TPU v7x, 32 devices: a whole 2x2x4 slice. The times are simulated.
32 devices in a mesh: copies: 2 (over x), tensor: 8 (over z, y), dp: 2 (over core).
Axes of the slice: x: 2, y: 2, z: 4, core: 2. Of those that a mesh axis runs over, the one named last changes fastest.
Arguments:
- activations: bfloat16 [32768, 28672], P(('copies', 'dp'), 'tensor'), parts along dimension 0, may hold values from -6 to 6
- out_grads: bfloat16 [32768, 8192], P(('copies', 'dp'), 'tensor'), parts along dimension 0, may hold values from -6 to 6
- proj_in: int32 [28672, 64], P('tensor'), may hold values from 0 to 1
- proj_out: int32 [8192, 64], P('tensor'), may hold values from 0 to 1
- segment_ids: int32 [4, 8192], P(('copies', 'dp')), parts along dimension 0, may hold values from 0 to 63, never falling along the last dimension, each value on 1 to 256 neighbouring positions
- queries: bfloat16 [1024, 4096], P(('copies', 'dp'), 'tensor'), parts along dimension 0, may hold values from -0.0078125 to 0.0078125
Outputs:
- scores: float32 [256, 512], P(('copies', 'dp')), parts along dimension 0
There are 2 independent parts, one for each index of `copies`. A program takes and returns all parts, laid end to end along the dimension named above; an argument that names none is the same for every part. Nothing has to cross between parts.
Inputs may be any that keep to these rules, and one draw needn't show every extreme that they name: `proj_in`: 0 or 1; the projection entry is 2 v - 1. `proj_out`: 0 or 1; the projection entry is 2 v - 1. `segment_ids`: in each row the ids never fall, every id 0 to 63 appears, each sequence has 1 to 256 tokens and one has exactly 256.
All inputs are finite; a program needn't handle non-finite values.
Results may differ from a plain program's by a relative error of at most 0.0052.
Values may be sent and summed in bfloat16 or wider, within the bound.
No kernel may reach another device: no remote copies, remote signals or barrier semaphores. Data moves between devices by JAX's collectives and lax.ppermute only.
A program may use at most 192 MiB of HBM per device.

v0:
```python
import math

import jax
import jax.numpy as jnp
from jax import lax
from jax.sharding import PartitionSpec as P

D = 8192
FF = 28672
SEQ_DEV = 64


def sketch_rows(seq_ids, seq_count, columns, proj_g):
    tok_count = seq_ids.shape[0]
    width_left = columns.shape[1]
    width_right = proj_g.shape[1]
    block = math.gcd(tok_count, 512)
    turns = tok_count // block
    seq_numbers = jnp.arange(seq_count, dtype=jnp.int32)
    ids_blocks = seq_ids.reshape(turns, block)
    left_blocks = columns.reshape(turns, block, width_left)
    right_blocks = proj_g.reshape(turns, block, width_right)

    def add_block(total, pieces):
        ids_part, left_part, right_part = pieces
        member = (ids_part[:, None] == seq_numbers[None, :]).astype(jnp.bfloat16)
        spread = (member[:, :, None] * left_part[:, None, :]).reshape(block, seq_count * width_left)
        term = lax.dot_general(
            spread, right_part, (((0,), (0,)), ((), ())), preferred_element_type=jnp.float32
        )
        return (total + term, None)

    start_total = jnp.zeros((seq_count * width_left, width_right), jnp.float32)
    total, unused = lax.scan(add_block, start_total, (ids_blocks, left_blocks, right_blocks))
    return total.reshape(seq_count, width_left * width_right).astype(jnp.bfloat16)


def body(activations, out_grads, proj_in, proj_out, segment_ids, queries):
    signs_in = (2 * proj_in - 1).astype(jnp.bfloat16)
    signs_out = (2 * proj_out - 1).astype(jnp.bfloat16)
    part_in = jnp.dot(activations, signs_in, preferred_element_type=jnp.float32)
    part_out = jnp.dot(out_grads, signs_out, preferred_element_type=jnp.float32)
    total_in, total_out = lax.psum((part_in, part_out), "tensor")
    proj_a = (total_in * FF ** (-0.5)).astype(jnp.bfloat16)
    proj_g = (total_out * D ** (-0.5)).astype(jnp.bfloat16)
    seq_ids = segment_ids[0]
    sketch = sketch_rows(seq_ids, SEQ_DEV, proj_a, proj_g)
    entries = lax.all_gather(queries, "tensor", axis=1, tiled=True)
    return lax.dot_general(
        sketch,
        lax.all_gather(entries, "dp", axis=0, tiled=True),
        (((1,), (1,)), ((), ())),
        preferred_element_type=jnp.float32,
    )


def solution(mesh):
    return jax.shard_map(
        body,
        mesh=mesh,
        in_specs=(
            P(("copies", "dp"), "tensor"),
            P(("copies", "dp"), "tensor"),
            P("tensor", None),
            P("tensor", None),
            P(("copies", "dp"), None),
            P(("copies", "dp"), "tensor"),
        ),
        out_specs=P(("copies", "dp"), None),
        check_vma=False,
    )
```

profile of v0, /device:TPU:0, one launch (start us, length us, event | category | flops | bytes accessed | tf_op | source)
XLA Modules:
  0.0 334.5 jit_solution(17459694957492993496)
XLA Ops:
  7.3 12.5 %convolution_bitcast_fusion.1 = f32[8192,64]{0,1:T(8,128)} fusion(bf16[8192,1024]{1,0:T(8,128)(2,1)} %param.9, s32[1024,64]{0,1:T(8,128)} %param.11), kind=kOutput, calls=%fused_computation.11 | convolution fusion | flops 1073938432 | bytes 19136512 | tf_op jit(solution)/shard_map/dot_general | solution.py:42
  19.8 25.8 %convolution_bitcast_fusion = f32[8192,64]{0,1:T(8,128)} fusion(bf16[8192,3584]{1,0:T(8,128)(2,1)} %param.8, s32[3584,64]{0,1:T(8,128)S(1)} %copy-done), kind=kOutput, calls=%fused_computation.10 | convolution fusion | flops 3758784512 | bytes 61734912 | tf_op jit(solution)/shard_map/dot_general | solution.py:41
  47.0 16.2 %all-gather.3.cloned.1.call-done = bf16[256,4096]{1,0:T(8,128)(2,1)} async-done(((bf16[256,512]{1,0:T(8,128)(2,1)}), bf16[256,4096]{1,0:T(8,128)(2,1)}) %all-gather.3.cloned.1.call-update) | async-done | bytes 2097168 | tf_op jit(solution)/shard_map/all_gather | solution.py:48
  63.2 158.6 %all-reduce.3.cloned.1.call-done = (f32[8192,64]{0,1:T(8,128)}, f32[8192,64]{0,1:T(8,128)}) async-done(((f32[8192,64]{0,1:T(8,128)}, f32[8192,64]{0,1:T(8,128)}), (f32[8192,64]{0,1:T(8,128)}, f32[8192,64]{0,1:T(8,128)})) %all-reduce.3.cloned.1.call-update) | async-done | bytes 4194320 | tf_op jit(solution)/shard_map/psum | solution.py:43
  221.8 2.6 multiply_convert_fusion
  226.4 96.0 %while.11 = (s32[]{:T(128)}, f32[4096,64]{0,1:T(8,128)S(1)}, s32[16,512]{1,0:T(8,128)S(1)}, bf16[16,512,64]{1,2,0:T(8,128)(2,1)S(1)}, bf16[16,512,64]{2,1,0:T(8,128)(2,1)}, /*index=5*/s32[]{:T(128)}, s32[]{:T(128)}) while((s32[]{:T(128)}, f32[4096,64]{0,1:T(8,128)S(1)}, s32[16,512]{1,0:T(8,128)S(1)}, ...), condition=%wide.region_3.4_spmd.clone, body=%wide.region_2.3_spmd.clone.sunk | while | flops 271122432 | bytes 10951263 | solution.py:34
  226.4 2.2 broadcast_multiply_fusion.2
  228.7 4.2 %convolution_add_fusion.2 = f32[4096,64]{0,1:T(8,128)S(1)} fusion(bf16[512,4096]{0,1:T(8,128)(2,1)} %bitcast.31, f32[4096,64]{0,1:T(8,128)S(1)} %get-tuple-element.121, pred[]{:T(512)S(6)} %compare.3, bf16[16,512,64]{2,1,0:T(8,128)(2,1)} %get-tuple-element.131, s32[]{:T(128)} %get-tuple-element.120), kind=kOutput, calls=%fused_computation.1.clone.1 | convolution fusion | flops 268959744 | bytes 6423041 | tf_op jit(solution)/shard_map/while/body/eval_jaxpr/dot_general | solution.py:28
  233.0 2.2 broadcast_multiply_fusion.2
  235.3 3.6 %convolution_add_fusion.2 = f32[4096,64]{0,1:T(8,128)S(1)} fusion(bf16[512,4096]{0,1:T(8,128)(2,1)} %bitcast.31, f32[4096,64]{0,1:T(8,128)S(1)} %get-tuple-element.121, pred[]{:T(512)S(6)} %compare.3, bf16[16,512,64]{2,1,0:T(8,128)(2,1)} %get-tuple-element.131, s32[]{:T(128)} %get-tuple-element.120), kind=kOutput, calls=%fused_computation.1.clone.1 | convolution fusion | flops 268959744 | bytes 6423041 | tf_op jit(solution)/shard_map/while/body/eval_jaxpr/dot_general | solution.py:28
  239.0 2.2 broadcast_multiply_fusion.2
  241.2 3.6 %convolution_add_fusion.2 = f32[4096,64]{0,1:T(8,128)S(1)} fusion(bf16[512,4096]{0,1:T(8,128)(2,1)} %bitcast.31, f32[4096,64]{0,1:T(8,128)S(1)} %get-tuple-element.121, pred[]{:T(512)S(6)} %compare.3, bf16[16,512,64]{2,1,0:T(8,128)(2,1)} %get-tuple-element.131, s32[]{:T(128)} %get-tuple-element.120), kind=kOutput, calls=%fused_computation.1.clone.1 | convolution fusion | flops 268959744 | bytes 6423041 | tf_op jit(solution)/shard_map/while/body/eval_jaxpr/dot_general | solution.py:28
  244.9 2.2 broadcast_multiply_fusion.2
  247.2 3.6 %convolution_add_fusion.2 = f32[4096,64]{0,1:T(8,128)S(1)} fusion(bf16[512,4096]{0,1:T(8,128)(2,1)} %bitcast.31, f32[4096,64]{0,1:T(8,128)S(1)} %get-tuple-element.121, pred[]{:T(512)S(6)} %compare.3, bf16[16,512,64]{2,1,0:T(8,128)(2,1)} %get-tuple-element.131, s32[]{:T(128)} %get-tuple-element.120), kind=kOutput, calls=%fused_computation.1.clone.1 | convolution fusion | flops 268959744 | bytes 6423041 | tf_op jit(solution)/shard_map/while/body/eval_jaxpr/dot_general | solution.py:28
  250.9 2.2 broadcast_multiply_fusion.2
  253.1 3.6 %convolution_add_fusion.2 = f32[4096,64]{0,1:T(8,128)S(1)} fusion(bf16[512,4096]{0,1:T(8,128)(2,1)} %bitcast.31, f32[4096,64]{0,1:T(8,128)S(1)} %get-tuple-element.121, pred[]{:T(512)S(6)} %compare.3, bf16[16,512,64]{2,1,0:T(8,128)(2,1)} %get-tuple-element.131, s32[]{:T(128)} %get-tuple-element.120), kind=kOutput, calls=%fused_computation.1.clone.1 | convolution fusion | flops 268959744 | bytes 6423041 | tf_op jit(solution)/shard_map/while/body/eval_jaxpr/dot_general | solution.py:28
  256.9 2.2 broadcast_multiply_fusion.2
  259.1 3.6 %convolution_add_fusion.2 = f32[4096,64]{0,1:T(8,128)S(1)} fusion(bf16[512,4096]{0,1:T(8,128)(2,1)} %bitcast.31, f32[4096,64]{0,1:T(8,128)S(1)} %get-tuple-element.121, pred[]{:T(512)S(6)} %compare.3, bf16[16,512,64]{2,1,0:T(8,128)(2,1)} %get-tuple-element.131, s32[]{:T(128)} %get-tuple-element.120), kind=kOutput, calls=%fused_computation.1.clone.1 | convolution fusion | flops 268959744 | bytes 6423041 | tf_op jit(solution)/shard_map/while/body/eval_jaxpr/dot_general | solution.py:28
  262.8 2.2 broadcast_multiply_fusion.2
  265.1 3.6 %convolution_add_fusion.2 = f32[4096,64]{0,1:T(8,128)S(1)} fusion(bf16[512,4096]{0,1:T(8,128)(2,1)} %bitcast.31, f32[4096,64]{0,1:T(8,128)S(1)} %get-tuple-element.121, pred[]{:T(512)S(6)} %compare.3, bf16[16,512,64]{2,1,0:T(8,128)(2,1)} %get-tuple-element.131, s32[]{:T(128)} %get-tuple-element.120), kind=kOutput, calls=%fused_computation.1.clone.1 | convolution fusion | flops 268959744 | bytes 6423041 | tf_op jit(solution)/shard_map/while/body/eval_jaxpr/dot_general | solution.py:28
  268.8 2.2 broadcast_multiply_fusion.2
  271.0 3.6 %convolution_add_fusion.2 = f32[4096,64]{0,1:T(8,128)S(1)} fusion(bf16[512,4096]{0,1:T(8,128)(2,1)} %bitcast.31, f32[4096,64]{0,1:T(8,128)S(1)} %get-tuple-element.121, pred[]{:T(512)S(6)} %compare.3, bf16[16,512,64]{2,1,0:T(8,128)(2,1)} %get-tuple-element.131, s32[]{:T(128)} %get-tuple-element.120), kind=kOutput, calls=%fused_computation.1.clone.1 | convolution fusion | flops 268959744 | bytes 6423041 | tf_op jit(solution)/shard_map/while/body/eval_jaxpr/dot_general | solution.py:28
  274.7 2.2 broadcast_multiply_fusion.2
  277.0 3.6 %convolution_add_fusion.2 = f32[4096,64]{0,1:T(8,128)S(1)} fusion(bf16[512,4096]{0,1:T(8,128)(2,1)} %bitcast.31, f32[4096,64]{0,1:T(8,128)S(1)} %get-tuple-element.121, pred[]{:T(512)S(6)} %compare.3, bf16[16,512,64]{2,1,0:T(8,128)(2,1)} %get-tuple-element.131, s32[]{:T(128)} %get-tuple-element.120), kind=kOutput, calls=%fused_computation.1.clone.1 | convolution fusion | flops 268959744 | bytes 6423041 | tf_op jit(solution)/shard_map/while/body/eval_jaxpr/dot_general | solution.py:28
  283.0 3.6 %convolution_add_fusion.2 = f32[4096,64]{0,1:T(8,128)S(1)} fusion(bf16[512,4096]{0,1:T(8,128)(2,1)} %bitcast.31, f32[4096,64]{0,1:T(8,128)S(1)} %get-tuple-element.121, pred[]{:T(512)S(6)} %compare.3, bf16[16,512,64]{2,1,0:T(8,128)(2,1)} %get-tuple-element.131, s32[]{:T(128)} %get-tuple-element.120), kind=kOutput, calls=%fused_computation.1.clone.1 | convolution fusion | flops 268959744 | bytes 6423041 | tf_op jit(solution)/shard_map/while/body/eval_jaxpr/dot_general | solution.py:28
  288.9 3.6 %convolution_add_fusion.2 = f32[4096,64]{0,1:T(8,128)S(1)} fusion(bf16[512,4096]{0,1:T(8,128)(2,1)} %bitcast.31, f32[4096,64]{0,1:T(8,128)S(1)} %get-tuple-element.121, pred[]{:T(512)S(6)} %compare.3, bf16[16,512,64]{2,1,0:T(8,128)(2,1)} %get-tuple-element.131, s32[]{:T(128)} %get-tuple-element.120), kind=kOutput, calls=%fused_computation.1.clone.1 | convolution fusion | flops 268959744 | bytes 6423041 | tf_op jit(solution)/shard_map/while/body/eval_jaxpr/dot_general | solution.py:28
  294.9 3.6 %convolution_add_fusion.2 = f32[4096,64]{0,1:T(8,128)S(1)} fusion(bf16[512,4096]{0,1:T(8,128)(2,1)} %bitcast.31, f32[4096,64]{0,1:T(8,128)S(1)} %get-tuple-element.121, pred[]{:T(512)S(6)} %compare.3, bf16[16,512,64]{2,1,0:T(8,128)(2,1)} %get-tuple-element.131, s32[]{:T(128)} %get-tuple-element.120), kind=kOutput, calls=%fused_computation.1.clone.1 | convolution fusion | flops 268959744 | bytes 6423041 | tf_op jit(solution)/shard_map/while/body/eval_jaxpr/dot_general | solution.py:28
  300.8 3.6 %convolution_add_fusion.2 = f32[4096,64]{0,1:T(8,128)S(1)} fusion(bf16[512,4096]{0,1:T(8,128)(2,1)} %bitcast.31, f32[4096,64]{0,1:T(8,128)S(1)} %get-tuple-element.121, pred[]{:T(512)S(6)} %compare.3, bf16[16,512,64]{2,1,0:T(8,128)(2,1)} %get-tuple-element.131, s32[]{:T(128)} %get-tuple-element.120), kind=kOutput, calls=%fused_computation.1.clone.1 | convolution fusion | flops 268959744 | bytes 6423041 | tf_op jit(solution)/shard_map/while/body/eval_jaxpr/dot_general | solution.py:28
  306.8 3.6 %convolution_add_fusion.2 = f32[4096,64]{0,1:T(8,128)S(1)} fusion(bf16[512,4096]{0,1:T(8,128)(2,1)} %bitcast.31, f32[4096,64]{0,1:T(8,128)S(1)} %get-tuple-element.121, pred[]{:T(512)S(6)} %compare.3, bf16[16,512,64]{2,1,0:T(8,128)(2,1)} %get-tuple-element.131, s32[]{:T(128)} %get-tuple-element.120), kind=kOutput, calls=%fused_computation.1.clone.1 | convolution fusion | flops 268959744 | bytes 6423041 | tf_op jit(solution)/shard_map/while/body/eval_jaxpr/dot_general | solution.py:28
  312.8 3.6 %convolution_add_fusion.2 = f32[4096,64]{0,1:T(8,128)S(1)} fusion(bf16[512,4096]{0,1:T(8,128)(2,1)} %bitcast.31, f32[4096,64]{0,1:T(8,128)S(1)} %get-tuple-element.121, pred[]{:T(512)S(6)} %compare.3, bf16[16,512,64]{2,1,0:T(8,128)(2,1)} %get-tuple-element.131, s32[]{:T(128)} %get-tuple-element.120), kind=kOutput, calls=%fused_computation.1.clone.1 | convolution fusion | flops 268959744 | bytes 6423041 | tf_op jit(solution)/shard_map/while/body/eval_jaxpr/dot_general | solution.py:28
  318.7 3.6 %convolution_add_fusion.2 = f32[4096,64]{0,1:T(8,128)S(1)} fusion(bf16[512,4096]{0,1:T(8,128)(2,1)} %bitcast.31, f32[4096,64]{0,1:T(8,128)S(1)} %get-tuple-element.121, pred[]{:T(512)S(6)} %compare.3, bf16[16,512,64]{2,1,0:T(8,128)(2,1)} %get-tuple-element.131, s32[]{:T(128)} %get-tuple-element.120), kind=kOutput, calls=%fused_computation.1.clone.1 | convolution fusion | flops 268959744 | bytes 6423041 | tf_op jit(solution)/shard_map/while/body/eval_jaxpr/dot_general | solution.py:28
  323.8 4.2 %fusion.14 = f32[64,512]{1,0:T(8,128)} fusion(bf16[64,4096]{1,0:T(8,128)(2,1)S(1)} %convert_element_type.30, bf16[512,4096]{1,0:T(8,128)(2,1)} %all-gather.5.cloned.1.call-done), kind=kOutput, calls=%fused_computation.25 | convolution fusion | flops 268435456 | bytes 4849664 | tf_op jit(solution)/shard_map/dot_general | solution.py:49
  (75 shorter events, 21.9 us)
Async XLA Ops:
  6.5 56.7 %all-gather.3.cloned.1.call-start = ((), (), s32[]{:S(2)}) async-start(), calls=%async_computation | async-start | bytes 2359296 | tf_op jit(solution)/shard_map/all_gather | solution.py:48
  7.3 12.5 %copy-start = (s32[3584,64]{0,1:T(8,128)S(1)}, s32[3584,64]{0,1:T(8,128)}, u32[]{:S(2)}) copy-start(s32[3584,64]{0,1:T(8,128)} %param.10) | copy-start | bytes 2752516
  7.3 214.6 %all-reduce.3.cloned.1.call-start = ((), (), s32[]{:S(2)}) async-start(), calls=%async_computation.2 | async-start | bytes 8388608 | tf_op jit(solution)/shard_map/psum | solution.py:43
  45.6 0.8 copy-start.1
  45.6 278.2 %all-gather.5.cloned.1.call-start = ((), (), s32[]{:S(2)}) async-start(), calls=%async_computation.1 | async-start | bytes 6291456 | tf_op jit(solution)/shard_map/all_gather | solution.py:51
Sparse Core Ops, SparseCore 0:
  9.4 53.7 all-gather.2
  66.9 154.8 all-reduce.2
  223.4 12.6 all-gather.4
where the time goes:
time: 335 us
  waiting for transfers between devices  176 us (53%)
  matrix products  101 us (30%)
  other arithmetic  39.6 us (12%)
  between operations  13.2 us (4%)
  local copies, waits for them, and re-layouts  4.26 us (1%)
    psum x1, waiting for transfers between devices, body(): total_in, total_out = lax.psum((part_in, part_out), 'tensor')  159 us
    dot_general x16, matrix products, add_block(): lax.dot_general(spread, right_part, (((0,), (0,)), ((), ())), preferred_e...  58.6 us
    mul x16, other arithmetic, add_block(): member[:, :, None] * left_part[:, None, :]  36 us
    dot_general x1, matrix products, body(): part_in = jnp.dot(activations, signs_in, preferred_element_type=jnp.float32)  25.8 us
    all_gather x1, waiting for transfers between devices, body(): entries = lax.all_gather(queries, 'tensor', axis=1, tiled=True)  16.2 us
    dot_general x1, matrix products, body(): part_out = jnp.dot(out_grads, signs_out, preferred_element_type=jnp.float32)  12.5 us
  transfers between devices with their start and end apart: 3, of which 2 were waited for; matrix products, arithmetic and copies ran while one was open for 42% of the time, Pallas kernels for 0%

commit v1 on v0

v1 whole, which is shorter than its diff:
```python
import functools

import jax
import jax.numpy as jnp
from jax import lax
from jax.experimental import pallas as pl
from jax.experimental.pallas import tpu as pltpu
from jax.sharding import PartitionSpec as P

D = 8192
FF = 28672
R = 64
SEQ_DEV = 64
CHUNKS = 4
VMEM = 56 * 1024 * 1024


def project_kernel(quarters, half_ref, act_ref, grad_ref, sin_ref, sout_ref, sent_ref, kept_ref):
    step = pl.program_id(0)
    part_a = jnp.dot(act_ref[...], sin_ref[...], preferred_element_type=jnp.float32)
    part_g = jnp.dot(grad_ref[...], sout_ref[...], preferred_element_type=jnp.float32)
    part_a = (part_a * FF ** -0.5).T
    part_g = (part_g * D ** -0.5).T

    @pl.when(step < quarters)
    def _():
        sent_ref[0, :R, :] = part_a.astype(jnp.bfloat16)
        sent_ref[0, R:, :] = part_g.astype(jnp.bfloat16)

    @pl.when(step >= quarters)
    def _():
        kept_ref[0, :R, :] = part_a
        kept_ref[0, R:, :] = part_g


def project(chunk, quarters, half, activations, out_grads, signs_in, signs_out):
    tokens, width_in = activations.shape
    width_out = out_grads.shape[1]
    steps = 2 * quarters
    tile = tokens // (CHUNKS * steps)

    def rows(s, half_ref):
        mine = (s >= quarters).astype(jnp.int32)
        side = half_ref[0] * mine + (1 - half_ref[0]) * (1 - mine)
        return (chunk * steps + side * quarters + s - mine * quarters, 0)

    fixed = lambda s, half_ref: (0, 0)
    return pl.pallas_call(
        functools.partial(project_kernel, quarters),
        grid_spec=pltpu.PrefetchScalarGridSpec(
            num_scalar_prefetch=1,
            grid=(steps,),
            in_specs=[
                pl.BlockSpec((tile, width_in), rows),
                pl.BlockSpec((tile, width_out), rows),
                pl.BlockSpec((width_in, R), fixed),
                pl.BlockSpec((width_out, R), fixed),
            ],
            out_specs=[
                pl.BlockSpec((1, 2 * R, tile), lambda s, half_ref: (jnp.minimum(s, quarters - 1), 0, 0)),
                pl.BlockSpec((1, 2 * R, tile), lambda s, half_ref: (jnp.maximum(s - quarters, 0), 0, 0)),
            ],
        ),
        out_shape=[
            jax.ShapeDtypeStruct((quarters, 2 * R, tile), jnp.bfloat16),
            jax.ShapeDtypeStruct((quarters, 2 * R, tile), jnp.float32),
        ],
        compiler_params=pltpu.CompilerParams(vmem_limit_bytes=VMEM),
        cost_estimate=pl.CostEstimate(
            flops=2 * tile * steps * (width_in + width_out) * R,
            bytes_accessed=2 * tile * steps * (width_in + width_out),
            transcendentals=0,
        ),
        name="project",
    )(half, activations, out_grads, signs_in, signs_out)


def sketch_kernel(per_dest, ids_ref, *refs):
    piece_refs, out_ref, proj_ref, spread_ref = refs[:-3], refs[-3], refs[-2], refs[-1]
    dest = pl.program_id(0)
    tile = piece_refs[0].shape[-1]

    @pl.when(dest == 0)
    def _():
        for c, piece_ref in enumerate(piece_refs):
            proj_ref[:, c * tile:(c + 1) * tile] = jnp.sum(piece_ref[...].astype(jnp.float32), axis=0)

    for r in range(per_dest):
        row = proj_ref[pl.ds(dest * per_dest + r, 1), :]
        spread_ref[r * R:(r + 1) * R, :] = (row * proj_ref[R:, :]).astype(jnp.bfloat16)
    numbers = lax.broadcasted_iota(jnp.int32, (SEQ_DEV, 1), 0)
    member = (ids_ref[...] == numbers).astype(jnp.bfloat16)
    part = lax.dot_general(
        spread_ref[...], member, (((1,), (1,)), ((), ())), preferred_element_type=jnp.float32
    )
    out_ref[0] = part.T.astype(jnp.bfloat16)


def sketch(ids, pieces, dests):
    per_dest = R // dests
    sources, both, tile = pieces[0].shape
    owned = tile * len(pieces)
    return pl.pallas_call(
        functools.partial(sketch_kernel, per_dest),
        grid=(dests,),
        in_specs=[pl.BlockSpec((1, owned), lambda s: (0, 0))]
        + [pl.BlockSpec((sources, both, tile), lambda s: (0, 0, 0))] * len(pieces),
        out_specs=pl.BlockSpec((1, SEQ_DEV, per_dest * R), lambda s: (s, 0, 0)),
        out_shape=jax.ShapeDtypeStruct((dests, SEQ_DEV, per_dest * R), jnp.bfloat16),
        scratch_shapes=[
            pltpu.VMEM((both, owned), jnp.float32),
            pltpu.VMEM((per_dest * R, owned), jnp.bfloat16),
        ],
        compiler_params=pltpu.CompilerParams(vmem_limit_bytes=VMEM),
        name="sketch",
    )(ids, *pieces)


def body(n_tensor, activations, out_grads, proj_in, proj_out, segment_ids, queries):
    halves = 2
    quarters = n_tensor // halves
    me = lax.axis_index("tensor")
    swap = [(k, k + 1 - 2 * (k % 2)) for k in range(n_tensor)]
    half = (me % halves).reshape(1)
    by_quarter = [[q * halves + h for q in range(quarters)] for h in range(halves)]

    signs_in = (2 * proj_in - 1).astype(jnp.bfloat16)
    signs_out = (2 * proj_out - 1).astype(jnp.bfloat16)

    other = lax.ppermute(queries, "dp", [(0, 1), (1, 0)])
    first = lax.axis_index("dp") == 0
    queries_0 = jnp.where(first, queries, other)
    queries_1 = jnp.where(first, other, queries)
    all_queries = jnp.concatenate([queries_0, queries_1], axis=0)

    pieces = []
    for c in range(CHUNKS):
        sent, kept = project(c, quarters, half, activations, out_grads, signs_in, signs_out)
        pair = (kept + lax.ppermute(sent, "tensor", swap)).astype(jnp.bfloat16)
        pieces.append(lax.all_to_all(pair, "tensor", 0, 0, axis_index_groups=by_quarter))

    tile = pieces[0].shape[-1]
    ids = segment_ids.reshape(CHUNKS, halves, quarters, tile)
    ids = lax.dynamic_slice(ids, (0, me % halves, me // halves, 0), (CHUNKS, 1, 1, tile)).reshape(1, CHUNKS * tile)
    parts = sketch(ids, pieces, n_tensor)
    entries = jnp.sum(lax.all_to_all(parts, "tensor", 0, 0).astype(jnp.float32), axis=0)
    rounded = lax.reduce_precision(entries, 8, 7)
    high = rounded.astype(jnp.bfloat16)
    low = (entries - rounded).astype(jnp.bfloat16)
    along = (((1,), (1,)), ((), ()))
    scores = lax.dot_general(high, all_queries, along, preferred_element_type=jnp.float32)
    scores = scores + lax.dot_general(low, all_queries, along, preferred_element_type=jnp.float32)
    split = scores.reshape(n_tensor, SEQ_DEV // n_tensor, scores.shape[1])
    mine = jnp.sum(lax.all_to_all(split, "tensor", 0, 0), axis=0)
    spread = jnp.broadcast_to(mine[None], split.shape)
    return lax.all_to_all(spread, "tensor", 0, 0).reshape(scores.shape)


def solution(mesh):
    return jax.shard_map(
        functools.partial(body, mesh.shape["tensor"]),
        mesh=mesh,
        in_specs=(
            P(("copies", "dp"), "tensor"),
            P(("copies", "dp"), "tensor"),
            P("tensor", None),
            P("tensor", None),
            P(("copies", "dp"), None),
            P(("copies", "dp"), "tensor"),
        ),
        out_specs=P(("copies", "dp"), None),
        check_vma=False,
    )
```

time: 335 us -> 139 us (0.41)
  waiting for transfers between devices: 176 us -> 21.1 us
  matrix products: 101 us -> 0.57 us
  Pallas kernels: 0 us -> 55.5 us
  other arithmetic: 39.6 us -> 5.9 us
  starting transfers between devices: 0.08 us -> 28.5 us
  blocking collectives: 0 us -> 21.2 us
  between operations: 13.2 us -> 0.13 us
    psum x1 -> x0, waiting for transfers between devices: 159 us -> none  [body(): total_in, total_out = lax.psum((part_in, part_out), 'tensor')]
    dot_general x19 -> x2, matrix products: 101 us -> 0.57 us  [the longest x1 0.3 us: body(): lax.dot_general(high, all_queries, along, preferred_element_type=jnp.floa...]
    pallas_call x0 -> x5, Pallas kernels: none -> 55.5 us  [the longest x4 49.1 us: project(): pl.pallas_call(functools.partial(project_kernel, quarters), grid_spec=plt...]
    mul x16 -> x0, other arithmetic: 36 us -> none  [add_block(): member[:, :, None] * left_part[:, None, :]]
    all_to_all x0 -> x5, starting transfers between devices: none -> 23.3 us  [the longest x4 18.9 us: body(): lax.all_to_all(pair, 'tensor', 0, 0, axis_index_groups=by_quarter)]
    all_to_all x0 -> x2, blocking collectives: none -> 21.2 us  [the longest x1 10.8 us: body(): mine = jnp.sum(lax.all_to_all(split, 'tensor', 0, 0), axis=0)]
    all_to_all x0 -> x5, waiting for transfers between devices: none -> 19.3 us  [the longest x4 10.7 us: body(): lax.all_to_all(pair, 'tensor', 0, 0, axis_index_groups=by_quarter)]
    all_gather x2 -> x0, waiting for transfers between devices: 16.2 us -> none  [the longest x1 16.2 us: body(): entries = lax.all_gather(queries, 'tensor', axis=1, tiled=True)]
  transfers between devices with their start and end apart: 3 -> 10, of which waited for: 2 -> 5; matrix products, arithmetic and copies ran while one was open for 42% -> 4% of each run, Pallas kernels for 0% -> 27%
where the time goes in v1:
time: 139 us; the launch traced here: 137 us
  Pallas kernels  55.5 us (40%)
  starting transfers between devices  28.5 us (21%)
  blocking collectives  21.2 us (15%)
  waiting for transfers between devices  21.1 us (15%)
  other arithmetic  5.9 us (4%)
  local copies, waits for them, and re-layouts  4.45 us (3%)
    pallas_call x4, Pallas kernels, project(): pl.pallas_call(functools.partial(project_kernel, quarters), grid_spec=plt...  49.1 us
    all_to_all x4, starting transfers between devices, body(): lax.all_to_all(pair, 'tensor', 0, 0, axis_index_groups=by_quarter)  18.9 us
    all_to_all x1, blocking collectives, body(): mine = jnp.sum(lax.all_to_all(split, 'tensor', 0, 0), axis=0)  10.8 us
    all_to_all x4, waiting for transfers between devices, body(): lax.all_to_all(pair, 'tensor', 0, 0, axis_index_groups=by_quarter)  10.7 us
    all_to_all x1, blocking collectives, body(): return lax.all_to_all(spread, 'tensor', 0, 0).reshape(scores.shape)  10.4 us
    all_to_all x1, waiting for transfers between devices, body(): lax.all_to_all(parts, 'tensor', 0, 0).astype(jnp.float32)  8.63 us
    pallas_call x1, Pallas kernels, sketch(): pl.pallas_call(functools.partial(sketch_kernel, per_dest), grid=(dests,),...  6.35 us
    ppermute x4, starting transfers between devices, body(): pair = (kept + lax.ppermute(sent, 'tensor', swap)).astype(jnp.bfloat16)  5.19 us
  transfers between devices with their start and end apart: 10, of which 5 were waited for; matrix products, arithmetic and copies ran while one was open for 4% of the time, Pallas kernels for 27%

profile of v1, /device:TPU:0, one launch (start us, length us, event | category | flops | bytes accessed | tf_op | source)
XLA Modules:
  0.0 137.3 jit_solution(11926253289764875390)
XLA Ops:
  0.0 1.7 %copy.8 = s32[3584,64]{1,0:T(8,128)S(1)} copy(s32[3584,64]{0,1:T(8,128)} %param.8) | data formatting | bytes 1835008 | tf_op args[2]
  1.7 1.2 add_convert_fusion.sin_ref
  3.1 0.8 add_convert_fusion.5.sout_ref
  3.9 12.2 %project.7 = (bf16[4,128,256]{2,1,0:T(8,128)(2,1)}, f32[4,128,256]{2,1,0:T(8,128)}) custom-call(s32[1]{0:T(128)} %bitcast.half_ref, bf16[8192,3584]{1,0:T(8,128)(2,1)} %act_ref.7, bf16[8192,1024]{1,0:T(8,128)(2,1)} %grad_ref.7, bf16[3584,64]{1,0:T(8,128)(2,1)} %add_convert_fusion.sin_ref, bf16[1024,64]{1,0:T(8,128)(2,1)} %add_convert_fusion.5.sout_ref), custom_call_target="tpu_custom_call" | custom-call | flops 1207959552 | bytes 18874368 | tf_op jit(solution)/shard_map/project/pallas_call | solution.py:48
  16.2 3.0 %collective-permute-start.3 = (bf16[4,128,256]{2,1,0:T(8,128)(2,1)}, bf16[4,128,256]{2,1,0:T(8,128)(2,1)S(1)}, u32[]{:S(2)}, u32[]{:S(2)}) collective-permute-start(bf16[4,128,256]{2,1,0:T(8,128)(2,1)} %get-tuple-element.20), channel_id=1, source_target_pairs={{0,2},{2,0},{4,6},{6,4},{8,10},{10,8},{12,14},{14,12},{1,3},{3,1},... | collective-permute-start | bytes 786440 | tf_op jit(solution)/shard_map/ppermute | solution.py:139
  19.2 12.2 %project.6 = (bf16[4,128,256]{2,1,0:T(8,128)(2,1)}, f32[4,128,256]{2,1,0:T(8,128)}) custom-call(s32[1]{0:T(128)} %bitcast.half_ref, bf16[8192,3584]{1,0:T(8,128)(2,1)} %act_ref.7, bf16[8192,1024]{1,0:T(8,128)(2,1)} %grad_ref.7, bf16[3584,64]{1,0:T(8,128)(2,1)} %add_convert_fusion.sin_ref, bf16[1024,64]{1,0:T(8,128)(2,1)} %add_convert_fusion.5.sout_ref), custom_call_target="tpu_custom_call" | custom-call | flops 1207959552 | bytes 18874368 | tf_op jit(solution)/shard_map/project/pallas_call | solution.py:48
  31.5 0.8 add_convert_fusion.1
  32.3 5.3 %all-to-all-start.3 = ((bf16[4,128,256]{2,1,0:T(8,128)(2,1)}), bf16[4,128,256]{2,1,0:T(8,128)(2,1)S(1)}, u32[]{:S(2)}, u32[]{:S(2)}) async-start(bf16[4,128,256]{2,1,0:T(8,128)(2,1)} %add_convert_fusion.1), calls=%async_computation.3 | async-start | bytes 524288 | tf_op jit(solution)/shard_map/all_to_all | solution.py:140
  37.5 12.3 %project.5 = (bf16[4,128,256]{2,1,0:T(8,128)(2,1)}, f32[4,128,256]{2,1,0:T(8,128)}) custom-call(s32[1]{0:T(128)} %bitcast.half_ref, bf16[8192,3584]{1,0:T(8,128)(2,1)} %act_ref.7, bf16[8192,1024]{1,0:T(8,128)(2,1)} %grad_ref.7, bf16[3584,64]{1,0:T(8,128)(2,1)} %add_convert_fusion.sin_ref, bf16[1024,64]{1,0:T(8,128)(2,1)} %add_convert_fusion.5.sout_ref), custom_call_target="tpu_custom_call" | custom-call | flops 1207959552 | bytes 18874368 | tf_op jit(solution)/shard_map/project/pallas_call | solution.py:48
  49.9 1.5 %collective-permute-start.1 = (bf16[4,128,256]{2,1,0:T(8,128)(2,1)}, bf16[4,128,256]{2,1,0:T(8,128)(2,1)S(1)}, u32[]{:S(2)}, u32[]{:S(2)}) collective-permute-start(bf16[4,128,256]{2,1,0:T(8,128)(2,1)} %get-tuple-element.16), channel_id=1, source_target_pairs={{0,2},{2,0},{4,6},{6,4},{8,10},{10,8},{12,14},{14,12},{1,3},{3,1},... | collective-permute-start | bytes 786440 | tf_op jit(solution)/shard_map/ppermute | solution.py:139
  51.4 0.8 add_convert_fusion.2
  52.2 5.1 %all-to-all-start.2 = ((bf16[4,128,256]{2,1,0:T(8,128)(2,1)}), bf16[4,128,256]{2,1,0:T(8,128)(2,1)S(1)}, u32[]{:S(2)}, u32[]{:S(2)}) async-start(bf16[4,128,256]{2,1,0:T(8,128)(2,1)} %add_convert_fusion.2), calls=%async_computation.2 | async-start | bytes 524288 | tf_op jit(solution)/shard_map/all_to_all | solution.py:140
  57.3 12.3 %project.4 = (bf16[4,128,256]{2,1,0:T(8,128)(2,1)}, f32[4,128,256]{2,1,0:T(8,128)}) custom-call(s32[1]{0:T(128)} %bitcast.half_ref, bf16[8192,3584]{1,0:T(8,128)(2,1)} %act_ref.7, bf16[8192,1024]{1,0:T(8,128)(2,1)} %grad_ref.7, bf16[3584,64]{1,0:T(8,128)(2,1)} %add_convert_fusion.sin_ref, bf16[1024,64]{1,0:T(8,128)(2,1)} %add_convert_fusion.5.sout_ref), custom_call_target="tpu_custom_call" | custom-call | flops 1207959552 | bytes 18874368 | tf_op jit(solution)/shard_map/project/pallas_call | solution.py:48
  69.6 0.6 collective-permute-start
  70.2 0.8 add_convert_fusion.3
  71.0 5.1 %all-to-all-start.1 = ((bf16[4,128,256]{2,1,0:T(8,128)(2,1)}), bf16[4,128,256]{2,1,0:T(8,128)(2,1)S(1)}, u32[]{:S(2)}, u32[]{:S(2)}) async-start(bf16[4,128,256]{2,1,0:T(8,128)(2,1)} %add_convert_fusion.3), calls=%async_computation.1 | async-start | bytes 524288 | tf_op jit(solution)/shard_map/all_to_all | solution.py:140
  76.3 0.8 add_convert_fusion.4
  77.0 5.8 %all-to-all-done.1.refs_1_ = bf16[4,128,256]{2,1,0:T(8,128)(2,1)S(1)} async-done(((bf16[4,128,256]{2,1,0:T(8,128)(2,1)}), bf16[4,128,256]{2,1,0:T(8,128)(2,1)S(1)}, u32[]{:S(2)}, u32[]{:S(2)}) %all-to-all-start.1) | async-done | bytes 262176 | tf_op jit(solution)/shard_map/all_to_all | solution.py:140
  82.8 3.4 %all-to-all-start = ((bf16[4,128,256]{2,1,0:T(8,128)(2,1)}), bf16[4,128,256]{2,1,0:T(8,128)(2,1)S(1)}, u32[]{:S(2)}, u32[]{:S(2)}) async-start(bf16[4,128,256]{2,1,0:T(8,128)(2,1)} %add_convert_fusion.4), calls=%async_computation | async-start | bytes 524288 | tf_op jit(solution)/shard_map/all_to_all | solution.py:140
  86.3 0.5 broadcast.16
  86.8 0.7 reduce.3
  87.5 0.6 constant_dynamic-slice_fusion
  88.1 4.9 %all-to-all-done.refs_0_ = bf16[4,128,256]{2,1,0:T(8,128)(2,1)S(1)} async-done(((bf16[4,128,256]{2,1,0:T(8,128)(2,1)}), bf16[4,128,256]{2,1,0:T(8,128)(2,1)S(1)}, u32[]{:S(2)}, u32[]{:S(2)}) %all-to-all-start) | async-done | bytes 262176 | tf_op jit(solution)/shard_map/all_to_all | solution.py:140
  93.0 0.7 copy-done.3
  93.7 6.4 %sketch.1 = bf16[8,64,512]{2,1,0:T(8,128)(2,1)} custom-call(s32[1,1024]{1,0:T(1,128)} %bitcast.6, bf16[4,128,256]{2,1,0:T(8,128)(2,1)} %copy-done.3, bf16[4,128,256]{2,1,0:T(8,128)(2,1)} %copy-done.2, bf16[4,128,256]{2,1,0:T(8,128)(2,1)} %copy-done.1, bf16[4,128,256]{2,1,0:T(8,128)(2,1)} %copy-done), custom_call_target="tpu_custom_call" | custom-call | tf_op jit(solution)/shard_map/sketch/pallas_call | solution.py:103
  100.1 4.4 %all-to-all-start.4 = ((bf16[8,64,512]{2,1,0:T(8,128)(2,1)}), bf16[8,64,512]{2,1,0:T(8,128)(2,1)S(1)}, u32[]{:S(2)}, u32[]{:S(2)}) async-start(bf16[8,64,512]{2,1,0:T(8,128)(2,1)} %sketch.1), calls=%async_computation.4 | async-start | bytes 1048576 | tf_op jit(solution)/shard_map/all_to_all | solution.py:146
  104.6 1.5 %collective-permute-done.4 = bf16[256,512]{1,0:T(8,128)(2,1)S(1)} collective-permute-done((bf16[256,512]{1,0:T(8,128)(2,1)S(1)}, bf16[256,512]{1,0:T(8,128)(2,1)S(1)}, u32[]{:S(2)}, u32[]{:S(2)}) %collective-permute-start.4) | collective-permute-done | bytes 262176 | tf_op jit(solution)/shard_map/ppermute | solution.py:130
  106.1 8.6 %all-to-all-done.4 = bf16[8,64,512]{2,1,0:T(8,128)(2,1)S(1)} async-done(((bf16[8,64,512]{2,1,0:T(8,128)(2,1)}), bf16[8,64,512]{2,1,0:T(8,128)(2,1)S(1)}, u32[]{:S(2)}, u32[]{:S(2)}) %all-to-all-start.4) | async-done | bytes 524320 | tf_op jit(solution)/shard_map/all_to_all | solution.py:146
  115.1 0.3 fusion
  115.4 10.8 %all_to_all.35 = f32[8,8,512]{2,1,0:T(8,128)S(1)} all-to-all(f32[8,8,512]{2,1,0:T(8,128)S(1)} %fusion), channel_id=1, replica_groups=mesh['copies'=2,'tensor'=8,'dp'=2] {'tensor'}, dimensions={0} | all-to-all | bytes 262144 | tf_op jit(solution)/shard_map/all_to_all | solution.py:154
  126.3 10.4 %all_to_all.36 = f32[8,8,512]{2,1,0:T(8,128)S(1)} all-to-all(f32[8,8,512]{2,1,0:T(8,128)S(1)} %broadcast_in_dim.2), channel_id=1, replica_groups=mesh['copies'=2,'tensor'=8,'dp'=2] {'tensor'}, dimensions={0} | all-to-all | bytes 262144 | tf_op jit(solution)/shard_map/all_to_all | solution.py:156
  136.7 0.7 copy.12
  (36 shorter events, 1.1 us)
Async XLA Ops:
  1.7 1.2 copy-start.8
  16.2 15.3 %copy-start.7 = (f32[4,128,256]{2,1,0:T(8,128)S(1)}, f32[4,128,256]{2,1,0:T(8,128)}, u32[]{:S(2)}) copy-start(f32[4,128,256]{2,1,0:T(8,128)} %get-tuple-element.19) | copy-start | bytes 1572868
  16.2 15.3 %collective-permute-start.3 = (bf16[4,128,256]{2,1,0:T(8,128)(2,1)}, bf16[4,128,256]{2,1,0:T(8,128)(2,1)S(1)}, u32[]{:S(2)}, u32[]{:S(2)}) collective-permute-start(bf16[4,128,256]{2,1,0:T(8,128)(2,1)} %get-tuple-element.20), channel_id=1, source_target_pairs={{0,2},{2,0},{4,6},{6,4},{8,10},{10,8},{12,14},{14,12},{1,3},{3,1},... | collective-permute-start | bytes 786440 | tf_op jit(solution)/shard_map/ppermute | solution.py:139
  31.4 20.0 %collective-permute-start.2 = (bf16[4,128,256]{2,1,0:T(8,128)(2,1)}, bf16[4,128,256]{2,1,0:T(8,128)(2,1)S(1)}, u32[]{:S(2)}, u32[]{:S(2)}) collective-permute-start(bf16[4,128,256]{2,1,0:T(8,128)(2,1)} %get-tuple-element.18), channel_id=1, source_target_pairs={{0,2},{2,0},{4,6},{6,4},{8,10},{10,8},{12,14},{14,12},{1,3},{3,1},... | collective-permute-start | bytes 786440 | tf_op jit(solution)/shard_map/ppermute | solution.py:139
  32.3 19.9 %all-to-all-start.3 = ((bf16[4,128,256]{2,1,0:T(8,128)(2,1)}), bf16[4,128,256]{2,1,0:T(8,128)(2,1)S(1)}, u32[]{:S(2)}, u32[]{:S(2)}) async-start(bf16[4,128,256]{2,1,0:T(8,128)(2,1)} %add_convert_fusion.1), calls=%async_computation.3 | async-start | bytes 524288 | tf_op jit(solution)/shard_map/all_to_all | solution.py:140
  37.5 13.9 %copy-start.5 = (f32[4,128,256]{2,1,0:T(8,128)S(1)}, f32[4,128,256]{2,1,0:T(8,128)}, u32[]{:S(2)}) copy-start(f32[4,128,256]{2,1,0:T(8,128)} %get-tuple-element.17) | copy-start | bytes 1572868
  49.9 20.3 %collective-permute-start.1 = (bf16[4,128,256]{2,1,0:T(8,128)(2,1)}, bf16[4,128,256]{2,1,0:T(8,128)(2,1)S(1)}, u32[]{:S(2)}, u32[]{:S(2)}) collective-permute-start(bf16[4,128,256]{2,1,0:T(8,128)(2,1)} %get-tuple-element.16), channel_id=1, source_target_pairs={{0,2},{2,0},{4,6},{6,4},{8,10},{10,8},{12,14},{14,12},{1,3},{3,1},... | collective-permute-start | bytes 786440 | tf_op jit(solution)/shard_map/ppermute | solution.py:139
  52.2 17.4 %copy-start = (bf16[4,128,256]{2,1,0:T(8,128)(2,1)}, bf16[4,128,256]{2,1,0:T(8,128)(2,1)S(1)}, u32[]{:S(2)}) copy-start(bf16[4,128,256]{2,1,0:T(8,128)(2,1)S(1)} %all-to-all-done.3.refs_3_) | copy-start | bytes 786436
  52.2 18.8 %all-to-all-start.2 = ((bf16[4,128,256]{2,1,0:T(8,128)(2,1)}), bf16[4,128,256]{2,1,0:T(8,128)(2,1)S(1)}, u32[]{:S(2)}, u32[]{:S(2)}) async-start(bf16[4,128,256]{2,1,0:T(8,128)(2,1)} %add_convert_fusion.2), calls=%async_computation.2 | async-start | bytes 524288 | tf_op jit(solution)/shard_map/all_to_all | solution.py:140
  57.3 12.9 %copy-start.4 = (f32[4,128,256]{2,1,0:T(8,128)S(1)}, f32[4,128,256]{2,1,0:T(8,128)}, u32[]{:S(2)}) copy-start(f32[4,128,256]{2,1,0:T(8,128)} %get-tuple-element.15) | copy-start | bytes 1572868
  69.6 6.7 %copy-start.6 = (f32[4,128,256]{2,1,0:T(8,128)S(1)}, f32[4,128,256]{2,1,0:T(8,128)}, u32[]{:S(2)}) copy-start(f32[4,128,256]{2,1,0:T(8,128)} %get-tuple-element.13) | copy-start | bytes 1572868
  69.6 17.2 %copy-start.10 = (s32[1,8192]{1,0:T(1,128)S(1)}, s32[1,8192]{1,0:T(1,128)}, u32[]{:S(2)}) copy-start(s32[1,8192]{1,0:T(1,128)} %param.10) | copy-start | bytes 98308
  69.6 6.6 %collective-permute-start = (bf16[4,128,256]{2,1,0:T(8,128)(2,1)}, bf16[4,128,256]{2,1,0:T(8,128)(2,1)S(1)}, u32[]{:S(2)}, u32[]{:S(2)}) collective-permute-start(bf16[4,128,256]{2,1,0:T(8,128)(2,1)} %get-tuple-element.14), channel_id=1, source_target_pairs={{0,2},{2,0},{4,6},{6,4},{8,10},{10,8},{12,14},{14,12},{1,3},{3,1},... | collective-permute-start | bytes 786440 | tf_op jit(solution)/shard_map/ppermute | solution.py:139
  71.0 22.1 %copy-start.1 = (bf16[4,128,256]{2,1,0:T(8,128)(2,1)}, bf16[4,128,256]{2,1,0:T(8,128)(2,1)S(1)}, u32[]{:S(2)}) copy-start(bf16[4,128,256]{2,1,0:T(8,128)(2,1)S(1)} %all-to-all-done.2.refs_2_) | copy-start | bytes 786436
  71.0 11.9 %all-to-all-start.1 = ((bf16[4,128,256]{2,1,0:T(8,128)(2,1)}), bf16[4,128,256]{2,1,0:T(8,128)(2,1)S(1)}, u32[]{:S(2)}, u32[]{:S(2)}) async-start(bf16[4,128,256]{2,1,0:T(8,128)(2,1)} %add_convert_fusion.3), calls=%async_computation.1 | async-start | bytes 524288 | tf_op jit(solution)/shard_map/all_to_all | solution.py:140
  77.0 27.5 %copy-start.9 = (bf16[256,512]{1,0:T(8,128)(2,1)S(1)}, bf16[256,512]{1,0:T(8,128)(2,1)}, u32[]{:S(2)}) copy-start(bf16[256,512]{1,0:T(8,128)(2,1)} %param.11) | copy-start | bytes 786436
  82.8 10.2 %copy-start.2 = (bf16[4,128,256]{2,1,0:T(8,128)(2,1)}, bf16[4,128,256]{2,1,0:T(8,128)(2,1)S(1)}, u32[]{:S(2)}) copy-start(bf16[4,128,256]{2,1,0:T(8,128)(2,1)S(1)} %all-to-all-done.1.refs_1_) | copy-start | bytes 786436
  82.8 10.2 %all-to-all-start = ((bf16[4,128,256]{2,1,0:T(8,128)(2,1)}), bf16[4,128,256]{2,1,0:T(8,128)(2,1)S(1)}, u32[]{:S(2)}, u32[]{:S(2)}) async-start(bf16[4,128,256]{2,1,0:T(8,128)(2,1)} %add_convert_fusion.4), calls=%async_computation | async-start | bytes 524288 | tf_op jit(solution)/shard_map/all_to_all | solution.py:140
  93.0 0.7 copy-start.3
  100.1 14.7 %all-to-all-start.4 = ((bf16[8,64,512]{2,1,0:T(8,128)(2,1)}), bf16[8,64,512]{2,1,0:T(8,128)(2,1)S(1)}, u32[]{:S(2)}, u32[]{:S(2)}) async-start(bf16[8,64,512]{2,1,0:T(8,128)(2,1)} %sketch.1), calls=%async_computation.4 | async-start | bytes 1048576 | tf_op jit(solution)/shard_map/all_to_all | solution.py:146
  104.5 1.6 %collective-permute-start.4 = (bf16[256,512]{1,0:T(8,128)(2,1)S(1)}, bf16[256,512]{1,0:T(8,128)(2,1)S(1)}, u32[]{:S(2)}, u32[]{:S(2)}) collective-permute-start(bf16[256,512]{1,0:T(8,128)(2,1)S(1)} %copy-done.9), channel_id=1, source_target_pairs={{0,1},{1,0},{2,3},{3,2},{4,5},{5,4},{6,7},{7,6},{8,9},{9,8},{10,11... | collective-permute-start | bytes 786440 | tf_op jit(solution)/shard_map/ppermute | solution.py:130

commit v2 on v0

v2 whole, which is shorter than its diff:
```python
import functools

import jax
import jax.numpy as jnp
from jax import lax
from jax.experimental import pallas as pl
from jax.experimental.pallas import tpu as pltpu
from jax.sharding import PartitionSpec as P

D = 8192
FF = 28672
R = 64
SEQ_DEV = 64
CHUNKS = 4
GROUP = 512
VMEM = 56 * 1024 * 1024
LAST = (((1,), (1,)), ((), ()))


def project_kernel(first, quarters, piece, who_ref, act_hbm, grad_hbm, sin_ref, sout_ref, sent_ref, kept_ref, act_buf, grad_buf, sems):
    half, quarter = who_ref[0], who_ref[1]
    count = 2 * quarters

    def copies(p):
        side = 1 - half if p < quarters else half
        row = pl.multiple_of(first + (side * quarters + ((p % quarters) ^ quarter)) * piece, piece)
        here = pl.ds(p * piece, piece)
        return (
            pltpu.make_async_copy(act_hbm.at[pl.ds(row, piece)], act_buf.at[here], sems.at[0, p]),
            pltpu.make_async_copy(grad_hbm.at[pl.ds(row, piece)], grad_buf.at[here], sems.at[1, p]),
        )

    for p in range(count):
        for copy in copies(p):
            copy.start()
    signs_in = (2 * sin_ref[...] - 1).astype(jnp.bfloat16)
    signs_out = (2 * sout_ref[...] - 1).astype(jnp.bfloat16)
    per_group = max(1, min(GROUP, count * piece) // piece)
    for start in range(0, count, per_group):
        for p in range(start, start + per_group):
            for copy in copies(p):
                copy.wait()
        rows = pl.ds(start * piece, per_group * piece)
        part_a = lax.dot_general(act_buf[rows, :], signs_in, LAST, preferred_element_type=jnp.float32)
        part_g = lax.dot_general(grad_buf[rows, :], signs_out, LAST, preferred_element_type=jnp.float32)
        part_a = (part_a * FF ** -0.5).T
        part_g = (part_g * D ** -0.5).T
        for p in range(start, start + per_group):
            at = (p - start) * piece
            out_ref = sent_ref if p < quarters else kept_ref
            out_ref[p % quarters, :R, :] = part_a[:, at:at + piece].astype(out_ref.dtype)
            out_ref[p % quarters, R:, :] = part_g[:, at:at + piece].astype(out_ref.dtype)


def project(first, quarters, piece, who, activations, out_grads, signs_in, signs_out):
    count = 2 * quarters
    rows = count * piece
    width_in, width_out = activations.shape[1], out_grads.shape[1]
    whole = pl.BlockSpec(memory_space=pltpu.VMEM)
    hbm = pl.BlockSpec(memory_space=pl.ANY)
    return pl.pallas_call(
        functools.partial(project_kernel, first, quarters, piece),
        in_specs=[pl.BlockSpec(memory_space=pltpu.SMEM), hbm, hbm, whole, whole],
        out_specs=[whole, whole],
        out_shape=[
            jax.ShapeDtypeStruct((quarters, 2 * R, piece), jnp.bfloat16),
            jax.ShapeDtypeStruct((quarters, 2 * R, piece), jnp.float32),
        ],
        scratch_shapes=[
            pltpu.VMEM((rows, width_in), jnp.bfloat16),
            pltpu.VMEM((rows, width_out), jnp.bfloat16),
            pltpu.SemaphoreType.DMA((2, count)),
        ],
        compiler_params=pltpu.CompilerParams(vmem_limit_bytes=VMEM),
        cost_estimate=pl.CostEstimate(
            flops=2 * rows * (width_in + width_out) * R,
            bytes_accessed=2 * rows * (width_in + width_out),
            transcendentals=0,
        ),
        name="project",
    )(who, activations, out_grads, signs_in, signs_out)


def sketch_kernel(quarters, chunks, has_base, last, who_ref, ids_ref, *refs):
    pieces = refs[:chunks * quarters]
    refs = refs[chunks * quarters:]
    if has_base:
        base_ref, refs = refs[0], refs[1:]
    outs, proj_ref, spread_ref = refs[:-2], refs[-2], refs[-1]
    quarter = who_ref[1]
    piece = pieces[0].shape[1]
    per_dest = R // quarters
    group = min(per_dest, 8)
    width = group * R
    for c in range(chunks):
        total = pieces[c * quarters][...]
        for q in range(1, quarters):
            total = total + pieces[c * quarters + q][...].astype(jnp.float32)
        proj_ref[:, c * piece:(c + 1) * piece] = total
    numbers = lax.broadcasted_iota(jnp.int32, (SEQ_DEV, 1), 0)
    member = (ids_ref[...] == numbers).astype(jnp.float32).T.astype(jnp.bfloat16)
    right = proj_ref[R:, :]
    for d in list(range(1, quarters)) + [0]:
        for s in range(per_dest // group):
            at = (quarter ^ d) * per_dest + s * group
            for r in range(group):
                spread_ref[r * R:(r + 1) * R, :] = (proj_ref[pl.ds(at + r, 1), :] * right).astype(jnp.bfloat16)
            part = jnp.dot(spread_ref[...], member, preferred_element_type=jnp.float32).T
            if has_base:
                part = part + base_ref[d, :, s * width:(s + 1) * width]
            if last:
                outs[d][:, s * width:(s + 1) * width] = part.astype(outs[d].dtype)
            else:
                outs[0][d, :, s * width:(s + 1) * width] = part


def sketch(quarters, last, who, ids, pieces, base):
    chunks = len(pieces) // quarters
    owned = chunks * pieces[0].shape[1]
    width = R // quarters * R
    whole = pl.BlockSpec(memory_space=pltpu.VMEM)
    operands = [who, ids] + pieces + ([] if base is None else [base])
    if last:
        shapes = [jax.ShapeDtypeStruct((SEQ_DEV, width), jnp.bfloat16 if d else jnp.float32) for d in range(quarters)]
    else:
        shapes = [jax.ShapeDtypeStruct((quarters, SEQ_DEV, width), jnp.float32)]
    return pl.pallas_call(
        functools.partial(sketch_kernel, quarters, chunks, base is not None, last),
        in_specs=[pl.BlockSpec(memory_space=pltpu.SMEM)] + [whole] * (len(operands) - 1),
        out_specs=[whole] * len(shapes),
        out_shape=shapes,
        scratch_shapes=[
            pltpu.VMEM((2 * R, owned), jnp.float32),
            pltpu.VMEM((min(R // quarters, 8) * R, owned), jnp.bfloat16),
        ],
        compiler_params=pltpu.CompilerParams(vmem_limit_bytes=VMEM),
        cost_estimate=pl.CostEstimate(flops=2 * owned * R * R * SEQ_DEV, bytes_accessed=4 * quarters * SEQ_DEV * width, transcendentals=0),
        name="sketch",
    )(*operands)


def score_kernel(quarters, who_ref, *refs):
    pieces, query_refs = refs[:quarters], refs[quarters:quarters + 4]
    outs, total_ref = refs[quarters + 4:-1], refs[-1]
    half, quarter, data = who_ref[0], who_ref[1], who_ref[2]
    width = query_refs[0].shape[1]
    count = query_refs[0].shape[0]
    entries = pieces[0][...]
    for piece_ref in pieces[1:]:
        entries = entries + piece_ref[...].astype(jnp.float32)
    high = entries.astype(jnp.bfloat16)
    low = (entries - high.astype(jnp.float32)).astype(jnp.bfloat16)
    both = jnp.concatenate([high, low], axis=0)
    swapped = half == 1
    near = jnp.where(swapped, both[:, width:], both[:, :width])
    far = jnp.where(swapped, both[:, :width], both[:, width:])
    for side in range(2):
        part = lax.dot_general(near, query_refs[2 * side][...], LAST, preferred_element_type=jnp.float32)
        part = part + lax.dot_general(far, query_refs[2 * side + 1][...], LAST, preferred_element_type=jnp.float32)
        place = data if side == 0 else 1 - data
        total_ref[:, pl.ds(pl.multiple_of(place * count, count), count)] = part[:SEQ_DEV] + part[SEQ_DEV:]
    rows = SEQ_DEV // quarters
    for d, out_ref in enumerate(outs):
        out_ref[...] = total_ref[pl.ds(pl.multiple_of((quarter ^ d) * rows, rows), rows), :]


def score(quarters, who, pieces, queries):
    whole = pl.BlockSpec(memory_space=pltpu.VMEM)
    columns = 2 * queries[0].shape[0]
    return pl.pallas_call(
        functools.partial(score_kernel, quarters),
        in_specs=[pl.BlockSpec(memory_space=pltpu.SMEM)] + [whole] * (quarters + 4),
        out_specs=[whole] * quarters,
        out_shape=[jax.ShapeDtypeStruct((SEQ_DEV // quarters, columns), jnp.float32)] * quarters,
        scratch_shapes=[pltpu.VMEM((SEQ_DEV, columns), jnp.float32)],
        compiler_params=pltpu.CompilerParams(vmem_limit_bytes=VMEM),
        name="score",
    )(who, *pieces, *queries)


def place_kernel(quarters, who_ref, *refs):
    rows = refs[0].shape[0]
    for d in range(quarters):
        refs[-1][pl.ds(pl.multiple_of((who_ref[1] ^ d) * rows, rows), rows), :] = refs[d][...]


def place(quarters, who, blocks):
    whole = pl.BlockSpec(memory_space=pltpu.VMEM)
    return pl.pallas_call(
        functools.partial(place_kernel, quarters),
        in_specs=[pl.BlockSpec(memory_space=pltpu.SMEM)] + [whole] * quarters,
        out_specs=whole,
        out_shape=jax.ShapeDtypeStruct((SEQ_DEV, blocks[0].shape[1]), jnp.float32),
        name="place",
    )(who, *blocks)


def plain_scores(half, first, pieces, queries):
    entries = sum([piece.astype(jnp.float32) for piece in pieces])
    near, near_far, far, far_far = queries
    mine = jnp.where(half == 0, jnp.concatenate([near, near_far], 1), jnp.concatenate([near_far, near], 1))
    other = jnp.where(half == 0, jnp.concatenate([far, far_far], 1), jnp.concatenate([far_far, far], 1))
    every = jnp.where(first, jnp.concatenate([mine, other], 0), jnp.concatenate([other, mine], 0))
    rounded = lax.reduce_precision(entries, 8, 7)
    high, low = rounded.astype(jnp.bfloat16), (entries - rounded).astype(jnp.bfloat16)
    total = lax.dot_general(high, every, LAST, preferred_element_type=jnp.float32)
    return lax.psum(total + lax.dot_general(low, every, LAST, preferred_element_type=jnp.float32), "tensor")


def body(n_tensor, activations, out_grads, proj_in, proj_out, segment_ids, queries):
    halves = 2
    quarters = n_tensor // halves
    me = lax.axis_index("tensor")
    half, quarter, data = me % halves, me // halves, lax.axis_index("dp")
    who = jnp.stack([half, quarter, data]).astype(jnp.int32)
    swap = [(k, k ^ 1) for k in range(n_tensor)]

    def across(array):
        return lax.ppermute(array, "tensor", swap)

    def along(array, d):
        return lax.ppermute(array, "tensor", [(k, k ^ (halves * d)) for k in range(n_tensor)])

    signs_in, signs_out = proj_in.T, proj_out.T
    near = across(queries)
    cores = [(0, 1), (1, 0)]
    all_queries = [queries, near, lax.ppermute(queries, "dp", cores), lax.ppermute(near, "dp", cores)]

    tokens = activations.shape[0]
    piece = tokens // (CHUNKS * n_tensor)
    pieces = []
    for c in range(CHUNKS):
        first = c * n_tensor * piece
        sent, kept = project(first, quarters, piece, who, activations, out_grads, signs_in, signs_out)
        got = across(sent)
        pieces.append(kept[0] + got[0].astype(jnp.float32))
        for d in range(1, quarters):
            pieces.append(along((kept[d] + got[d].astype(jnp.float32)).astype(jnp.bfloat16), d))

    ids = segment_ids.reshape(CHUNKS, halves, quarters, piece)
    ids = lax.dynamic_slice(ids, (0, half, quarter, 0), (CHUNKS, 1, 1, piece)).reshape(1, CHUNKS * piece)
    early = (CHUNKS - 1) * piece
    base = sketch(quarters, False, who, ids[:, :early], pieces[:(CHUNKS - 1) * quarters], None)[0]
    parts = sketch(quarters, True, who, ids[:, early:], pieces[(CHUNKS - 1) * quarters:], base)
    entries = [parts[0]] + [along(parts[d], d) for d in range(1, quarters)]
    if queries.shape[1] % 128 or SEQ_DEV % (8 * quarters):
        return plain_scores(half, data == 0, entries, all_queries)
    blocks = score(quarters, who, entries, all_queries)
    mine = blocks[0]
    for d in range(1, quarters):
        mine = mine + along(blocks[d], d)
    mine = mine + across(mine)
    return place(quarters, who, [mine] + [along(mine, d) for d in range(1, quarters)])


def solution(mesh):
    return jax.shard_map(
        functools.partial(body, mesh.shape["tensor"]),
        mesh=mesh,
        in_specs=(
            P(("copies", "dp"), "tensor"),
            P(("copies", "dp"), "tensor"),
            P("tensor", None),
            P("tensor", None),
            P(("copies", "dp"), None),
            P(("copies", "dp"), "tensor"),
        ),
        out_specs=P(("copies", "dp"), None),
        check_vma=False,
    )
```

time: 335 us -> 137 us (0.41)
  waiting for transfers between devices: 176 us -> 21.9 us
  matrix products: 101 us -> 0 us
  Pallas kernels: 0 us -> 63.2 us
  starting transfers between devices: 0.08 us -> 40.9 us
  other arithmetic: 39.6 us -> 6.01 us
  between operations: 13.2 us -> 0.36 us
    psum x1 -> x0, waiting for transfers between devices: 159 us -> none  [body(): total_in, total_out = lax.psum((part_in, part_out), 'tensor')]
    dot_general x19 -> x0, matrix products: 101 us -> none  [the longest x16 58.6 us: add_block(): lax.dot_general(spread, right_part, (((0,), (0,)), ((), ())), preferred_e...]
    pallas_call x0 -> x8, Pallas kernels: none -> 63.2 us  [the longest x4 51.8 us: project(): pl.pallas_call(functools.partial(project_kernel, first, quarters, piece),...]
    ppermute x0 -> x29, starting transfers between devices: none -> 40.9 us  [the longest x21 33 us: along(): lax.ppermute(array, 'tensor', [(k, k ^ halves * d) for k in range(n_tenso...]
    mul x16 -> x0, other arithmetic: 36 us -> none  [add_block(): member[:, :, None] * left_part[:, None, :]]
    ppermute x0 -> x29, waiting for transfers between devices: none -> 21.9 us  [the longest x21 17.7 us: along(): lax.ppermute(array, 'tensor', [(k, k ^ halves * d) for k in range(n_tenso...]
    all_gather x2 -> x0, waiting for transfers between devices: 16.2 us -> none  [the longest x1 16.2 us: body(): entries = lax.all_gather(queries, 'tensor', axis=1, tiled=True)]
  transfers between devices with their start and end apart: 3 -> 29, of which waited for: 2 -> 9; matrix products, arithmetic and copies ran while one was open for 42% -> 5% of each run, Pallas kernels for 0% -> 34%
where the time goes in v2:
time: 137 us; the launch traced here: 136 us
  Pallas kernels  63.2 us (46%)
  starting transfers between devices  40.9 us (30%)
  waiting for transfers between devices  21.9 us (16%)
  other arithmetic  6.01 us (4%)
  local copies, waits for them, and re-layouts  3.78 us (3%)
    pallas_call x4, Pallas kernels, project(): pl.pallas_call(functools.partial(project_kernel, first, quarters, piece),...  51.8 us
    ppermute x21, starting transfers between devices, along(): lax.ppermute(array, 'tensor', [(k, k ^ halves * d) for k in range(n_tenso...  33 us
    ppermute x21, waiting for transfers between devices, along(): lax.ppermute(array, 'tensor', [(k, k ^ halves * d) for k in range(n_tenso...  17.7 us
    ppermute x6, starting transfers between devices, across(): return lax.ppermute(array, 'tensor', swap)  7.84 us
    pallas_call x2, Pallas kernels, sketch(): pl.pallas_call(functools.partial(sketch_kernel, quarters, chunks, base is...  7.28 us
    ppermute x6, waiting for transfers between devices, across(): return lax.ppermute(array, 'tensor', swap)  4.18 us
    convert_element_type x4, other arithmetic, body(): (kept[d] + got[d].astype(jnp.float32)).astype(jnp.bfloat16)  3.92 us
  transfers between devices with their start and end apart: 29, of which 9 were waited for; matrix products, arithmetic and copies ran while one was open for 5% of the time, Pallas kernels for 34%

profile of v2, /device:TPU:0, one launch (start us, length us, event | category | flops | bytes accessed | tf_op | source)
XLA Modules:
  0.0 136.1 jit_solution(16769157835449596399)
XLA Ops:
  0.6 12.9 %project.6 = (bf16[4,128,256]{2,1,0:T(8,128)(2,1)}, f32[4,128,256]{2,1,0:T(8,128)}) custom-call(s32[3]{0:T(128)} %pad_add_fusion.who_ref, bf16[8192,3584]{1,0:T(8,128)(2,1)} %act_hbm.7, bf16[8192,1024]{1,0:T(8,128)(2,1)} %grad_hbm.7, s32[64,3584]{1,0:T(8,128)} %bitcast.38, s32[64,1024]{1,0:T(8,128)} %bitcast.42), custom_call_target="tpu_custom_call" | custom-call | flops 1207959552 | bytes 18874368 | tf_op jit(solution)/shard_map/project/pallas_call | solution.py:61
  13.5 3.0 %collective-permute-start.8 = (bf16[4,128,256]{2,1,0:T(8,128)(2,1)}, bf16[4,128,256]{2,1,0:T(8,128)(2,1)S(1)}, u32[]{:S(2)}, u32[]{:S(2)}) collective-permute-start(bf16[4,128,256]{2,1,0:T(8,128)(2,1)} %get-tuple-element.26), channel_id=1, source_target_pairs={{0,2},{2,0},{4,6},{6,4},{8,10},{10,8},{12,14},{14,12},{1,3},{3,1},... | collective-permute-start | bytes 786440 | tf_op jit(solution)/shard_map/ppermute | solution.py:219
  16.6 12.9 %project.7 = (bf16[4,128,256]{2,1,0:T(8,128)(2,1)}, f32[4,128,256]{2,1,0:T(8,128)}) custom-call(s32[3]{0:T(128)} %pad_add_fusion.who_ref, bf16[8192,3584]{1,0:T(8,128)(2,1)} %act_hbm.7, bf16[8192,1024]{1,0:T(8,128)(2,1)} %grad_hbm.7, s32[64,3584]{1,0:T(8,128)} %bitcast.39, s32[64,1024]{1,0:T(8,128)} %bitcast.43), custom_call_target="tpu_custom_call" | custom-call | flops 1207959552 | bytes 18874368 | tf_op jit(solution)/shard_map/project/pallas_call | solution.py:61
  29.6 13.0 %project.5 = (bf16[4,128,256]{2,1,0:T(8,128)(2,1)}, f32[4,128,256]{2,1,0:T(8,128)}) custom-call(s32[3]{0:T(128)} %pad_add_fusion.who_ref, bf16[8192,3584]{1,0:T(8,128)(2,1)} %act_hbm.7, bf16[8192,1024]{1,0:T(8,128)(2,1)} %grad_hbm.7, s32[64,3584]{1,0:T(8,128)} %bitcast.40, s32[64,1024]{1,0:T(8,128)} %bitcast.44), custom_call_target="tpu_custom_call" | custom-call | flops 1207959552 | bytes 18874368 | tf_op jit(solution)/shard_map/project/pallas_call | solution.py:61
  42.7 2.0 %collective-permute-start.4 = (bf16[4,128,256]{2,1,0:T(8,128)(2,1)}, bf16[4,128,256]{2,1,0:T(8,128)(2,1)S(1)}, u32[]{:S(2)}, u32[]{:S(2)}) collective-permute-start(bf16[4,128,256]{2,1,0:T(8,128)(2,1)} %get-tuple-element.24), channel_id=1, source_target_pairs={{0,2},{2,0},{4,6},{6,4},{8,10},{10,8},{12,14},{14,12},{1,3},{3,1},... | collective-permute-start | bytes 786440 | tf_op jit(solution)/shard_map/ppermute | solution.py:219
  44.7 12.9 %project.4 = (bf16[4,128,256]{2,1,0:T(8,128)(2,1)}, f32[4,128,256]{2,1,0:T(8,128)}) custom-call(s32[3]{0:T(128)} %pad_add_fusion.who_ref, bf16[8192,3584]{1,0:T(8,128)(2,1)} %act_hbm.7, bf16[8192,1024]{1,0:T(8,128)(2,1)} %grad_hbm.7, s32[64,3584]{1,0:T(8,128)} %bitcast.41, s32[64,1024]{1,0:T(8,128)} %bitcast.45), custom_call_target="tpu_custom_call" | custom-call | flops 1207959552 | bytes 18874368 | tf_op jit(solution)/shard_map/project/pallas_call | solution.py:61
  57.8 1.9 %collective-permute-start.19 = (bf16[256,512]{1,0:T(8,128)(2,1)S(1)}, bf16[256,512]{1,0:T(8,128)(2,1)S(1)}, u32[]{:S(2)}, u32[]{:S(2)}) collective-permute-start(bf16[256,512]{1,0:T(8,128)(2,1)S(1)} %copy-done.3), channel_id=1, source_target_pairs={{0,2},{2,0},{4,6},{6,4},{8,10},{10,8},{12,14},{14,12},{1,3},{3,1},... | collective-permute-start | bytes 786440 | tf_op jit(solution)/shard_map/ppermute | solution.py:219
  61.7 2.6 %collective-permute-start.10 = (bf16[128,256]{1,0:T(8,128)(2,1)S(1)}, bf16[128,256]{1,0:T(8,128)(2,1)S(1)}, u32[]{:S(2)}, u32[]{:S(2)}) collective-permute-start(bf16[128,256]{1,0:T(8,128)(2,1)S(1)} %get-tuple-element.42), channel_id=1, source_target_pairs={{0,8},{2,10},{4,12},{6,14},{8,0},{10,2},{12,4},{14,6},{1,9},{3,11}... | collective-permute-start | bytes 196616 | tf_op jit(solution)/shard_map/ppermute | solution.py:222
  64.3 1.3 collective-permute-start.11
  67.2 2.6 %collective-permute-start.14 = (bf16[128,256]{1,0:T(8,128)(2,1)S(1)}, bf16[128,256]{1,0:T(8,128)(2,1)S(1)}, u32[]{:S(2)}, u32[]{:S(2)}) collective-permute-start(bf16[128,256]{1,0:T(8,128)(2,1)S(1)} %get-tuple-element.38), channel_id=1, source_target_pairs={{0,8},{2,10},{4,12},{6,14},{8,0},{10,2},{12,4},{14,6},{1,9},{3,11}... | collective-permute-start | bytes 196616 | tf_op jit(solution)/shard_map/ppermute | solution.py:222
  70.7 3.6 %collective-permute-start.15 = (bf16[128,256]{1,0:T(8,128)(2,1)S(1)}, bf16[128,256]{1,0:T(8,128)(2,1)S(1)}, u32[]{:S(2)}, u32[]{:S(2)}) collective-permute-start(bf16[128,256]{1,0:T(8,128)(2,1)S(1)} %get-tuple-element.37), channel_id=1, source_target_pairs={{0,12},{2,14},{4,8},{6,10},{8,4},{10,6},{12,0},{14,2},{1,13},{3,15... | collective-permute-start | bytes 196616 | tf_op jit(solution)/shard_map/ppermute | solution.py:222
  75.1 3.6 %collective-permute-start.7 = (bf16[128,256]{1,0:T(8,128)(2,1)S(1)}, bf16[128,256]{1,0:T(8,128)(2,1)S(1)}, u32[]{:S(2)}, u32[]{:S(2)}) collective-permute-start(bf16[128,256]{1,0:T(8,128)(2,1)S(1)} %get-tuple-element.45), channel_id=1, source_target_pairs={{0,12},{2,14},{4,8},{6,10},{8,4},{10,6},{12,0},{14,2},{1,13},{3,15... | collective-permute-start | bytes 196616 | tf_op jit(solution)/shard_map/ppermute | solution.py:222
  78.8 1.8 %fusion.2 = (bf16[128,256]{1,0:T(8,128)(2,1)S(1)}, bf16[128,256]{1,0:T(8,128)(2,1)S(1)}, bf16[128,256]{1,0:T(8,128)(2,1)S(1)}, f32[128,256]{1,0:T(8,128)}) fusion(f32[4,128,256]{2,1,0:T(8,128)} %get-tuple-element.21, bf16[4,128,256]{2,1,0:T(8,128)(2,1)S(1)} %collective-permute-done), kind=kLoop, calls=%fused_computation.18 | loop fusion | flops 360448 | bytes 1114112 | tf_op jit(solution)/shard_map/convert_element_type | solution.py:238
  80.6 2.1 %collective-permute-start.1 = (bf16[128,256]{1,0:T(8,128)(2,1)S(1)}, bf16[128,256]{1,0:T(8,128)(2,1)S(1)}, u32[]{:S(2)}, u32[]{:S(2)}) collective-permute-start(bf16[128,256]{1,0:T(8,128)(2,1)S(1)} %get-tuple-element.51), channel_id=1, source_target_pairs={{0,4},{2,6},{4,0},{6,2},{8,12},{10,14},{12,8},{14,10},{1,5},{3,7},... | collective-permute-start | bytes 196616 | tf_op jit(solution)/shard_map/ppermute | solution.py:222
  82.7 2.4 %collective-permute-start.3 = (bf16[128,256]{1,0:T(8,128)(2,1)S(1)}, bf16[128,256]{1,0:T(8,128)(2,1)S(1)}, u32[]{:S(2)}, u32[]{:S(2)}) collective-permute-start(bf16[128,256]{1,0:T(8,128)(2,1)S(1)} %get-tuple-element.49), channel_id=1, source_target_pairs={{0,12},{2,14},{4,8},{6,10},{8,4},{10,6},{12,0},{14,2},{1,13},{3,15... | collective-permute-start | bytes 196616 | tf_op jit(solution)/shard_map/ppermute | solution.py:222
  86.4 4.3 %sketch.2.refs_4_ = f32[4,64,1024]{2,1,0:T(8,128)} custom-call(s32[3]{0:T(128)} %pad_add_fusion.who_ref, s32[1,768]{1,0:T(1,128)} %slice.141.ids_ref, f32[128,256]{1,0:T(8,128)} %get-tuple-element.48.refs_0_, bf16[128,256]{1,0:T(8,128)(2,1)} %copy-done.16, bf16[128,256]{1,0:T(8,128)(2,1)} %copy-done.17, bf16[128,256]{1,0:T(8,128)(2,1)} %copy-done.18, ...), custom_call_target="tpu_custom_call" | custom-call | flops 402653184 | bytes 1048576 | tf_op jit(solution)/shard_map/sketch/pallas_call | solution.py:127
  91.3 3.0 %sketch.3 = (f32[64,1024]{1,0:T(8,128)}, bf16[64,1024]{1,0:T(8,128)(2,1)}, bf16[64,1024]{1,0:T(8,128)(2,1)}, bf16[64,1024]{1,0:T(8,128)(2,1)}) custom-call(s32[3]{0:T(128)} %pad_add_fusion.who_ref, s32[1,256]{1,0:T(1,128)} %slice.136.ids_ref, f32[128,256]{1,0:T(8,128)} %get-tuple-element.52.refs_0_, bf16[128,256]{1,0:T(8,128)(2,1)} %copy-done.20, ...), custom_call_target="tpu_custom_call" | custom-call | flops 134217728 | bytes 1048576 | tf_op jit(solution)/shard_map/sketch/pallas_call | solution.py:127
  94.3 1.6 %collective-permute-start.16 = (bf16[64,1024]{1,0:T(8,128)(2,1)}, bf16[64,1024]{1,0:T(8,128)(2,1)S(1)}, u32[]{:S(2)}, u32[]{:S(2)}) collective-permute-start(bf16[64,1024]{1,0:T(8,128)(2,1)} %get-tuple-element.30), channel_id=1, source_target_pairs={{0,4},{2,6},{4,0},{6,2},{8,12},{10,14},{12,8},{14,10},{1,5},{3,7},... | collective-permute-start | bytes 393224 | tf_op jit(solution)/shard_map/ppermute | solution.py:222
  96.4 2.4 %collective-permute-start.18 = (bf16[64,1024]{1,0:T(8,128)(2,1)}, bf16[64,1024]{1,0:T(8,128)(2,1)S(1)}, u32[]{:S(2)}, u32[]{:S(2)}) collective-permute-start(bf16[64,1024]{1,0:T(8,128)(2,1)} %get-tuple-element.32), channel_id=1, source_target_pairs={{0,12},{2,14},{4,8},{6,10},{8,4},{10,6},{12,0},{14,2},{1,13},{3,15... | collective-permute-start | bytes 393224 | tf_op jit(solution)/shard_map/ppermute | solution.py:222
  98.7 2.8 %collective-permute-done.16.refs_1_ = bf16[64,1024]{1,0:T(8,128)(2,1)S(1)} collective-permute-done((bf16[64,1024]{1,0:T(8,128)(2,1)}, bf16[64,1024]{1,0:T(8,128)(2,1)S(1)}, u32[]{:S(2)}, u32[]{:S(2)}) %collective-permute-start.16) | collective-permute-done | bytes 131104 | tf_op jit(solution)/shard_map/ppermute | solution.py:222
  101.6 7.0 %collective-permute-done.17.refs_2_ = bf16[64,1024]{1,0:T(8,128)(2,1)S(1)} collective-permute-done((bf16[64,1024]{1,0:T(8,128)(2,1)}, bf16[64,1024]{1,0:T(8,128)(2,1)S(1)}, u32[]{:S(2)}, u32[]{:S(2)}) %collective-permute-start.17) | collective-permute-done | bytes 131104 | tf_op jit(solution)/shard_map/ppermute | solution.py:222
  109.4 2.6 %score.1 = (f32[16,512]{1,0:T(8,128)}, f32[16,512]{1,0:T(8,128)}, f32[16,512]{1,0:T(8,128)}, f32[16,512]{1,0:T(8,128)}) custom-call(s32[3]{0:T(128)} %pad_add_fusion.who_ref, f32[64,1024]{1,0:T(8,128)} %get-tuple-element.29.refs_0_, bf16[64,1024]{1,0:T(8,128)(2,1)} %copy-done.7, bf16[64,1024]{1,0:T(8,128)(2,1)} %copy-done.8, bf16[64,1024]{1,0:T(8,128)(2,1)} %copy-done.9, ...), custom_call_target="tpu_custom_call" | custom-call | tf_op jit(solution)/shard_map/score/pallas_call | solution.py:170
  112.0 2.5 %collective-permute-start.22 = (f32[16,512]{1,0:T(8,128)}, f32[16,512]{1,0:T(8,128)S(1)}, u32[]{:S(2)}, u32[]{:S(2)}) collective-permute-start(f32[16,512]{1,0:T(8,128)} %get-tuple-element.34), channel_id=1, source_target_pairs={{0,4},{2,6},{4,0},{6,2},{8,12},{10,14},{12,8},{14,10},{1,5},{3,7},... | collective-permute-start | bytes 98312 | tf_op jit(solution)/shard_map/ppermute | solution.py:222
  114.6 2.4 %collective-permute-start.24 = (f32[16,512]{1,0:T(8,128)}, f32[16,512]{1,0:T(8,128)S(1)}, u32[]{:S(2)}, u32[]{:S(2)}) collective-permute-start(f32[16,512]{1,0:T(8,128)} %get-tuple-element.36), channel_id=1, source_target_pairs={{0,12},{2,14},{4,8},{6,10},{8,4},{10,6},{12,0},{14,2},{1,13},{3,15... | collective-permute-start | bytes 98312 | tf_op jit(solution)/shard_map/ppermute | solution.py:222
  117.0 2.6 %collective-permute-done.23 = f32[16,512]{1,0:T(8,128)S(1)} collective-permute-done((f32[16,512]{1,0:T(8,128)}, f32[16,512]{1,0:T(8,128)S(1)}, u32[]{:S(2)}, u32[]{:S(2)}) %collective-permute-start.23) | collective-permute-done | bytes 32800 | tf_op jit(solution)/shard_map/ppermute | solution.py:222
  119.6 0.9 collective-permute-done.24
  120.5 0.8 add_add_fusion
  121.9 3.3 %collective-permute-done.25 = f32[16,512]{1,0:T(8,128)S(1)} collective-permute-done((f32[16,512]{1,0:T(8,128)S(1)}, f32[16,512]{1,0:T(8,128)S(1)}, u32[]{:S(2)}, u32[]{:S(2)}) %collective-permute-start.25) | collective-permute-done | bytes 32800 | tf_op jit(solution)/shard_map/ppermute | solution.py:219
  125.3 3.0 %collective-permute-start.27 = (f32[16,512]{1,0:T(8,128)S(1)}, f32[16,512]{1,0:T(8,128)S(1)}, u32[]{:S(2)}, u32[]{:S(2)}) collective-permute-start(f32[16,512]{1,0:T(8,128)S(1)} %add.117.refs_0_), channel_id=1, source_target_pairs={{0,8},{2,10},{4,12},{6,14},{8,0},{10,2},{12,4},{14,6},{1,9},{3,11}... | collective-permute-start | bytes 98312 | tf_op jit(solution)/shard_map/ppermute | solution.py:222
  128.3 1.4 %collective-permute-start.28 = (f32[16,512]{1,0:T(8,128)S(1)}, f32[16,512]{1,0:T(8,128)S(1)}, u32[]{:S(2)}, u32[]{:S(2)}) collective-permute-start(f32[16,512]{1,0:T(8,128)S(1)} %add.117.refs_0_), channel_id=1, source_target_pairs={{0,12},{2,14},{4,8},{6,10},{8,4},{10,6},{12,0},{14,2},{1,13},{3,15... | collective-permute-start | bytes 98312 | tf_op jit(solution)/shard_map/ppermute | solution.py:222
  130.2 3.8 %collective-permute-done.28.refs_3_ = f32[16,512]{1,0:T(8,128)S(1)} collective-permute-done((f32[16,512]{1,0:T(8,128)S(1)}, f32[16,512]{1,0:T(8,128)S(1)}, u32[]{:S(2)}, u32[]{:S(2)}) %collective-permute-start.28) | collective-permute-done | bytes 32800 | tf_op jit(solution)/shard_map/ppermute | solution.py:222
  134.6 1.5 %place.1 = f32[64,512]{1,0:T(8,128)} custom-call(s32[3]{0:T(128)} %pad_add_fusion.who_ref, f32[16,512]{1,0:T(8,128)} %copy-done.10, f32[16,512]{1,0:T(8,128)} %copy-done.24, f32[16,512]{1,0:T(8,128)} %copy-done.25, f32[16,512]{1,0:T(8,128)} %copy-done.26), custom_call_target="tpu_custom_call" | custom-call | tf_op jit(solution)/shard_map/place/pallas_call | solution.py:189
  (101 shorter events, 11.0 us)
Async XLA Ops:
  13.5 47.5 %collective-permute-start.8 = (bf16[4,128,256]{2,1,0:T(8,128)(2,1)}, bf16[4,128,256]{2,1,0:T(8,128)(2,1)S(1)}, u32[]{:S(2)}, u32[]{:S(2)}) collective-permute-start(bf16[4,128,256]{2,1,0:T(8,128)(2,1)} %get-tuple-element.26), channel_id=1, source_target_pairs={{0,2},{2,0},{4,6},{6,4},{8,10},{10,8},{12,14},{14,12},{1,3},{3,1},... | collective-permute-start | bytes 786440 | tf_op jit(solution)/shard_map/ppermute | solution.py:219
  29.5 31.5 %copy-start.2 = (f32[4,128,256]{2,1,0:T(8,128)S(1)}, f32[4,128,256]{2,1,0:T(8,128)}, u32[]{:S(2)}) copy-start(f32[4,128,256]{2,1,0:T(8,128)} %get-tuple-element.25) | copy-start | bytes 1572868
  29.5 36.1 %copy-start.1 = (f32[4,128,256]{2,1,0:T(8,128)S(1)}, f32[4,128,256]{2,1,0:T(8,128)}, u32[]{:S(2)}) copy-start(f32[4,128,256]{2,1,0:T(8,128)} %get-tuple-element.27) | copy-start | bytes 1572868
  29.6 34.8 %collective-permute-start.12 = (bf16[4,128,256]{2,1,0:T(8,128)(2,1)}, bf16[4,128,256]{2,1,0:T(8,128)(2,1)S(1)}, u32[]{:S(2)}, u32[]{:S(2)}) collective-permute-start(bf16[4,128,256]{2,1,0:T(8,128)(2,1)} %get-tuple-element.28), channel_id=1, source_target_pairs={{0,2},{2,0},{4,6},{6,4},{8,10},{10,8},{12,14},{14,12},{1,3},{3,1},... | collective-permute-start | bytes 786440 | tf_op jit(solution)/shard_map/ppermute | solution.py:219
  42.7 23.7 %collective-permute-start.4 = (bf16[4,128,256]{2,1,0:T(8,128)(2,1)}, bf16[4,128,256]{2,1,0:T(8,128)(2,1)S(1)}, u32[]{:S(2)}, u32[]{:S(2)}) collective-permute-start(bf16[4,128,256]{2,1,0:T(8,128)(2,1)} %get-tuple-element.24), channel_id=1, source_target_pairs={{0,2},{2,0},{4,6},{6,4},{8,10},{10,8},{12,14},{14,12},{1,3},{3,1},... | collective-permute-start | bytes 786440 | tf_op jit(solution)/shard_map/ppermute | solution.py:219
  57.6 9.5 %collective-permute-start = (bf16[4,128,256]{2,1,0:T(8,128)(2,1)}, bf16[4,128,256]{2,1,0:T(8,128)(2,1)S(1)}, u32[]{:S(2)}, u32[]{:S(2)}) collective-permute-start(bf16[4,128,256]{2,1,0:T(8,128)(2,1)} %get-tuple-element.22), channel_id=1, source_target_pairs={{0,2},{2,0},{4,6},{6,4},{8,10},{10,8},{12,14},{14,12},{1,3},{3,1},... | collective-permute-start | bytes 786440 | tf_op jit(solution)/shard_map/ppermute | solution.py:219
  57.8 12.9 %collective-permute-start.19 = (bf16[256,512]{1,0:T(8,128)(2,1)S(1)}, bf16[256,512]{1,0:T(8,128)(2,1)S(1)}, u32[]{:S(2)}, u32[]{:S(2)}) collective-permute-start(bf16[256,512]{1,0:T(8,128)(2,1)S(1)} %copy-done.3), channel_id=1, source_target_pairs={{0,2},{2,0},{4,6},{6,4},{8,10},{10,8},{12,14},{14,12},{1,3},{3,1},... | collective-permute-start | bytes 786440 | tf_op jit(solution)/shard_map/ppermute | solution.py:219
  61.7 12.6 %collective-permute-start.10 = (bf16[128,256]{1,0:T(8,128)(2,1)S(1)}, bf16[128,256]{1,0:T(8,128)(2,1)S(1)}, u32[]{:S(2)}, u32[]{:S(2)}) collective-permute-start(bf16[128,256]{1,0:T(8,128)(2,1)S(1)} %get-tuple-element.42), channel_id=1, source_target_pairs={{0,8},{2,10},{4,12},{6,14},{8,0},{10,2},{12,4},{14,6},{1,9},{3,11}... | collective-permute-start | bytes 196616 | tf_op jit(solution)/shard_map/ppermute | solution.py:222
  64.3 10.0 %collective-permute-start.11 = (bf16[128,256]{1,0:T(8,128)(2,1)S(1)}, bf16[128,256]{1,0:T(8,128)(2,1)S(1)}, u32[]{:S(2)}, u32[]{:S(2)}) collective-permute-start(bf16[128,256]{1,0:T(8,128)(2,1)S(1)} %get-tuple-element.41), channel_id=1, source_target_pairs={{0,12},{2,14},{4,8},{6,10},{8,4},{10,6},{12,0},{14,2},{1,13},{3,15... | collective-permute-start | bytes 196616 | tf_op jit(solution)/shard_map/ppermute | solution.py:222
  66.4 8.8 %collective-permute-start.13 = (bf16[128,256]{1,0:T(8,128)(2,1)S(1)}, bf16[128,256]{1,0:T(8,128)(2,1)S(1)}, u32[]{:S(2)}, u32[]{:S(2)}) collective-permute-start(bf16[128,256]{1,0:T(8,128)(2,1)S(1)} %get-tuple-element.39), channel_id=1, source_target_pairs={{0,4},{2,6},{4,0},{6,2},{8,12},{10,14},{12,8},{14,10},{1,5},{3,7},... | collective-permute-start | bytes 196616 | tf_op jit(solution)/shard_map/ppermute | solution.py:222
  67.2 11.6 %collective-permute-start.14 = (bf16[128,256]{1,0:T(8,128)(2,1)S(1)}, bf16[128,256]{1,0:T(8,128)(2,1)S(1)}, u32[]{:S(2)}, u32[]{:S(2)}) collective-permute-start(bf16[128,256]{1,0:T(8,128)(2,1)S(1)} %get-tuple-element.38), channel_id=1, source_target_pairs={{0,8},{2,10},{4,12},{6,14},{8,0},{10,2},{12,4},{14,6},{1,9},{3,11}... | collective-permute-start | bytes 196616 | tf_op jit(solution)/shard_map/ppermute | solution.py:222
  70.7 37.9 %copy-start.4 = (bf16[256,512]{1,0:T(8,128)(2,1)}, bf16[256,512]{1,0:T(8,128)(2,1)S(1)}, u32[]{:S(2)}) copy-start(bf16[256,512]{1,0:T(8,128)(2,1)S(1)} %collective-permute-done.19.refs_5_) | copy-start | bytes 786436
  70.7 9.8 %collective-permute-start.15 = (bf16[128,256]{1,0:T(8,128)(2,1)S(1)}, bf16[128,256]{1,0:T(8,128)(2,1)S(1)}, u32[]{:S(2)}, u32[]{:S(2)}) collective-permute-start(bf16[128,256]{1,0:T(8,128)(2,1)S(1)} %get-tuple-element.37), channel_id=1, source_target_pairs={{0,12},{2,14},{4,8},{6,10},{8,4},{10,6},{12,0},{14,2},{1,13},{3,15... | collective-permute-start | bytes 196616 | tf_op jit(solution)/shard_map/ppermute | solution.py:222
  74.3 6.3 %collective-permute-start.5 = (bf16[128,256]{1,0:T(8,128)(2,1)S(1)}, bf16[128,256]{1,0:T(8,128)(2,1)S(1)}, u32[]{:S(2)}, u32[]{:S(2)}) collective-permute-start(bf16[128,256]{1,0:T(8,128)(2,1)S(1)} %get-tuple-element.47), channel_id=1, source_target_pairs={{0,4},{2,6},{4,0},{6,2},{8,12},{10,14},{12,8},{14,10},{1,5},{3,7},... | collective-permute-start | bytes 196616 | tf_op jit(solution)/shard_map/ppermute | solution.py:222
  74.4 8.3 %collective-permute-start.6 = (bf16[128,256]{1,0:T(8,128)(2,1)S(1)}, bf16[128,256]{1,0:T(8,128)(2,1)S(1)}, u32[]{:S(2)}, u32[]{:S(2)}) collective-permute-start(bf16[128,256]{1,0:T(8,128)(2,1)S(1)} %get-tuple-element.46), channel_id=1, source_target_pairs={{0,8},{2,10},{4,12},{6,14},{8,0},{10,2},{12,4},{14,6},{1,9},{3,11}... | collective-permute-start | bytes 196616 | tf_op jit(solution)/shard_map/ppermute | solution.py:222
  75.1 7.5 %collective-permute-start.7 = (bf16[128,256]{1,0:T(8,128)(2,1)S(1)}, bf16[128,256]{1,0:T(8,128)(2,1)S(1)}, u32[]{:S(2)}, u32[]{:S(2)}) collective-permute-start(bf16[128,256]{1,0:T(8,128)(2,1)S(1)} %get-tuple-element.45), channel_id=1, source_target_pairs={{0,12},{2,14},{4,8},{6,10},{8,4},{10,6},{12,0},{14,2},{1,13},{3,15... | collective-permute-start | bytes 196616 | tf_op jit(solution)/shard_map/ppermute | solution.py:222
  78.7 6.4 %collective-permute-start.9 = (bf16[128,256]{1,0:T(8,128)(2,1)S(1)}, bf16[128,256]{1,0:T(8,128)(2,1)S(1)}, u32[]{:S(2)}, u32[]{:S(2)}) collective-permute-start(bf16[128,256]{1,0:T(8,128)(2,1)S(1)} %get-tuple-element.43), channel_id=1, source_target_pairs={{0,4},{2,6},{4,0},{6,2},{8,12},{10,14},{12,8},{14,10},{1,5},{3,7},... | collective-permute-start | bytes 196616 | tf_op jit(solution)/shard_map/ppermute | solution.py:222
  80.6 18.2 %collective-permute-start.20 = (bf16[256,512]{1,0:T(8,128)(2,1)S(1)}, bf16[256,512]{1,0:T(8,128)(2,1)S(1)}, u32[]{:S(2)}, u32[]{:S(2)}) collective-permute-start(bf16[256,512]{1,0:T(8,128)(2,1)S(1)} %copy-done.3), channel_id=1, source_target_pairs={{0,1},{1,0},{2,3},{3,2},{4,5},{5,4},{6,7},{7,6},{8,9},{9,8},{10,11... | collective-permute-start | bytes 786440 | tf_op jit(solution)/shard_map/ppermute | solution.py:227
  80.6 10.0 %collective-permute-start.1 = (bf16[128,256]{1,0:T(8,128)(2,1)S(1)}, bf16[128,256]{1,0:T(8,128)(2,1)S(1)}, u32[]{:S(2)}, u32[]{:S(2)}) collective-permute-start(bf16[128,256]{1,0:T(8,128)(2,1)S(1)} %get-tuple-element.51), channel_id=1, source_target_pairs={{0,4},{2,6},{4,0},{6,2},{8,12},{10,14},{12,8},{14,10},{1,5},{3,7},... | collective-permute-start | bytes 196616 | tf_op jit(solution)/shard_map/ppermute | solution.py:222
  82.7 8.0 %collective-permute-start.2 = (bf16[128,256]{1,0:T(8,128)(2,1)S(1)}, bf16[128,256]{1,0:T(8,128)(2,1)S(1)}, u32[]{:S(2)}, u32[]{:S(2)}) collective-permute-start(bf16[128,256]{1,0:T(8,128)(2,1)S(1)} %get-tuple-element.50), channel_id=1, source_target_pairs={{0,8},{2,10},{4,12},{6,14},{8,0},{10,2},{12,4},{14,6},{1,9},{3,11}... | collective-permute-start | bytes 196616 | tf_op jit(solution)/shard_map/ppermute | solution.py:222
  82.7 8.0 %collective-permute-start.3 = (bf16[128,256]{1,0:T(8,128)(2,1)S(1)}, bf16[128,256]{1,0:T(8,128)(2,1)S(1)}, u32[]{:S(2)}, u32[]{:S(2)}) collective-permute-start(bf16[128,256]{1,0:T(8,128)(2,1)S(1)} %get-tuple-element.49), channel_id=1, source_target_pairs={{0,12},{2,14},{4,8},{6,10},{8,4},{10,6},{12,0},{14,2},{1,13},{3,15... | collective-permute-start | bytes 196616 | tf_op jit(solution)/shard_map/ppermute | solution.py:222
  85.1 23.5 %collective-permute-start.21 = (bf16[256,512]{1,0:T(8,128)(2,1)S(1)}, bf16[256,512]{1,0:T(8,128)(2,1)S(1)}, u32[]{:S(2)}, u32[]{:S(2)}) collective-permute-start(bf16[256,512]{1,0:T(8,128)(2,1)S(1)} %collective-permute-done.19.refs_5_), channel_id=1, source_target_pairs={{0,1},{1,0},{2,3},{3,2},{4,5},{5,4},{6,7},{7,6},{8,9},{9,8},{10,11... | collective-permute-start | bytes 786440 | tf_op jit(solution)/shard_map/ppermute | solution.py:227
  94.3 7.2 %collective-permute-start.16 = (bf16[64,1024]{1,0:T(8,128)(2,1)}, bf16[64,1024]{1,0:T(8,128)(2,1)S(1)}, u32[]{:S(2)}, u32[]{:S(2)}) collective-permute-start(bf16[64,1024]{1,0:T(8,128)(2,1)} %get-tuple-element.30), channel_id=1, source_target_pairs={{0,4},{2,6},{4,0},{6,2},{8,12},{10,14},{12,8},{14,10},{1,5},{3,7},... | collective-permute-start | bytes 393224 | tf_op jit(solution)/shard_map/ppermute | solution.py:222
  96.0 12.7 %collective-permute-start.17 = (bf16[64,1024]{1,0:T(8,128)(2,1)}, bf16[64,1024]{1,0:T(8,128)(2,1)S(1)}, u32[]{:S(2)}, u32[]{:S(2)}) collective-permute-start(bf16[64,1024]{1,0:T(8,128)(2,1)} %get-tuple-element.31), channel_id=1, source_target_pairs={{0,8},{2,10},{4,12},{6,14},{8,0},{10,2},{12,4},{14,6},{1,9},{3,11}... | collective-permute-start | bytes 393224 | tf_op jit(solution)/shard_map/ppermute | solution.py:222
  96.4 12.2 %collective-permute-start.18 = (bf16[64,1024]{1,0:T(8,128)(2,1)}, bf16[64,1024]{1,0:T(8,128)(2,1)S(1)}, u32[]{:S(2)}, u32[]{:S(2)}) collective-permute-start(bf16[64,1024]{1,0:T(8,128)(2,1)} %get-tuple-element.32), channel_id=1, source_target_pairs={{0,12},{2,14},{4,8},{6,10},{8,4},{10,6},{12,0},{14,2},{1,13},{3,15... | collective-permute-start | bytes 393224 | tf_op jit(solution)/shard_map/ppermute | solution.py:222
  112.0 5.0 %collective-permute-start.22 = (f32[16,512]{1,0:T(8,128)}, f32[16,512]{1,0:T(8,128)S(1)}, u32[]{:S(2)}, u32[]{:S(2)}) collective-permute-start(f32[16,512]{1,0:T(8,128)} %get-tuple-element.34), channel_id=1, source_target_pairs={{0,4},{2,6},{4,0},{6,2},{8,12},{10,14},{12,8},{14,10},{1,5},{3,7},... | collective-permute-start | bytes 98312 | tf_op jit(solution)/shard_map/ppermute | solution.py:222
  114.6 5.0 %collective-permute-start.23 = (f32[16,512]{1,0:T(8,128)}, f32[16,512]{1,0:T(8,128)S(1)}, u32[]{:S(2)}, u32[]{:S(2)}) collective-permute-start(f32[16,512]{1,0:T(8,128)} %get-tuple-element.35), channel_id=1, source_target_pairs={{0,8},{2,10},{4,12},{6,14},{8,0},{10,2},{12,4},{14,6},{1,9},{3,11}... | collective-permute-start | bytes 98312 | tf_op jit(solution)/shard_map/ppermute | solution.py:222
  114.6 5.9 %collective-permute-start.24 = (f32[16,512]{1,0:T(8,128)}, f32[16,512]{1,0:T(8,128)S(1)}, u32[]{:S(2)}, u32[]{:S(2)}) collective-permute-start(f32[16,512]{1,0:T(8,128)} %get-tuple-element.36), channel_id=1, source_target_pairs={{0,12},{2,14},{4,8},{6,10},{8,4},{10,6},{12,0},{14,2},{1,13},{3,15... | collective-permute-start | bytes 98312 | tf_op jit(solution)/shard_map/ppermute | solution.py:222
  121.3 4.0 %collective-permute-start.25 = (f32[16,512]{1,0:T(8,128)S(1)}, f32[16,512]{1,0:T(8,128)S(1)}, u32[]{:S(2)}, u32[]{:S(2)}) collective-permute-start(f32[16,512]{1,0:T(8,128)S(1)} %add_add_fusion), channel_id=1, source_target_pairs={{0,2},{2,0},{4,6},{6,4},{8,10},{10,8},{12,14},{14,12},{1,3},{3,1},... | collective-permute-start | bytes 98312 | tf_op jit(solution)/shard_map/ppermute | solution.py:219
  125.3 4.5 %collective-permute-start.26 = (f32[16,512]{1,0:T(8,128)S(1)}, f32[16,512]{1,0:T(8,128)S(1)}, u32[]{:S(2)}, u32[]{:S(2)}) collective-permute-start(f32[16,512]{1,0:T(8,128)S(1)} %add.117.refs_0_), channel_id=1, source_target_pairs={{0,4},{2,6},{4,0},{6,2},{8,12},{10,14},{12,8},{14,10},{1,5},{3,7},... | collective-permute-start | bytes 98312 | tf_op jit(solution)/shard_map/ppermute | solution.py:222
  125.3 4.9 %collective-permute-start.27 = (f32[16,512]{1,0:T(8,128)S(1)}, f32[16,512]{1,0:T(8,128)S(1)}, u32[]{:S(2)}, u32[]{:S(2)}) collective-permute-start(f32[16,512]{1,0:T(8,128)S(1)} %add.117.refs_0_), channel_id=1, source_target_pairs={{0,8},{2,10},{4,12},{6,14},{8,0},{10,2},{12,4},{14,6},{1,9},{3,11}... | collective-permute-start | bytes 98312 | tf_op jit(solution)/shard_map/ppermute | solution.py:222
  128.3 5.7 %collective-permute-start.28 = (f32[16,512]{1,0:T(8,128)S(1)}, f32[16,512]{1,0:T(8,128)S(1)}, u32[]{:S(2)}, u32[]{:S(2)}) collective-permute-start(f32[16,512]{1,0:T(8,128)S(1)} %add.117.refs_0_), channel_id=1, source_target_pairs={{0,12},{2,14},{4,8},{6,10},{8,4},{10,6},{12,0},{14,2},{1,13},{3,15... | collective-permute-start | bytes 98312 | tf_op jit(solution)/shard_map/ppermute | solution.py:222
  (24 other events, 187.3 us)

commit v3 on v0

v3 whole, which is shorter than its diff:
```python
import functools

import jax
import jax.numpy as jnp
from jax import lax
from jax.experimental import pallas as pl
from jax.experimental.pallas import tpu as pltpu
from jax.sharding import PartitionSpec as P

D = 8192
FF = 28672
R = 64
SEQ_DEV = 64
VMEM = 56 * 1024 * 1024
LAST = (((1,), (1,)), ((), ()))


def project_kernel(scale, by_column, x_ref, bits_ref, out_ref, signs_ref):
    @pl.when(pl.program_id(0) == 0)
    def _():
        signs_ref[...] = (2 * bits_ref[...] - 1).astype(jnp.bfloat16)

    part = lax.dot_general(signs_ref[...], x_ref[...], LAST, preferred_element_type=jnp.float32)
    part = (part * scale).astype(jnp.bfloat16)
    if by_column:
        out_ref[:, 0] = part.reshape(out_ref.shape[0], out_ref.shape[2], part.shape[1])
    else:
        across = out_ref.shape[0]
        tokens = part.shape[1] // across
        for q in range(across):
            out_ref[q, 0] = part[:, q * tokens:(q + 1) * tokens]


def project(x, bits, scale, quarters, by_column, tile):
    tokens, width = x.shape
    per_half = tokens // 2 // tile
    if by_column:
        shape = (quarters, 2, R // quarters, tokens // 2)
        block = (quarters, 1, R // quarters, tile)
        place = lambda s: (0, s // per_half, 0, s % per_half)
    else:
        piece = tokens // 2 // quarters
        shape = (quarters, 2, R, piece)
        across = max(1, tile // piece)
        block = (across, 1, R, min(tile, piece))
        split = max(1, piece // tile)
        place = lambda s: ((s % per_half) // split, s // per_half, 0, (s % per_half) % split)
    out = pl.pallas_call(
        functools.partial(project_kernel, scale, by_column),
        grid=(tokens // tile,),
        in_specs=[pl.BlockSpec((tile, width), lambda s: (s, 0)), pl.BlockSpec((R, width), lambda s: (0, 0))],
        out_specs=pl.BlockSpec(block, place),
        out_shape=jax.ShapeDtypeStruct(shape, jnp.bfloat16),
        scratch_shapes=[pltpu.VMEM((R, width), jnp.bfloat16)],
        compiler_params=pltpu.CompilerParams(vmem_limit_bytes=VMEM),
        cost_estimate=pl.CostEstimate(flops=2 * tokens * width * R, bytes_accessed=2 * tokens * width, transcendentals=0),
        name="project",
    )(x, bits)
    return out.reshape((2 * quarters,) + shape[2:])


def score_kernel(width, ids_ref, left_ref, right_ref, query_ref, out_ref, row_ref, col_ref, member_ref, spread_ref, sketch_ref):
    total = left_ref[0].astype(jnp.float32)
    for source in range(1, left_ref.shape[0]):
        total = total + left_ref[source].astype(jnp.float32)
    row_ref[...] = total
    piece = right_ref.shape[2]
    for q in range(right_ref.shape[0]):
        col_ref[:, q * piece:(q + 1) * piece] = right_ref[q].astype(jnp.float32)
    numbers = lax.broadcasted_iota(jnp.int32, (SEQ_DEV, 1), 0)
    member_ref[...] = (ids_ref[...] == numbers).astype(jnp.bfloat16)
    rows = spread_ref.shape[0] // R
    for first in range(0, row_ref.shape[0], rows):
        for at in range(0, col_ref.shape[1], width):
            right = col_ref[:, at:at + width]
            for r in range(rows):
                spread_ref[r * R:(r + 1) * R, at:at + width] = (row_ref[first + r:first + r + 1, at:at + width] * right).astype(jnp.bfloat16)
        sketch_ref[:, first * R:(first + rows) * R] = lax.dot_general(
            member_ref[...], spread_ref[...], LAST, preferred_element_type=jnp.float32
        )
    entries = sketch_ref[...]
    high = entries.astype(jnp.bfloat16)
    low = (entries - high.astype(jnp.float32)).astype(jnp.bfloat16)
    out_ref[...] = lax.dot_general(high, query_ref[...], LAST, preferred_element_type=jnp.float32) + lax.dot_general(
        low, query_ref[...], LAST, preferred_element_type=jnp.float32
    )


def score(ids, left, right, queries):
    whole = pl.BlockSpec(memory_space=pltpu.VMEM)
    sources, columns, tokens = left.shape
    rows = min(4, columns)
    return pl.pallas_call(
        functools.partial(score_kernel, min(512, tokens)),
        in_specs=[whole] * 4,
        out_specs=whole,
        out_shape=jax.ShapeDtypeStruct((SEQ_DEV, queries.shape[0]), jnp.float32),
        scratch_shapes=[
            pltpu.VMEM((columns, tokens), jnp.float32),
            pltpu.VMEM((R, tokens), jnp.float32),
            pltpu.VMEM((SEQ_DEV, tokens), jnp.bfloat16),
            pltpu.VMEM((rows * R, tokens), jnp.bfloat16),
            pltpu.VMEM((SEQ_DEV, columns * R), jnp.float32),
        ],
        compiler_params=pltpu.CompilerParams(vmem_limit_bytes=VMEM),
        cost_estimate=pl.CostEstimate(flops=2 * tokens * columns * R * SEQ_DEV, bytes_accessed=2 * left.size, transcendentals=0),
        name="score",
    )(ids, left, right, queries)


def body(n_tensor, activations, out_grads, proj_in, proj_out, segment_ids, queries):
    quarters = n_tensor // 2
    by_half = [[2 * q, 2 * q + 1] for q in range(quarters)]
    by_quarter = [[2 * q + h for q in range(quarters)] for h in range(2)]
    half = lax.axis_index("tensor") % 2
    tokens = activations.shape[0]

    part_g = project(out_grads, proj_out.T, D ** -0.5, quarters, False, 1024)
    got_g = lax.all_to_all(part_g, "tensor", 0, 0)
    part_a = project(activations, proj_in.T, FF ** -0.5, quarters, True, 512)
    own_g = jnp.sum(got_g.astype(jnp.float32), axis=0).astype(jnp.bfloat16)
    right = lax.all_gather(own_g, "tensor", axis=0, axis_index_groups=by_quarter)
    left = lax.all_to_all(part_a, "tensor", 0, 0)

    all_queries = lax.all_gather(queries, "dp", axis=0, tiled=True)
    all_queries = lax.all_gather(all_queries, "tensor", axis=1, tiled=True, axis_index_groups=by_half)
    ids = lax.dynamic_slice(segment_ids, (0, half * (tokens // 2)), (1, tokens // 2))
    return lax.psum(score(ids, left, right, all_queries), "tensor")


def solution(mesh):
    return jax.shard_map(
        functools.partial(body, mesh.shape["tensor"]),
        mesh=mesh,
        in_specs=(
            P(("copies", "dp"), "tensor"),
            P(("copies", "dp"), "tensor"),
            P("tensor", None),
            P("tensor", None),
            P(("copies", "dp"), None),
            P(("copies", "dp"), "tensor"),
        ),
        out_specs=P(("copies", "dp"), None),
        check_vma=False,
    )
```

time: 335 us -> 183 us (0.55)
  waiting for transfers between devices: 176 us -> 70.8 us
  matrix products: 101 us -> 0 us
  Pallas kernels: 0 us -> 46.9 us
  other arithmetic: 39.6 us -> 0.18 us
  blocking collectives: 0 us -> 34.5 us
  starting transfers between devices: 0.08 us -> 13.3 us
    dot_general x19 -> x0, matrix products: 101 us -> none  [the longest x16 58.6 us: add_block(): lax.dot_general(spread, right_part, (((0,), (0,)), ((), ())), preferred_e...]
    psum x1, waiting for transfers between devices: 159 us -> 70.8 us  [body(): return lax.psum(score(ids, left, right, all_queries), 'tensor')]
    pallas_call x0 -> x3, Pallas kernels: none -> 46.9 us  [the longest x2 41.2 us: project(): pl.pallas_call(functools.partial(project_kernel, scale, by_column), grid=...]
    mul x16 -> x0, other arithmetic: 36 us -> none  [add_block(): member[:, :, None] * left_part[:, None, :]]
    all_gather x0 -> x2, blocking collectives: none -> 34.5 us  [the longest x1 32.2 us: body(): lax.all_gather(own_g, 'tensor', axis=0, axis_index_groups=by_quarter)]
    all_gather x2 -> x1, waiting for transfers between devices: 16.2 us -> 0.01 us  [body(): lax.all_gather(all_queries, 'tensor', axis=1, tiled=True, axis_index_grou...]
    all_to_all x0 -> x2, starting transfers between devices: none -> 13.3 us  [the longest x1 7.28 us: body(): got_g = lax.all_to_all(part_g, 'tensor', 0, 0)]
  transfers between devices with their start and end apart: 3 -> 4, of which waited for: 2 -> 1; matrix products, arithmetic and copies ran while one was open for 42% -> 0% of each run, Pallas kernels for 0% -> 16%
where the time goes in v3:
time: 183 us; the launch traced here: 182 us
  waiting for transfers between devices  70.8 us (39%)
  Pallas kernels  46.9 us (26%)
  blocking collectives  34.5 us (19%)
  between operations  13.4 us (7%)
  starting transfers between devices  13.3 us (7%)
  local copies, waits for them, and re-layouts  3.15 us (2%)
    psum x1, waiting for transfers between devices, body(): return lax.psum(score(ids, left, right, all_queries), 'tensor')  70.8 us
    pallas_call x2, Pallas kernels, project(): pl.pallas_call(functools.partial(project_kernel, scale, by_column), grid=...  41.2 us
    all_gather x1, blocking collectives, body(): lax.all_gather(own_g, 'tensor', axis=0, axis_index_groups=by_quarter)  32.2 us
    all_to_all x1, starting transfers between devices, body(): got_g = lax.all_to_all(part_g, 'tensor', 0, 0)  7.28 us
    all_to_all x1, starting transfers between devices, body(): left = lax.all_to_all(part_a, 'tensor', 0, 0)  5.98 us
    pallas_call x1, Pallas kernels, score(): pl.pallas_call(functools.partial(score_kernel, min(512, tokens)), in_spec...  5.67 us
  transfers between devices with their start and end apart: 4, of which 1 were waited for; matrix products, arithmetic and copies ran while one was open for 0% of the time, Pallas kernels for 16%

profile of v3, /device:TPU:0, one launch (start us, length us, event | category | flops | bytes accessed | tf_op | source)
XLA Modules:
  0.0 182.4 jit_solution(1852471779712490260)
XLA Ops:
  6.5 0.0 copy-start
  6.5 0.0 copy-start.2
  6.5 11.6 %project.3 = bf16[4,2,64,1024]{3,2,1,0:T(8,128)(2,1)} custom-call(bf16[8192,1024]{1,0:T(8,128)(2,1)} %x_ref.3, s32[64,1024]{1,0:T(8,128)} %bitcast.9), custom_call_target="tpu_custom_call" | custom-call | flops 1073741824 | bytes 16777216 | tf_op jit(solution)/shard_map/project/pallas_call | solution.py:48
  18.1 7.3 %all-to-all-start.1 = ((bf16[8,64,1024]{2,1,0:T(8,128)(2,1)}), bf16[8,64,1024]{2,1,0:T(8,128)(2,1)S(1)}, u32[]{:S(2)}, u32[]{:S(2)}) async-start(bf16[8,64,1024]{2,1,0:T(8,128)(2,1)} %bitcast.5), calls=%async_computation.1 | async-start | bytes 2097152 | tf_op jit(solution)/shard_map/all_to_all | solution.py:119
  25.4 29.6 %project.2 = bf16[4,2,16,4096]{3,2,1,0:T(8,128)(2,1)} custom-call(bf16[8192,3584]{1,0:T(8,128)(2,1)} %x_ref.2, s32[64,3584]{1,0:T(8,128)} %bitcast.8), custom_call_target="tpu_custom_call" | custom-call | flops 3758096384 | bytes 58720256 | tf_op jit(solution)/shard_map/project/pallas_call | solution.py:48
  55.1 0.0 all-to-all-done.1
  55.1 6.0 %all-to-all-start = ((bf16[8,16,4096]{2,1,0:T(8,128)(2,1)}), bf16[8,16,4096]{2,1,0:T(8,128)(2,1)S(1)}, u32[]{:S(2)}, u32[]{:S(2)}) async-start(bf16[8,16,4096]{2,1,0:T(8,128)(2,1)} %bitcast.6), calls=%async_computation | async-start | bytes 2097152 | tf_op jit(solution)/shard_map/all_to_all | solution.py:123
  61.0 0.0 all-gather.3.cloned.1.call-start
  61.1 0.0 copy-done.2
  61.1 2.3 %all_gather.14 = bf16[512,512]{1,0:T(8,128)(2,1)} all-gather(bf16[256,512]{1,0:T(8,128)(2,1)S(1)} %copy-done.2), channel_id=1, replica_groups=mesh['copies'=2,'tensor'=8,'dp'=2] {'dp'}, dimensions={0}, use_global_device_ids=true | all-gather | bytes 786432 | tf_op jit(solution)/shard_map/all_gather | solution.py:125
  63.4 0.0 all-gather.3.cloned.1.call-update
  63.4 0.0 all-reduce.2.cloned.1.call-start
  63.5 0.0 copy-done
  63.5 0.6 constant_dynamic-slice_fusion.ids_ref
  64.1 0.2 reduce_sum.12
  64.3 32.2 %all-gather = bf16[256,1024]{1,0:T(8,128)(2,1)} all-gather(bf16[64,1024]{1,0:T(8,128)(2,1)S(1)} %reduce_sum.12), channel_id=2, replica_groups={{0,4,8,12},{2,6,10,14},{1,5,9,13},{3,7,11,15},{16,20,24,28},{18,22,26,3..., dimensions={0}, use_global_device_ids=true | all-gather | bytes 655360 | tf_op jit(solution)/shard_map/all_gather | solution.py:122
  96.5 0.0 all-gather.3.cloned.1.call-done.query_ref
  96.5 0.0 all-to-all-done.left_ref
  96.5 0.0 copy-start.1
  96.5 1.0 copy-done.1
  97.5 5.7 %score.1 = f32[64,512]{1,0:T(8,128)} custom-call(s32[1,4096]{1,0:T(1,128)} %constant_dynamic-slice_fusion.ids_ref, bf16[8,16,4096]{2,1,0:T(8,128)(2,1)} %copy-done.1, bf16[4,64,1024]{2,1,0:T(8,128)(2,1)} %bitcast.7, bf16[512,1024]{1,0:T(8,128)(2,1)} %all-gather.3.cloned.1.call-done.query_ref), custom_call_target="tpu_custom_call" | custom-call | flops 536870912 | bytes 1048576 | tf_op jit(solution)/shard_map/score/pallas_call | solution.py:93
  103.2 0.0 all-reduce.2.cloned.1.call-update
  103.2 70.8 %all-reduce.2.cloned.1.call-done = f32[64,512]{1,0:T(8,128)} async-done(((f32[64,512]{1,0:T(8,128)}), f32[64,512]{1,0:T(8,128)}) %all-reduce.2.cloned.1.call-update) | async-done | bytes 131088 | tf_op jit(solution)/shard_map/psum | solution.py:128
  174.0 1.6 copy.8
Async XLA Ops:
  6.5 57.0 %copy-start = (s32[1,8192]{1,0:T(1,128)S(1)}, s32[1,8192]{1,0:T(1,128)}, u32[]{:S(2)}) copy-start(s32[1,8192]{1,0:T(1,128)} %param.10) | copy-start | bytes 98308
  6.5 54.6 %copy-start.2 = (bf16[256,512]{1,0:T(8,128)(2,1)S(1)}, bf16[256,512]{1,0:T(8,128)(2,1)}, u32[]{:S(2)}) copy-start(bf16[256,512]{1,0:T(8,128)(2,1)} %param.11) | copy-start | bytes 786436
  18.1 36.9 %all-to-all-start.1 = ((bf16[8,64,1024]{2,1,0:T(8,128)(2,1)}), bf16[8,64,1024]{2,1,0:T(8,128)(2,1)S(1)}, u32[]{:S(2)}, u32[]{:S(2)}) async-start(bf16[8,64,1024]{2,1,0:T(8,128)(2,1)} %bitcast.5), calls=%async_computation.1 | async-start | bytes 2097152 | tf_op jit(solution)/shard_map/all_to_all | solution.py:119
  55.1 41.5 %all-to-all-start = ((bf16[8,16,4096]{2,1,0:T(8,128)(2,1)}), bf16[8,16,4096]{2,1,0:T(8,128)(2,1)S(1)}, u32[]{:S(2)}, u32[]{:S(2)}) async-start(bf16[8,16,4096]{2,1,0:T(8,128)(2,1)} %bitcast.6), calls=%async_computation | async-start | bytes 2097152 | tf_op jit(solution)/shard_map/all_to_all | solution.py:123
  61.0 35.5 %all-gather.3.cloned.1.call-start = ((), (), s32[]{:S(2)}) async-start(), calls=%async_computation.2 | async-start | bytes 1572864 | tf_op jit(solution)/shard_map/all_gather | solution.py:126
  63.4 110.5 %all-reduce.2.cloned.1.call-start = ((), (), s32[]{:S(2)}) async-start(), calls=%async_computation.3 | async-start | bytes 262144 | tf_op jit(solution)/shard_map/psum | solution.py:128
  96.5 1.0 copy-start.1
Sparse Core Ops, SparseCore 0:
  63.6 25.7 all-gather.2
  103.3 70.5 all-reduce.1

commit v4 on v3

v4 whole, which is shorter than its diff:
```python
import functools
import math

import jax
import jax.numpy as jnp
from jax import lax
from jax.experimental import pallas as pl
from jax.experimental.pallas import tpu as pltpu
from jax.sharding import PartitionSpec as P

D = 8192
FF = 28672
R = 64
SEQ_DEV = 64
VMEM = 56 * 1024 * 1024
LAST = (((1,), (1,)), ((), ()))


def project_kernel(scale, per, depth, by_column, half_ref, x_ref, bits_ref, *refs):
    sent_ref, kept_ref, signs_ref, total_ref = refs[-4:]
    step = pl.program_id(0)

    @pl.when(step == 0)
    def _():
        signs_ref[...] = (2 * bits_ref[...] - 1).astype(jnp.bfloat16)

    for at in range(0, x_ref.shape[1], depth):
        here = slice(at, at + depth)
        part = lax.dot_general(x_ref[:, here], signs_ref[:, here], LAST, preferred_element_type=jnp.float32)
        total_ref[...] = part if at == 0 else total_ref[...] + part
    part = (total_ref[...] * scale).T

    def store(out_ref):
        if by_column:
            out_ref[...] = part.astype(out_ref.dtype).reshape(out_ref.shape)
        else:
            tokens = out_ref.shape[2]
            for q in range(out_ref.shape[0]):
                out_ref[q] = part[:, q * tokens:(q + 1) * tokens].astype(out_ref.dtype)

    @pl.when(step < per)
    def _():
        store(sent_ref)

    @pl.when(step >= per)
    def _():
        store(kept_ref)


def project(x, bits, half, scale, quarters, by_column, first, count, tile, after=()):
    tokens, width = x.shape
    depth = math.gcd(width, 256)
    per = count // tile
    if by_column:
        shape = (quarters, R // quarters, count)
        block = (quarters, R // quarters, tile)
        place = lambda s: (0, 0, s)
    else:
        piece = count // quarters
        across = max(1, tile // piece)
        split = max(1, piece // tile)
        shape = (quarters, R, piece)
        block = (across, R, min(tile, piece))
        place = lambda s: (s // split, 0, s % split)

    def rows(s, half_ref):
        mine = (s >= per).astype(jnp.int32)
        side = half_ref[0] * mine + (1 - half_ref[0]) * (1 - mine)
        return (side * (tokens // 2 // tile) + first // tile + s - mine * per, 0)

    return pl.pallas_call(
        functools.partial(project_kernel, scale, per, depth, by_column),
        grid_spec=pltpu.PrefetchScalarGridSpec(
            num_scalar_prefetch=1,
            grid=(2 * per,),
            in_specs=[pl.BlockSpec((tile, width), rows), pl.BlockSpec((R, width), lambda s, half_ref: (0, 0))]
            + [pl.BlockSpec(memory_space=pl.ANY)] * len(after),
            out_specs=[
                pl.BlockSpec(block, lambda s, half_ref: place(jnp.minimum(s, per - 1))),
                pl.BlockSpec(block, lambda s, half_ref: place(jnp.maximum(s - per, 0))),
            ],
            scratch_shapes=[pltpu.VMEM((R, width), jnp.bfloat16), pltpu.VMEM((tile, R), jnp.float32)],
        ),
        out_shape=[jax.ShapeDtypeStruct(shape, jnp.bfloat16), jax.ShapeDtypeStruct(shape, jnp.float32)],
        compiler_params=pltpu.CompilerParams(vmem_limit_bytes=VMEM),
        cost_estimate=pl.CostEstimate(flops=4 * count * width * R, bytes_accessed=4 * count * width, transcendentals=0),
        name="project",
    )(half, x, bits, *after)


def score_kernel(width, half_ref, ids_ref, left_ref, right_ref, near_ref, far_ref, out_ref, row_ref, col_ref, member_ref, spread_ref, sketch_ref):
    total = left_ref[0].astype(jnp.float32)
    for source in range(1, left_ref.shape[0]):
        total = total + left_ref[source].astype(jnp.float32)
    row_ref[...] = total
    piece = right_ref.shape[2]
    for q in range(right_ref.shape[0]):
        col_ref[:, q * piece:(q + 1) * piece] = right_ref[q].astype(jnp.float32)
    numbers = lax.broadcasted_iota(jnp.int32, (SEQ_DEV, 1), 0)
    member_ref[...] = (ids_ref[...] == numbers).astype(jnp.bfloat16)
    rows = spread_ref.shape[0] // R
    for first in range(0, row_ref.shape[0], rows):
        for at in range(0, col_ref.shape[1], width):
            right = col_ref[:, at:at + width]
            for r in range(rows):
                spread_ref[r * R:(r + 1) * R, at:at + width] = (row_ref[first + r:first + r + 1, at:at + width] * right).astype(jnp.bfloat16)
        sketch_ref[:, first * R:(first + rows) * R] = lax.dot_general(
            member_ref[...], spread_ref[...], LAST, preferred_element_type=jnp.float32
        )
    entries = sketch_ref[...]
    high = entries.astype(jnp.bfloat16)
    low = (entries - high.astype(jnp.float32)).astype(jnp.bfloat16)
    both = jnp.concatenate([high, low], axis=0)
    middle = both.shape[1] // 2
    swapped = half_ref[0] == 1
    near = jnp.where(swapped, both[:, middle:], both[:, :middle])
    far = jnp.where(swapped, both[:, :middle], both[:, middle:])
    part = lax.dot_general(near, near_ref[...], LAST, preferred_element_type=jnp.float32)
    part = part + lax.dot_general(far, far_ref[...], LAST, preferred_element_type=jnp.float32)
    out_ref[...] = part[:SEQ_DEV] + part[SEQ_DEV:]


def score(half, ids, left, right, near, far):
    whole = pl.BlockSpec(memory_space=pltpu.VMEM)
    sources, columns, tokens = left.shape
    rows = min(4, columns)
    return pl.pallas_call(
        functools.partial(score_kernel, min(512, tokens)),
        in_specs=[pl.BlockSpec(memory_space=pltpu.SMEM)] + [whole] * 5,
        out_specs=whole,
        out_shape=jax.ShapeDtypeStruct((SEQ_DEV, near.shape[0]), jnp.float32),
        scratch_shapes=[
            pltpu.VMEM((columns, tokens), jnp.float32),
            pltpu.VMEM((R, tokens), jnp.float32),
            pltpu.VMEM((SEQ_DEV, tokens), jnp.bfloat16),
            pltpu.VMEM((rows * R, tokens), jnp.bfloat16),
            pltpu.VMEM((SEQ_DEV, columns * R), jnp.float32),
        ],
        compiler_params=pltpu.CompilerParams(vmem_limit_bytes=VMEM),
        cost_estimate=pl.CostEstimate(flops=2 * tokens * columns * R * SEQ_DEV, bytes_accessed=2 * left.size, transcendentals=0),
        name="score",
    )(half, ids, left, right, near, far)


def body(n_tensor, activations, out_grads, proj_in, proj_out, segment_ids, queries):
    quarters = n_tensor // 2
    by_quarter = [[2 * q + h for q in range(quarters)] for h in range(2)]
    half = (lax.axis_index("tensor") % 2).astype(jnp.int32)
    side = half.reshape(1)
    owned = activations.shape[0] // 2

    def swap(array, distance):
        return lax.ppermute(array, "tensor", [(k, k ^ distance) for k in range(n_tensor)])

    def along(array):
        return lax.all_to_all(array, "tensor", 0, 0, axis_index_groups=by_quarter)

    near = lax.all_gather(queries, "dp", axis=0, tiled=True)
    far = swap(near, 1)

    bits_in, bits_out = proj_in.T, proj_out.T
    sent_g, kept_g = project(out_grads, bits_out, side, D ** -0.5, quarters, False, 0, owned, 1024)
    got_g = swap(sent_g, 1)
    sent_0, kept_0 = project(activations, bits_in, side, FF ** -0.5, quarters, True, 0, owned // 2, 1024)
    got_0 = swap(sent_0, 1)
    pair_g = (kept_g + got_g.astype(jnp.float32)).astype(jnp.bfloat16)
    pieces_g = along(pair_g)
    sent_1, kept_1 = project(activations, bits_in, side, FF ** -0.5, quarters, True, owned // 2, owned // 2, 1024, (pair_g,))
    got_1 = swap(sent_1, 1)
    own_g = jnp.sum(pieces_g.astype(jnp.float32), axis=0).astype(jnp.bfloat16)
    right = along(jnp.broadcast_to(own_g[None], pieces_g.shape))
    pair_0 = (kept_0 + got_0.astype(jnp.float32)).astype(jnp.bfloat16)
    pair_1 = (kept_1 + got_1.astype(jnp.float32)).astype(jnp.bfloat16)
    left = along(jnp.concatenate([pair_0, pair_1], axis=2))

    ids = lax.dynamic_slice(segment_ids, (0, half * owned), (1, owned))
    total = score(side, ids, left, right, near, far)
    distance = 1
    while 2 * distance < n_tensor:
        total = total + swap(total, distance)
        distance = 2 * distance
    rounded = total.astype(jnp.bfloat16)
    return rounded.astype(jnp.float32) + swap(rounded, distance).astype(jnp.float32)


def solution(mesh):
    return jax.shard_map(
        functools.partial(body, mesh.shape["tensor"]),
        mesh=mesh,
        in_specs=(
            P(("copies", "dp"), "tensor"),
            P(("copies", "dp"), "tensor"),
            P("tensor", None),
            P("tensor", None),
            P(("copies", "dp"), None),
            P(("copies", "dp"), "tensor"),
        ),
        out_specs=P(("copies", "dp"), None),
        check_vma=False,
    )
```

time: 183 us -> 132 us (0.72)
  blocking collectives: 34.5 us -> 2.18 us
  waiting for transfers between devices: 70.8 us -> 48.3 us
  between operations: 13.4 us -> 0.07 us
  starting transfers between devices: 13.3 us -> 23.2 us
  other arithmetic: 0.18 us -> 4.62 us
  Pallas kernels: 46.9 us -> 49.5 us
    psum x1 -> x0, waiting for transfers between devices: 70.8 us -> none  [body(): return lax.psum(score(ids, left, right, all_queries), 'tensor')]
    all_gather x2 -> x1, blocking collectives: 34.5 us -> 2.18 us  [body(): near = lax.all_gather(queries, 'dp', axis=0, tiled=True)]
    all_to_all x2 -> x3, waiting for transfers between devices: 0.01 us -> 24.5 us  [along(): return lax.all_to_all(array, 'tensor', 0, 0, axis_index_groups=by_quarter)]
    ppermute x0 -> x7, waiting for transfers between devices: none -> 23.8 us  [swap(): lax.ppermute(array, 'tensor', [(k, k ^ distance) for k in range(n_tensor)])]
    ppermute x0 -> x7, starting transfers between devices: none -> 11.4 us  [swap(): lax.ppermute(array, 'tensor', [(k, k ^ distance) for k in range(n_tensor)])]
    pallas_call x2 -> x3, Pallas kernels: 41.2 us -> 44.3 us  [project(): pl.pallas_call(functools.partial(project_kernel, scale, per, depth, by_co...]
    convert_element_type x0 -> x4, other arithmetic: none -> 2.11 us  [the longest x1 1.09 us: body(): pair_1 = (kept_1 + got_1.astype(jnp.float32)).astype(jnp.bfloat16)]
    all_to_all x2 -> x3, starting transfers between devices: 13.3 us -> 11.8 us  [along(): return lax.all_to_all(array, 'tensor', 0, 0, axis_index_groups=by_quarter)]
  transfers between devices with their start and end apart: 4 -> 10, of which waited for: 1 -> 7; matrix products, arithmetic and copies ran while one was open for 0% -> 3% of each run, Pallas kernels for 16% -> 24%
where the time goes in v4:
time: 132 us; the launch traced here: 131 us
  Pallas kernels  49.5 us (38%)
  waiting for transfers between devices  48.3 us (37%)
  starting transfers between devices  23.2 us (18%)
  other arithmetic  4.62 us (4%)
  local copies, waits for them, and re-layouts  3.16 us (2%)
  blocking collectives  2.18 us (2%)
    pallas_call x3, Pallas kernels, project(): pl.pallas_call(functools.partial(project_kernel, scale, per, depth, by_co...  44.3 us
    all_to_all x3, waiting for transfers between devices, along(): return lax.all_to_all(array, 'tensor', 0, 0, axis_index_groups=by_quarter)  24.5 us
    ppermute x7, waiting for transfers between devices, swap(): lax.ppermute(array, 'tensor', [(k, k ^ distance) for k in range(n_tensor)])  23.8 us
    all_to_all x3, starting transfers between devices, along(): return lax.all_to_all(array, 'tensor', 0, 0, axis_index_groups=by_quarter)  11.8 us
    ppermute x7, starting transfers between devices, swap(): lax.ppermute(array, 'tensor', [(k, k ^ distance) for k in range(n_tensor)])  11.4 us
    pallas_call x1, Pallas kernels, score(): pl.pallas_call(functools.partial(score_kernel, min(512, tokens)), in_spec...  5.24 us
  transfers between devices with their start and end apart: 10, of which 7 were waited for; matrix products, arithmetic and copies ran while one was open for 3% of the time, Pallas kernels for 24%

profile of v4, /device:TPU:0, one launch (start us, length us, event | category | flops | bytes accessed | tf_op | source)
XLA Modules:
  0.0 131.1 jit_solution(16402711560584444600)
XLA Ops:
  0.0 12.6 %project.4 = (bf16[4,64,1024]{2,1,0:T(8,128)(2,1)}, f32[4,64,1024]{2,1,0:T(8,128)}) custom-call(s32[1]{0:T(128)} %bitcast.half_ref, bf16[8192,1024]{1,0:T(8,128)(2,1)} %x_ref.4, s32[64,1024]{1,0:T(8,128)} %bitcast.5), custom_call_target="tpu_custom_call" | custom-call | flops 1073741824 | bytes 16777216 | tf_op jit(solution)/shard_map/project/pallas_call | solution.py:71
  12.6 3.0 %collective-permute-start.1 = (bf16[4,64,1024]{2,1,0:T(8,128)(2,1)}, bf16[4,64,1024]{2,1,0:T(8,128)(2,1)S(1)}, u32[]{:S(2)}, u32[]{:S(2)}) collective-permute-start(bf16[4,64,1024]{2,1,0:T(8,128)(2,1)} %get-tuple-element.14), channel_id=1, source_target_pairs={{0,2},{2,0},{4,6},{6,4},{8,10},{10,8},{12,14},{14,12},{1,3},{3,1},... | collective-permute-start | bytes 1572872 | tf_op jit(solution)/shard_map/ppermute | solution.py:153
  15.6 15.8 %project.3 = (bf16[4,16,2048]{2,1,0:T(8,128)(2,1)}, f32[4,16,2048]{2,1,0:T(8,128)}) custom-call(s32[1]{0:T(128)} %bitcast.half_ref, bf16[8192,3584]{1,0:T(8,128)(2,1)} %x_ref.5, s32[64,3584]{1,0:T(8,128)} %bitcast.3), custom_call_target="tpu_custom_call" | custom-call | flops 1879048192 | bytes 29360128 | tf_op jit(solution)/shard_map/project/pallas_call | solution.py:71
  31.5 0.1 collective-permute-start
  31.6 1.0 add_convert_fusion.refs_0_
  32.5 15.8 %project.5 = (bf16[4,16,2048]{2,1,0:T(8,128)(2,1)}, f32[4,16,2048]{2,1,0:T(8,128)}) custom-call(s32[1]{0:T(128)} %bitcast.half_ref, bf16[8192,3584]{1,0:T(8,128)(2,1)} %x_ref.5, s32[64,3584]{1,0:T(8,128)} %bitcast.4, bf16[4,64,1024]{2,1,0:T(8,128)(2,1)} %add_convert_fusion.refs_0_), custom_call_target="tpu_custom_call" | custom-call | flops 1879048192 | bytes 29360128 | tf_op jit(solution)/shard_map/project/pallas_call | solution.py:71
  48.4 1.9 %collective-permute-start.2 = (bf16[4,16,2048]{2,1,0:T(8,128)(2,1)}, bf16[4,16,2048]{2,1,0:T(8,128)(2,1)S(1)}, u32[]{:S(2)}, u32[]{:S(2)}) collective-permute-start(bf16[4,16,2048]{2,1,0:T(8,128)(2,1)} %get-tuple-element.16), channel_id=1, source_target_pairs={{0,2},{2,0},{4,6},{6,4},{8,10},{10,8},{12,14},{14,12},{1,3},{3,1},... | collective-permute-start | bytes 786440 | tf_op jit(solution)/shard_map/ppermute | solution.py:153
  50.4 4.9 %all-to-all-start.1 = ((bf16[4,64,1024]{2,1,0:T(8,128)(2,1)}), bf16[4,64,1024]{2,1,0:T(8,128)(2,1)S(1)}, u32[]{:S(2)}, u32[]{:S(2)}) async-start(bf16[4,64,1024]{2,1,0:T(8,128)(2,1)} %add_convert_fusion.refs_0_), calls=%async_computation.1 | async-start | bytes 1048576 | tf_op jit(solution)/shard_map/all_to_all | solution.py:156
  55.2 1.1 collective-permute-done.2
  56.3 1.1 add_convert_fusion.1
  57.4 0.8 pad_maximum_fusion
  58.3 10.7 %all-to-all-done.1 = bf16[4,64,1024]{2,1,0:T(8,128)(2,1)S(1)} async-done(((bf16[4,64,1024]{2,1,0:T(8,128)(2,1)}), bf16[4,64,1024]{2,1,0:T(8,128)(2,1)S(1)}, u32[]{:S(2)}, u32[]{:S(2)}) %all-to-all-start.1) | async-done | bytes 524320 | tf_op jit(solution)/shard_map/all_to_all | solution.py:156
  68.9 3.5 %all-to-all-start = ((bf16[4,16,4096]{2,1,0:T(8,128)(2,1)}), bf16[4,16,4096]{2,1,0:T(8,128)(2,1)S(1)}, u32[]{:S(2)}, u32[]{:S(2)}) async-start(bf16[4,16,4096]{2,1,0:T(8,128)(2,1)} %pad_maximum_fusion), calls=%async_computation | async-start | bytes 1048576 | tf_op jit(solution)/shard_map/all_to_all | solution.py:156
  72.4 0.1 reduce_sum.12
  72.5 13.9 %all-to-all-done.left_ref = bf16[4,16,4096]{2,1,0:T(8,128)(2,1)S(1)} async-done(((bf16[4,16,4096]{2,1,0:T(8,128)(2,1)}), bf16[4,16,4096]{2,1,0:T(8,128)(2,1)S(1)}, u32[]{:S(2)}, u32[]{:S(2)}) %all-to-all-start) | async-done | bytes 524320 | tf_op jit(solution)/shard_map/all_to_all | solution.py:156
  86.3 0.9 broadcast_in_dim.2
  87.3 3.5 %all-to-all-start.2 = ((bf16[4,64,1024]{2,1,0:T(8,128)(2,1)}), bf16[4,64,1024]{2,1,0:T(8,128)(2,1)S(1)}, u32[]{:S(2)}, u32[]{:S(2)}) async-start(bf16[4,64,1024]{2,1,0:T(8,128)(2,1)} %broadcast_in_dim.2), calls=%async_computation.2 | async-start | bytes 1048576 | tf_op jit(solution)/shard_map/all_to_all | solution.py:156
  90.8 2.2 %all_gather.3.near_ref = bf16[512,512]{1,0:T(8,128)(2,1)S(1)} all-gather(bf16[256,512]{1,0:T(8,128)(2,1)S(1)} %copy-done.7), channel_id=1, replica_groups=mesh['copies'=2,'tensor'=8,'dp'=2] {'dp'}, dimensions={0}, use_global_device_ids=true | all-gather | bytes 786432 | tf_op jit(solution)/shard_map/all_gather | solution.py:158
  93.0 0.5 collective-permute-start.3
  93.5 0.6 constant_dynamic-slice_fusion.ids_ref
  94.1 12.8 %collective-permute-done.3.far_ref = bf16[512,512]{1,0:T(8,128)(2,1)S(1)} collective-permute-done((bf16[512,512]{1,0:T(8,128)(2,1)S(1)}, bf16[512,512]{1,0:T(8,128)(2,1)S(1)}, u32[]{:S(2)}, u32[]{:S(2)}) %collective-permute-start.3) | collective-permute-done | bytes 524320 | tf_op jit(solution)/shard_map/ppermute | solution.py:153
  106.9 0.8 copy-done.5
  107.7 0.8 copy-done.2
  108.5 5.2 %score.1 = f32[64,512]{1,0:T(8,128)} custom-call(s32[1]{0:T(128)} %bitcast.half_ref, s32[1,4096]{1,0:T(1,128)} %constant_dynamic-slice_fusion.ids_ref, bf16[4,16,4096]{2,1,0:T(8,128)(2,1)} %copy-done.1, bf16[4,64,1024]{2,1,0:T(8,128)(2,1)} %copy-done.2, bf16[512,512]{1,0:T(8,128)(2,1)} %copy-done.3, bf16[512,512]{1,0:T(8,128)(2,1)} %copy-done.5), custom_call_target="tpu_custom_call" | custom-call | flops 536870912 | bytes 524288 | tf_op jit(solution)/shard_map/score/pallas_call | solution.py:127
  113.8 0.6 collective-permute-start.4
  114.3 4.6 %collective-permute-done.4 = f32[64,512]{1,0:T(8,128)S(1)} collective-permute-done((f32[64,512]{1,0:T(8,128)}, f32[64,512]{1,0:T(8,128)S(1)}, u32[]{:S(2)}, u32[]{:S(2)}) %collective-permute-start.4) | collective-permute-done | bytes 131104 | tf_op jit(solution)/shard_map/ppermute | solution.py:153
  119.0 0.9 add.30
  119.9 2.0 %collective-permute-start.5 = (f32[64,512]{1,0:T(8,128)S(1)}, f32[64,512]{1,0:T(8,128)S(1)}, u32[]{:S(2)}, u32[]{:S(2)}) collective-permute-start(f32[64,512]{1,0:T(8,128)S(1)} %add.30), channel_id=1, source_target_pairs={{0,4},{2,6},{4,0},{6,2},{8,12},{10,14},{12,8},{14,10},{1,5},{3,7},... | collective-permute-start | bytes 393224 | tf_op jit(solution)/shard_map/ppermute | solution.py:153
  121.9 3.0 %collective-permute-done.5 = f32[64,512]{1,0:T(8,128)S(1)} collective-permute-done((f32[64,512]{1,0:T(8,128)S(1)}, f32[64,512]{1,0:T(8,128)S(1)}, u32[]{:S(2)}, u32[]{:S(2)}) %collective-permute-start.5) | collective-permute-done | bytes 131104 | tf_op jit(solution)/shard_map/ppermute | solution.py:153
  124.9 3.2 %collective-permute-start.6 = (bf16[64,512]{1,0:T(8,128)(2,1)S(1)}, bf16[64,512]{1,0:T(8,128)(2,1)S(1)}, u32[]{:S(2)}, u32[]{:S(2)}) collective-permute-start(bf16[64,512]{1,0:T(8,128)(2,1)S(1)} %add_convert_fusion.3), channel_id=1, source_target_pairs={{0,8},{2,10},{4,12},{6,14},{8,0},{10,2},{12,4},{14,6},{1,9},{3,11}... | collective-permute-start | bytes 196616 | tf_op jit(solution)/shard_map/ppermute | solution.py:153
  128.2 2.2 %collective-permute-done.6 = bf16[64,512]{1,0:T(8,128)(2,1)S(1)} collective-permute-done((bf16[64,512]{1,0:T(8,128)(2,1)S(1)}, bf16[64,512]{1,0:T(8,128)(2,1)S(1)}, u32[]{:S(2)}, u32[]{:S(2)}) %collective-permute-start.6) | collective-permute-done | bytes 65568 | tf_op jit(solution)/shard_map/ppermute | solution.py:153
  130.4 0.7 convert_add_fusion
  (19 shorter events, 0.1 us)
Async XLA Ops:
  0.0 93.5 %copy-start = (s32[1,8192]{1,0:T(1,128)S(1)}, s32[1,8192]{1,0:T(1,128)}, u32[]{:S(2)}) copy-start(s32[1,8192]{1,0:T(1,128)} %param.10) | copy-start | bytes 98308
  12.6 19.0 %copy-start.4 = (f32[4,64,1024]{2,1,0:T(8,128)S(1)}, f32[4,64,1024]{2,1,0:T(8,128)}, u32[]{:S(2)}) copy-start(f32[4,64,1024]{2,1,0:T(8,128)} %get-tuple-element.13) | copy-start | bytes 3145732
  12.6 18.9 %collective-permute-start.1 = (bf16[4,64,1024]{2,1,0:T(8,128)(2,1)}, bf16[4,64,1024]{2,1,0:T(8,128)(2,1)S(1)}, u32[]{:S(2)}, u32[]{:S(2)}) collective-permute-start(bf16[4,64,1024]{2,1,0:T(8,128)(2,1)} %get-tuple-element.14), channel_id=1, source_target_pairs={{0,2},{2,0},{4,6},{6,4},{8,10},{10,8},{12,14},{14,12},{1,3},{3,1},... | collective-permute-start | bytes 1572872 | tf_op jit(solution)/shard_map/ppermute | solution.py:153
  15.6 75.1 %copy-start.7 = (bf16[256,512]{1,0:T(8,128)(2,1)S(1)}, bf16[256,512]{1,0:T(8,128)(2,1)}, u32[]{:S(2)}) copy-start(bf16[256,512]{1,0:T(8,128)(2,1)} %param.11) | copy-start | bytes 786436
  31.5 18.8 %copy-start.6 = (f32[4,16,2048]{2,1,0:T(8,128)S(1)}, f32[4,16,2048]{2,1,0:T(8,128)}, u32[]{:S(2)}) copy-start(f32[4,16,2048]{2,1,0:T(8,128)} %get-tuple-element.11) | copy-start | bytes 1572868
  31.5 18.8 %collective-permute-start = (bf16[4,16,2048]{2,1,0:T(8,128)(2,1)}, bf16[4,16,2048]{2,1,0:T(8,128)(2,1)S(1)}, u32[]{:S(2)}, u32[]{:S(2)}) collective-permute-start(bf16[4,16,2048]{2,1,0:T(8,128)(2,1)} %get-tuple-element.12), channel_id=1, source_target_pairs={{0,2},{2,0},{4,6},{6,4},{8,10},{10,8},{12,14},{14,12},{1,3},{3,1},... | collective-permute-start | bytes 786440 | tf_op jit(solution)/shard_map/ppermute | solution.py:153
  48.4 8.0 %collective-permute-start.2 = (bf16[4,16,2048]{2,1,0:T(8,128)(2,1)}, bf16[4,16,2048]{2,1,0:T(8,128)(2,1)S(1)}, u32[]{:S(2)}, u32[]{:S(2)}) collective-permute-start(bf16[4,16,2048]{2,1,0:T(8,128)(2,1)} %get-tuple-element.16), channel_id=1, source_target_pairs={{0,2},{2,0},{4,6},{6,4},{8,10},{10,8},{12,14},{14,12},{1,3},{3,1},... | collective-permute-start | bytes 786440 | tf_op jit(solution)/shard_map/ppermute | solution.py:153
  50.4 18.5 %all-to-all-start.1 = ((bf16[4,64,1024]{2,1,0:T(8,128)(2,1)}), bf16[4,64,1024]{2,1,0:T(8,128)(2,1)S(1)}, u32[]{:S(2)}, u32[]{:S(2)}) async-start(bf16[4,64,1024]{2,1,0:T(8,128)(2,1)} %add_convert_fusion.refs_0_), calls=%async_computation.1 | async-start | bytes 1048576 | tf_op jit(solution)/shard_map/all_to_all | solution.py:156
  68.9 17.4 %all-to-all-start = ((bf16[4,16,4096]{2,1,0:T(8,128)(2,1)}), bf16[4,16,4096]{2,1,0:T(8,128)(2,1)S(1)}, u32[]{:S(2)}, u32[]{:S(2)}) async-start(bf16[4,16,4096]{2,1,0:T(8,128)(2,1)} %pad_maximum_fusion), calls=%async_computation | async-start | bytes 1048576 | tf_op jit(solution)/shard_map/all_to_all | solution.py:156
  86.3 20.6 %copy-start.1 = (bf16[4,16,4096]{2,1,0:T(8,128)(2,1)}, bf16[4,16,4096]{2,1,0:T(8,128)(2,1)S(1)}, u32[]{:S(2)}) copy-start(bf16[4,16,4096]{2,1,0:T(8,128)(2,1)S(1)} %all-to-all-done.left_ref) | copy-start | bytes 1572868
  87.3 19.6 %all-to-all-start.2 = ((bf16[4,64,1024]{2,1,0:T(8,128)(2,1)}), bf16[4,64,1024]{2,1,0:T(8,128)(2,1)S(1)}, u32[]{:S(2)}, u32[]{:S(2)}) async-start(bf16[4,64,1024]{2,1,0:T(8,128)(2,1)} %broadcast_in_dim.2), calls=%async_computation.2 | async-start | bytes 1048576 | tf_op jit(solution)/shard_map/all_to_all | solution.py:156
  92.9 14.0 %copy-start.3 = (bf16[512,512]{1,0:T(8,128)(2,1)}, bf16[512,512]{1,0:T(8,128)(2,1)S(1)}, u32[]{:S(2)}) copy-start(bf16[512,512]{1,0:T(8,128)(2,1)S(1)} %all_gather.3.near_ref) | copy-start | bytes 1572868
  93.0 14.0 %collective-permute-start.3 = (bf16[512,512]{1,0:T(8,128)(2,1)S(1)}, bf16[512,512]{1,0:T(8,128)(2,1)S(1)}, u32[]{:S(2)}, u32[]{:S(2)}) collective-permute-start(bf16[512,512]{1,0:T(8,128)(2,1)S(1)} %all_gather.3.near_ref), channel_id=1, source_target_pairs={{0,2},{2,0},{4,6},{6,4},{8,10},{10,8},{12,14},{14,12},{1,3},{3,1},... | collective-permute-start | bytes 1572872 | tf_op jit(solution)/shard_map/ppermute | solution.py:153
  106.9 0.8 copy-start.5
  107.7 0.8 copy-start.2
  113.8 5.2 %collective-permute-start.4 = (f32[64,512]{1,0:T(8,128)}, f32[64,512]{1,0:T(8,128)S(1)}, u32[]{:S(2)}, u32[]{:S(2)}) collective-permute-start(f32[64,512]{1,0:T(8,128)} %score.1), channel_id=1, source_target_pairs={{0,2},{2,0},{4,6},{6,4},{8,10},{10,8},{12,14},{14,12},{1,3},{3,1},... | collective-permute-start | bytes 393224 | tf_op jit(solution)/shard_map/ppermute | solution.py:153
  119.9 5.0 %collective-permute-start.5 = (f32[64,512]{1,0:T(8,128)S(1)}, f32[64,512]{1,0:T(8,128)S(1)}, u32[]{:S(2)}, u32[]{:S(2)}) collective-permute-start(f32[64,512]{1,0:T(8,128)S(1)} %add.30), channel_id=1, source_target_pairs={{0,4},{2,6},{4,0},{6,2},{8,12},{10,14},{12,8},{14,10},{1,5},{3,7},... | collective-permute-start | bytes 393224 | tf_op jit(solution)/shard_map/ppermute | solution.py:153
  124.9 5.5 %collective-permute-start.6 = (bf16[64,512]{1,0:T(8,128)(2,1)S(1)}, bf16[64,512]{1,0:T(8,128)(2,1)S(1)}, u32[]{:S(2)}, u32[]{:S(2)}) collective-permute-start(bf16[64,512]{1,0:T(8,128)(2,1)S(1)} %add_convert_fusion.3), channel_id=1, source_target_pairs={{0,8},{2,10},{4,12},{6,14},{8,0},{10,2},{12,4},{14,6},{1,9},{3,11}... | collective-permute-start | bytes 196616 | tf_op jit(solution)/shard_map/ppermute | solution.py:153

commit v5 on v4

v5 whole, which is shorter than its diff:
```python
import functools

import jax
import jax.numpy as jnp
from jax import lax
from jax.experimental import pallas as pl
from jax.experimental.pallas import tpu as pltpu
from jax.sharding import PartitionSpec as P

D = 8192
FF = 28672
R = 64
SEQ_DEV = 64
BUFFERS = 4
VMEM = 56 * 1024 * 1024
LAST = (((1,), (1,)), ((), ()))


def project_kernel(scale, per, order, start, who_ref, x_hbm, bits_ref, *refs):
    sent_ref, kept_ref, signs_ref, x_buf, sems = refs[-5:]
    step = pl.program_id(0)
    steps = 2 * per
    buffers, tile = x_buf.shape[0], x_buf.shape[1]
    slot = lax.rem(step, buffers)

    def copy(s, slot):
        mine = (s >= per).astype(jnp.int32) if isinstance(s, jax.Array) else int(s >= per)
        side = who_ref[0] * mine + (1 - who_ref[0]) * (1 - mine)
        row = pl.multiple_of(side * (x_hbm.shape[0] // 2) + start + (s - mine * per) * tile, tile)
        return pltpu.make_async_copy(x_hbm.at[pl.ds(row, tile)], x_buf.at[slot], sems.at[slot])

    @pl.when(step == 0)
    def _():
        for s in range(min(buffers, steps)):
            copy(s, s).start()
        if order:
            for q in range(order):
                rows = R // order
                bits = bits_ref[pl.ds(pl.multiple_of((q ^ who_ref[1]) * rows, rows), rows), :]
                signs_ref[q * rows:(q + 1) * rows, :] = (2 * bits - 1).astype(jnp.bfloat16)
        else:
            signs_ref[...] = (2 * bits_ref[...] - 1).astype(jnp.bfloat16)

    copy(step, slot).wait()
    part = lax.dot_general(signs_ref[...], x_buf[slot], LAST, preferred_element_type=jnp.float32) * scale

    @pl.when(step + buffers < steps)
    def _():
        copy(step + buffers, slot).start()

    def store(out_ref):
        out_ref[...] = part.astype(out_ref.dtype).reshape(out_ref.shape)

    @pl.when(step < per)
    def _():
        store(sent_ref)

    @pl.when(step >= per)
    def _():
        store(kept_ref)


def project(x, bits, who, scale, quarters, by_column, first, count, tile, after=()):
    tokens, width = x.shape
    piece = count // quarters
    if not by_column:
        tile = min(tile, piece)
    per = count // tile
    order = quarters if by_column and (R // quarters) % 8 == 0 else 0
    if by_column and not order:
        rows = jnp.arange(R, dtype=jnp.int32)
        bits = jnp.take(bits, rows ^ (who[1] * (R // quarters)), axis=0)
    if by_column:
        shape = (quarters, R // quarters, count)
        block = (quarters, R // quarters, tile)
        place = lambda s, who_ref: (0, 0, s)
    else:
        split = piece // tile
        shape = (quarters, R, piece)
        block = (1, R, tile)
        place = lambda s, who_ref: ((s // split) ^ who_ref[1], 0, s % split)

    return pl.pallas_call(
        functools.partial(project_kernel, scale, per, order, first),
        grid_spec=pltpu.PrefetchScalarGridSpec(
            num_scalar_prefetch=1,
            grid=(2 * per,),
            in_specs=[
                pl.BlockSpec(memory_space=pl.ANY),
                pl.BlockSpec((R, width), lambda s, who_ref: (0, 0)),
            ]
            + [pl.BlockSpec(memory_space=pl.ANY)] * len(after),
            out_specs=[
                pl.BlockSpec(block, lambda s, who_ref: place(jnp.minimum(s, per - 1), who_ref)),
                pl.BlockSpec(block, lambda s, who_ref: place(jnp.maximum(s - per, 0), who_ref)),
            ],
            scratch_shapes=[
                pltpu.VMEM((R, width), jnp.bfloat16),
                pltpu.VMEM((BUFFERS, tile, width), jnp.bfloat16),
                pltpu.SemaphoreType.DMA((BUFFERS,)),
            ],
        ),
        out_shape=[jax.ShapeDtypeStruct(shape, jnp.bfloat16), jax.ShapeDtypeStruct(shape, jnp.float32)],
        compiler_params=pltpu.CompilerParams(vmem_limit_bytes=VMEM),
        cost_estimate=pl.CostEstimate(flops=4 * count * width * R, bytes_accessed=4 * count * width, transcendentals=0),
        name="project",
    )(who, x, bits, *after)


def score_kernel(quarters, width, who_ref, ids_ref, near_ref, far_ref, *refs):
    left_refs, right_refs = refs[:quarters], refs[quarters:2 * quarters]
    out_ref, row_ref, col_ref, member_ref, spread_ref, sketch_ref = refs[2 * quarters:]
    half, quarter = who_ref[0], who_ref[1]
    total = left_refs[0][...]
    for left_ref in left_refs[1:]:
        total = total + left_ref[...].astype(jnp.float32)
    row_ref[...] = total
    piece = right_refs[0].shape[1]
    for d, right_ref in enumerate(right_refs):
        col_ref[:, pl.ds(pl.multiple_of((quarter ^ d) * piece, piece), piece)] = right_ref[...].astype(jnp.float32)
    numbers = lax.broadcasted_iota(jnp.int32, (SEQ_DEV, 1), 0)
    member_ref[...] = (ids_ref[...] == numbers).astype(jnp.bfloat16)
    rows = spread_ref.shape[0] // R
    for first in range(0, row_ref.shape[0], rows):
        for at in range(0, col_ref.shape[1], width):
            right = col_ref[:, at:at + width]
            for r in range(rows):
                spread_ref[r * R:(r + 1) * R, at:at + width] = (row_ref[first + r:first + r + 1, at:at + width] * right).astype(jnp.bfloat16)
        sketch_ref[:, first * R:(first + rows) * R] = lax.dot_general(
            member_ref[...], spread_ref[...], LAST, preferred_element_type=jnp.float32
        )
    entries = sketch_ref[...]
    high = entries.astype(jnp.bfloat16)
    low = (entries - high.astype(jnp.float32)).astype(jnp.bfloat16)
    both = jnp.concatenate([high, low], axis=0)
    middle = both.shape[1] // 2
    swapped = half == 1
    near = jnp.where(swapped, both[:, middle:], both[:, :middle])
    far = jnp.where(swapped, both[:, :middle], both[:, middle:])
    part = lax.dot_general(near, near_ref[...], LAST, preferred_element_type=jnp.float32)
    part = part + lax.dot_general(far, far_ref[...], LAST, preferred_element_type=jnp.float32)
    out_ref[...] = part[:SEQ_DEV] + part[SEQ_DEV:]


def score(who, ids, near, far, left, right):
    whole = pl.BlockSpec(memory_space=pltpu.VMEM)
    columns, tokens = left[0].shape
    rows = min(4, columns)
    return pl.pallas_call(
        functools.partial(score_kernel, len(left), min(512, tokens)),
        in_specs=[pl.BlockSpec(memory_space=pltpu.SMEM)] + [whole] * (3 + len(left) + len(right)),
        out_specs=whole,
        out_shape=jax.ShapeDtypeStruct((SEQ_DEV, near.shape[0]), jnp.float32),
        scratch_shapes=[
            pltpu.VMEM((columns, tokens), jnp.float32),
            pltpu.VMEM((R, tokens), jnp.float32),
            pltpu.VMEM((SEQ_DEV, tokens), jnp.bfloat16),
            pltpu.VMEM((rows * R, tokens), jnp.bfloat16),
            pltpu.VMEM((SEQ_DEV, columns * R), jnp.float32),
        ],
        compiler_params=pltpu.CompilerParams(vmem_limit_bytes=VMEM),
        cost_estimate=pl.CostEstimate(flops=2 * tokens * columns * R * SEQ_DEV, bytes_accessed=4 * columns * tokens, transcendentals=0),
        name="score",
    )(who, ids, near, far, *left, *right)


def body(n_tensor, activations, out_grads, proj_in, proj_out, segment_ids, queries):
    quarters = n_tensor // 2
    me = lax.axis_index("tensor").astype(jnp.int32)
    half = me % 2
    who = jnp.stack([half, me // 2])
    owned = activations.shape[0] // 2
    early = owned * 5 // 8

    def swap(array, distance):
        return lax.ppermute(array, "tensor", [(k, k ^ distance) for k in range(n_tensor)])

    near = lax.all_gather(queries, "dp", axis=0, tiled=True)
    far = swap(near, 1)

    bits_in, bits_out = proj_in.T, proj_out.T
    scale_in, scale_out = FF ** -0.5, D ** -0.5
    sent_g, kept_g = project(out_grads, bits_out, who, scale_out, quarters, False, 0, owned, 1024)
    got_g = swap(sent_g, 1)
    sent_0, kept_0 = project(activations, bits_in, who, scale_in, quarters, True, 0, early, 512)
    got_0 = swap(sent_0, 1)
    pair_g = [kept_g[d] + got_g[d].astype(jnp.float32) for d in range(quarters)]
    pair_g = [pair_g[0]] + [pair.astype(jnp.bfloat16) for pair in pair_g[1:]]
    moved_g = [swap(pair_g[d], 2 * d) for d in range(1, quarters)]
    sent_1, kept_1 = project(activations, bits_in, who, scale_in, quarters, True, early, owned - early, 512, pair_g[1:2])
    got_1 = swap(sent_1, 1)
    own_g = sum([moved.astype(jnp.float32) for moved in moved_g], pair_g[0]).astype(jnp.bfloat16)
    right = [own_g] + [swap(own_g, 2 * d) for d in range(1, quarters)]
    left = []
    for d in range(quarters):
        parts = [kept_0[d] + got_0[d].astype(jnp.float32), kept_1[d] + got_1[d].astype(jnp.float32)]
        if d:
            left.append(swap(jnp.concatenate([part.astype(jnp.bfloat16) for part in parts], axis=1), 2 * d))
        else:
            left.append(jnp.concatenate(parts, axis=1))

    ids = lax.dynamic_slice(segment_ids, (0, half * owned), (1, owned))
    total = score(who, ids, near, far, left, right)
    distance = 1
    while 2 * distance < n_tensor:
        total = total + swap(total, distance)
        distance = 2 * distance
    rounded = total.astype(jnp.bfloat16)
    return rounded.astype(jnp.float32) + swap(rounded, distance).astype(jnp.float32)


def solution(mesh):
    return jax.shard_map(
        functools.partial(body, mesh.shape["tensor"]),
        mesh=mesh,
        in_specs=(
            P(("copies", "dp"), "tensor"),
            P(("copies", "dp"), "tensor"),
            P("tensor", None),
            P("tensor", None),
            P(("copies", "dp"), None),
            P(("copies", "dp"), "tensor"),
        ),
        out_specs=P(("copies", "dp"), None),
        check_vma=False,
    )
```

time: 132 us -> 110 us (0.83)
  waiting for transfers between devices: 48.3 us -> 33.3 us
  Pallas kernels: 49.5 us -> 45.5 us
  starting transfers between devices: 23.2 us -> 21 us
    all_to_all x3 -> x0, waiting for transfers between devices: 24.5 us -> none  [along(): return lax.all_to_all(array, 'tensor', 0, 0, axis_index_groups=by_quarter)]
    all_to_all x3 -> x0, starting transfers between devices: 11.8 us -> none  [along(): return lax.all_to_all(array, 'tensor', 0, 0, axis_index_groups=by_quarter)]
    ppermute x7 -> x16, starting transfers between devices: 11.4 us -> 21 us  [swap(): lax.ppermute(array, 'tensor', [(k, k ^ distance) for k in range(n_tensor)])]
    ppermute x7 -> x16, waiting for transfers between devices: 23.8 us -> 33.3 us  [swap(): lax.ppermute(array, 'tensor', [(k, k ^ distance) for k in range(n_tensor)])]
    pallas_call x4, Pallas kernels: 49.5 us -> 45.5 us  [the longest x3 40.2 us: project(): pl.pallas_call(functools.partial(project_kernel, scale, per, order, first...]
  transfers between devices with their start and end apart: 10 -> 16, of which waited for: 7 -> 7; matrix products, arithmetic and copies ran while one was open for 3% -> 3% of each run, Pallas kernels for 24% -> 27%
where the time goes in v5:
time: 110 us
  Pallas kernels  45.5 us (41%)
  waiting for transfers between devices  33.3 us (30%)
  starting transfers between devices  21 us (19%)
  other arithmetic  5.4 us (5%)
  blocking collectives  2.17 us (2%)
  local copies, waits for them, and re-layouts  1.87 us (2%)
    pallas_call x3, Pallas kernels, project(): pl.pallas_call(functools.partial(project_kernel, scale, per, order, first...  40.2 us
    ppermute x16, waiting for transfers between devices, swap(): lax.ppermute(array, 'tensor', [(k, k ^ distance) for k in range(n_tensor)])  33.3 us
    ppermute x16, starting transfers between devices, swap(): lax.ppermute(array, 'tensor', [(k, k ^ distance) for k in range(n_tensor)])  21 us
    pallas_call x1, Pallas kernels, score(): pl.pallas_call(functools.partial(score_kernel, len(left), min(512, tokens...  5.35 us
    convert_element_type x2, other arithmetic, body(): part.astype(jnp.bfloat16)  2.27 us
  transfers between devices with their start and end apart: 16, of which 7 were waited for; matrix products, arithmetic and copies ran while one was open for 3% of the time, Pallas kernels for 27%

profile of v5, /device:TPU:0, one launch (start us, length us, event | category | flops | bytes accessed | tf_op | source)
XLA Modules:
  0.0 109.5 jit_solution(7799807050258704584)
XLA Ops:
  0.0 0.6 pad_add_fusion.who_ref
  0.6 10.6 %project.4 = (bf16[4,64,1024]{2,1,0:T(8,128)(2,1)}, f32[4,64,1024]{2,1,0:T(8,128)}) custom-call(s32[2]{0:T(128)} %pad_add_fusion.who_ref, bf16[8192,1024]{1,0:T(8,128)(2,1)} %x_hbm.4, s32[64,1024]{1,0:T(8,128)} %bitcast.36), custom_call_target="tpu_custom_call" | custom-call | flops 1073741824 | bytes 16777216 | tf_op jit(solution)/shard_map/project/pallas_call | solution.py:83
  11.2 3.0 %collective-permute-start.2 = (bf16[4,64,1024]{2,1,0:T(8,128)(2,1)}, bf16[4,64,1024]{2,1,0:T(8,128)(2,1)S(1)}, u32[]{:S(2)}, u32[]{:S(2)}) collective-permute-start(bf16[4,64,1024]{2,1,0:T(8,128)(2,1)} %get-tuple-element.14), channel_id=1, source_target_pairs={{0,2},{2,0},{4,6},{6,4},{8,10},{10,8},{12,14},{14,12},{1,3},{3,1},... | collective-permute-start | bytes 1572872 | tf_op jit(solution)/shard_map/ppermute | solution.py:176
  14.2 17.4 %project.3 = (bf16[4,16,2560]{2,1,0:T(8,128)(2,1)}, f32[4,16,2560]{2,1,0:T(8,128)}) custom-call(s32[2]{0:T(128)} %pad_add_fusion.who_ref, bf16[8192,3584]{1,0:T(8,128)(2,1)} %x_hbm.5, s32[64,3584]{1,0:T(8,128)} %bitcast.34), custom_call_target="tpu_custom_call" | custom-call | flops 2348810240 | bytes 36700160 | tf_op jit(solution)/shard_map/project/pallas_call | solution.py:83
  31.8 2.2 %all_gather.3.near_ref = bf16[512,512]{1,0:T(8,128)(2,1)S(1)} all-gather(bf16[256,512]{1,0:T(8,128)(2,1)S(1)} %copy-done.6), channel_id=1, replica_groups=mesh['copies'=2,'tensor'=8,'dp'=2] {'dp'}, dimensions={0}, use_global_device_ids=true | all-gather | bytes 786432 | tf_op jit(solution)/shard_map/all_gather | solution.py:178
  34.0 1.9 %collective-permute-start = (bf16[512,512]{1,0:T(8,128)(2,1)S(1)}, bf16[512,512]{1,0:T(8,128)(2,1)S(1)}, u32[]{:S(2)}, u32[]{:S(2)}) collective-permute-start(bf16[512,512]{1,0:T(8,128)(2,1)S(1)} %all_gather.3.near_ref), channel_id=1, source_target_pairs={{0,2},{2,0},{4,6},{6,4},{8,10},{10,8},{12,14},{14,12},{1,3},{3,1},... | collective-permute-start | bytes 1572872 | tf_op jit(solution)/shard_map/ppermute | solution.py:176
  35.8 0.6 constant_dynamic-slice_fusion.ids_ref
  36.4 6.0 %collective-permute-done.1 = bf16[4,16,2560]{2,1,0:T(8,128)(2,1)S(1)} collective-permute-done((bf16[4,16,2560]{2,1,0:T(8,128)(2,1)}, bf16[4,16,2560]{2,1,0:T(8,128)(2,1)S(1)}, u32[]{:S(2)}, u32[]{:S(2)}) %collective-permute-start.1) | collective-permute-done | bytes 327712 | tf_op jit(solution)/shard_map/ppermute | solution.py:176
  42.5 1.2 %fusion.8 = (bf16[16,2560]{1,0:T(8,128)(2,1)S(1)}, bf16[16,2560]{1,0:T(8,128)(2,1)S(1)}, bf16[16,2560]{1,0:T(8,128)(2,1)S(1)}, f32[16,2560]{1,0:T(8,128)S(1)}) fusion(f32[4,16,2560]{2,1,0:T(8,128)} %get-tuple-element.11, bf16[4,16,2560]{2,1,0:T(8,128)(2,1)S(1)} %collective-permute-done.1), kind=kLoop, calls=%fused_computation.26 | loop fusion | flops 450560 | bytes 1392640 | tf_op jit(solution)/shard_map/convert_element_type | solution.py:198
  43.8 1.7 %collective-permute-start.7 = (bf16[64,1024]{1,0:T(8,128)(2,1)S(1)}, bf16[64,1024]{1,0:T(8,128)(2,1)S(1)}, u32[]{:S(2)}, u32[]{:S(2)}) collective-permute-start(bf16[64,1024]{1,0:T(8,128)(2,1)S(1)} %get-tuple-element.19.refs_0_), channel_id=1, source_target_pairs={{0,4},{2,6},{4,0},{6,2},{8,12},{10,14},{12,8},{14,10},{1,5},{3,7},... | collective-permute-start | bytes 393224 | tf_op jit(solution)/shard_map/ppermute | solution.py:176
  45.5 2.6 %collective-permute-start.8 = (bf16[64,1024]{1,0:T(8,128)(2,1)S(1)}, bf16[64,1024]{1,0:T(8,128)(2,1)S(1)}, u32[]{:S(2)}, u32[]{:S(2)}) collective-permute-start(bf16[64,1024]{1,0:T(8,128)(2,1)S(1)} %get-tuple-element.17), channel_id=1, source_target_pairs={{0,8},{2,10},{4,12},{6,14},{8,0},{10,2},{12,4},{14,6},{1,9},{3,11}... | collective-permute-start | bytes 393224 | tf_op jit(solution)/shard_map/ppermute | solution.py:176
  48.3 12.3 %project.5 = (bf16[4,16,1536]{2,1,0:T(8,128)(2,1)}, f32[4,16,1536]{2,1,0:T(8,128)}) custom-call(s32[2]{0:T(128)} %pad_add_fusion.who_ref, bf16[8192,3584]{1,0:T(8,128)(2,1)} %x_hbm.5, s32[64,3584]{1,0:T(8,128)} %bitcast.35, bf16[64,1024]{1,0:T(8,128)(2,1)} %copy-done.3), custom_call_target="tpu_custom_call" | custom-call | flops 1409286144 | bytes 22020096 | tf_op jit(solution)/shard_map/project/pallas_call | solution.py:83
  60.6 0.3 collective-permute-start.3
  61.0 1.0 collective-permute-start.10
  62.0 3.5 %collective-permute-start.11 = (bf16[64,1024]{1,0:T(8,128)(2,1)S(1)}, bf16[64,1024]{1,0:T(8,128)(2,1)S(1)}, u32[]{:S(2)}, u32[]{:S(2)}) collective-permute-start(bf16[64,1024]{1,0:T(8,128)(2,1)S(1)} %fusion.2.refs_4_), channel_id=1, source_target_pairs={{0,8},{2,10},{4,12},{6,14},{8,0},{10,2},{12,4},{14,6},{1,9},{3,11}... | collective-permute-start | bytes 393224 | tf_op jit(solution)/shard_map/ppermute | solution.py:176
  65.5 1.0 collective-permute-done.3
  66.5 1.1 fusion.11
  67.6 3.7 %collective-permute-start.6 = (bf16[16,4096]{1,0:T(8,128)(2,1)S(1)}, bf16[16,4096]{1,0:T(8,128)(2,1)S(1)}, u32[]{:S(2)}, u32[]{:S(2)}) collective-permute-start(bf16[16,4096]{1,0:T(8,128)(2,1)S(1)} %pad_maximum_fusion.3), channel_id=1, source_target_pairs={{0,12},{2,14},{4,8},{6,10},{8,4},{10,6},{12,0},{14,2},{1,13},{3,15... | collective-permute-start | bytes 393224 | tf_op jit(solution)/shard_map/ppermute | solution.py:176
  71.4 0.8 collective-permute-start.4
  72.2 0.7 pad_maximum_fusion.refs_0_
  72.9 5.7 %collective-permute-done.11.refs_6_ = bf16[64,1024]{1,0:T(8,128)(2,1)S(1)} collective-permute-done((bf16[64,1024]{1,0:T(8,128)(2,1)S(1)}, bf16[64,1024]{1,0:T(8,128)(2,1)S(1)}, u32[]{:S(2)}, u32[]{:S(2)}) %collective-permute-start.11) | collective-permute-done | bytes 131104 | tf_op jit(solution)/shard_map/ppermute | solution.py:176
  78.7 6.2 %collective-permute-done.5.refs_2_ = bf16[16,4096]{1,0:T(8,128)(2,1)S(1)} collective-permute-done((bf16[16,4096]{1,0:T(8,128)(2,1)S(1)}, bf16[16,4096]{1,0:T(8,128)(2,1)S(1)}, u32[]{:S(2)}, u32[]{:S(2)}) %collective-permute-start.5) | collective-permute-done | bytes 131104 | tf_op jit(solution)/shard_map/ppermute | solution.py:176
  84.9 0.6 copy-done.11
  85.5 0.7 copy-done.12
  86.1 5.3 %score.1 = f32[64,512]{1,0:T(8,128)} custom-call(s32[2]{0:T(128)} %pad_add_fusion.who_ref, s32[1,4096]{1,0:T(1,128)} %constant_dynamic-slice_fusion.ids_ref, bf16[512,512]{1,0:T(8,128)(2,1)} %copy-done.1, bf16[512,512]{1,0:T(8,128)(2,1)} %copy-done.4, f32[16,4096]{1,0:T(8,128)} %pad_maximum_fusion.refs_0_, bf16[16,4096]{1,0:T(8,128)(2,1)} %copy-done.12, ...), custom_call_target="tpu_custom_call" | custom-call | flops 536870912 | bytes 262144 | tf_op jit(solution)/shard_map/score/pallas_call | solution.py:149
  91.5 1.2 %collective-permute-start.13 = (f32[64,512]{1,0:T(8,128)}, f32[64,512]{1,0:T(8,128)S(1)}, u32[]{:S(2)}, u32[]{:S(2)}) collective-permute-start(f32[64,512]{1,0:T(8,128)} %score.1), channel_id=1, source_target_pairs={{0,2},{2,0},{4,6},{6,4},{8,10},{10,8},{12,14},{14,12},{1,3},{3,1},... | collective-permute-start | bytes 393224 | tf_op jit(solution)/shard_map/ppermute | solution.py:176
  92.7 3.9 %collective-permute-done.13 = f32[64,512]{1,0:T(8,128)S(1)} collective-permute-done((f32[64,512]{1,0:T(8,128)}, f32[64,512]{1,0:T(8,128)S(1)}, u32[]{:S(2)}, u32[]{:S(2)}) %collective-permute-start.13) | collective-permute-done | bytes 131104 | tf_op jit(solution)/shard_map/ppermute | solution.py:176
  96.7 0.9 add.100
  97.7 5.7 %collective-permute-done.14 = f32[64,512]{1,0:T(8,128)S(1)} collective-permute-done((f32[64,512]{1,0:T(8,128)S(1)}, f32[64,512]{1,0:T(8,128)S(1)}, u32[]{:S(2)}, u32[]{:S(2)}) %collective-permute-start.14) | collective-permute-done | bytes 131104 | tf_op jit(solution)/shard_map/ppermute | solution.py:176
  103.3 0.8 collective-permute-start.15
  104.2 4.7 %collective-permute-done.15 = bf16[64,512]{1,0:T(8,128)(2,1)S(1)} collective-permute-done((bf16[64,512]{1,0:T(8,128)(2,1)S(1)}, bf16[64,512]{1,0:T(8,128)(2,1)S(1)}, u32[]{:S(2)}, u32[]{:S(2)}) %collective-permute-start.15) | collective-permute-done | bytes 65568 | tf_op jit(solution)/shard_map/ppermute | solution.py:176
  108.8 0.7 convert_add_fusion
  (44 shorter events, 0.9 us)
Async XLA Ops:
  0.0 35.8 %copy-start = (s32[1,8192]{1,0:T(1,128)S(1)}, s32[1,8192]{1,0:T(1,128)}, u32[]{:S(2)}) copy-start(s32[1,8192]{1,0:T(1,128)} %param.10) | copy-start | bytes 98308
  0.0 31.8 %copy-start.6 = (bf16[256,512]{1,0:T(8,128)(2,1)S(1)}, bf16[256,512]{1,0:T(8,128)(2,1)}, u32[]{:S(2)}) copy-start(bf16[256,512]{1,0:T(8,128)(2,1)} %param.11) | copy-start | bytes 786436
  11.2 32.5 %copy-start.2 = (f32[4,64,1024]{2,1,0:T(8,128)S(1)}, f32[4,64,1024]{2,1,0:T(8,128)}, u32[]{:S(2)}) copy-start(f32[4,64,1024]{2,1,0:T(8,128)} %get-tuple-element.13) | copy-start | bytes 3145732
  11.2 32.5 %collective-permute-start.2 = (bf16[4,64,1024]{2,1,0:T(8,128)(2,1)}, bf16[4,64,1024]{2,1,0:T(8,128)(2,1)S(1)}, u32[]{:S(2)}, u32[]{:S(2)}) collective-permute-start(bf16[4,64,1024]{2,1,0:T(8,128)(2,1)} %get-tuple-element.14), channel_id=1, source_target_pairs={{0,2},{2,0},{4,6},{6,4},{8,10},{10,8},{12,14},{14,12},{1,3},{3,1},... | collective-permute-start | bytes 1572872 | tf_op jit(solution)/shard_map/ppermute | solution.py:176
  31.6 10.9 %collective-permute-start.1 = (bf16[4,16,2560]{2,1,0:T(8,128)(2,1)}, bf16[4,16,2560]{2,1,0:T(8,128)(2,1)S(1)}, u32[]{:S(2)}, u32[]{:S(2)}) collective-permute-start(bf16[4,16,2560]{2,1,0:T(8,128)(2,1)} %get-tuple-element.12), channel_id=1, source_target_pairs={{0,2},{2,0},{4,6},{6,4},{8,10},{10,8},{12,14},{14,12},{1,3},{3,1},... | collective-permute-start | bytes 983048 | tf_op jit(solution)/shard_map/ppermute | solution.py:176
  34.0 50.9 %copy-start.1 = (bf16[512,512]{1,0:T(8,128)(2,1)}, bf16[512,512]{1,0:T(8,128)(2,1)S(1)}, u32[]{:S(2)}) copy-start(bf16[512,512]{1,0:T(8,128)(2,1)S(1)} %all_gather.3.near_ref) | copy-start | bytes 1572868
  34.0 37.3 %collective-permute-start = (bf16[512,512]{1,0:T(8,128)(2,1)S(1)}, bf16[512,512]{1,0:T(8,128)(2,1)S(1)}, u32[]{:S(2)}, u32[]{:S(2)}) collective-permute-start(bf16[512,512]{1,0:T(8,128)(2,1)S(1)} %all_gather.3.near_ref), channel_id=1, source_target_pairs={{0,2},{2,0},{4,6},{6,4},{8,10},{10,8},{12,14},{14,12},{1,3},{3,1},... | collective-permute-start | bytes 1572872 | tf_op jit(solution)/shard_map/ppermute | solution.py:176
  43.8 4.5 %copy-start.3 = (bf16[64,1024]{1,0:T(8,128)(2,1)}, bf16[64,1024]{1,0:T(8,128)(2,1)S(1)}, u32[]{:S(2)}) copy-start(bf16[64,1024]{1,0:T(8,128)(2,1)S(1)} %get-tuple-element.19.refs_0_) | copy-start | bytes 393220
  43.8 17.1 %collective-permute-start.7 = (bf16[64,1024]{1,0:T(8,128)(2,1)S(1)}, bf16[64,1024]{1,0:T(8,128)(2,1)S(1)}, u32[]{:S(2)}, u32[]{:S(2)}) collective-permute-start(bf16[64,1024]{1,0:T(8,128)(2,1)S(1)} %get-tuple-element.19.refs_0_), channel_id=1, source_target_pairs={{0,4},{2,6},{4,0},{6,2},{8,12},{10,14},{12,8},{14,10},{1,5},{3,7},... | collective-permute-start | bytes 393224 | tf_op jit(solution)/shard_map/ppermute | solution.py:176
  45.5 15.4 %collective-permute-start.8 = (bf16[64,1024]{1,0:T(8,128)(2,1)S(1)}, bf16[64,1024]{1,0:T(8,128)(2,1)S(1)}, u32[]{:S(2)}, u32[]{:S(2)}) collective-permute-start(bf16[64,1024]{1,0:T(8,128)(2,1)S(1)} %get-tuple-element.17), channel_id=1, source_target_pairs={{0,8},{2,10},{4,12},{6,14},{8,0},{10,2},{12,4},{14,6},{1,9},{3,11}... | collective-permute-start | bytes 393224 | tf_op jit(solution)/shard_map/ppermute | solution.py:176
  48.0 12.8 %collective-permute-start.9 = (bf16[64,1024]{1,0:T(8,128)(2,1)S(1)}, bf16[64,1024]{1,0:T(8,128)(2,1)S(1)}, u32[]{:S(2)}, u32[]{:S(2)}) collective-permute-start(bf16[64,1024]{1,0:T(8,128)(2,1)S(1)} %get-tuple-element.18), channel_id=1, source_target_pairs={{0,12},{2,14},{4,8},{6,10},{8,4},{10,6},{12,0},{14,2},{1,13},{3,15... | collective-permute-start | bytes 393224 | tf_op jit(solution)/shard_map/ppermute | solution.py:176
  60.6 5.9 %collective-permute-start.3 = (bf16[4,16,1536]{2,1,0:T(8,128)(2,1)}, bf16[4,16,1536]{2,1,0:T(8,128)(2,1)S(1)}, u32[]{:S(2)}, u32[]{:S(2)}) collective-permute-start(bf16[4,16,1536]{2,1,0:T(8,128)(2,1)} %get-tuple-element.16), channel_id=1, source_target_pairs={{0,2},{2,0},{4,6},{6,4},{8,10},{10,8},{12,14},{14,12},{1,3},{3,1},... | collective-permute-start | bytes 589832 | tf_op jit(solution)/shard_map/ppermute | solution.py:176
  61.0 23.9 %copy-start.5 = (bf16[64,1024]{1,0:T(8,128)(2,1)}, bf16[64,1024]{1,0:T(8,128)(2,1)S(1)}, u32[]{:S(2)}) copy-start(bf16[64,1024]{1,0:T(8,128)(2,1)S(1)} %fusion.2.refs_4_) | copy-start | bytes 393220
  61.0 10.4 %collective-permute-start.10 = (bf16[64,1024]{1,0:T(8,128)(2,1)S(1)}, bf16[64,1024]{1,0:T(8,128)(2,1)S(1)}, u32[]{:S(2)}, u32[]{:S(2)}) collective-permute-start(bf16[64,1024]{1,0:T(8,128)(2,1)S(1)} %fusion.2.refs_4_), channel_id=1, source_target_pairs={{0,4},{2,6},{4,0},{6,2},{8,12},{10,14},{12,8},{14,10},{1,5},{3,7},... | collective-permute-start | bytes 393224 | tf_op jit(solution)/shard_map/ppermute | solution.py:176
  62.0 16.6 %collective-permute-start.11 = (bf16[64,1024]{1,0:T(8,128)(2,1)S(1)}, bf16[64,1024]{1,0:T(8,128)(2,1)S(1)}, u32[]{:S(2)}, u32[]{:S(2)}) collective-permute-start(bf16[64,1024]{1,0:T(8,128)(2,1)S(1)} %fusion.2.refs_4_), channel_id=1, source_target_pairs={{0,8},{2,10},{4,12},{6,14},{8,0},{10,2},{12,4},{14,6},{1,9},{3,11}... | collective-permute-start | bytes 393224 | tf_op jit(solution)/shard_map/ppermute | solution.py:176
  65.5 13.2 %collective-permute-start.12 = (bf16[64,1024]{1,0:T(8,128)(2,1)S(1)}, bf16[64,1024]{1,0:T(8,128)(2,1)S(1)}, u32[]{:S(2)}, u32[]{:S(2)}) collective-permute-start(bf16[64,1024]{1,0:T(8,128)(2,1)S(1)} %fusion.2.refs_4_), channel_id=1, source_target_pairs={{0,12},{2,14},{4,8},{6,10},{8,4},{10,6},{12,0},{14,2},{1,13},{3,15... | collective-permute-start | bytes 393224 | tf_op jit(solution)/shard_map/ppermute | solution.py:176
  67.6 11.1 %collective-permute-start.6 = (bf16[16,4096]{1,0:T(8,128)(2,1)S(1)}, bf16[16,4096]{1,0:T(8,128)(2,1)S(1)}, u32[]{:S(2)}, u32[]{:S(2)}) collective-permute-start(bf16[16,4096]{1,0:T(8,128)(2,1)S(1)} %pad_maximum_fusion.3), channel_id=1, source_target_pairs={{0,12},{2,14},{4,8},{6,10},{8,4},{10,6},{12,0},{14,2},{1,13},{3,15... | collective-permute-start | bytes 393224 | tf_op jit(solution)/shard_map/ppermute | solution.py:176
  71.3 13.6 %copy-start.4 = (bf16[512,512]{1,0:T(8,128)(2,1)}, bf16[512,512]{1,0:T(8,128)(2,1)S(1)}, u32[]{:S(2)}) copy-start(bf16[512,512]{1,0:T(8,128)(2,1)S(1)} %collective-permute-done.far_ref) | copy-start | bytes 1572868
  71.3 13.5 %collective-permute-start.5 = (bf16[16,4096]{1,0:T(8,128)(2,1)S(1)}, bf16[16,4096]{1,0:T(8,128)(2,1)S(1)}, u32[]{:S(2)}, u32[]{:S(2)}) collective-permute-start(bf16[16,4096]{1,0:T(8,128)(2,1)S(1)} %pad_maximum_fusion.2), channel_id=1, source_target_pairs={{0,8},{2,10},{4,12},{6,14},{8,0},{10,2},{12,4},{14,6},{1,9},{3,11}... | collective-permute-start | bytes 393224 | tf_op jit(solution)/shard_map/ppermute | solution.py:176
  71.4 13.5 %copy-start.7 = (bf16[64,1024]{1,0:T(8,128)(2,1)}, bf16[64,1024]{1,0:T(8,128)(2,1)S(1)}, u32[]{:S(2)}) copy-start(bf16[64,1024]{1,0:T(8,128)(2,1)S(1)} %collective-permute-done.10.refs_5_) | copy-start | bytes 393220
  71.4 13.4 %collective-permute-start.4 = (bf16[16,4096]{1,0:T(8,128)(2,1)S(1)}, bf16[16,4096]{1,0:T(8,128)(2,1)S(1)}, u32[]{:S(2)}, u32[]{:S(2)}) collective-permute-start(bf16[16,4096]{1,0:T(8,128)(2,1)S(1)} %pad_maximum_fusion.1), channel_id=1, source_target_pairs={{0,4},{2,6},{4,0},{6,2},{8,12},{10,14},{12,8},{14,10},{1,5},{3,7},... | collective-permute-start | bytes 393224 | tf_op jit(solution)/shard_map/ppermute | solution.py:176
  78.6 6.3 %copy-start.8 = (bf16[64,1024]{1,0:T(8,128)(2,1)}, bf16[64,1024]{1,0:T(8,128)(2,1)S(1)}, u32[]{:S(2)}) copy-start(bf16[64,1024]{1,0:T(8,128)(2,1)S(1)} %collective-permute-done.11.refs_6_) | copy-start | bytes 393220
  78.6 6.3 %copy-start.9 = (bf16[64,1024]{1,0:T(8,128)(2,1)}, bf16[64,1024]{1,0:T(8,128)(2,1)S(1)}, u32[]{:S(2)}) copy-start(bf16[64,1024]{1,0:T(8,128)(2,1)S(1)} %collective-permute-done.12.refs_7_) | copy-start | bytes 393220
  78.6 6.3 %copy-start.10 = (bf16[16,4096]{1,0:T(8,128)(2,1)}, bf16[16,4096]{1,0:T(8,128)(2,1)S(1)}, u32[]{:S(2)}) copy-start(bf16[16,4096]{1,0:T(8,128)(2,1)S(1)} %collective-permute-done.6.refs_3_) | copy-start | bytes 393220
  84.8 0.6 copy-start.11
  85.5 0.7 copy-start.12
  91.5 5.2 %collective-permute-start.13 = (f32[64,512]{1,0:T(8,128)}, f32[64,512]{1,0:T(8,128)S(1)}, u32[]{:S(2)}, u32[]{:S(2)}) collective-permute-start(f32[64,512]{1,0:T(8,128)} %score.1), channel_id=1, source_target_pairs={{0,2},{2,0},{4,6},{6,4},{8,10},{10,8},{12,14},{14,12},{1,3},{3,1},... | collective-permute-start | bytes 393224 | tf_op jit(solution)/shard_map/ppermute | solution.py:176
  97.6 5.7 %collective-permute-start.14 = (f32[64,512]{1,0:T(8,128)S(1)}, f32[64,512]{1,0:T(8,128)S(1)}, u32[]{:S(2)}, u32[]{:S(2)}) collective-permute-start(f32[64,512]{1,0:T(8,128)S(1)} %add.100), channel_id=1, source_target_pairs={{0,4},{2,6},{4,0},{6,2},{8,12},{10,14},{12,8},{14,10},{1,5},{3,7},... | collective-permute-start | bytes 393224 | tf_op jit(solution)/shard_map/ppermute | solution.py:176
  103.3 5.5 %collective-permute-start.15 = (bf16[64,512]{1,0:T(8,128)(2,1)S(1)}, bf16[64,512]{1,0:T(8,128)(2,1)S(1)}, u32[]{:S(2)}, u32[]{:S(2)}) collective-permute-start(bf16[64,512]{1,0:T(8,128)(2,1)S(1)} %add_convert_fusion.6), channel_id=1, source_target_pairs={{0,8},{2,10},{4,12},{6,14},{8,0},{10,2},{12,4},{14,6},{1,9},{3,11}... | collective-permute-start | bytes 196616 | tf_op jit(solution)/shard_map/ppermute | solution.py:176

commit v6 on v5

v6 whole, which is shorter than its diff:
```python
import functools

import jax
import jax.numpy as jnp
from jax import lax
from jax.experimental import pallas as pl
from jax.experimental.pallas import tpu as pltpu
from jax.sharding import PartitionSpec as P

D = 8192
FF = 28672
R = 64
SEQ_DEV = 64
BUFFERS = 4
VMEM = 48 * 1024 * 1024
LAST = (((1,), (1,)), ((), ()))


def project_kernel(scale, order, first, split, who_ref, x_hbm, bits_hbm, *refs):
    sent_ref, kept_ref, bits_ref, signs_ref, x_buf, bits_sem, sems = refs[-7:]
    half, quarter = who_ref[0], who_ref[1]
    buffers, tile = x_buf.shape[0], x_buf.shape[1]
    steps = sent_ref.size // R // tile

    def copy(s, mine):
        slot = lax.rem(s + mine * steps, buffers)
        row = pl.multiple_of((half ^ 1 ^ mine) * (x_hbm.shape[0] // 2) + first + s * tile, tile)
        return pltpu.make_async_copy(x_hbm.at[pl.ds(row, tile)], x_buf.at[slot], sems.at[slot])

    bits_copy = pltpu.make_async_copy(bits_hbm, bits_ref, bits_sem)
    bits_copy.start()
    ahead = min(buffers, steps)
    for s in range(ahead):
        copy(s, 0).start()
    bits_copy.wait()
    for q in range(max(order, 1)):
        rows = R // max(order, 1)
        at = pl.multiple_of((q ^ quarter) * rows, rows) if order else 0
        signs_ref[q * rows:(q + 1) * rows, :] = (2 * bits_ref[pl.ds(at, rows), :] - 1).astype(jnp.bfloat16)

    for mine, out_ref in enumerate((sent_ref, kept_ref)):
        def one(s, carry):
            copy(s, mine).wait()
            slot = lax.rem(s + mine * steps, buffers)
            part = lax.dot_general(signs_ref[...], x_buf[slot], LAST, preferred_element_type=jnp.float32) * scale
            part = part.astype(out_ref.dtype)
            if split:
                here = pl.ds(pl.multiple_of(lax.rem(s, split) * tile, tile), tile)
                out_ref[(s // split) ^ quarter, :, here] = part
            else:
                here = pl.ds(pl.multiple_of(s * tile, tile), tile)
                out_ref[:, :, here] = part.reshape(out_ref.shape[0], out_ref.shape[1], tile)

            @pl.when(s + ahead < steps)
            def _():
                copy(s + ahead, mine).start()

            if not mine:
                @pl.when(s + ahead >= steps)
                def _():
                    copy(s + ahead - steps, 1).start()

            return carry

        lax.fori_loop(0, steps, one, 0)


def project(x, bits, who, scale, quarters, by_column, first, count, tile, after=()):
    width = x.shape[1]
    piece = count // quarters
    order, split = 0, 0
    if not by_column:
        tile = min(tile, piece)
        split = piece // tile
        shape = (quarters, R, piece)
    else:
        shape = (quarters, R // quarters, count)
        if (R // quarters) % 8:
            rows = jnp.arange(R, dtype=jnp.int32)
            bits = jnp.take(bits, rows ^ (who[1] * (R // quarters)), axis=0)
        else:
            order = quarters
    whole = pl.BlockSpec(memory_space=pltpu.VMEM)
    buffers = min(BUFFERS, count // tile)
    return pl.pallas_call(
        functools.partial(project_kernel, scale, order, first, split),
        in_specs=[pl.BlockSpec(memory_space=pltpu.SMEM)] + [pl.BlockSpec(memory_space=pl.ANY)] * (2 + len(after)),
        out_specs=[whole, whole],
        scratch_shapes=[
            pltpu.VMEM((R, width), jnp.int32),
            pltpu.VMEM((R, width), jnp.bfloat16),
            pltpu.VMEM((buffers, tile, width), jnp.bfloat16),
            pltpu.SemaphoreType.DMA,
            pltpu.SemaphoreType.DMA((buffers,)),
        ],
        out_shape=[jax.ShapeDtypeStruct(shape, jnp.bfloat16), jax.ShapeDtypeStruct(shape, jnp.float32)],
        compiler_params=pltpu.CompilerParams(vmem_limit_bytes=VMEM),
        cost_estimate=pl.CostEstimate(flops=4 * count * width * R, bytes_accessed=4 * count * width, transcendentals=0),
        name="project",
    )(who, x, bits, *after)


def fetch_all(sources, targets, sems):
    copies = [pltpu.make_async_copy(source, target, sems.at[k]) for k, (source, target) in enumerate(zip(sources, targets))]
    for copy in copies:
        copy.start()
    return copies


def merge_kernel(chunks, *refs):
    sources, outs = refs[:2 * chunks], refs[2 * chunks:-2 * chunks - 1]
    targets, sems = refs[-2 * chunks - 1:-1], refs[-1]
    copies = fetch_all(sources, targets, sems)
    at = 0
    for c in range(chunks):
        kept_ref, got_ref = targets[2 * c], targets[2 * c + 1]
        copies[2 * c].wait()
        copies[2 * c + 1].wait()
        width = kept_ref.shape[2]
        for d, out_ref in enumerate(outs):
            out_ref[:, at:at + width] = (kept_ref[d] + got_ref[d].astype(jnp.float32)).astype(out_ref.dtype)
        at = at + width


def merge(arrays):
    quarters, rows = arrays[0].shape[:2]
    tokens = sum(array.shape[2] for array in arrays[::2])
    whole = pl.BlockSpec(memory_space=pltpu.VMEM)
    return pl.pallas_call(
        functools.partial(merge_kernel, len(arrays) // 2),
        in_specs=[pl.BlockSpec(memory_space=pl.ANY)] * len(arrays),
        out_specs=[whole] * quarters,
        out_shape=[jax.ShapeDtypeStruct((rows, tokens), jnp.bfloat16 if d else jnp.float32) for d in range(quarters)],
        scratch_shapes=[pltpu.VMEM(array.shape, array.dtype) for array in arrays] + [pltpu.SemaphoreType.DMA((len(arrays),))],
        compiler_params=pltpu.CompilerParams(vmem_limit_bytes=VMEM // 6),
        cost_estimate=pl.CostEstimate(flops=quarters * rows * tokens, bytes_accessed=8 * quarters * rows * tokens, transcendentals=0),
        name="merge",
    )(*arrays)


def score_kernel(quarters, width, who_ref, *refs):
    count = 2 * quarters + 5
    sources, out_ref, targets = refs[:count], refs[count], refs[count + 1:2 * count + 1]
    sems, row_ref, col_ref, member_ref, spread_ref, sketch_ref = refs[2 * count + 1:]
    copies = fetch_all(sources, targets, sems)
    left_refs, right_refs = targets[:quarters], targets[quarters:2 * quarters]
    ids_ref, query_refs = targets[2 * quarters], targets[2 * quarters + 1:]
    half, quarter, data = who_ref[0], who_ref[1], who_ref[2]
    for copy in copies[:2 * quarters + 1]:
        copy.wait()
    total = left_refs[0][...]
    for left_ref in left_refs[1:]:
        total = total + left_ref[...].astype(jnp.float32)
    row_ref[...] = total
    piece = right_refs[0].shape[1]
    for d, right_ref in enumerate(right_refs):
        col_ref[:, pl.ds(pl.multiple_of((quarter ^ d) * piece, piece), piece)] = right_ref[...].astype(jnp.float32)
    numbers = lax.broadcasted_iota(jnp.int32, (SEQ_DEV, 1), 0)
    member_ref[...] = (ids_ref[...] == numbers).astype(jnp.bfloat16)
    rows = spread_ref.shape[0] // R
    for first in range(0, row_ref.shape[0], rows):
        for at in range(0, col_ref.shape[1], width):
            right = col_ref[:, at:at + width]
            for r in range(rows):
                spread_ref[r * R:(r + 1) * R, at:at + width] = (row_ref[first + r:first + r + 1, at:at + width] * right).astype(jnp.bfloat16)
        sketch_ref[:, first * R:(first + rows) * R] = lax.dot_general(
            member_ref[...], spread_ref[...], LAST, preferred_element_type=jnp.float32
        )
    entries = sketch_ref[...]
    high = entries.astype(jnp.bfloat16)
    low = (entries - high.astype(jnp.float32)).astype(jnp.bfloat16)
    both = jnp.concatenate([high, low], axis=0)
    middle = both.shape[1] // 2
    swapped = half == 1
    near = jnp.where(swapped, both[:, middle:], both[:, :middle])
    far = jnp.where(swapped, both[:, :middle], both[:, middle:])
    for copy in copies[2 * quarters + 1:]:
        copy.wait()
    rows = query_refs[0].shape[0]
    for side in range(2):
        part = lax.dot_general(near, query_refs[2 * side][...], LAST, preferred_element_type=jnp.float32)
        part = part + lax.dot_general(far, query_refs[2 * side + 1][...], LAST, preferred_element_type=jnp.float32)
        out_ref[:, pl.ds(pl.multiple_of((data ^ side) * rows, rows), rows)] = part[:SEQ_DEV] + part[SEQ_DEV:]


def score(who, left, right, ids, queries):
    operands = left + right + [ids] + queries
    columns, tokens = left[0].shape
    rows = min(4, columns)
    shape = (SEQ_DEV, 2 * queries[0].shape[0])
    return pl.pallas_call(
        functools.partial(score_kernel, len(left), min(512, tokens)),
        in_specs=[pl.BlockSpec(memory_space=pltpu.SMEM)] + [pl.BlockSpec(memory_space=pl.ANY)] * len(operands),
        out_specs=pl.BlockSpec(memory_space=pltpu.VMEM),
        out_shape=jax.ShapeDtypeStruct(shape, jnp.float32),
        scratch_shapes=[pltpu.VMEM(operand.shape, operand.dtype) for operand in operands]
        + [
            pltpu.SemaphoreType.DMA((len(operands),)),
            pltpu.VMEM((columns, tokens), jnp.float32),
            pltpu.VMEM((R, tokens), jnp.float32),
            pltpu.VMEM((SEQ_DEV, tokens), jnp.bfloat16),
            pltpu.VMEM((rows * R, tokens), jnp.bfloat16),
            pltpu.VMEM((SEQ_DEV, columns * R), jnp.float32),
        ],
        compiler_params=pltpu.CompilerParams(vmem_limit_bytes=VMEM // 3),
        cost_estimate=pl.CostEstimate(flops=2 * tokens * columns * R * SEQ_DEV, bytes_accessed=4 * columns * tokens, transcendentals=0),
        name="score",
    )(who, *operands)


def body(n_tensor, activations, out_grads, proj_in, proj_out, segment_ids, queries):
    quarters = n_tensor // 2
    me = lax.axis_index("tensor").astype(jnp.int32)
    half = me % 2
    who = jnp.stack([half, me // 2, lax.axis_index("dp").astype(jnp.int32)])
    owned = activations.shape[0] // 2
    early = owned * 5 // 8

    def swap(array, distance):
        return lax.ppermute(array, "tensor", [(k, k ^ distance) for k in range(n_tensor)])

    def cross(array):
        return lax.ppermute(array, "dp", [(0, 1), (1, 0)])

    far = swap(queries, 1)
    every = [queries, far, cross(queries), cross(far)]

    bits_in, bits_out = proj_in.T, proj_out.T
    scale_in, scale_out = FF ** -0.5, D ** -0.5
    sent_g, kept_g = project(out_grads, bits_out, who, scale_out, quarters, False, 0, owned, 1024)
    got_g = swap(sent_g, 1)
    sent_0, kept_0 = project(activations, bits_in, who, scale_in, quarters, True, 0, early, 512)
    got_0 = swap(sent_0, 1)
    pair_g = [kept_g[d] + got_g[d].astype(jnp.float32) for d in range(quarters)]
    pair_g = [pair_g[0]] + [pair.astype(jnp.bfloat16) for pair in pair_g[1:]]
    moved_g = [swap(pair_g[d], 2 * d) for d in range(1, quarters)]
    sent_1, kept_1 = project(activations, bits_in, who, scale_in, quarters, True, early, owned - early, 512, [pair_g[1], far])
    got_1 = swap(sent_1, 1)
    own_g = sum([moved.astype(jnp.float32) for moved in moved_g], pair_g[0]).astype(jnp.bfloat16)
    right = [own_g] + [swap(own_g, 2 * d) for d in range(1, quarters)]
    pair_a = merge([kept_0, got_0, kept_1, got_1])
    left = [pair_a[0]] + [swap(pair_a[d], 2 * d) for d in range(1, quarters)]

    ids = lax.dynamic_slice(segment_ids, (0, half * owned), (1, owned))
    total = score(who, left, right, ids, every)
    distance = 1
    while 2 * distance < n_tensor:
        total = total + swap(total, distance)
        distance = 2 * distance
    rounded = total.astype(jnp.bfloat16)
    return rounded.astype(jnp.float32) + swap(rounded, distance).astype(jnp.float32)


def solution(mesh):
    return jax.shard_map(
        functools.partial(body, mesh.shape["tensor"]),
        mesh=mesh,
        in_specs=(
            P(("copies", "dp"), "tensor"),
            P(("copies", "dp"), "tensor"),
            P("tensor", None),
            P("tensor", None),
            P(("copies", "dp"), None),
            P(("copies", "dp"), "tensor"),
        ),
        out_specs=P(("copies", "dp"), None),
        check_vma=False,
    )
```

time: 110 us -> 94 us (0.85)
  waiting for transfers between devices: 33.3 us -> 20.7 us
  starting transfers between devices: 21 us -> 30.3 us
  Pallas kernels: 45.5 us -> 39.6 us
  other arithmetic: 5.4 us -> 0.95 us
  blocking collectives: 2.17 us -> 0 us
    ppermute x16, waiting for transfers between devices: 33.3 us -> 20.7 us  [swap(): lax.ppermute(array, 'tensor', [(k, k ^ distance) for k in range(n_tensor)])]
    ppermute x16, starting transfers between devices: 21 us -> 30.2 us  [swap(): lax.ppermute(array, 'tensor', [(k, k ^ distance) for k in range(n_tensor)])]
    pallas_call x3 -> x4, Pallas kernels: 40.2 us -> 34.5 us  [the longest x3 33.6 us: project(): pl.pallas_call(functools.partial(project_kernel, scale, order, first, spl...]
    convert_element_type x2 -> x0, other arithmetic: 2.27 us -> none  [body(): part.astype(jnp.bfloat16)]
    all_gather x1 -> x0, blocking collectives: 2.17 us -> none  [body(): near = lax.all_gather(queries, 'dp', axis=0, tiled=True)]
  transfers between devices with their start and end apart: 16 -> 18, of which waited for: 7 -> 6; matrix products, arithmetic and copies ran while one was open for 3% -> 0% of each run, Pallas kernels for 27% -> 28%
where the time goes in v6:
time: 94 us; the launch traced here: 93.9 us
  Pallas kernels  39.6 us (42%)
  starting transfers between devices  30.3 us (32%)
  waiting for transfers between devices  20.7 us (22%)
  local copies, waits for them, and re-layouts  2.14 us (2%)
  other arithmetic  0.95 us (1%)
    pallas_call x3, Pallas kernels, project(): pl.pallas_call(functools.partial(project_kernel, scale, order, first, spl...  33.6 us
    ppermute x16, starting transfers between devices, swap(): lax.ppermute(array, 'tensor', [(k, k ^ distance) for k in range(n_tensor)])  30.2 us
    ppermute x16, waiting for transfers between devices, swap(): lax.ppermute(array, 'tensor', [(k, k ^ distance) for k in range(n_tensor)])  20.7 us
    pallas_call x1, Pallas kernels, score(): pl.pallas_call(functools.partial(score_kernel, len(left), min(512, tokens...  5.19 us
    unnamed x8, local copies, waits for them, and re-layouts  2.14 us
  transfers between devices with their start and end apart: 18, of which 6 were waited for; matrix products, arithmetic and copies ran while one was open for 0% of the time, Pallas kernels for 28%

profile of v6, /device:TPU:0, one launch (start us, length us, event | category | flops | bytes accessed | tf_op | source)
XLA Modules:
  0.0 93.9 jit_solution(17178092405635951239)
XLA Ops:
  0.0 0.1 pad_add_fusion.who_ref
  0.1 0.9 %copy-done.2 = s32[1024,64]{0,1:T(8,128)S(1)} copy-done((s32[1024,64]{0,1:T(8,128)S(1)}, s32[1024,64]{0,1:T(8,128)}, u32[]{:S(2)}) %copy-start.2) | copy-done | bytes 262168
  1.0 8.3 %project.4 = (bf16[4,64,1024]{2,1,0:T(8,128)(2,1)S(1)}, f32[4,64,1024]{2,1,0:T(8,128)S(1)}) custom-call(s32[3]{0:T(128)S(1)} %pad_add_fusion.who_ref, bf16[8192,1024]{1,0:T(8,128)(2,1)} %x_hbm.4, s32[64,1024]{1,0:T(8,128)S(1)} %bitcast.21), custom_call_target="tpu_custom_call" | custom-call | flops 1073741824 | bytes 16777216 | tf_op jit(solution)/shard_map/project/pallas_call | solution.py:85
  9.3 3.0 %collective-permute-start.1 = (bf16[4,64,1024]{2,1,0:T(8,128)(2,1)S(1)}, bf16[4,64,1024]{2,1,0:T(8,128)(2,1)S(1)}, u32[]{:S(2)}, u32[]{:S(2)}) collective-permute-start(bf16[4,64,1024]{2,1,0:T(8,128)(2,1)S(1)} %get-tuple-element.18), channel_id=1, source_target_pairs={{0,2},{2,0},{4,6},{6,4},{8,10},{10,8},{12,14},{14,12},{1,3},{3,1},... | collective-permute-start | bytes 1572872 | tf_op jit(solution)/shard_map/ppermute | solution.py:220
  12.4 0.1 collective-permute-start.2
  12.5 1.2 %copy-done.1 = s32[3584,64]{0,1:T(8,128)S(1)} copy-done((s32[3584,64]{0,1:T(8,128)S(1)}, s32[3584,64]{0,1:T(8,128)}, u32[]{:S(2)}) %copy-start.1) | copy-done | bytes 917528
  13.6 15.1 %project.3 = (bf16[4,16,2560]{2,1,0:T(8,128)(2,1)S(1)}, f32[4,16,2560]{2,1,0:T(8,128)S(1)}) custom-call(s32[3]{0:T(128)S(1)} %pad_add_fusion.who_ref, bf16[8192,3584]{1,0:T(8,128)(2,1)} %x_hbm.5, s32[64,3584]{1,0:T(8,128)S(1)} %bitcast.19), custom_call_target="tpu_custom_call" | custom-call | flops 2348810240 | bytes 36700160 | tf_op jit(solution)/shard_map/project/pallas_call | solution.py:85
  28.7 2.0 %collective-permute-start = (bf16[4,16,2560]{2,1,0:T(8,128)(2,1)S(1)}, bf16[4,16,2560]{2,1,0:T(8,128)(2,1)S(1)}, u32[]{:S(2)}, u32[]{:S(2)}) collective-permute-start(bf16[4,16,2560]{2,1,0:T(8,128)(2,1)S(1)} %get-tuple-element.16), channel_id=1, source_target_pairs={{0,2},{2,0},{4,6},{6,4},{8,10},{10,8},{12,14},{14,12},{1,3},{3,1},... | collective-permute-start | bytes 983048 | tf_op jit(solution)/shard_map/ppermute | solution.py:220
  30.8 0.1 fusion.4
  30.8 1.6 %collective-permute-start.7 = (bf16[64,1024]{1,0:T(8,128)(2,1)S(1)}, bf16[64,1024]{1,0:T(8,128)(2,1)S(1)}, u32[]{:S(2)}, u32[]{:S(2)}) collective-permute-start(bf16[64,1024]{1,0:T(8,128)(2,1)S(1)} %get-tuple-element.27.refs_0_), channel_id=1, source_target_pairs={{0,4},{2,6},{4,0},{6,2},{8,12},{10,14},{12,8},{14,10},{1,5},{3,7},... | collective-permute-start | bytes 393224 | tf_op jit(solution)/shard_map/ppermute | solution.py:220
  32.5 2.6 %collective-permute-start.8 = (bf16[64,1024]{1,0:T(8,128)(2,1)S(1)}, bf16[64,1024]{1,0:T(8,128)(2,1)S(1)}, u32[]{:S(2)}, u32[]{:S(2)}) collective-permute-start(bf16[64,1024]{1,0:T(8,128)(2,1)S(1)} %get-tuple-element.25), channel_id=1, source_target_pairs={{0,8},{2,10},{4,12},{6,14},{8,0},{10,2},{12,4},{14,6},{1,9},{3,11}... | collective-permute-start | bytes 393224 | tf_op jit(solution)/shard_map/ppermute | solution.py:220
  35.1 0.2 collective-permute-start.9
  35.3 10.2 %project.5 = (bf16[4,16,1536]{2,1,0:T(8,128)(2,1)S(1)}, f32[4,16,1536]{2,1,0:T(8,128)S(1)}) custom-call(s32[3]{0:T(128)S(1)} %pad_add_fusion.who_ref, bf16[8192,3584]{1,0:T(8,128)(2,1)} %x_hbm.5, s32[64,3584]{1,0:T(8,128)S(1)} %bitcast.20, bf16[64,1024]{1,0:T(8,128)(2,1)S(1)} %get-tuple-element.27.refs_0_, ...), custom_call_target="tpu_custom_call" | custom-call | flops 1409286144 | bytes 22020096 | tf_op jit(solution)/shard_map/project/pallas_call | solution.py:85
  45.6 0.3 collective-permute-start.3
  45.9 0.1 fusion.2.refs_4_
  46.0 1.9 %collective-permute-start.10 = (bf16[64,1024]{1,0:T(8,128)(2,1)S(1)}, bf16[64,1024]{1,0:T(8,128)(2,1)S(1)}, u32[]{:S(2)}, u32[]{:S(2)}) collective-permute-start(bf16[64,1024]{1,0:T(8,128)(2,1)S(1)} %fusion.2.refs_4_), channel_id=1, source_target_pairs={{0,4},{2,6},{4,0},{6,2},{8,12},{10,14},{12,8},{14,10},{1,5},{3,7},... | collective-permute-start | bytes 393224 | tf_op jit(solution)/shard_map/ppermute | solution.py:220
  47.9 2.6 %collective-permute-start.11 = (bf16[64,1024]{1,0:T(8,128)(2,1)S(1)}, bf16[64,1024]{1,0:T(8,128)(2,1)S(1)}, u32[]{:S(2)}, u32[]{:S(2)}) collective-permute-start(bf16[64,1024]{1,0:T(8,128)(2,1)S(1)} %fusion.2.refs_4_), channel_id=1, source_target_pairs={{0,8},{2,10},{4,12},{6,14},{8,0},{10,2},{12,4},{14,6},{1,9},{3,11}... | collective-permute-start | bytes 393224 | tf_op jit(solution)/shard_map/ppermute | solution.py:220
  50.5 2.4 %collective-permute-done.3.refs_3_ = bf16[4,16,1536]{2,1,0:T(8,128)(2,1)S(1)} collective-permute-done((bf16[4,16,1536]{2,1,0:T(8,128)(2,1)S(1)}, bf16[4,16,1536]{2,1,0:T(8,128)(2,1)S(1)}, u32[]{:S(2)}, u32[]{:S(2)}) %collective-permute-start.3) | collective-permute-done | bytes 196640 | tf_op jit(solution)/shard_map/ppermute | solution.py:220
  52.9 3.6 %collective-permute-start.12 = (bf16[64,1024]{1,0:T(8,128)(2,1)S(1)}, bf16[64,1024]{1,0:T(8,128)(2,1)S(1)}, u32[]{:S(2)}, u32[]{:S(2)}) collective-permute-start(bf16[64,1024]{1,0:T(8,128)(2,1)S(1)} %fusion.2.refs_4_), channel_id=1, source_target_pairs={{0,12},{2,14},{4,8},{6,10},{8,4},{10,6},{12,0},{14,2},{1,13},{3,15... | collective-permute-start | bytes 393224 | tf_op jit(solution)/shard_map/ppermute | solution.py:220
  56.5 0.9 merge.1
  57.5 0.8 collective-permute-start.5
  58.3 3.6 %collective-permute-start.6 = (bf16[16,4096]{1,0:T(8,128)(2,1)S(1)}, bf16[16,4096]{1,0:T(8,128)(2,1)S(1)}, u32[]{:S(2)}, u32[]{:S(2)}) collective-permute-start(bf16[16,4096]{1,0:T(8,128)(2,1)S(1)} %get-tuple-element.24), channel_id=1, source_target_pairs={{0,12},{2,14},{4,8},{6,10},{8,4},{10,6},{12,0},{14,2},{1,13},{3,15... | collective-permute-start | bytes 393224 | tf_op jit(solution)/shard_map/ppermute | solution.py:220
  61.9 1.4 %collective-permute-done.4.refs_1_ = bf16[16,4096]{1,0:T(8,128)(2,1)S(1)} collective-permute-done((bf16[16,4096]{1,0:T(8,128)(2,1)S(1)}, bf16[16,4096]{1,0:T(8,128)(2,1)S(1)}, u32[]{:S(2)}, u32[]{:S(2)}) %collective-permute-start.4) | collective-permute-done | bytes 131104 | tf_op jit(solution)/shard_map/ppermute | solution.py:220
  63.3 7.8 %collective-permute-done.5.refs_2_ = bf16[16,4096]{1,0:T(8,128)(2,1)S(1)} collective-permute-done((bf16[16,4096]{1,0:T(8,128)(2,1)S(1)}, bf16[16,4096]{1,0:T(8,128)(2,1)S(1)}, u32[]{:S(2)}, u32[]{:S(2)}) %collective-permute-start.5) | collective-permute-done | bytes 131104 | tf_op jit(solution)/shard_map/ppermute | solution.py:220
  71.1 5.2 %score.1 = f32[64,512]{1,0:T(8,128)S(1)} custom-call(s32[3]{0:T(128)S(1)} %pad_add_fusion.who_ref, f32[16,4096]{1,0:T(8,128)S(1)} %get-tuple-element.21.refs_0_, bf16[16,4096]{1,0:T(8,128)(2,1)S(1)} %collective-permute-done.4.refs_1_, bf16[16,4096]{1,0:T(8,128)(2,1)S(1)} %collective-permute-done.5.refs_2_, ...), custom_call_target="tpu_custom_call" | custom-call | flops 536870912 | bytes 262144 | tf_op jit(solution)/shard_map/score/pallas_call | solution.py:191
  76.3 1.7 %collective-permute-start.15 = (f32[64,512]{1,0:T(8,128)S(1)}, f32[64,512]{1,0:T(8,128)S(1)}, u32[]{:S(2)}, u32[]{:S(2)}) collective-permute-start(f32[64,512]{1,0:T(8,128)S(1)} %score.1), channel_id=1, source_target_pairs={{0,2},{2,0},{4,6},{6,4},{8,10},{10,8},{12,14},{14,12},{1,3},{3,1},... | collective-permute-start | bytes 393224 | tf_op jit(solution)/shard_map/ppermute | solution.py:220
  78.0 3.6 %collective-permute-done.15 = f32[64,512]{1,0:T(8,128)S(1)} collective-permute-done((f32[64,512]{1,0:T(8,128)S(1)}, f32[64,512]{1,0:T(8,128)S(1)}, u32[]{:S(2)}, u32[]{:S(2)}) %collective-permute-start.15) | collective-permute-done | bytes 131104 | tf_op jit(solution)/shard_map/ppermute | solution.py:220
  81.6 3.4 %collective-permute-start.16 = (f32[64,512]{1,0:T(8,128)S(1)}, f32[64,512]{1,0:T(8,128)S(1)}, u32[]{:S(2)}, u32[]{:S(2)}) collective-permute-start(f32[64,512]{1,0:T(8,128)S(1)} %add.54), channel_id=1, source_target_pairs={{0,4},{2,6},{4,0},{6,2},{8,12},{10,14},{12,8},{14,10},{1,5},{3,7},... | collective-permute-start | bytes 393224 | tf_op jit(solution)/shard_map/ppermute | solution.py:220
  85.0 2.9 %collective-permute-done.16 = f32[64,512]{1,0:T(8,128)S(1)} collective-permute-done((f32[64,512]{1,0:T(8,128)S(1)}, f32[64,512]{1,0:T(8,128)S(1)}, u32[]{:S(2)}, u32[]{:S(2)}) %collective-permute-start.16) | collective-permute-done | bytes 131104 | tf_op jit(solution)/shard_map/ppermute | solution.py:220
  88.0 2.7 %collective-permute-start.17 = (bf16[64,512]{1,0:T(8,128)(2,1)S(1)}, bf16[64,512]{1,0:T(8,128)(2,1)S(1)}, u32[]{:S(2)}, u32[]{:S(2)}) collective-permute-start(bf16[64,512]{1,0:T(8,128)(2,1)S(1)} %add_convert_fusion.3), channel_id=1, source_target_pairs={{0,8},{2,10},{4,12},{6,14},{8,0},{10,2},{12,4},{14,6},{1,9},{3,11}... | collective-permute-start | bytes 196616 | tf_op jit(solution)/shard_map/ppermute | solution.py:220
  90.7 2.5 %collective-permute-done.17 = bf16[64,512]{1,0:T(8,128)(2,1)S(1)} collective-permute-done((bf16[64,512]{1,0:T(8,128)(2,1)S(1)}, bf16[64,512]{1,0:T(8,128)(2,1)S(1)}, u32[]{:S(2)}, u32[]{:S(2)}) %collective-permute-start.17) | collective-permute-done | bytes 65568 | tf_op jit(solution)/shard_map/ppermute | solution.py:220
  93.2 0.7 convert_add_fusion
  (24 shorter events, 0.2 us)
Async XLA Ops:
  0.0 61.9 %copy-start = (s32[1,8192]{1,0:T(1,128)S(1)}, s32[1,8192]{1,0:T(1,128)}, u32[]{:S(2)}) copy-start(s32[1,8192]{1,0:T(1,128)} %param.10) | copy-start | bytes 98308
  0.1 1.0 %copy-start.2 = (s32[1024,64]{0,1:T(8,128)S(1)}, s32[1024,64]{0,1:T(8,128)}, u32[]{:S(2)}) copy-start(s32[1024,64]{0,1:T(8,128)} %param.9) | copy-start | bytes 786436
  9.3 21.4 %collective-permute-start.1 = (bf16[4,64,1024]{2,1,0:T(8,128)(2,1)S(1)}, bf16[4,64,1024]{2,1,0:T(8,128)(2,1)S(1)}, u32[]{:S(2)}, u32[]{:S(2)}) collective-permute-start(bf16[4,64,1024]{2,1,0:T(8,128)(2,1)S(1)} %get-tuple-element.18), channel_id=1, source_target_pairs={{0,2},{2,0},{4,6},{6,4},{8,10},{10,8},{12,14},{14,12},{1,3},{3,1},... | collective-permute-start | bytes 1572872 | tf_op jit(solution)/shard_map/ppermute | solution.py:220
  12.4 22.7 %collective-permute-start.2 = (bf16[256,512]{1,0:T(8,128)(2,1)}, bf16[256,512]{1,0:T(8,128)(2,1)S(1)}, u32[]{:S(2)}, u32[]{:S(2)}) collective-permute-start(bf16[256,512]{1,0:T(8,128)(2,1)} %refs_9_.1), channel_id=1, source_target_pairs={{0,2},{2,0},{4,6},{6,4},{8,10},{10,8},{12,14},{14,12},{1,3},{3,1},... | collective-permute-start | bytes 786440 | tf_op jit(solution)/shard_map/ppermute | solution.py:220
  12.5 44.9 %collective-permute-start.13 = (bf16[256,512]{1,0:T(8,128)(2,1)}, bf16[256,512]{1,0:T(8,128)(2,1)S(1)}, u32[]{:S(2)}, u32[]{:S(2)}) collective-permute-start(bf16[256,512]{1,0:T(8,128)(2,1)} %refs_9_.1), channel_id=1, source_target_pairs={{0,1},{1,0},{2,3},{3,2},{4,5},{5,4},{6,7},{7,6},{8,9},{9,8},{10,11... | collective-permute-start | bytes 786440 | tf_op jit(solution)/shard_map/ppermute | solution.py:223
  12.5 1.2 %copy-start.1 = (s32[3584,64]{0,1:T(8,128)S(1)}, s32[3584,64]{0,1:T(8,128)}, u32[]{:S(2)}) copy-start(s32[3584,64]{0,1:T(8,128)} %param.8) | copy-start | bytes 2752516
  13.6 57.5 %copy-start.3 = (bf16[256,512]{1,0:T(8,128)(2,1)S(1)}, bf16[256,512]{1,0:T(8,128)(2,1)}, u32[]{:S(2)}) copy-start(bf16[256,512]{1,0:T(8,128)(2,1)} %refs_9_.1) | copy-start | bytes 786436
  28.7 19.2 %collective-permute-start = (bf16[4,16,2560]{2,1,0:T(8,128)(2,1)S(1)}, bf16[4,16,2560]{2,1,0:T(8,128)(2,1)S(1)}, u32[]{:S(2)}, u32[]{:S(2)}) collective-permute-start(bf16[4,16,2560]{2,1,0:T(8,128)(2,1)S(1)} %get-tuple-element.16), channel_id=1, source_target_pairs={{0,2},{2,0},{4,6},{6,4},{8,10},{10,8},{12,14},{14,12},{1,3},{3,1},... | collective-permute-start | bytes 983048 | tf_op jit(solution)/shard_map/ppermute | solution.py:220
  30.8 14.7 %collective-permute-start.7 = (bf16[64,1024]{1,0:T(8,128)(2,1)S(1)}, bf16[64,1024]{1,0:T(8,128)(2,1)S(1)}, u32[]{:S(2)}, u32[]{:S(2)}) collective-permute-start(bf16[64,1024]{1,0:T(8,128)(2,1)S(1)} %get-tuple-element.27.refs_0_), channel_id=1, source_target_pairs={{0,4},{2,6},{4,0},{6,2},{8,12},{10,14},{12,8},{14,10},{1,5},{3,7},... | collective-permute-start | bytes 393224 | tf_op jit(solution)/shard_map/ppermute | solution.py:220
  32.5 13.1 %collective-permute-start.8 = (bf16[64,1024]{1,0:T(8,128)(2,1)S(1)}, bf16[64,1024]{1,0:T(8,128)(2,1)S(1)}, u32[]{:S(2)}, u32[]{:S(2)}) collective-permute-start(bf16[64,1024]{1,0:T(8,128)(2,1)S(1)} %get-tuple-element.25), channel_id=1, source_target_pairs={{0,8},{2,10},{4,12},{6,14},{8,0},{10,2},{12,4},{14,6},{1,9},{3,11}... | collective-permute-start | bytes 393224 | tf_op jit(solution)/shard_map/ppermute | solution.py:220
  35.1 10.9 %collective-permute-start.9 = (bf16[64,1024]{1,0:T(8,128)(2,1)S(1)}, bf16[64,1024]{1,0:T(8,128)(2,1)S(1)}, u32[]{:S(2)}, u32[]{:S(2)}) collective-permute-start(bf16[64,1024]{1,0:T(8,128)(2,1)S(1)} %get-tuple-element.26), channel_id=1, source_target_pairs={{0,12},{2,14},{4,8},{6,10},{8,4},{10,6},{12,0},{14,2},{1,13},{3,15... | collective-permute-start | bytes 393224 | tf_op jit(solution)/shard_map/ppermute | solution.py:220
  45.5 12.0 %collective-permute-start.14 = (bf16[256,512]{1,0:T(8,128)(2,1)S(1)}, bf16[256,512]{1,0:T(8,128)(2,1)S(1)}, u32[]{:S(2)}, u32[]{:S(2)}) collective-permute-start(bf16[256,512]{1,0:T(8,128)(2,1)S(1)} %collective-permute-done.2.refs_1_.refs_10_), channel_id=1, source_target_pairs={{0,1},{1,0},{2,3},{3,2},{4,5},{5,4},{6,7},{7,6},{8,9},{9,8},{10,11... | collective-permute-start | bytes 786440 | tf_op jit(solution)/shard_map/ppermute | solution.py:223
  45.6 7.3 %collective-permute-start.3 = (bf16[4,16,1536]{2,1,0:T(8,128)(2,1)S(1)}, bf16[4,16,1536]{2,1,0:T(8,128)(2,1)S(1)}, u32[]{:S(2)}, u32[]{:S(2)}) collective-permute-start(bf16[4,16,1536]{2,1,0:T(8,128)(2,1)S(1)} %get-tuple-element.20), channel_id=1, source_target_pairs={{0,2},{2,0},{4,6},{6,4},{8,10},{10,8},{12,14},{14,12},{1,3},{3,1},... | collective-permute-start | bytes 589832 | tf_op jit(solution)/shard_map/ppermute | solution.py:220
  46.0 12.2 %collective-permute-start.10 = (bf16[64,1024]{1,0:T(8,128)(2,1)S(1)}, bf16[64,1024]{1,0:T(8,128)(2,1)S(1)}, u32[]{:S(2)}, u32[]{:S(2)}) collective-permute-start(bf16[64,1024]{1,0:T(8,128)(2,1)S(1)} %fusion.2.refs_4_), channel_id=1, source_target_pairs={{0,4},{2,6},{4,0},{6,2},{8,12},{10,14},{12,8},{14,10},{1,5},{3,7},... | collective-permute-start | bytes 393224 | tf_op jit(solution)/shard_map/ppermute | solution.py:220
  47.9 13.9 %collective-permute-start.11 = (bf16[64,1024]{1,0:T(8,128)(2,1)S(1)}, bf16[64,1024]{1,0:T(8,128)(2,1)S(1)}, u32[]{:S(2)}, u32[]{:S(2)}) collective-permute-start(bf16[64,1024]{1,0:T(8,128)(2,1)S(1)} %fusion.2.refs_4_), channel_id=1, source_target_pairs={{0,8},{2,10},{4,12},{6,14},{8,0},{10,2},{12,4},{14,6},{1,9},{3,11}... | collective-permute-start | bytes 393224 | tf_op jit(solution)/shard_map/ppermute | solution.py:220
  52.9 9.0 %collective-permute-start.12 = (bf16[64,1024]{1,0:T(8,128)(2,1)S(1)}, bf16[64,1024]{1,0:T(8,128)(2,1)S(1)}, u32[]{:S(2)}, u32[]{:S(2)}) collective-permute-start(bf16[64,1024]{1,0:T(8,128)(2,1)S(1)} %fusion.2.refs_4_), channel_id=1, source_target_pairs={{0,12},{2,14},{4,8},{6,10},{8,4},{10,6},{12,0},{14,2},{1,13},{3,15... | collective-permute-start | bytes 393224 | tf_op jit(solution)/shard_map/ppermute | solution.py:220
  57.4 5.8 %collective-permute-start.4 = (bf16[16,4096]{1,0:T(8,128)(2,1)S(1)}, bf16[16,4096]{1,0:T(8,128)(2,1)S(1)}, u32[]{:S(2)}, u32[]{:S(2)}) collective-permute-start(bf16[16,4096]{1,0:T(8,128)(2,1)S(1)} %get-tuple-element.22), channel_id=1, source_target_pairs={{0,4},{2,6},{4,0},{6,2},{8,12},{10,14},{12,8},{14,10},{1,5},{3,7},... | collective-permute-start | bytes 393224 | tf_op jit(solution)/shard_map/ppermute | solution.py:220
  57.5 13.6 %collective-permute-start.5 = (bf16[16,4096]{1,0:T(8,128)(2,1)S(1)}, bf16[16,4096]{1,0:T(8,128)(2,1)S(1)}, u32[]{:S(2)}, u32[]{:S(2)}) collective-permute-start(bf16[16,4096]{1,0:T(8,128)(2,1)S(1)} %get-tuple-element.23), channel_id=1, source_target_pairs={{0,8},{2,10},{4,12},{6,14},{8,0},{10,2},{12,4},{14,6},{1,9},{3,11}... | collective-permute-start | bytes 393224 | tf_op jit(solution)/shard_map/ppermute | solution.py:220
  58.3 12.8 %collective-permute-start.6 = (bf16[16,4096]{1,0:T(8,128)(2,1)S(1)}, bf16[16,4096]{1,0:T(8,128)(2,1)S(1)}, u32[]{:S(2)}, u32[]{:S(2)}) collective-permute-start(bf16[16,4096]{1,0:T(8,128)(2,1)S(1)} %get-tuple-element.24), channel_id=1, source_target_pairs={{0,12},{2,14},{4,8},{6,10},{8,4},{10,6},{12,0},{14,2},{1,13},{3,15... | collective-permute-start | bytes 393224 | tf_op jit(solution)/shard_map/ppermute | solution.py:220
  76.3 5.2 %collective-permute-start.15 = (f32[64,512]{1,0:T(8,128)S(1)}, f32[64,512]{1,0:T(8,128)S(1)}, u32[]{:S(2)}, u32[]{:S(2)}) collective-permute-start(f32[64,512]{1,0:T(8,128)S(1)} %score.1), channel_id=1, source_target_pairs={{0,2},{2,0},{4,6},{6,4},{8,10},{10,8},{12,14},{14,12},{1,3},{3,1},... | collective-permute-start | bytes 393224 | tf_op jit(solution)/shard_map/ppermute | solution.py:220
  81.6 6.4 %collective-permute-start.16 = (f32[64,512]{1,0:T(8,128)S(1)}, f32[64,512]{1,0:T(8,128)S(1)}, u32[]{:S(2)}, u32[]{:S(2)}) collective-permute-start(f32[64,512]{1,0:T(8,128)S(1)} %add.54), channel_id=1, source_target_pairs={{0,4},{2,6},{4,0},{6,2},{8,12},{10,14},{12,8},{14,10},{1,5},{3,7},... | collective-permute-start | bytes 393224 | tf_op jit(solution)/shard_map/ppermute | solution.py:220
  88.0 5.2 %collective-permute-start.17 = (bf16[64,512]{1,0:T(8,128)(2,1)S(1)}, bf16[64,512]{1,0:T(8,128)(2,1)S(1)}, u32[]{:S(2)}, u32[]{:S(2)}) collective-permute-start(bf16[64,512]{1,0:T(8,128)(2,1)S(1)} %add_convert_fusion.3), channel_id=1, source_target_pairs={{0,8},{2,10},{4,12},{6,14},{8,0},{10,2},{12,4},{14,6},{1,9},{3,11}... | collective-permute-start | bytes 196616 | tf_op jit(solution)/shard_map/ppermute | solution.py:220

commit v7 on v6

v7 whole, which is shorter than its diff:
```python
import functools
import math

import jax
import jax.numpy as jnp
from jax import lax
from jax.experimental import pallas as pl
from jax.experimental.pallas import tpu as pltpu
from jax.sharding import PartitionSpec as P

D = 8192
FF = 28672
R = 64
SEQ_DEV = 64
BUFFERS = 4
VMEM = 48 * 1024 * 1024
LAST = (((1,), (1,)), ((), ()))


def project_kernel(scale, first, split, order, direct, makes, waits, who_ref, x_hbm, sign_source, *refs):
    outs = 1 if direct else 2
    other_source, refs = refs[0], refs[makes + waits:]
    out_refs, refs = refs[:outs], refs[outs:]
    made_ref, refs = refs[0], refs[makes:]
    bits_ref, other_ref = refs[0], refs[1]
    signs_ref, x_buf, sign_sem, sems = refs[-4:]
    half, quarter = who_ref[0], who_ref[1]
    buffers, tile = x_buf.shape[0], x_buf.shape[1]
    subs = sems.shape[1]
    sub = tile // subs
    steps = out_refs[0].size // (R * tile) // (2 if direct else 1)

    def copies(p):
        mine = (p >= steps).astype(jnp.int32) if isinstance(p, jax.Array) else int(p >= steps)
        side = mine if direct else half ^ 1 ^ mine
        slot = lax.rem(p, buffers)
        row = pl.multiple_of(side * (x_hbm.shape[0] // 2) + first + (p - mine * steps) * tile, sub)
        return [
            pltpu.make_async_copy(x_hbm.at[pl.ds(row + h * sub, sub)], x_buf.at[slot, pl.ds(h * sub, sub)], sems.at[slot, h])
            for h in range(subs)
        ]

    sign_copy = pltpu.make_async_copy(sign_source, bits_ref, sign_sem.at[0])
    if makes:
        other_copy = pltpu.make_async_copy(other_source, other_ref, sign_sem.at[1])
    sign_copy.start()
    for p in range(min(buffers, 2 * steps)):
        for copy in copies(p):
            copy.start()
    if makes:
        other_copy.start()
    sign_copy.wait()
    if makes:
        signs_ref[...] = (2 * bits_ref[...] - 1).astype(jnp.bfloat16)
    else:
        rows = R // max(order, 1)
        for q in range(max(order, 1)):
            at = pl.multiple_of((q ^ quarter) * rows, rows) if order else 0
            signs_ref[q * rows:(q + 1) * rows, :] = bits_ref[pl.ds(at, rows), :]

    def product(p, mine, at, size):
        s = p - mine * steps
        slot = lax.rem(p, buffers)
        part = lax.dot_general(
            signs_ref[...], x_buf[slot, at:at + size, :], LAST, preferred_element_type=jnp.float32
        ) * scale
        out_ref = out_refs[0] if direct else out_refs[mine]
        part = part.astype(out_ref.dtype)
        if split:
            here = pl.ds(pl.multiple_of(lax.rem(s, split) * tile + at, size), size)
            out_ref[s // split, mine, :, here] = part
        else:
            here = pl.ds(pl.multiple_of(s * tile + at, size), size)
            if direct:
                out_ref[:, mine, :, here] = part.reshape(out_ref.shape[0], out_ref.shape[2], size)
            else:
                out_ref[:, :, here] = part.reshape(out_ref.shape[0], out_ref.shape[1], size)

    def one(p, mine):
        for copy in copies(p):
            copy.wait()
        product(p, mine, 0, tile)

        @pl.when(p + buffers < 2 * steps)
        def _():
            for copy in copies(p + buffers):
                copy.start()

    def halves(p, mine):
        for h, copy in enumerate(copies(p)):
            copy.wait()
            product(p, mine, h * sub, sub)
        if p + buffers < 2 * steps:
            for copy in copies(p + buffers):
                copy.start()

    def run(low, high, mine):
        def loop(p, carry):
            one(p, mine)
            return carry

        lax.fori_loop(low, high, loop, 0)

    halves(0, 0)
    run(1, steps, 0)
    run(steps, 2 * steps - 1, 1)
    halves(2 * steps - 1, 1)
    if makes:
        other_copy.wait()
        made_ref[...] = (2 * other_ref[...] - 1).astype(jnp.bfloat16)


def project(x, signs, who, scale, quarters, by_column, direct, first, count, tile, other=None, after=()):
    width = x.shape[1]
    piece = count // quarters
    order, split = 0, 0
    makes = other is not None
    if by_column:
        shape = (quarters, R // quarters, count)
        if not direct and (R // quarters) % 16:
            rows = jnp.arange(R, dtype=jnp.int32)
            signs = jnp.take(signs, rows ^ (who[1] * (R // quarters)), axis=0)
        elif not direct:
            order = quarters
    else:
        tile = min(tile, piece)
        split = piece // tile
        shape = (quarters, R, piece)
    if direct:
        shapes = [jax.ShapeDtypeStruct((quarters, 2) + shape[1:], jnp.bfloat16)]
    else:
        shapes = [jax.ShapeDtypeStruct(shape, jnp.bfloat16), jax.ShapeDtypeStruct(shape, jnp.float32)]
    scratch = [pltpu.VMEM(signs.shape, signs.dtype)]
    if makes:
        shapes.append(jax.ShapeDtypeStruct(other.shape, jnp.bfloat16))
        scratch.append(pltpu.VMEM(other.shape, other.dtype))
    hbm = pl.BlockSpec(memory_space=pltpu.HBM)
    buffers = min(BUFFERS, 2 * (count // tile))
    subs = 2 if tile % 256 == 0 else 1
    operands = [x, signs] + ([other] if makes else []) + list(after)
    specs = [hbm, hbm if makes else pl.BlockSpec(memory_space=pl.ANY)] + ([hbm] if makes else [])
    return pl.pallas_call(
        functools.partial(project_kernel, scale, first, split, order, direct, int(makes), len(after)),
        in_specs=[pl.BlockSpec(memory_space=pltpu.SMEM)] + specs + [pl.BlockSpec(memory_space=pl.ANY)] * len(after),
        out_specs=[pl.BlockSpec(memory_space=pltpu.VMEM)] * len(shapes),
        scratch_shapes=scratch
        + [
            pltpu.VMEM(signs.shape, jnp.bfloat16),
            pltpu.VMEM((buffers, tile, width), jnp.bfloat16),
            pltpu.SemaphoreType.DMA((2,)),
            pltpu.SemaphoreType.DMA((buffers, subs)),
        ],
        out_shape=shapes,
        compiler_params=pltpu.CompilerParams(vmem_limit_bytes=VMEM),
        cost_estimate=pl.CostEstimate(flops=4 * count * width * R, bytes_accessed=4 * count * width, transcendentals=0),
        name="project",
    )(who, *operands)


def fetch_all(sources, targets, sems):
    copies = [pltpu.make_async_copy(source, target, sems.at[k]) for k, (source, target) in enumerate(zip(sources, targets))]
    for copy in copies:
        copy.start()
    return copies


def merge_kernel(chunks, *refs):
    sources, outs = refs[:2 * chunks], refs[2 * chunks:-2 * chunks - 1]
    targets, sems = refs[-2 * chunks - 1:-1], refs[-1]
    copies = fetch_all(sources, targets, sems)
    at = 0
    for c in range(chunks):
        kept_ref, got_ref = targets[2 * c], targets[2 * c + 1]
        copies[2 * c].wait()
        copies[2 * c + 1].wait()
        width = kept_ref.shape[2]
        for d, out_ref in enumerate(outs):
            out_ref[:, at:at + width] = (kept_ref[d] + got_ref[d].astype(jnp.float32)).astype(out_ref.dtype)
        at = at + width


def merge(arrays):
    quarters, rows = arrays[0].shape[:2]
    tokens = sum(array.shape[2] for array in arrays[::2])
    whole = pl.BlockSpec(memory_space=pltpu.VMEM)
    return pl.pallas_call(
        functools.partial(merge_kernel, len(arrays) // 2),
        in_specs=[pl.BlockSpec(memory_space=pl.ANY)] * len(arrays),
        out_specs=[whole] * quarters,
        out_shape=[jax.ShapeDtypeStruct((rows, tokens), jnp.bfloat16 if d else jnp.float32) for d in range(quarters)],
        scratch_shapes=[pltpu.VMEM(array.shape, array.dtype) for array in arrays] + [pltpu.SemaphoreType.DMA((len(arrays),))],
        compiler_params=pltpu.CompilerParams(vmem_limit_bytes=VMEM // 6),
        cost_estimate=pl.CostEstimate(flops=quarters * rows * tokens, bytes_accessed=8 * quarters * rows * tokens, transcendentals=0),
        name="merge",
    )(*arrays)


def add_sources(refs, stacked):
    parts = [refs[0][k] for k in range(refs[0].shape[0])] if stacked else [ref[...] for ref in refs]
    return sum([part.astype(jnp.float32) for part in parts[1:]], parts[0].astype(jnp.float32))


def sketch_rows(half, quarter, first, left_refs, right_refs, ids_ref, base_ref, stores, scratch):
    row_ref, col_ref, member_ref, spread_ref = scratch
    owned = ids_ref.shape[1] // 2
    tokens = row_ref.shape[1]
    width = math.gcd(tokens, 512)
    row_ref[...] = add_sources(left_refs, len(left_refs) == 1)
    piece = right_refs[0].shape[1]
    for d, right_ref in enumerate(right_refs):
        col_ref[:, pl.ds(pl.multiple_of((quarter ^ d) * piece, piece), piece)] = right_ref[...].astype(jnp.float32)
    numbers = lax.broadcasted_iota(jnp.int32, (SEQ_DEV, 1), 0)
    ids = ids_ref[:, pl.ds(pl.multiple_of(half * owned + first, 128), tokens)]
    member_ref[...] = (ids == numbers).astype(jnp.bfloat16)
    rows = spread_ref.shape[0] // R
    for top in range(0, row_ref.shape[0], rows):
        for at in range(0, tokens, width):
            right = col_ref[:, first + at:first + at + width]
            for r in range(rows):
                spread_ref[r * R:(r + 1) * R, at:at + width] = (row_ref[top + r:top + r + 1, at:at + width] * right).astype(jnp.bfloat16)
        part = lax.dot_general(member_ref[...], spread_ref[...], LAST, preferred_element_type=jnp.float32)
        here = slice(top * R, (top + rows) * R)
        stores[:, here] = part if base_ref is None else base_ref[:, here] + part


def sketch_kernel(quarters, lefts, first, who_ref, *refs):
    count = lefts + quarters + 1
    sources, out_ref, targets = refs[:count], refs[count], refs[count + 1:2 * count + 1]
    copies = fetch_all(sources, targets, refs[2 * count + 1])
    for copy in copies:
        copy.wait()
    sketch_rows(who_ref[0], who_ref[1], first, targets[:lefts], targets[lefts:-1], targets[-1], None, out_ref, refs[2 * count + 2:])


def score_kernel(quarters, lefts, first, who_ref, *refs):
    count = lefts + quarters + 6
    sources, out_ref, targets = refs[:count], refs[count], refs[count + 1:2 * count + 1]
    sketch_ref, scratch = refs[2 * count + 2], refs[2 * count + 3:]
    copies = fetch_all(sources, targets, refs[2 * count + 1])
    half, quarter, data = who_ref[0], who_ref[1], who_ref[2]
    for copy in copies[:-4]:
        copy.wait()
    sketch_rows(half, quarter, first, targets[:lefts], targets[lefts:-6], targets[-6], targets[-5], sketch_ref, scratch)
    entries = sketch_ref[...]
    high = entries.astype(jnp.bfloat16)
    low = (entries - high.astype(jnp.float32)).astype(jnp.bfloat16)
    both = jnp.concatenate([high, low], axis=0)
    middle = both.shape[1] // 2
    swapped = half == 1
    near = jnp.where(swapped, both[:, middle:], both[:, :middle])
    far = jnp.where(swapped, both[:, :middle], both[:, middle:])
    for copy in copies[-4:]:
        copy.wait()
    query_refs = targets[-4:]
    rows = query_refs[0].shape[0]
    for side in range(2):
        part = lax.dot_general(near, query_refs[2 * side][...], LAST, preferred_element_type=jnp.float32)
        part = part + lax.dot_general(far, query_refs[2 * side + 1][...], LAST, preferred_element_type=jnp.float32)
        out_ref[:, pl.ds(pl.multiple_of((data ^ side) * rows, rows), rows)] = part[:SEQ_DEV] + part[SEQ_DEV:]


def call_sketch(kernel, first, who, left, right, rest, shape, extra):
    operands = left + right + rest
    columns, tokens = left[0].shape[-2:]
    rows = min(4, columns)
    return pl.pallas_call(
        functools.partial(kernel, len(right), len(left), first),
        in_specs=[pl.BlockSpec(memory_space=pltpu.SMEM)] + [pl.BlockSpec(memory_space=pl.ANY)] * len(operands),
        out_specs=pl.BlockSpec(memory_space=pltpu.VMEM),
        out_shape=jax.ShapeDtypeStruct(shape, jnp.float32),
        scratch_shapes=[pltpu.VMEM(operand.shape, operand.dtype) for operand in operands]
        + [pltpu.SemaphoreType.DMA((len(operands),))]
        + extra
        + [
            pltpu.VMEM((columns, tokens), jnp.float32),
            pltpu.VMEM((R, rest[0].shape[1] // 2), jnp.float32),
            pltpu.VMEM((SEQ_DEV, tokens), jnp.bfloat16),
            pltpu.VMEM((rows * R, tokens), jnp.bfloat16),
        ],
        compiler_params=pltpu.CompilerParams(vmem_limit_bytes=VMEM // 3),
        cost_estimate=pl.CostEstimate(flops=2 * tokens * columns * R * SEQ_DEV, bytes_accessed=4 * columns * tokens, transcendentals=0),
        name="sketch" if not extra else "score",
    )(who, *operands)


def body(n_tensor, activations, out_grads, proj_in, proj_out, segment_ids, queries):
    quarters = n_tensor // 2
    me = lax.axis_index("tensor").astype(jnp.int32)
    half = me % 2
    who = jnp.stack([half, me // 2, lax.axis_index("dp").astype(jnp.int32)])
    owned = activations.shape[0] // 2
    early = owned * 3 // 4

    def swap(array, distance):
        return lax.ppermute(array, "tensor", [(k, k ^ distance) for k in range(n_tensor)])

    def cross(array):
        return lax.ppermute(array, "dp", [(0, 1), (1, 0)])

    far = swap(queries, 1)
    every = [queries, far, cross(queries), cross(far)]

    bits_in, bits_out = proj_in.T, proj_out.T
    scale_in, scale_out = FF ** -0.5, D ** -0.5
    part_g, signs_in = project(out_grads, bits_out, who, scale_out, quarters, False, True, 0, owned, 1024, bits_in)
    moved_g = lax.all_to_all(part_g.reshape((n_tensor,) + part_g.shape[2:]), "tensor", 0, 0)
    sent_0, kept_0 = project(activations, signs_in, who, scale_in, quarters, True, False, 0, early, 512)
    got_0 = swap(sent_0, 1)
    own_g = sum([moved_g[k].astype(jnp.float32) for k in range(1, n_tensor)], moved_g[0].astype(jnp.float32)).astype(jnp.bfloat16)
    right = [own_g] + [swap(own_g, 2 * d) for d in range(1, quarters)]
    late = owned - early
    part_1 = project(activations, signs_in, who, scale_in, quarters, True, True, early, late, 512, None, [own_g, far])[0]
    pair_0 = merge([kept_0, got_0])
    left_0 = [pair_0[0]] + [swap(pair_0[d], 2 * d) for d in range(1, quarters)]
    left_1 = [lax.all_to_all(part_1.reshape((n_tensor,) + part_1.shape[2:]), "tensor", 0, 0)]

    entries = R // quarters * R
    base = call_sketch(sketch_kernel, 0, who, left_0, right, [segment_ids], (SEQ_DEV, entries), [])
    rest = [segment_ids, base] + every
    shape = (SEQ_DEV, 2 * queries.shape[0])
    total = call_sketch(score_kernel, early, who, left_1, right, rest, shape, [pltpu.VMEM((SEQ_DEV, entries), jnp.float32)])
    distance = 1
    while 2 * distance < n_tensor:
        total = total + swap(total, distance)
        distance = 2 * distance
    rounded = total.astype(jnp.bfloat16)
    return rounded.astype(jnp.float32) + swap(rounded, distance).astype(jnp.float32)


def solution(mesh):
    return jax.shard_map(
        functools.partial(body, mesh.shape["tensor"]),
        mesh=mesh,
        in_specs=(
            P(("copies", "dp"), "tensor"),
            P(("copies", "dp"), "tensor"),
            P("tensor", None),
            P("tensor", None),
            P(("copies", "dp"), None),
            P(("copies", "dp"), "tensor"),
        ),
        out_specs=P(("copies", "dp"), None),
        check_vma=False,
    )
```

time: 94 us -> 111 us (1.18)
  waiting for transfers between devices: 20.7 us -> 36.9 us
  starting transfers between devices: 30.3 us -> 24.4 us
  Pallas kernels: 39.6 us -> 45.3 us
  other arithmetic: 0.95 us -> 2.24 us
    ppermute x16 -> x11, starting transfers between devices: 30.2 us -> 13 us  [swap(): lax.ppermute(array, 'tensor', [(k, k ^ distance) for k in range(n_tensor)])]
    ppermute x16 -> x11, waiting for transfers between devices: 20.7 us -> 32.2 us  [swap(): lax.ppermute(array, 'tensor', [(k, k ^ distance) for k in range(n_tensor)])]
    all_to_all x0 -> x2, starting transfers between devices: none -> 10.9 us  [the longest x1 7.3 us: body(): lax.all_to_all(part_g.reshape((n_tensor,) + part_g.shape[2:]), 'tensor',...]
    pallas_call x4 -> x5, Pallas kernels: 38.8 us -> 45 us  [the longest x3 38.1 us: project(): pl.pallas_call(functools.partial(project_kernel, scale, first, split, ord...]
    all_to_all x0 -> x2, waiting for transfers between devices: none -> 4.75 us  [the longest x1 4.75 us: body(): lax.all_to_all(part_g.reshape((n_tensor,) + part_g.shape[2:]), 'tensor',...]
    convert_element_type x2 -> x1, other arithmetic: 0.17 us -> 1.45 us  [body(): sum([moved_g[k].astype(jnp.float32) for k in range(1, n_tensor)], moved_g...]
  transfers between devices with their start and end apart: 18 -> 15, of which waited for: 6 -> 7; matrix products, arithmetic and copies ran while one was open for 0% -> 1% of each run, Pallas kernels for 28% -> 30%
where the time goes in v7:
time: 111 us
  Pallas kernels  45.3 us (41%)
  waiting for transfers between devices  36.9 us (33%)
  starting transfers between devices  24.4 us (22%)
  other arithmetic  2.24 us (2%)
  local copies, waits for them, and re-layouts  2.14 us (2%)
    pallas_call x3, Pallas kernels, project(): pl.pallas_call(functools.partial(project_kernel, scale, first, split, ord...  38.1 us
    ppermute x11, waiting for transfers between devices, swap(): lax.ppermute(array, 'tensor', [(k, k ^ distance) for k in range(n_tensor)])  32.2 us
    ppermute x11, starting transfers between devices, swap(): lax.ppermute(array, 'tensor', [(k, k ^ distance) for k in range(n_tensor)])  13 us
    all_to_all x1, starting transfers between devices, body(): lax.all_to_all(part_g.reshape((n_tensor,) + part_g.shape[2:]), 'tensor',...  7.3 us
    pallas_call x2, Pallas kernels, call_sketch(): pl.pallas_call(functools.partial(kernel, len(right), len(left), first), i...  6.89 us
    all_to_all x1, waiting for transfers between devices, body(): lax.all_to_all(part_g.reshape((n_tensor,) + part_g.shape[2:]), 'tensor',...  4.75 us
    all_to_all x1, starting transfers between devices, body(): lax.all_to_all(part_1.reshape((n_tensor,) + part_1.shape[2:]), 'tensor',...  3.6 us
  transfers between devices with their start and end apart: 15, of which 7 were waited for; matrix products, arithmetic and copies ran while one was open for 1% of the time, Pallas kernels for 30%

profile of v7, /device:TPU:0, one launch (start us, length us, event | category | flops | bytes accessed | tf_op | source)
XLA Modules:
  0.0 111.1 jit_solution(16724039070159150711)
XLA Ops:
  0.0 0.1 pad_add_fusion.who_ref
  0.1 1.2 %copy-done = s32[3584,64]{0,1:T(8,128)S(1)} copy-done((s32[3584,64]{0,1:T(8,128)S(1)}, s32[3584,64]{0,1:T(8,128)}, u32[]{:S(2)}) %copy-start) | copy-done | bytes 917528
  1.3 0.9 copy-done.2
  2.2 9.3 %project.3 = (bf16[4,2,64,1024]{3,2,1,0:T(8,128)(2,1)}, bf16[64,3584]{1,0:T(8,128)(2,1)S(1)}) custom-call(s32[3]{0:T(128)S(1)} %pad_add_fusion.who_ref, bf16[8192,1024]{1,0:T(8,128)(2,1)} %x_hbm.3, s32[64,1024]{1,0:T(8,128)S(1)} %bitcast.10, s32[64,3584]{1,0:T(8,128)S(1)} %bitcast.9), custom_call_target="tpu_custom_call" | custom-call | flops 1073741824 | bytes 16777216 | tf_op jit(solution)/shard_map/project/pallas_call | solution.py:142
  11.5 7.3 %all-to-all-start = ((bf16[8,64,1024]{2,1,0:T(8,128)(2,1)}), bf16[8,64,1024]{2,1,0:T(8,128)(2,1)}, u32[]{:S(2)}, u32[]{:S(2)}) async-start(bf16[8,64,1024]{2,1,0:T(8,128)(2,1)} %bitcast.5), calls=%async_computation | async-start | bytes 2097152 | tf_op jit(solution)/shard_map/all_to_all | solution.py:306
  18.8 2.0 %collective-permute-start = (bf16[256,512]{1,0:T(8,128)(2,1)}, bf16[256,512]{1,0:T(8,128)(2,1)S(1)}, u32[]{:S(2)}, u32[]{:S(2)}) collective-permute-start(bf16[256,512]{1,0:T(8,128)(2,1)} %refs_7_.1), channel_id=1, source_target_pairs={{0,2},{2,0},{4,6},{6,4},{8,10},{10,8},{12,14},{14,12},{1,3},{3,1},... | collective-permute-start | bytes 786440 | tf_op jit(solution)/shard_map/ppermute | solution.py:295
  20.8 19.0 %project.5 = (bf16[4,16,3072]{2,1,0:T(8,128)(2,1)S(1)}, f32[4,16,3072]{2,1,0:T(8,128)S(1)}) custom-call(s32[3]{0:T(128)S(1)} %pad_add_fusion.who_ref, bf16[8192,3584]{1,0:T(8,128)(2,1)} %x_hbm.5, bf16[64,3584]{1,0:T(8,128)(2,1)S(1)} %get-tuple-element.13.sign_source), custom_call_target="tpu_custom_call" | custom-call | flops 2818572288 | bytes 44040192 | tf_op jit(solution)/shard_map/project/pallas_call | solution.py:142
  39.8 0.1 collective-permute-start.4
  39.9 4.8 %all-to-all-done = bf16[8,64,1024]{2,1,0:T(8,128)(2,1)} async-done(((bf16[8,64,1024]{2,1,0:T(8,128)(2,1)}), bf16[8,64,1024]{2,1,0:T(8,128)(2,1)}, u32[]{:S(2)}, u32[]{:S(2)}) %all-to-all-start) | async-done | bytes 1048608 | tf_op jit(solution)/shard_map/all_to_all | solution.py:306
  44.7 1.4 %fusion.refs_0_.refs_4_.refs_1_ = bf16[64,1024]{1,0:T(8,128)(2,1)S(1)} fusion(bf16[8,64,1024]{2,1,0:T(8,128)(2,1)} %all-to-all-done), kind=kLoop, calls=%fused_computation.1 | loop fusion | flops 1048576 | bytes 1179648 | tf_op jit(solution)/shard_map/convert_element_type | solution.py:309
  46.1 0.0 collective-permute-done.refs_1_.refs_8_
  46.1 9.9 %project.4 = bf16[4,2,16,1024]{3,2,1,0:T(8,128)(2,1)} custom-call(s32[3]{0:T(128)S(1)} %pad_add_fusion.who_ref, bf16[8192,3584]{1,0:T(8,128)(2,1)} %x_hbm.5, bf16[64,3584]{1,0:T(8,128)(2,1)S(1)} %get-tuple-element.13.sign_source, bf16[64,1024]{1,0:T(8,128)(2,1)S(1)} %fusion.refs_0_.refs_4_.refs_1_, bf16[256,512]{1,0:T(8,128)(2,1)S(1)} %collective-permute-done.refs_1_.refs_8_), custom_call_target="tpu_custom_call" | custom-call | flops 939524096 | bytes 14680064 | tf_op jit(solution)/shard_map/project/pallas_call | solution.py:142
  56.0 3.6 %all-to-all-start.1 = ((bf16[8,16,1024]{2,1,0:T(8,128)(2,1)}), bf16[8,16,1024]{2,1,0:T(8,128)(2,1)S(1)}, u32[]{:S(2)}, u32[]{:S(2)}) async-start(bf16[8,16,1024]{2,1,0:T(8,128)(2,1)} %bitcast.7), calls=%async_computation.1 | async-start | bytes 524288 | tf_op jit(solution)/shard_map/all_to_all | solution.py:315
  59.6 0.3 merge.1
  59.9 2.1 %collective-permute-start.5 = (bf16[16,3072]{1,0:T(8,128)(2,1)S(1)}, bf16[16,3072]{1,0:T(8,128)(2,1)S(1)}, u32[]{:S(2)}, u32[]{:S(2)}) collective-permute-start(bf16[16,3072]{1,0:T(8,128)(2,1)S(1)} %get-tuple-element.18), channel_id=1, source_target_pairs={{0,4},{2,6},{4,0},{6,2},{8,12},{10,14},{12,8},{14,10},{1,5},{3,7},... | collective-permute-start | bytes 294920 | tf_op jit(solution)/shard_map/ppermute | solution.py:295
  62.0 2.4 %collective-permute-start.6 = (bf16[16,3072]{1,0:T(8,128)(2,1)S(1)}, bf16[16,3072]{1,0:T(8,128)(2,1)S(1)}, u32[]{:S(2)}, u32[]{:S(2)}) collective-permute-start(bf16[16,3072]{1,0:T(8,128)(2,1)S(1)} %get-tuple-element.19), channel_id=1, source_target_pairs={{0,8},{2,10},{4,12},{6,14},{8,0},{10,2},{12,4},{14,6},{1,9},{3,11}... | collective-permute-start | bytes 294920 | tf_op jit(solution)/shard_map/ppermute | solution.py:295
  64.4 0.1 collective-permute-start.7
  64.5 0.5 collective-permute-start.9
  65.0 4.1 %collective-permute-done.5.refs_1_ = bf16[16,3072]{1,0:T(8,128)(2,1)S(1)} collective-permute-done((bf16[16,3072]{1,0:T(8,128)(2,1)S(1)}, bf16[16,3072]{1,0:T(8,128)(2,1)S(1)}, u32[]{:S(2)}, u32[]{:S(2)}) %collective-permute-start.5) | collective-permute-done | bytes 98336 | tf_op jit(solution)/shard_map/ppermute | solution.py:295
  69.0 0.6 collective-permute-start.1
  69.7 6.6 %collective-permute-done.6.refs_2_ = bf16[16,3072]{1,0:T(8,128)(2,1)S(1)} collective-permute-done((bf16[16,3072]{1,0:T(8,128)(2,1)S(1)}, bf16[16,3072]{1,0:T(8,128)(2,1)S(1)}, u32[]{:S(2)}, u32[]{:S(2)}) %collective-permute-start.6) | collective-permute-done | bytes 98336 | tf_op jit(solution)/shard_map/ppermute | solution.py:295
  76.3 0.5 collective-permute-start.3
  76.7 10.0 %collective-permute-done.2.refs_6_.refs_3_ = bf16[64,1024]{1,0:T(8,128)(2,1)S(1)} collective-permute-done((bf16[64,1024]{1,0:T(8,128)(2,1)S(1)}, bf16[64,1024]{1,0:T(8,128)(2,1)S(1)}, u32[]{:S(2)}, u32[]{:S(2)}) %collective-permute-start.2) | collective-permute-done | bytes 131104 | tf_op jit(solution)/shard_map/ppermute | solution.py:295
  86.8 4.1 %sketch.1.refs_6_ = f32[64,1024]{1,0:T(8,128)S(1)} custom-call(s32[3]{0:T(128)S(1)} %pad_add_fusion.who_ref, f32[16,3072]{1,0:T(8,128)S(1)} %get-tuple-element.17.refs_0_, bf16[16,3072]{1,0:T(8,128)(2,1)S(1)} %collective-permute-done.5.refs_1_, bf16[16,3072]{1,0:T(8,128)(2,1)S(1)} %collective-permute-done.6.refs_2_, ...), custom_call_target="tpu_custom_call" | custom-call | flops 402653184 | bytes 196608 | tf_op jit(solution)/shard_map/sketch/pallas_call | solution.py:266
  90.9 2.8 %score.1 = f32[64,512]{1,0:T(8,128)S(1)} custom-call(s32[3]{0:T(128)S(1)} %pad_add_fusion.who_ref, bf16[8,16,1024]{2,1,0:T(8,128)(2,1)S(1)} %all-to-all-done.1.refs_0_, bf16[64,1024]{1,0:T(8,128)(2,1)S(1)} %fusion.refs_0_.refs_4_.refs_1_, bf16[64,1024]{1,0:T(8,128)(2,1)S(1)} %collective-permute-done.1.refs_5_.refs_2_, ...), custom_call_target="tpu_custom_call" | custom-call | flops 134217728 | bytes 65536 | tf_op jit(solution)/shard_map/score/pallas_call | solution.py:266
  93.7 1.3 %collective-permute-start.10 = (f32[64,512]{1,0:T(8,128)S(1)}, f32[64,512]{1,0:T(8,128)S(1)}, u32[]{:S(2)}, u32[]{:S(2)}) collective-permute-start(f32[64,512]{1,0:T(8,128)S(1)} %score.1), channel_id=1, source_target_pairs={{0,2},{2,0},{4,6},{6,4},{8,10},{10,8},{12,14},{14,12},{1,3},{3,1},... | collective-permute-start | bytes 393224 | tf_op jit(solution)/shard_map/ppermute | solution.py:295
  95.0 3.7 %collective-permute-done.10 = f32[64,512]{1,0:T(8,128)S(1)} collective-permute-done((f32[64,512]{1,0:T(8,128)S(1)}, f32[64,512]{1,0:T(8,128)S(1)}, u32[]{:S(2)}, u32[]{:S(2)}) %collective-permute-start.10) | collective-permute-done | bytes 131104 | tf_op jit(solution)/shard_map/ppermute | solution.py:295
  98.7 2.8 %collective-permute-start.11 = (f32[64,512]{1,0:T(8,128)S(1)}, f32[64,512]{1,0:T(8,128)S(1)}, u32[]{:S(2)}, u32[]{:S(2)}) collective-permute-start(f32[64,512]{1,0:T(8,128)S(1)} %add.49), channel_id=1, source_target_pairs={{0,4},{2,6},{4,0},{6,2},{8,12},{10,14},{12,8},{14,10},{1,5},{3,7},... | collective-permute-start | bytes 393224 | tf_op jit(solution)/shard_map/ppermute | solution.py:295
  101.5 3.6 %collective-permute-done.11 = f32[64,512]{1,0:T(8,128)S(1)} collective-permute-done((f32[64,512]{1,0:T(8,128)S(1)}, f32[64,512]{1,0:T(8,128)S(1)}, u32[]{:S(2)}, u32[]{:S(2)}) %collective-permute-start.11) | collective-permute-done | bytes 131104 | tf_op jit(solution)/shard_map/ppermute | solution.py:295
  105.2 1.2 %collective-permute-start.12 = (bf16[64,512]{1,0:T(8,128)(2,1)S(1)}, bf16[64,512]{1,0:T(8,128)(2,1)S(1)}, u32[]{:S(2)}, u32[]{:S(2)}) collective-permute-start(bf16[64,512]{1,0:T(8,128)(2,1)S(1)} %add_convert_fusion.1), channel_id=1, source_target_pairs={{0,8},{2,10},{4,12},{6,14},{8,0},{10,2},{12,4},{14,6},{1,9},{3,11}... | collective-permute-start | bytes 196616 | tf_op jit(solution)/shard_map/ppermute | solution.py:295
  106.4 4.1 %collective-permute-done.12 = bf16[64,512]{1,0:T(8,128)(2,1)S(1)} collective-permute-done((bf16[64,512]{1,0:T(8,128)(2,1)S(1)}, bf16[64,512]{1,0:T(8,128)(2,1)S(1)}, u32[]{:S(2)}, u32[]{:S(2)}) %collective-permute-start.12) | collective-permute-done | bytes 65568 | tf_op jit(solution)/shard_map/ppermute | solution.py:295
  110.4 0.7 convert_add_fusion
  (17 shorter events, 0.1 us)
Async XLA Ops:
  0.1 1.2 %copy-start = (s32[3584,64]{0,1:T(8,128)S(1)}, s32[3584,64]{0,1:T(8,128)}, u32[]{:S(2)}) copy-start(s32[3584,64]{0,1:T(8,128)} %param.8) | copy-start | bytes 2752516
  1.3 0.9 copy-start.2
  11.5 33.2 %all-to-all-start = ((bf16[8,64,1024]{2,1,0:T(8,128)(2,1)}), bf16[8,64,1024]{2,1,0:T(8,128)(2,1)}, u32[]{:S(2)}, u32[]{:S(2)}) async-start(bf16[8,64,1024]{2,1,0:T(8,128)(2,1)} %bitcast.5), calls=%async_computation | async-start | bytes 2097152 | tf_op jit(solution)/shard_map/all_to_all | solution.py:306
  18.8 27.3 %collective-permute-start = (bf16[256,512]{1,0:T(8,128)(2,1)}, bf16[256,512]{1,0:T(8,128)(2,1)S(1)}, u32[]{:S(2)}, u32[]{:S(2)}) collective-permute-start(bf16[256,512]{1,0:T(8,128)(2,1)} %refs_7_.1), channel_id=1, source_target_pairs={{0,2},{2,0},{4,6},{6,4},{8,10},{10,8},{12,14},{14,12},{1,3},{3,1},... | collective-permute-start | bytes 786440 | tf_op jit(solution)/shard_map/ppermute | solution.py:295
  20.8 43.6 %copy-start.1 = (bf16[256,512]{1,0:T(8,128)(2,1)S(1)}, bf16[256,512]{1,0:T(8,128)(2,1)}, u32[]{:S(2)}) copy-start(bf16[256,512]{1,0:T(8,128)(2,1)} %refs_7_.1) | copy-start | bytes 786436
  20.8 65.9 %copy-start.3 = (s32[1,8192]{1,0:T(1,128)S(1)}, s32[1,8192]{1,0:T(1,128)}, u32[]{:S(2)}) copy-start(s32[1,8192]{1,0:T(1,128)} %refs_5_.1) | copy-start | bytes 98308
  39.8 19.8 %collective-permute-start.4 = (bf16[4,16,3072]{2,1,0:T(8,128)(2,1)S(1)}, bf16[4,16,3072]{2,1,0:T(8,128)(2,1)S(1)}, u32[]{:S(2)}, u32[]{:S(2)}) collective-permute-start(bf16[4,16,3072]{2,1,0:T(8,128)(2,1)S(1)} %get-tuple-element.16), channel_id=1, source_target_pairs={{0,2},{2,0},{4,6},{6,4},{8,10},{10,8},{12,14},{14,12},{1,3},{3,1},... | collective-permute-start | bytes 1179656 | tf_op jit(solution)/shard_map/ppermute | solution.py:295
  56.0 34.9 %all-to-all-start.1 = ((bf16[8,16,1024]{2,1,0:T(8,128)(2,1)}), bf16[8,16,1024]{2,1,0:T(8,128)(2,1)S(1)}, u32[]{:S(2)}, u32[]{:S(2)}) async-start(bf16[8,16,1024]{2,1,0:T(8,128)(2,1)} %bitcast.7), calls=%async_computation.1 | async-start | bytes 524288 | tf_op jit(solution)/shard_map/all_to_all | solution.py:315
  59.9 9.1 %collective-permute-start.5 = (bf16[16,3072]{1,0:T(8,128)(2,1)S(1)}, bf16[16,3072]{1,0:T(8,128)(2,1)S(1)}, u32[]{:S(2)}, u32[]{:S(2)}) collective-permute-start(bf16[16,3072]{1,0:T(8,128)(2,1)S(1)} %get-tuple-element.18), channel_id=1, source_target_pairs={{0,4},{2,6},{4,0},{6,2},{8,12},{10,14},{12,8},{14,10},{1,5},{3,7},... | collective-permute-start | bytes 294920 | tf_op jit(solution)/shard_map/ppermute | solution.py:295
  62.0 14.2 %collective-permute-start.6 = (bf16[16,3072]{1,0:T(8,128)(2,1)S(1)}, bf16[16,3072]{1,0:T(8,128)(2,1)S(1)}, u32[]{:S(2)}, u32[]{:S(2)}) collective-permute-start(bf16[16,3072]{1,0:T(8,128)(2,1)S(1)} %get-tuple-element.19), channel_id=1, source_target_pairs={{0,8},{2,10},{4,12},{6,14},{8,0},{10,2},{12,4},{14,6},{1,9},{3,11}... | collective-permute-start | bytes 294920 | tf_op jit(solution)/shard_map/ppermute | solution.py:295
  64.4 11.9 %collective-permute-start.7 = (bf16[16,3072]{1,0:T(8,128)(2,1)S(1)}, bf16[16,3072]{1,0:T(8,128)(2,1)S(1)}, u32[]{:S(2)}, u32[]{:S(2)}) collective-permute-start(bf16[16,3072]{1,0:T(8,128)(2,1)S(1)} %get-tuple-element.20), channel_id=1, source_target_pairs={{0,12},{2,14},{4,8},{6,10},{8,4},{10,6},{12,0},{14,2},{1,13},{3,15... | collective-permute-start | bytes 294920 | tf_op jit(solution)/shard_map/ppermute | solution.py:295
  64.5 26.4 %collective-permute-start.8 = (bf16[256,512]{1,0:T(8,128)(2,1)S(1)}, bf16[256,512]{1,0:T(8,128)(2,1)S(1)}, u32[]{:S(2)}, u32[]{:S(2)}) collective-permute-start(bf16[256,512]{1,0:T(8,128)(2,1)S(1)} %copy-done.1), channel_id=1, source_target_pairs={{0,1},{1,0},{2,3},{3,2},{4,5},{5,4},{6,7},{7,6},{8,9},{9,8},{10,11... | collective-permute-start | bytes 786440 | tf_op jit(solution)/shard_map/ppermute | solution.py:298
  64.5 26.4 %collective-permute-start.9 = (bf16[256,512]{1,0:T(8,128)(2,1)S(1)}, bf16[256,512]{1,0:T(8,128)(2,1)S(1)}, u32[]{:S(2)}, u32[]{:S(2)}) collective-permute-start(bf16[256,512]{1,0:T(8,128)(2,1)S(1)} %collective-permute-done.refs_1_.refs_8_), channel_id=1, source_target_pairs={{0,1},{1,0},{2,3},{3,2},{4,5},{5,4},{6,7},{7,6},{8,9},{9,8},{10,11... | collective-permute-start | bytes 786440 | tf_op jit(solution)/shard_map/ppermute | solution.py:298
  69.0 7.7 %collective-permute-start.1 = (bf16[64,1024]{1,0:T(8,128)(2,1)S(1)}, bf16[64,1024]{1,0:T(8,128)(2,1)S(1)}, u32[]{:S(2)}, u32[]{:S(2)}) collective-permute-start(bf16[64,1024]{1,0:T(8,128)(2,1)S(1)} %fusion.refs_0_.refs_4_.refs_1_), channel_id=1, source_target_pairs={{0,4},{2,6},{4,0},{6,2},{8,12},{10,14},{12,8},{14,10},{1,5},{3,7},... | collective-permute-start | bytes 393224 | tf_op jit(solution)/shard_map/ppermute | solution.py:295
  76.3 10.5 %collective-permute-start.2 = (bf16[64,1024]{1,0:T(8,128)(2,1)S(1)}, bf16[64,1024]{1,0:T(8,128)(2,1)S(1)}, u32[]{:S(2)}, u32[]{:S(2)}) collective-permute-start(bf16[64,1024]{1,0:T(8,128)(2,1)S(1)} %fusion.refs_0_.refs_4_.refs_1_), channel_id=1, source_target_pairs={{0,8},{2,10},{4,12},{6,14},{8,0},{10,2},{12,4},{14,6},{1,9},{3,11}... | collective-permute-start | bytes 393224 | tf_op jit(solution)/shard_map/ppermute | solution.py:295
  76.3 10.5 %collective-permute-start.3 = (bf16[64,1024]{1,0:T(8,128)(2,1)S(1)}, bf16[64,1024]{1,0:T(8,128)(2,1)S(1)}, u32[]{:S(2)}, u32[]{:S(2)}) collective-permute-start(bf16[64,1024]{1,0:T(8,128)(2,1)S(1)} %fusion.refs_0_.refs_4_.refs_1_), channel_id=1, source_target_pairs={{0,12},{2,14},{4,8},{6,10},{8,4},{10,6},{12,0},{14,2},{1,13},{3,15... | collective-permute-start | bytes 393224 | tf_op jit(solution)/shard_map/ppermute | solution.py:295
  93.7 5.0 %collective-permute-start.10 = (f32[64,512]{1,0:T(8,128)S(1)}, f32[64,512]{1,0:T(8,128)S(1)}, u32[]{:S(2)}, u32[]{:S(2)}) collective-permute-start(f32[64,512]{1,0:T(8,128)S(1)} %score.1), channel_id=1, source_target_pairs={{0,2},{2,0},{4,6},{6,4},{8,10},{10,8},{12,14},{14,12},{1,3},{3,1},... | collective-permute-start | bytes 393224 | tf_op jit(solution)/shard_map/ppermute | solution.py:295
  98.7 6.4 %collective-permute-start.11 = (f32[64,512]{1,0:T(8,128)S(1)}, f32[64,512]{1,0:T(8,128)S(1)}, u32[]{:S(2)}, u32[]{:S(2)}) collective-permute-start(f32[64,512]{1,0:T(8,128)S(1)} %add.49), channel_id=1, source_target_pairs={{0,4},{2,6},{4,0},{6,2},{8,12},{10,14},{12,8},{14,10},{1,5},{3,7},... | collective-permute-start | bytes 393224 | tf_op jit(solution)/shard_map/ppermute | solution.py:295
  105.2 5.2 %collective-permute-start.12 = (bf16[64,512]{1,0:T(8,128)(2,1)S(1)}, bf16[64,512]{1,0:T(8,128)(2,1)S(1)}, u32[]{:S(2)}, u32[]{:S(2)}) collective-permute-start(bf16[64,512]{1,0:T(8,128)(2,1)S(1)} %add_convert_fusion.1), channel_id=1, source_target_pairs={{0,8},{2,10},{4,12},{6,14},{8,0},{10,2},{12,4},{14,6},{1,9},{3,11}... | collective-permute-start | bytes 196616 | tf_op jit(solution)/shard_map/ppermute | solution.py:295

commit v8 on v6

v8 whole, which is shorter than its diff:
```python
import functools

import jax
import jax.numpy as jnp
from jax import lax
from jax.experimental import pallas as pl
from jax.experimental.pallas import tpu as pltpu
from jax.sharding import PartitionSpec as P

D = 8192
FF = 28672
R = 64
SEQ_DEV = 64
BUFFERS = 4
VMEM = 48 * 1024 * 1024
LAST = (((1,), (1,)), ((), ()))


def project_kernel(scale, first, split, order, makes, waits, who_ref, x_hbm, sign_source, *refs):
    other_source, refs = refs[0], refs[makes + waits:]
    sent_ref, kept_ref, made_ref, refs = refs[0], refs[1], refs[2], refs[2 + makes:]
    bits_ref, other_ref = refs[0], refs[1]
    signs_ref, x_buf, sign_sem, sems = refs[-4:]
    half, quarter = who_ref[0], who_ref[1]
    buffers, tile = x_buf.shape[0], x_buf.shape[1]
    steps = sent_ref.size // (R * tile)

    def copy(p):
        mine = (p >= steps).astype(jnp.int32)
        row = pl.multiple_of((half ^ 1 ^ mine) * (x_hbm.shape[0] // 2) + first + (p - mine * steps) * tile, tile)
        slot = lax.rem(p, buffers)
        return pltpu.make_async_copy(x_hbm.at[pl.ds(row, tile)], x_buf.at[slot], sems.at[slot])

    sign_copy = pltpu.make_async_copy(sign_source, bits_ref, sign_sem.at[0])
    sign_copy.start()

    def begin(p, carry):
        copy(p).start()
        return carry

    lax.fori_loop(0, buffers, begin, 0)
    if makes:
        other_copy = pltpu.make_async_copy(other_source, other_ref, sign_sem.at[1])
        other_copy.start()
    sign_copy.wait()
    if makes:
        signs_ref[...] = (2 * bits_ref[...] - 1).astype(jnp.bfloat16)
    else:
        rows = R // max(order, 1)
        for q in range(max(order, 1)):
            at = pl.multiple_of((q ^ quarter) * rows, rows) if order else 0
            signs_ref[q * rows:(q + 1) * rows, :] = bits_ref[pl.ds(at, rows), :]

    def one(p, carry):
        copy(p).wait()
        mine = (p >= steps).astype(jnp.int32)
        s = p - mine * steps
        part = lax.dot_general(
            signs_ref[...], x_buf[lax.rem(p, buffers)], LAST, preferred_element_type=jnp.float32
        ) * scale

        def store(out_ref):
            value = part.astype(out_ref.dtype)
            if split:
                here = pl.ds(pl.multiple_of(lax.rem(s, split) * tile, tile), tile)
                out_ref[(s // split) ^ quarter, :, here] = value
            else:
                here = pl.ds(pl.multiple_of(s * tile, tile), tile)
                out_ref[:, :, here] = value.reshape(out_ref.shape[0], out_ref.shape[1], tile)

        @pl.when(p < steps)
        def _():
            store(sent_ref)

        @pl.when(p >= steps)
        def _():
            store(kept_ref)

        @pl.when(p + buffers < 2 * steps)
        def _():
            copy(p + buffers).start()

        return carry

    lax.fori_loop(0, 2 * steps, one, 0)
    if makes:
        other_copy.wait()
        made_ref[...] = (2 * other_ref[...] - 1).astype(jnp.bfloat16)


def project(x, signs, who, scale, quarters, by_column, first, count, tile, other=None, after=()):
    width = x.shape[1]
    piece = count // quarters
    order, split = 0, 0
    makes = other is not None
    if by_column:
        shape = (quarters, R // quarters, count)
        if (R // quarters) % 16:
            rows = jnp.arange(R, dtype=jnp.int32)
            signs = jnp.take(signs, rows ^ (who[1] * (R // quarters)), axis=0)
        else:
            order = quarters
    else:
        tile = min(tile, piece)
        split = piece // tile
        shape = (quarters, R, piece)
    shapes = [jax.ShapeDtypeStruct(shape, jnp.bfloat16), jax.ShapeDtypeStruct(shape, jnp.float32)]
    scratch = [pltpu.VMEM(signs.shape, signs.dtype)]
    if makes:
        shapes.append(jax.ShapeDtypeStruct(other.shape, jnp.bfloat16))
        scratch.append(pltpu.VMEM(other.shape, other.dtype))
    buffers = min(BUFFERS, 2 * (count // tile))
    operands = [x, signs] + ([other] if makes else []) + list(after)
    return pl.pallas_call(
        functools.partial(project_kernel, scale, first, split, order, int(makes), len(after)),
        in_specs=[pl.BlockSpec(memory_space=pltpu.SMEM)] + [pl.BlockSpec(memory_space=pl.ANY)] * len(operands),
        out_specs=[pl.BlockSpec(memory_space=pltpu.VMEM)] * len(shapes),
        scratch_shapes=scratch
        + [
            pltpu.VMEM(signs.shape, jnp.bfloat16),
            pltpu.VMEM((buffers, tile, width), jnp.bfloat16),
            pltpu.SemaphoreType.DMA((2,)),
            pltpu.SemaphoreType.DMA((buffers,)),
        ],
        out_shape=shapes,
        compiler_params=pltpu.CompilerParams(vmem_limit_bytes=VMEM),
        cost_estimate=pl.CostEstimate(flops=4 * count * width * R, bytes_accessed=4 * count * width, transcendentals=0),
        name="project",
    )(who, *operands)


def fetch_all(sources, targets, sems):
    copies = [pltpu.make_async_copy(source, target, sems.at[k]) for k, (source, target) in enumerate(zip(sources, targets))]
    for copy in copies:
        copy.start()
    return copies


def merge_kernel(quarters, bases, pairs, waits, *refs):
    count = bases + 2 * pairs
    sources, outs = refs[:count], refs[count + waits:count + waits + quarters]
    targets, sems = refs[count + waits + quarters:-1], refs[-1]
    copies = fetch_all(sources, targets, sems)
    for copy in copies:
        copy.wait()
    for d, out_ref in enumerate(outs):
        at = 0
        if bases:
            at = targets[d].shape[1]
            out_ref[:, :at] = targets[d][...]
        for c in range(bases, count, 2):
            kept_ref, got_ref = targets[c], targets[c + 1]
            width = kept_ref.shape[2]
            out_ref[:, at:at + width] = (kept_ref[d] + got_ref[d].astype(jnp.float32)).astype(out_ref.dtype)
            at = at + width


def merge(base, arrays, after):
    quarters, rows = arrays[0].shape[:2]
    tokens = sum(array.shape[2] for array in arrays[::2]) + (base[0].shape[1] if base else 0)
    operands = list(base) + list(arrays)
    return pl.pallas_call(
        functools.partial(merge_kernel, quarters, len(base), len(arrays) // 2, len(after)),
        in_specs=[pl.BlockSpec(memory_space=pl.ANY)] * (len(operands) + len(after)),
        out_specs=[pl.BlockSpec(memory_space=pltpu.VMEM)] * quarters,
        out_shape=[jax.ShapeDtypeStruct((rows, tokens), jnp.bfloat16 if d else jnp.float32) for d in range(quarters)],
        scratch_shapes=[pltpu.VMEM(operand.shape, operand.dtype) for operand in operands] + [pltpu.SemaphoreType.DMA((len(operands),))],
        compiler_params=pltpu.CompilerParams(vmem_limit_bytes=VMEM // 6),
        cost_estimate=pl.CostEstimate(flops=quarters * rows * tokens, bytes_accessed=8 * quarters * rows * tokens, transcendentals=0),
        name="merge",
    )(*operands, *after)


def total_kernel(count, waits, *refs):
    sources, out_ref, targets, sems = refs[:count], refs[count + waits], refs[count + waits + 1:-1], refs[-1]
    for copy in fetch_all(sources, targets, sems):
        copy.wait()
    total = targets[0][...]
    for target in targets[1:]:
        total = total + target[...].astype(jnp.float32)
    out_ref[...] = total.astype(out_ref.dtype)


def total_of(parts, after):
    return pl.pallas_call(
        functools.partial(total_kernel, len(parts), len(after)),
        in_specs=[pl.BlockSpec(memory_space=pl.ANY)] * (len(parts) + len(after)),
        out_specs=pl.BlockSpec(memory_space=pltpu.VMEM),
        out_shape=jax.ShapeDtypeStruct(parts[0].shape, jnp.bfloat16),
        scratch_shapes=[pltpu.VMEM(part.shape, part.dtype) for part in parts] + [pltpu.SemaphoreType.DMA((len(parts),))],
        compiler_params=pltpu.CompilerParams(vmem_limit_bytes=VMEM // 6),
        cost_estimate=pl.CostEstimate(flops=parts[0].size * len(parts), bytes_accessed=2 * parts[0].size * len(parts), transcendentals=0),
        name="total",
    )(*parts, *after)


def score_kernel(quarters, width, who_ref, *refs):
    count = 2 * quarters + 5
    sources, out_ref, targets = refs[:count], refs[count], refs[count + 1:2 * count + 1]
    sems, row_ref, col_ref, member_ref, spread_ref, sketch_ref = refs[2 * count + 1:]
    copies = fetch_all(sources, targets, sems)
    left_refs, right_refs = targets[:quarters], targets[quarters:2 * quarters]
    ids_ref, query_refs = targets[2 * quarters], targets[2 * quarters + 1:]
    half, quarter, data = who_ref[0], who_ref[1], who_ref[2]
    for copy in copies[:2 * quarters + 1]:
        copy.wait()
    total = left_refs[0][...]
    for left_ref in left_refs[1:]:
        total = total + left_ref[...].astype(jnp.float32)
    row_ref[...] = total
    piece = right_refs[0].shape[1]
    for d, right_ref in enumerate(right_refs):
        col_ref[:, pl.ds(pl.multiple_of((quarter ^ d) * piece, piece), piece)] = right_ref[...].astype(jnp.float32)
    numbers = lax.broadcasted_iota(jnp.int32, (SEQ_DEV, 1), 0)
    owned = col_ref.shape[1]
    ids = ids_ref[:, pl.ds(pl.multiple_of(half * owned, 128), owned)]
    member_ref[...] = (ids == numbers).astype(jnp.bfloat16)
    rows = spread_ref.shape[0] // R

    def group(g, carry):
        for at in range(0, owned, width):
            right = col_ref[:, at:at + width]
            for r in range(rows):
                row = row_ref[pl.ds(g * rows + r, 1), at:at + width]
                spread_ref[r * R:(r + 1) * R, at:at + width] = (row * right).astype(jnp.bfloat16)
        here = pl.ds(pl.multiple_of(g * rows * R, rows * R), rows * R)
        sketch_ref[:, here] = lax.dot_general(member_ref[...], spread_ref[...], LAST, preferred_element_type=jnp.float32)
        return carry

    lax.fori_loop(0, row_ref.shape[0] // rows, group, 0)
    entries = sketch_ref[...]
    high = entries.astype(jnp.bfloat16)
    low = (entries - high.astype(jnp.float32)).astype(jnp.bfloat16)
    both = jnp.concatenate([high, low], axis=0)
    middle = both.shape[1] // 2
    swapped = half == 1
    near = jnp.where(swapped, both[:, middle:], both[:, :middle])
    far = jnp.where(swapped, both[:, :middle], both[:, middle:])
    for copy in copies[2 * quarters + 1:]:
        copy.wait()
    rows = query_refs[0].shape[0]
    for side in range(2):
        part = lax.dot_general(near, query_refs[2 * side][...], LAST, preferred_element_type=jnp.float32)
        part = part + lax.dot_general(far, query_refs[2 * side + 1][...], LAST, preferred_element_type=jnp.float32)
        out_ref[:, pl.ds(pl.multiple_of((data ^ side) * rows, rows), rows)] = part[:SEQ_DEV] + part[SEQ_DEV:]


def score(who, left, right, ids, queries):
    operands = left + right + [ids] + queries
    columns, tokens = left[0].shape
    rows = min(4, columns)
    shape = (SEQ_DEV, 2 * queries[0].shape[0])
    return pl.pallas_call(
        functools.partial(score_kernel, len(left), min(512, tokens)),
        in_specs=[pl.BlockSpec(memory_space=pltpu.SMEM)] + [pl.BlockSpec(memory_space=pl.ANY)] * len(operands),
        out_specs=pl.BlockSpec(memory_space=pltpu.VMEM),
        out_shape=jax.ShapeDtypeStruct(shape, jnp.float32),
        scratch_shapes=[pltpu.VMEM(operand.shape, operand.dtype) for operand in operands]
        + [
            pltpu.SemaphoreType.DMA((len(operands),)),
            pltpu.VMEM((columns, tokens), jnp.float32),
            pltpu.VMEM((R, tokens), jnp.float32),
            pltpu.VMEM((SEQ_DEV, tokens), jnp.bfloat16),
            pltpu.VMEM((rows * R, tokens), jnp.bfloat16),
            pltpu.VMEM((SEQ_DEV, columns * R), jnp.float32),
        ],
        compiler_params=pltpu.CompilerParams(vmem_limit_bytes=VMEM // 3),
        cost_estimate=pl.CostEstimate(flops=2 * tokens * columns * R * SEQ_DEV, bytes_accessed=4 * columns * tokens, transcendentals=0),
        name="score",
    )(who, *operands)


def body(n_tensor, activations, out_grads, proj_in, proj_out, segment_ids, queries):
    quarters = n_tensor // 2
    me = lax.axis_index("tensor").astype(jnp.int32)
    half = me % 2
    who = jnp.stack([half, me // 2, lax.axis_index("dp").astype(jnp.int32)])
    owned = activations.shape[0] // 2
    def swap(array, distance):
        return lax.ppermute(array, "tensor", [(k, k ^ distance) for k in range(n_tensor)])

    def cross(array):
        return lax.ppermute(array, "dp", [(0, 1), (1, 0)])

    far = swap(queries, 1)
    every = [queries, far, cross(queries), cross(far)]

    scale_in, scale_out = FF ** -0.5, D ** -0.5
    sent_g, kept_g, signs = project(out_grads, proj_out.T, who, scale_out, quarters, False, 0, owned, 1024, proj_in.T)
    got_g = swap(sent_g, 1)

    def chunk(eighth, eighths, after):
        first, count = owned * eighth // 8, owned * eighths // 8
        sent, kept = project(activations, signs, who, scale_in, quarters, True, first, count, 512, None, after)
        return sent, [kept, swap(sent, 1)]

    sent_0, chunk_0 = chunk(0, 4, [])
    pair_g = merge([], [kept_g, got_g], [sent_0])
    moved_g = [swap(pair_g[d], 2 * d) for d in range(1, quarters)]
    sent_1, chunk_1 = chunk(4, 3, [pair_g[1]])
    own_g = total_of([pair_g[0]] + moved_g, [sent_1])
    right = [own_g] + [swap(own_g, 2 * d) for d in range(1, quarters)]
    sent_2, chunk_2 = chunk(7, 1, [own_g, far])
    pair_a = merge([], chunk_0, right[1:])
    pair_a = merge(pair_a, chunk_1 + chunk_2, [])
    left = [pair_a[0]] + [swap(pair_a[d], 2 * d) for d in range(1, quarters)]

    total = score(who, left, right, segment_ids, every)
    total = (total + swap(total, 1)).astype(jnp.bfloat16)
    parts = [total] + [swap(total, 2 * d) for d in range(1, quarters)]
    parts = [part.astype(jnp.float32) for part in parts]
    while len(parts) > 1:
        parts = [parts[k] + parts[k + 1] for k in range(0, len(parts), 2)]
    return parts[0]


def solution(mesh):
    return jax.shard_map(
        functools.partial(body, mesh.shape["tensor"]),
        mesh=mesh,
        in_specs=(
            P(("copies", "dp"), "tensor"),
            P(("copies", "dp"), "tensor"),
            P("tensor", None),
            P("tensor", None),
            P(("copies", "dp"), None),
            P(("copies", "dp"), "tensor"),
        ),
        out_specs=P(("copies", "dp"), None),
        check_vma=False,
    )
```

time: 94 us -> 96.5 us (1.027)
  starting transfers between devices: 30.3 us -> 24.3 us
  Pallas kernels: 39.6 us -> 45.1 us
  waiting for transfers between devices: 20.7 us -> 23.8 us
    ppermute x16 -> x18, starting transfers between devices: 30.2 us -> 24.2 us  [swap(): lax.ppermute(array, 'tensor', [(k, k ^ distance) for k in range(n_tensor)])]
    pallas_call x4 -> x8, Pallas kernels: 34.5 us -> 39.3 us  [the longest x4 37.1 us: project(): pl.pallas_call(functools.partial(project_kernel, scale, first, split, ord...]
    ppermute x16 -> x18, waiting for transfers between devices: 20.7 us -> 23.8 us  [swap(): lax.ppermute(array, 'tensor', [(k, k ^ distance) for k in range(n_tensor)])]
  transfers between devices with their start and end apart: 18 -> 20, of which waited for: 6 -> 8; matrix products, arithmetic and copies ran while one was open for 0% -> 0% of each run, Pallas kernels for 28% -> 32%
where the time goes in v8:
time: 96.5 us; the launch traced here: 96.3 us
  Pallas kernels  45.1 us (47%)
  starting transfers between devices  24.3 us (25%)
  waiting for transfers between devices  23.8 us (25%)
  local copies, waits for them, and re-layouts  2.14 us (2%)
    pallas_call x4, Pallas kernels, project(): pl.pallas_call(functools.partial(project_kernel, scale, first, split, ord...  37.1 us
    ppermute x18, starting transfers between devices, swap(): lax.ppermute(array, 'tensor', [(k, k ^ distance) for k in range(n_tensor)])  24.2 us
    ppermute x18, waiting for transfers between devices, swap(): lax.ppermute(array, 'tensor', [(k, k ^ distance) for k in range(n_tensor)])  23.8 us
    pallas_call x1, Pallas kernels, score(): pl.pallas_call(functools.partial(score_kernel, len(left), min(512, tokens...  5.78 us
    unnamed x8, local copies, waits for them, and re-layouts  2.14 us
  transfers between devices with their start and end apart: 20, of which 8 were waited for; matrix products, arithmetic and copies ran while one was open for 0% of the time, Pallas kernels for 32%

profile of v8, /device:TPU:0, one launch (start us, length us, event | category | flops | bytes accessed | tf_op | source)
XLA Modules:
  0.0 96.3 jit_solution(2024083052663937921)
XLA Ops:
  0.1 1.2 %copy-done = s32[3584,64]{0,1:T(8,128)S(1)} copy-done((s32[3584,64]{0,1:T(8,128)S(1)}, s32[3584,64]{0,1:T(8,128)}, u32[]{:S(2)}) %copy-start) | copy-done | bytes 917528
  1.3 0.9 copy-done.2
  2.2 8.6 %project.4 = (bf16[4,64,1024]{2,1,0:T(8,128)(2,1)S(1)}, f32[4,64,1024]{2,1,0:T(8,128)S(1)}, bf16[64,3584]{1,0:T(8,128)(2,1)S(1)}) custom-call(s32[3]{0:T(128)S(1)} %pad_add_fusion.who_ref, bf16[8192,1024]{1,0:T(8,128)(2,1)} %x_hbm.4, s32[64,1024]{1,0:T(8,128)S(1)} %bitcast.6, s32[64,3584]{1,0:T(8,128)S(1)} %bitcast.5), custom_call_target="tpu_custom_call" | custom-call | flops 1073741824 | bytes 16777216 | tf_op jit(solution)/shard_map/project/pallas_call | solution.py:114
  10.9 3.0 %collective-permute-start.1 = (bf16[4,64,1024]{2,1,0:T(8,128)(2,1)S(1)}, bf16[4,64,1024]{2,1,0:T(8,128)(2,1)S(1)}, u32[]{:S(2)}, u32[]{:S(2)}) collective-permute-start(bf16[4,64,1024]{2,1,0:T(8,128)(2,1)S(1)} %get-tuple-element.30), channel_id=1, source_target_pairs={{0,2},{2,0},{4,6},{6,4},{8,10},{10,8},{12,14},{14,12},{1,3},{3,1},... | collective-permute-start | bytes 1572872 | tf_op jit(solution)/shard_map/ppermute | solution.py:280
  14.0 12.8 %project.5 = (bf16[4,16,2048]{2,1,0:T(8,128)(2,1)S(1)}, f32[4,16,2048]{2,1,0:T(8,128)S(1)}) custom-call(s32[3]{0:T(128)S(1)} %pad_add_fusion.who_ref, bf16[8192,3584]{1,0:T(8,128)(2,1)} %x_hbm.7, bf16[64,3584]{1,0:T(8,128)(2,1)S(1)} %get-tuple-element.26.sign_source), custom_call_target="tpu_custom_call" | custom-call | flops 1879048192 | bytes 29360128 | tf_op jit(solution)/shard_map/project/pallas_call | solution.py:114
  26.8 2.0 %collective-permute-start = (bf16[4,16,2048]{2,1,0:T(8,128)(2,1)S(1)}, bf16[4,16,2048]{2,1,0:T(8,128)(2,1)S(1)}, u32[]{:S(2)}, u32[]{:S(2)}) collective-permute-start(bf16[4,16,2048]{2,1,0:T(8,128)(2,1)S(1)} %get-tuple-element.28.refs_2_), channel_id=1, source_target_pairs={{0,2},{2,0},{4,6},{6,4},{8,10},{10,8},{12,14},{14,12},{1,3},{3,1},... | collective-permute-start | bytes 786440 | tf_op jit(solution)/shard_map/ppermute | solution.py:280
  29.0 1.6 %collective-permute-start.2 = (bf16[64,1024]{1,0:T(8,128)(2,1)S(1)}, bf16[64,1024]{1,0:T(8,128)(2,1)S(1)}, u32[]{:S(2)}, u32[]{:S(2)}) collective-permute-start(bf16[64,1024]{1,0:T(8,128)(2,1)S(1)} %get-tuple-element.32.refs_0_), channel_id=1, source_target_pairs={{0,4},{2,6},{4,0},{6,2},{8,12},{10,14},{12,8},{14,10},{1,5},{3,7},... | collective-permute-start | bytes 393224 | tf_op jit(solution)/shard_map/ppermute | solution.py:280
  30.6 2.6 %collective-permute-start.3 = (bf16[64,1024]{1,0:T(8,128)(2,1)S(1)}, bf16[64,1024]{1,0:T(8,128)(2,1)S(1)}, u32[]{:S(2)}, u32[]{:S(2)}) collective-permute-start(bf16[64,1024]{1,0:T(8,128)(2,1)S(1)} %get-tuple-element.33), channel_id=1, source_target_pairs={{0,8},{2,10},{4,12},{6,14},{8,0},{10,2},{12,4},{14,6},{1,9},{3,11}... | collective-permute-start | bytes 393224 | tf_op jit(solution)/shard_map/ppermute | solution.py:280
  33.5 10.3 %project.6 = (bf16[4,16,1536]{2,1,0:T(8,128)(2,1)S(1)}, f32[4,16,1536]{2,1,0:T(8,128)S(1)}) custom-call(s32[3]{0:T(128)S(1)} %pad_add_fusion.who_ref, bf16[8192,3584]{1,0:T(8,128)(2,1)} %x_hbm.7, bf16[64,3584]{1,0:T(8,128)(2,1)S(1)} %get-tuple-element.26.sign_source, bf16[64,1024]{1,0:T(8,128)(2,1)S(1)} %get-tuple-element.32.refs_0_), custom_call_target="tpu_custom_call" | custom-call | flops 1409286144 | bytes 22020096 | tf_op jit(solution)/shard_map/project/pallas_call | solution.py:114
  43.8 0.6 total.1.refs_0_.refs_4_
  44.5 0.9 collective-permute-start.5
  45.4 3.3 %collective-permute-start.6 = (bf16[64,1024]{1,0:T(8,128)(2,1)S(1)}, bf16[64,1024]{1,0:T(8,128)(2,1)S(1)}, u32[]{:S(2)}, u32[]{:S(2)}) collective-permute-start(bf16[64,1024]{1,0:T(8,128)(2,1)S(1)} %total.1.refs_0_.refs_4_), channel_id=1, source_target_pairs={{0,8},{2,10},{4,12},{6,14},{8,0},{10,2},{12,4},{14,6},{1,9},{3,11}... | collective-permute-start | bytes 393224 | tf_op jit(solution)/shard_map/ppermute | solution.py:280
  48.7 0.5 collective-permute-start.8
  49.3 0.9 collective-permute-done.5.refs_2_.refs_5_
  50.2 5.4 %project.7 = (bf16[4,16,512]{2,1,0:T(8,128)(2,1)S(1)}, f32[4,16,512]{2,1,0:T(8,128)S(1)}) custom-call(s32[3]{0:T(128)S(1)} %pad_add_fusion.who_ref, bf16[8192,3584]{1,0:T(8,128)(2,1)} %x_hbm.7, bf16[64,3584]{1,0:T(8,128)(2,1)S(1)} %get-tuple-element.26.sign_source, bf16[64,1024]{1,0:T(8,128)(2,1)S(1)} %total.1.refs_0_.refs_4_, ...), custom_call_target="tpu_custom_call" | custom-call | flops 469762048 | bytes 7340032 | tf_op jit(solution)/shard_map/project/pallas_call | solution.py:114
  55.6 1.6 %collective-permute-done.6.refs_3_.refs_6_ = bf16[64,1024]{1,0:T(8,128)(2,1)S(1)} collective-permute-done((bf16[64,1024]{1,0:T(8,128)(2,1)S(1)}, bf16[64,1024]{1,0:T(8,128)(2,1)S(1)}, u32[]{:S(2)}, u32[]{:S(2)}) %collective-permute-start.6) | collective-permute-done | bytes 131104 | tf_op jit(solution)/shard_map/ppermute | solution.py:280
  57.3 0.5 collective-permute-start.10
  57.9 3.6 %collective-permute-done.10.refs_7_ = bf16[4,16,512]{2,1,0:T(8,128)(2,1)S(1)} collective-permute-done((bf16[4,16,512]{2,1,0:T(8,128)(2,1)S(1)}, bf16[4,16,512]{2,1,0:T(8,128)(2,1)S(1)}, u32[]{:S(2)}, u32[]{:S(2)}) %collective-permute-start.10) | collective-permute-done | bytes 65568 | tf_op jit(solution)/shard_map/ppermute | solution.py:280
  61.5 1.2 %merge.5 = (f32[16,4096]{1,0:T(8,128)S(1)}, bf16[16,4096]{1,0:T(8,128)(2,1)S(1)}, bf16[16,4096]{1,0:T(8,128)(2,1)S(1)}, bf16[16,4096]{1,0:T(8,128)(2,1)S(1)}) custom-call(f32[16,2048]{1,0:T(8,128)S(1)} %get-tuple-element.36.refs_0_, bf16[16,2048]{1,0:T(8,128)(2,1)S(1)} %get-tuple-element.37.refs_1_, bf16[16,2048]{1,0:T(8,128)(2,1)S(1)} %get-tuple-element.38.refs_2_, ...), custom_call_target="tpu_custom_call" | custom-call | flops 262144 | bytes 2097152 | tf_op jit(solution)/shard_map/merge/pallas_call | solution.py:162
  62.9 3.0 %collective-permute-start.12 = (bf16[16,4096]{1,0:T(8,128)(2,1)S(1)}, bf16[16,4096]{1,0:T(8,128)(2,1)S(1)}, u32[]{:S(2)}, u32[]{:S(2)}) collective-permute-start(bf16[16,4096]{1,0:T(8,128)(2,1)S(1)} %get-tuple-element.45), channel_id=1, source_target_pairs={{0,8},{2,10},{4,12},{6,14},{8,0},{10,2},{12,4},{14,6},{1,9},{3,11}... | collective-permute-start | bytes 393224 | tf_op jit(solution)/shard_map/ppermute | solution.py:280
  65.9 1.3 %collective-permute-start.13 = (bf16[16,4096]{1,0:T(8,128)(2,1)S(1)}, bf16[16,4096]{1,0:T(8,128)(2,1)S(1)}, u32[]{:S(2)}, u32[]{:S(2)}) collective-permute-start(bf16[16,4096]{1,0:T(8,128)(2,1)S(1)} %get-tuple-element.46), channel_id=1, source_target_pairs={{0,12},{2,14},{4,8},{6,10},{8,4},{10,6},{12,0},{14,2},{1,13},{3,15... | collective-permute-start | bytes 393224 | tf_op jit(solution)/shard_map/ppermute | solution.py:280
  67.2 1.7 %collective-permute-done.11.refs_1_ = bf16[16,4096]{1,0:T(8,128)(2,1)S(1)} collective-permute-done((bf16[16,4096]{1,0:T(8,128)(2,1)S(1)}, bf16[16,4096]{1,0:T(8,128)(2,1)S(1)}, u32[]{:S(2)}, u32[]{:S(2)}) %collective-permute-start.11) | collective-permute-done | bytes 131104 | tf_op jit(solution)/shard_map/ppermute | solution.py:280
  68.9 6.7 %collective-permute-done.12.refs_2_ = bf16[16,4096]{1,0:T(8,128)(2,1)S(1)} collective-permute-done((bf16[16,4096]{1,0:T(8,128)(2,1)S(1)}, bf16[16,4096]{1,0:T(8,128)(2,1)S(1)}, u32[]{:S(2)}, u32[]{:S(2)}) %collective-permute-start.12) | collective-permute-done | bytes 131104 | tf_op jit(solution)/shard_map/ppermute | solution.py:280
  75.6 5.8 %score.1 = f32[64,512]{1,0:T(8,128)S(1)} custom-call(s32[3]{0:T(128)S(1)} %pad_add_fusion.who_ref, f32[16,4096]{1,0:T(8,128)S(1)} %get-tuple-element.43.refs_0_, bf16[16,4096]{1,0:T(8,128)(2,1)S(1)} %collective-permute-done.11.refs_1_, bf16[16,4096]{1,0:T(8,128)(2,1)S(1)} %collective-permute-done.12.refs_2_, ...), custom_call_target="tpu_custom_call" | custom-call | flops 536870912 | bytes 262144 | tf_op jit(solution)/shard_map/score/pallas_call | solution.py:253
  81.4 0.5 collective-permute-start.16
  81.9 4.5 %collective-permute-done.16 = f32[64,512]{1,0:T(8,128)S(1)} collective-permute-done((f32[64,512]{1,0:T(8,128)S(1)}, f32[64,512]{1,0:T(8,128)S(1)}, u32[]{:S(2)}, u32[]{:S(2)}) %collective-permute-start.16) | collective-permute-done | bytes 131104 | tf_op jit(solution)/shard_map/ppermute | solution.py:280
  86.4 2.0 %collective-permute-start.17 = (bf16[64,512]{1,0:T(8,128)(2,1)S(1)}, bf16[64,512]{1,0:T(8,128)(2,1)S(1)}, u32[]{:S(2)}, u32[]{:S(2)}) collective-permute-start(bf16[64,512]{1,0:T(8,128)(2,1)S(1)} %add_convert_fusion), channel_id=1, source_target_pairs={{0,4},{2,6},{4,0},{6,2},{8,12},{10,14},{12,8},{14,10},{1,5},{3,7},... | collective-permute-start | bytes 196616 | tf_op jit(solution)/shard_map/ppermute | solution.py:280
  88.5 0.9 collective-permute-start.18
  89.4 1.5 %collective-permute-start.19 = (bf16[64,512]{1,0:T(8,128)(2,1)S(1)}, bf16[64,512]{1,0:T(8,128)(2,1)S(1)}, u32[]{:S(2)}, u32[]{:S(2)}) collective-permute-start(bf16[64,512]{1,0:T(8,128)(2,1)S(1)} %add_convert_fusion), channel_id=1, source_target_pairs={{0,12},{2,14},{4,8},{6,10},{8,4},{10,6},{12,0},{14,2},{1,13},{3,15... | collective-permute-start | bytes 196616 | tf_op jit(solution)/shard_map/ppermute | solution.py:280
  90.9 3.4 %collective-permute-done.18 = bf16[64,512]{1,0:T(8,128)(2,1)S(1)} collective-permute-done((bf16[64,512]{1,0:T(8,128)(2,1)S(1)}, bf16[64,512]{1,0:T(8,128)(2,1)S(1)}, u32[]{:S(2)}, u32[]{:S(2)}) %collective-permute-start.18) | collective-permute-done | bytes 65568 | tf_op jit(solution)/shard_map/ppermute | solution.py:280
  94.3 1.3 %collective-permute-done.19 = bf16[64,512]{1,0:T(8,128)(2,1)S(1)} collective-permute-done((bf16[64,512]{1,0:T(8,128)(2,1)S(1)}, bf16[64,512]{1,0:T(8,128)(2,1)S(1)}, u32[]{:S(2)}, u32[]{:S(2)}) %collective-permute-start.19) | collective-permute-done | bytes 65568 | tf_op jit(solution)/shard_map/ppermute | solution.py:280
  95.6 0.7 add_add_fusion
  (28 shorter events, 0.9 us)
Async XLA Ops:
  0.1 1.2 %copy-start = (s32[3584,64]{0,1:T(8,128)S(1)}, s32[3584,64]{0,1:T(8,128)}, u32[]{:S(2)}) copy-start(s32[3584,64]{0,1:T(8,128)} %param.8) | copy-start | bytes 2752516
  1.3 0.9 copy-start.2
  10.9 17.9 %collective-permute-start.1 = (bf16[4,64,1024]{2,1,0:T(8,128)(2,1)S(1)}, bf16[4,64,1024]{2,1,0:T(8,128)(2,1)S(1)}, u32[]{:S(2)}, u32[]{:S(2)}) collective-permute-start(bf16[4,64,1024]{2,1,0:T(8,128)(2,1)S(1)} %get-tuple-element.30), channel_id=1, source_target_pairs={{0,2},{2,0},{4,6},{6,4},{8,10},{10,8},{12,14},{14,12},{1,3},{3,1},... | collective-permute-start | bytes 1572872 | tf_op jit(solution)/shard_map/ppermute | solution.py:280
  13.9 35.3 %collective-permute-start.9 = (bf16[256,512]{1,0:T(8,128)(2,1)}, bf16[256,512]{1,0:T(8,128)(2,1)S(1)}, u32[]{:S(2)}, u32[]{:S(2)}) collective-permute-start(bf16[256,512]{1,0:T(8,128)(2,1)} %refs_9_.1), channel_id=1, source_target_pairs={{0,2},{2,0},{4,6},{6,4},{8,10},{10,8},{12,14},{14,12},{1,3},{3,1},... | collective-permute-start | bytes 786440 | tf_op jit(solution)/shard_map/ppermute | solution.py:280
  14.0 35.2 %copy-start.1 = (bf16[256,512]{1,0:T(8,128)(2,1)S(1)}, bf16[256,512]{1,0:T(8,128)(2,1)}, u32[]{:S(2)}) copy-start(bf16[256,512]{1,0:T(8,128)(2,1)} %refs_9_.1) | copy-start | bytes 786436
  26.8 22.4 %collective-permute-start = (bf16[4,16,2048]{2,1,0:T(8,128)(2,1)S(1)}, bf16[4,16,2048]{2,1,0:T(8,128)(2,1)S(1)}, u32[]{:S(2)}, u32[]{:S(2)}) collective-permute-start(bf16[4,16,2048]{2,1,0:T(8,128)(2,1)S(1)} %get-tuple-element.28.refs_2_), channel_id=1, source_target_pairs={{0,2},{2,0},{4,6},{6,4},{8,10},{10,8},{12,14},{14,12},{1,3},{3,1},... | collective-permute-start | bytes 786440 | tf_op jit(solution)/shard_map/ppermute | solution.py:280
  29.0 14.8 %collective-permute-start.2 = (bf16[64,1024]{1,0:T(8,128)(2,1)S(1)}, bf16[64,1024]{1,0:T(8,128)(2,1)S(1)}, u32[]{:S(2)}, u32[]{:S(2)}) collective-permute-start(bf16[64,1024]{1,0:T(8,128)(2,1)S(1)} %get-tuple-element.32.refs_0_), channel_id=1, source_target_pairs={{0,4},{2,6},{4,0},{6,2},{8,12},{10,14},{12,8},{14,10},{1,5},{3,7},... | collective-permute-start | bytes 393224 | tf_op jit(solution)/shard_map/ppermute | solution.py:280
  30.6 13.2 %collective-permute-start.3 = (bf16[64,1024]{1,0:T(8,128)(2,1)S(1)}, bf16[64,1024]{1,0:T(8,128)(2,1)S(1)}, u32[]{:S(2)}, u32[]{:S(2)}) collective-permute-start(bf16[64,1024]{1,0:T(8,128)(2,1)S(1)} %get-tuple-element.33), channel_id=1, source_target_pairs={{0,8},{2,10},{4,12},{6,14},{8,0},{10,2},{12,4},{14,6},{1,9},{3,11}... | collective-permute-start | bytes 393224 | tf_op jit(solution)/shard_map/ppermute | solution.py:280
  33.2 42.4 %copy-start.3 = (s32[1,8192]{1,0:T(1,128)S(1)}, s32[1,8192]{1,0:T(1,128)}, u32[]{:S(2)}) copy-start(s32[1,8192]{1,0:T(1,128)} %refs_8_.1) | copy-start | bytes 98308
  33.2 10.6 %collective-permute-start.4 = (bf16[64,1024]{1,0:T(8,128)(2,1)S(1)}, bf16[64,1024]{1,0:T(8,128)(2,1)S(1)}, u32[]{:S(2)}, u32[]{:S(2)}) collective-permute-start(bf16[64,1024]{1,0:T(8,128)(2,1)S(1)} %get-tuple-element.34), channel_id=1, source_target_pairs={{0,12},{2,14},{4,8},{6,10},{8,4},{10,6},{12,0},{14,2},{1,13},{3,15... | collective-permute-start | bytes 393224 | tf_op jit(solution)/shard_map/ppermute | solution.py:280
  44.5 5.8 %collective-permute-start.5 = (bf16[64,1024]{1,0:T(8,128)(2,1)S(1)}, bf16[64,1024]{1,0:T(8,128)(2,1)S(1)}, u32[]{:S(2)}, u32[]{:S(2)}) collective-permute-start(bf16[64,1024]{1,0:T(8,128)(2,1)S(1)} %total.1.refs_0_.refs_4_), channel_id=1, source_target_pairs={{0,4},{2,6},{4,0},{6,2},{8,12},{10,14},{12,8},{14,10},{1,5},{3,7},... | collective-permute-start | bytes 393224 | tf_op jit(solution)/shard_map/ppermute | solution.py:280
  45.4 11.9 %collective-permute-start.6 = (bf16[64,1024]{1,0:T(8,128)(2,1)S(1)}, bf16[64,1024]{1,0:T(8,128)(2,1)S(1)}, u32[]{:S(2)}, u32[]{:S(2)}) collective-permute-start(bf16[64,1024]{1,0:T(8,128)(2,1)S(1)} %total.1.refs_0_.refs_4_), channel_id=1, source_target_pairs={{0,8},{2,10},{4,12},{6,14},{8,0},{10,2},{12,4},{14,6},{1,9},{3,11}... | collective-permute-start | bytes 393224 | tf_op jit(solution)/shard_map/ppermute | solution.py:280
  48.7 12.8 %collective-permute-start.8 = (bf16[4,16,1536]{2,1,0:T(8,128)(2,1)S(1)}, bf16[4,16,1536]{2,1,0:T(8,128)(2,1)S(1)}, u32[]{:S(2)}, u32[]{:S(2)}) collective-permute-start(bf16[4,16,1536]{2,1,0:T(8,128)(2,1)S(1)} %get-tuple-element.35.refs_4_), channel_id=1, source_target_pairs={{0,2},{2,0},{4,6},{6,4},{8,10},{10,8},{12,14},{14,12},{1,3},{3,1},... | collective-permute-start | bytes 589832 | tf_op jit(solution)/shard_map/ppermute | solution.py:280
  49.2 8.6 %collective-permute-start.7 = (bf16[64,1024]{1,0:T(8,128)(2,1)S(1)}, bf16[64,1024]{1,0:T(8,128)(2,1)S(1)}, u32[]{:S(2)}, u32[]{:S(2)}) collective-permute-start(bf16[64,1024]{1,0:T(8,128)(2,1)S(1)} %total.1.refs_0_.refs_4_), channel_id=1, source_target_pairs={{0,12},{2,14},{4,8},{6,10},{8,4},{10,6},{12,0},{14,2},{1,13},{3,15... | collective-permute-start | bytes 393224 | tf_op jit(solution)/shard_map/ppermute | solution.py:280
  49.2 18.0 %collective-permute-start.14 = (bf16[256,512]{1,0:T(8,128)(2,1)S(1)}, bf16[256,512]{1,0:T(8,128)(2,1)S(1)}, u32[]{:S(2)}, u32[]{:S(2)}) collective-permute-start(bf16[256,512]{1,0:T(8,128)(2,1)S(1)} %copy-done.1), channel_id=1, source_target_pairs={{0,1},{1,0},{2,3},{3,2},{4,5},{5,4},{6,7},{7,6},{8,9},{9,8},{10,11... | collective-permute-start | bytes 786440 | tf_op jit(solution)/shard_map/ppermute | solution.py:283
  50.2 17.0 %collective-permute-start.15 = (bf16[256,512]{1,0:T(8,128)(2,1)S(1)}, bf16[256,512]{1,0:T(8,128)(2,1)S(1)}, u32[]{:S(2)}, u32[]{:S(2)}) collective-permute-start(bf16[256,512]{1,0:T(8,128)(2,1)S(1)} %collective-permute-done.9.refs_1_.refs_10_), channel_id=1, source_target_pairs={{0,1},{1,0},{2,3},{3,2},{4,5},{5,4},{6,7},{7,6},{8,9},{9,8},{10,11... | collective-permute-start | bytes 786440 | tf_op jit(solution)/shard_map/ppermute | solution.py:283
  57.3 4.3 %collective-permute-start.10 = (bf16[4,16,512]{2,1,0:T(8,128)(2,1)S(1)}, bf16[4,16,512]{2,1,0:T(8,128)(2,1)S(1)}, u32[]{:S(2)}, u32[]{:S(2)}) collective-permute-start(bf16[4,16,512]{2,1,0:T(8,128)(2,1)S(1)} %get-tuple-element.42), channel_id=1, source_target_pairs={{0,2},{2,0},{4,6},{6,4},{8,10},{10,8},{12,14},{14,12},{1,3},{3,1},... | collective-permute-start | bytes 196616 | tf_op jit(solution)/shard_map/ppermute | solution.py:280
  62.8 6.1 %collective-permute-start.11 = (bf16[16,4096]{1,0:T(8,128)(2,1)S(1)}, bf16[16,4096]{1,0:T(8,128)(2,1)S(1)}, u32[]{:S(2)}, u32[]{:S(2)}) collective-permute-start(bf16[16,4096]{1,0:T(8,128)(2,1)S(1)} %get-tuple-element.44), channel_id=1, source_target_pairs={{0,4},{2,6},{4,0},{6,2},{8,12},{10,14},{12,8},{14,10},{1,5},{3,7},... | collective-permute-start | bytes 393224 | tf_op jit(solution)/shard_map/ppermute | solution.py:280
  62.9 12.7 %collective-permute-start.12 = (bf16[16,4096]{1,0:T(8,128)(2,1)S(1)}, bf16[16,4096]{1,0:T(8,128)(2,1)S(1)}, u32[]{:S(2)}, u32[]{:S(2)}) collective-permute-start(bf16[16,4096]{1,0:T(8,128)(2,1)S(1)} %get-tuple-element.45), channel_id=1, source_target_pairs={{0,8},{2,10},{4,12},{6,14},{8,0},{10,2},{12,4},{14,6},{1,9},{3,11}... | collective-permute-start | bytes 393224 | tf_op jit(solution)/shard_map/ppermute | solution.py:280
  65.9 9.7 %collective-permute-start.13 = (bf16[16,4096]{1,0:T(8,128)(2,1)S(1)}, bf16[16,4096]{1,0:T(8,128)(2,1)S(1)}, u32[]{:S(2)}, u32[]{:S(2)}) collective-permute-start(bf16[16,4096]{1,0:T(8,128)(2,1)S(1)} %get-tuple-element.46), channel_id=1, source_target_pairs={{0,12},{2,14},{4,8},{6,10},{8,4},{10,6},{12,0},{14,2},{1,13},{3,15... | collective-permute-start | bytes 393224 | tf_op jit(solution)/shard_map/ppermute | solution.py:280
  81.4 5.0 %collective-permute-start.16 = (f32[64,512]{1,0:T(8,128)S(1)}, f32[64,512]{1,0:T(8,128)S(1)}, u32[]{:S(2)}, u32[]{:S(2)}) collective-permute-start(f32[64,512]{1,0:T(8,128)S(1)} %score.1), channel_id=1, source_target_pairs={{0,2},{2,0},{4,6},{6,4},{8,10},{10,8},{12,14},{14,12},{1,3},{3,1},... | collective-permute-start | bytes 393224 | tf_op jit(solution)/shard_map/ppermute | solution.py:280
  86.4 4.5 %collective-permute-start.17 = (bf16[64,512]{1,0:T(8,128)(2,1)S(1)}, bf16[64,512]{1,0:T(8,128)(2,1)S(1)}, u32[]{:S(2)}, u32[]{:S(2)}) collective-permute-start(bf16[64,512]{1,0:T(8,128)(2,1)S(1)} %add_convert_fusion), channel_id=1, source_target_pairs={{0,4},{2,6},{4,0},{6,2},{8,12},{10,14},{12,8},{14,10},{1,5},{3,7},... | collective-permute-start | bytes 196616 | tf_op jit(solution)/shard_map/ppermute | solution.py:280
  88.5 5.9 %collective-permute-start.18 = (bf16[64,512]{1,0:T(8,128)(2,1)S(1)}, bf16[64,512]{1,0:T(8,128)(2,1)S(1)}, u32[]{:S(2)}, u32[]{:S(2)}) collective-permute-start(bf16[64,512]{1,0:T(8,128)(2,1)S(1)} %add_convert_fusion), channel_id=1, source_target_pairs={{0,8},{2,10},{4,12},{6,14},{8,0},{10,2},{12,4},{14,6},{1,9},{3,11}... | collective-permute-start | bytes 196616 | tf_op jit(solution)/shard_map/ppermute | solution.py:280
  89.4 6.2 %collective-permute-start.19 = (bf16[64,512]{1,0:T(8,128)(2,1)S(1)}, bf16[64,512]{1,0:T(8,128)(2,1)S(1)}, u32[]{:S(2)}, u32[]{:S(2)}) collective-permute-start(bf16[64,512]{1,0:T(8,128)(2,1)S(1)} %add_convert_fusion), channel_id=1, source_target_pairs={{0,12},{2,14},{4,8},{6,10},{8,4},{10,6},{12,0},{14,2},{1,13},{3,15... | collective-permute-start | bytes 196616 | tf_op jit(solution)/shard_map/ppermute | solution.py:280

commit v9 on v8

--- a/solution.py
+++ b/solution.py
@@ -1,4 +1,5 @@
 import functools
+import math
 
 import jax
 import jax.numpy as jnp
@@ -194,40 +195,126 @@
     )(*parts, *after)
 
 
-def score_kernel(quarters, width, who_ref, *refs):
-    count = 2 * quarters + 5
-    sources, out_ref, targets = refs[:count], refs[count], refs[count + 1:2 * count + 1]
-    sems, row_ref, col_ref, member_ref, spread_ref, sketch_ref = refs[2 * count + 1:]
-    copies = fetch_all(sources, targets, sems)
-    left_refs, right_refs = targets[:quarters], targets[quarters:2 * quarters]
-    ids_ref, query_refs = targets[2 * quarters], targets[2 * quarters + 1:]
-    half, quarter, data = who_ref[0], who_ref[1], who_ref[2]
-    for copy in copies[:2 * quarters + 1]:
-        copy.wait()
-    total = left_refs[0][...]
-    for left_ref in left_refs[1:]:
-        total = total + left_ref[...].astype(jnp.float32)
-    row_ref[...] = total
+def pack_kernel(quarters, waits, *refs):
+    count = quarters + 2
+    sources, refs = refs[:count], refs[count + waits:]
+    own_g_ref, own_a_ref, outs, refs = refs[0], refs[1], refs[2:quarters + 1], refs[quarters + 1:]
+    targets, sems = refs[:-1], refs[-1]
+    for copy in fetch_all(sources, targets, sems):
+        copy.wait()
+    total = targets[0][...]
+    for target in targets[1:quarters]:
+        total = total + target[...].astype(jnp.float32)
+    own = total.astype(jnp.bfloat16)
+    own_g_ref[...] = own
+    kept_ref, got_ref = targets[quarters], targets[quarters + 1]
+    own_a_ref[...] = kept_ref[0] + got_ref[0].astype(jnp.float32)
+    rows, at = kept_ref.shape[1], own.shape[1]
+    width = kept_ref.shape[2] * rows // R
+    for d, out_ref in enumerate(outs, 1):
+        out_ref[:, :at] = own
+        for f in range(R // rows):
+            here = slice(f * width, (f + 1) * width)
+            out_ref[f * rows:(f + 1) * rows, at:] = (kept_ref[d, :, here] + got_ref[d, :, here].astype(jnp.float32)).astype(jnp.bfloat16)
+
+
+def pack(parts, kept, got, after):
+    quarters, rows, tokens = kept.shape
+    operands = list(parts) + [kept, got]
+    packed = jax.ShapeDtypeStruct((R, parts[0].shape[1] + tokens * rows // R), jnp.bfloat16)
+    shapes = [jax.ShapeDtypeStruct(parts[0].shape, jnp.bfloat16), jax.ShapeDtypeStruct((rows, tokens), jnp.float32)]
+    shapes = shapes + [packed] * (quarters - 1)
+    return pl.pallas_call(
+        functools.partial(pack_kernel, quarters, len(after)),
+        in_specs=[pl.BlockSpec(memory_space=pl.ANY)] * (len(operands) + len(after)),
+        out_specs=[pl.BlockSpec(memory_space=pltpu.VMEM)] * len(shapes),
+        out_shape=shapes,
+        scratch_shapes=[pltpu.VMEM(operand.shape, operand.dtype) for operand in operands] + [pltpu.SemaphoreType.DMA((len(operands),))],
+        compiler_params=pltpu.CompilerParams(vmem_limit_bytes=VMEM // 6),
+        cost_estimate=pl.CostEstimate(flops=4 * kept.size, bytes_accessed=8 * kept.size, transcendentals=0),
+        name="pack",
+    )(*operands, *after)
+
+
+def touch_kernel(*refs):
+    refs[-1][...] = jnp.zeros(refs[-1].shape, refs[-1].dtype)
+
+
+def touch(after):
+    return pl.pallas_call(
+        touch_kernel,
+        in_specs=[pl.BlockSpec(memory_space=pl.ANY)] * len(after),
+        out_specs=pl.BlockSpec(memory_space=pltpu.VMEM),
+        out_shape=jax.ShapeDtypeStruct((8, 128), jnp.float32),
+        compiler_params=pltpu.CompilerParams(vmem_limit_bytes=VMEM // 6),
+        name="touch",
+    )(*after)
+
+
+def sketch_rows(half, first, row_ref, col_ref, ids_ref, member_ref, spread_refs, sink):
+    columns, tokens = row_ref.shape
+    owned = ids_ref.shape[1] // 2
+    width = math.gcd(tokens, 512)
+    numbers = lax.broadcasted_iota(jnp.int32, (SEQ_DEV, 1), 0)
+    ids = ids_ref[:, pl.ds(pl.multiple_of(half * owned + first, 128), tokens)]
+    member_ref[...] = (ids == numbers).astype(jnp.bfloat16)
+    rows = spread_refs[0].shape[0] // R
+    for g in range(columns // rows):
+        spread_ref = spread_refs[g % 2]
+        for at in range(0, tokens, width):
+            right = col_ref[:, first + at:first + at + width].astype(jnp.float32)
+            for r in range(rows):
+                row = row_ref[g * rows + r:g * rows + r + 1, at:at + width]
+                spread_ref[r * R:(r + 1) * R, at:at + width] = (row * right).astype(jnp.bfloat16)
+        part = lax.dot_general(member_ref[...], spread_ref[...], LAST, preferred_element_type=jnp.float32)
+        sink(slice(g * rows * R, (g + 1) * rows * R), part)
+
+
+def sketch_kernel(quarters, packed, who_ref, *refs):
+    count = quarters + 2 if packed else 2 * quarters + 1
+    sources, base_ref, col_ref, targets = refs[:count], refs[count], refs[count + 1], refs[count + 2:2 * count + 2]
+    sems, row_ref, member_ref, spread_0, spread_1 = refs[2 * count + 2:]
+    half, quarter = who_ref[0], who_ref[1]
+    for copy in fetch_all(sources, targets, sems):
+        copy.wait()
+    ids_ref, own_ref, right_refs = targets[0], targets[1], targets[2:2 + quarters]
     piece = right_refs[0].shape[1]
     for d, right_ref in enumerate(right_refs):
-        col_ref[:, pl.ds(pl.multiple_of((quarter ^ d) * piece, piece), piece)] = right_ref[...].astype(jnp.float32)
-    numbers = lax.broadcasted_iota(jnp.int32, (SEQ_DEV, 1), 0)
-    owned = col_ref.shape[1]
-    ids = ids_ref[:, pl.ds(pl.multiple_of(half * owned, 128), owned)]
-    member_ref[...] = (ids == numbers).astype(jnp.bfloat16)
-    rows = spread_ref.shape[0] // R
-
-    def group(g, carry):
-        for at in range(0, owned, width):
-            right = col_ref[:, at:at + width]
-            for r in range(rows):
-                row = row_ref[pl.ds(g * rows + r, 1), at:at + width]
-                spread_ref[r * R:(r + 1) * R, at:at + width] = (row * right).astype(jnp.bfloat16)
-        here = pl.ds(pl.multiple_of(g * rows * R, rows * R), rows * R)
-        sketch_ref[:, here] = lax.dot_general(member_ref[...], spread_ref[...], LAST, preferred_element_type=jnp.float32)
-        return carry
-
-    lax.fori_loop(0, row_ref.shape[0] // rows, group, 0)
+        here = pl.ds(pl.multiple_of((quarter ^ d) * piece, piece), piece)
+        col_ref[:, here] = right_ref[:, :piece]
+    if packed:
+        rows, tokens = row_ref.shape
+        width = tokens * rows // R
+        for f in range(R // rows):
+            here = slice(f * width, (f + 1) * width)
+            total = own_ref[:, here]
+            for right_ref in right_refs[1:]:
+                total = total + right_ref[f * rows:(f + 1) * rows, piece:].astype(jnp.float32)
+            row_ref[:, here] = total
+    else:
+        row_ref[...] = sum([ref[...].astype(jnp.float32) for ref in targets[2 + quarters:]], own_ref[...])
+
+    def sink(here, part):
+        base_ref[:, here] = part
+
+    sketch_rows(half, 0, row_ref, col_ref, ids_ref, member_ref, (spread_0, spread_1), sink)
+
+
+def score_kernel(lefts, first, who_ref, *refs):
+    count = lefts + 7
+    sources, out_ref, targets = refs[:count], refs[count], refs[count + 1:2 * count + 1]
+    sems, sketch_ref, row_ref, member_ref, spread_0, spread_1 = refs[2 * count + 1:]
+    copies = fetch_all(sources, targets, sems)
+    half, data = who_ref[0], who_ref[2]
+    ids_ref, col_ref, base_ref, left_refs, query_refs = targets[0], targets[1], targets[2], targets[3:-4], targets[-4:]
+    for copy in copies[:-4]:
+        copy.wait()
+    row_ref[...] = sum([ref[...].astype(jnp.float32) for ref in left_refs[1:]], left_refs[0][...])
+
+    def sink(here, part):
+        sketch_ref[:, here] = base_ref[:, here] + part
+
+    sketch_rows(half, first, row_ref, col_ref, ids_ref, member_ref, (spread_0, spread_1), sink)
     entries = sketch_ref[...]
     high = entries.astype(jnp.bfloat16)
     low = (entries - high.astype(jnp.float32)).astype(jnp.bfloat16)
@@ -236,7 +323,7 @@
     swapped = half == 1
     near = jnp.where(swapped, both[:, middle:], both[:, :middle])
     far = jnp.where(swapped, both[:, :middle], both[:, middle:])
-    for copy in copies[2 * quarters + 1:]:
+    for copy in copies[-4:]:
         copy.wait()
     rows = query_refs[0].shape[0]
     for side in range(2):
@@ -245,28 +332,25 @@
         out_ref[:, pl.ds(pl.multiple_of((data ^ side) * rows, rows), rows)] = part[:SEQ_DEV] + part[SEQ_DEV:]
 
 
-def score(who, left, right, ids, queries):
-    operands = left + right + [ids] + queries
-    columns, tokens = left[0].shape
+def call_sketch(kernel, who, operands, columns, tokens, shapes, extra, name):
     rows = min(4, columns)
-    shape = (SEQ_DEV, 2 * queries[0].shape[0])
-    return pl.pallas_call(
-        functools.partial(score_kernel, len(left), min(512, tokens)),
+    return pl.pallas_call(
+        kernel,
         in_specs=[pl.BlockSpec(memory_space=pltpu.SMEM)] + [pl.BlockSpec(memory_space=pl.ANY)] * len(operands),
-        out_specs=pl.BlockSpec(memory_space=pltpu.VMEM),
-        out_shape=jax.ShapeDtypeStruct(shape, jnp.float32),
+        out_specs=[pl.BlockSpec(memory_space=pltpu.VMEM)] * len(shapes),
+        out_shape=shapes,
         scratch_shapes=[pltpu.VMEM(operand.shape, operand.dtype) for operand in operands]
+        + [pltpu.SemaphoreType.DMA((len(operands),))]
+        + extra
         + [
-            pltpu.SemaphoreType.DMA((len(operands),)),
             pltpu.VMEM((columns, tokens), jnp.float32),
-            pltpu.VMEM((R, tokens), jnp.float32),
             pltpu.VMEM((SEQ_DEV, tokens), jnp.bfloat16),
             pltpu.VMEM((rows * R, tokens), jnp.bfloat16),
-            pltpu.VMEM((SEQ_DEV, columns * R), jnp.float32),
+            pltpu.VMEM((rows * R, tokens), jnp.bfloat16),
         ],
         compiler_params=pltpu.CompilerParams(vmem_limit_bytes=VMEM // 3),
         cost_estimate=pl.CostEstimate(flops=2 * tokens * columns * R * SEQ_DEV, bytes_accessed=4 * columns * tokens, transcendentals=0),
-        name="score",
+        name=name,
     )(who, *operands)
 
 
@@ -298,14 +382,29 @@
     pair_g = merge([], [kept_g, got_g], [sent_0])
     moved_g = [swap(pair_g[d], 2 * d) for d in range(1, quarters)]
     sent_1, chunk_1 = chunk(4, 3, [pair_g[1]])
-    own_g = total_of([pair_g[0]] + moved_g, [sent_1])
-    right = [own_g] + [swap(own_g, 2 * d) for d in range(1, quarters)]
+    columns = R // quarters
+    packed = columns % 16 == 0
+    if packed:
+        sums = pack([pair_g[0]] + moved_g, chunk_0[0], chunk_0[1], [sent_1])
+        own_g, own_a = sums[:2]
+        right = [own_g] + [swap(sums[d + 1], 2 * d) for d in range(1, quarters)]
+        first = [segment_ids, own_a] + right
+    else:
+        own_g = total_of([pair_g[0]] + moved_g, [sent_1])
+        right = [own_g] + [swap(own_g, 2 * d) for d in range(1, quarters)]
+        pair_0 = merge([], chunk_0, [])
+        first = [segment_ids, pair_0[0]] + right + [swap(pair_0[d], 2 * d) for d in range(1, quarters)]
     sent_2, chunk_2 = chunk(7, 1, [own_g, far])
-    pair_a = merge([], chunk_0, right[1:])
-    pair_a = merge(pair_a, chunk_1 + chunk_2, [])
-    left = [pair_a[0]] + [swap(pair_a[d], 2 * d) for d in range(1, quarters)]
-
-    total = score(who, left, right, segment_ids, every)
+    pair_1 = merge([], chunk_1 + chunk_2, [touch(right[1:])])
+    left = [pair_1[0]] + [swap(pair_1[d], 2 * d) for d in range(1, quarters)]
+
+    early, entries = owned // 2, columns * R
+    shapes = [jax.ShapeDtypeStruct((SEQ_DEV, entries), jnp.float32), jax.ShapeDtypeStruct((R, owned), jnp.bfloat16)]
+    base, col = call_sketch(functools.partial(sketch_kernel, quarters, packed), who, first, columns, early, shapes, [], "sketch")
+    shapes = [jax.ShapeDtypeStruct((SEQ_DEV, 2 * queries.shape[0]), jnp.float32)]
+    extra = [pltpu.VMEM((SEQ_DEV, entries), jnp.float32)]
+    rest = [segment_ids, col, base] + left + every
+    total = call_sketch(functools.partial(score_kernel, quarters, early), who, rest, columns, owned - early, shapes, extra, "score")[0]
     total = (total + swap(total, 1)).astype(jnp.bfloat16)
     parts = [total] + [swap(total, 2 * d) for d in range(1, quarters)]
     parts = [part.astype(jnp.float32) for part in parts]

time: 96.5 us -> 93.6 us (0.970)
  waiting for transfers between devices: 23.8 us -> 20.9 us
    ppermute x18, waiting for transfers between devices: 23.8 us -> 20.9 us  [swap(): lax.ppermute(array, 'tensor', [(k, k ^ distance) for k in range(n_tensor)])]
    pallas_call x2 -> x4, Pallas kernels: 6.4 us -> 7.06 us  [the longest x2 6.31 us: call_sketch(): pl.pallas_call(kernel, in_specs=[pl.BlockSpec(memory_space=pltpu.SMEM)] +...]
  transfers between devices with their start and end apart: 20 -> 20, of which waited for: 8 -> 7; matrix products, arithmetic and copies ran while one was open for 0% -> 0% of each run, Pallas kernels for 32% -> 36%
where the time goes in v9:
time: 93.6 us; the launch traced here: 93.5 us
  Pallas kernels  45.2 us (48%)
  starting transfers between devices  24.3 us (26%)
  waiting for transfers between devices  20.9 us (22%)
  local copies, waits for them, and re-layouts  2.14 us (2%)
    pallas_call x4, Pallas kernels, project(): pl.pallas_call(functools.partial(project_kernel, scale, first, split, ord...  37.1 us
    ppermute x18, starting transfers between devices, swap(): lax.ppermute(array, 'tensor', [(k, k ^ distance) for k in range(n_tensor)])  24.3 us
    ppermute x18, waiting for transfers between devices, swap(): lax.ppermute(array, 'tensor', [(k, k ^ distance) for k in range(n_tensor)])  20.9 us
    pallas_call x2, Pallas kernels, call_sketch(): pl.pallas_call(kernel, in_specs=[pl.BlockSpec(memory_space=pltpu.SMEM)] +...  6.31 us
    unnamed x8, local copies, waits for them, and re-layouts  2.14 us
  transfers between devices with their start and end apart: 20, of which 7 were waited for; matrix products, arithmetic and copies ran while one was open for 0% of the time, Pallas kernels for 36%

profile of v9, /device:TPU:0, one launch (start us, length us, event | category | flops | bytes accessed | tf_op | source)
XLA Modules:
  0.0 93.5 jit_solution(15393910063528592623)
XLA Ops:
  0.1 1.2 %copy-done = s32[3584,64]{0,1:T(8,128)S(1)} copy-done((s32[3584,64]{0,1:T(8,128)S(1)}, s32[3584,64]{0,1:T(8,128)}, u32[]{:S(2)}) %copy-start) | copy-done | bytes 917528
  1.3 0.9 %copy-done.2 = s32[1024,64]{0,1:T(8,128)S(1)} copy-done((s32[1024,64]{0,1:T(8,128)S(1)}, s32[1024,64]{0,1:T(8,128)}, u32[]{:S(2)}) %copy-start.2) | copy-done | bytes 262168
  2.2 8.6 %project.4 = (bf16[4,64,1024]{2,1,0:T(8,128)(2,1)S(1)}, f32[4,64,1024]{2,1,0:T(8,128)S(1)}, bf16[64,3584]{1,0:T(8,128)(2,1)S(1)}) custom-call(s32[3]{0:T(128)S(1)} %pad_add_fusion.who_ref, bf16[8192,1024]{1,0:T(8,128)(2,1)} %x_hbm.4, s32[64,1024]{1,0:T(8,128)S(1)} %bitcast.6, s32[64,3584]{1,0:T(8,128)S(1)} %bitcast.5), custom_call_target="tpu_custom_call" | custom-call | flops 1073741824 | bytes 16777216 | tf_op jit(solution)/shard_map/project/pallas_call | solution.py:115
  10.9 3.0 %collective-permute-start = (bf16[4,64,1024]{2,1,0:T(8,128)(2,1)S(1)}, bf16[4,64,1024]{2,1,0:T(8,128)(2,1)S(1)}, u32[]{:S(2)}, u32[]{:S(2)}) collective-permute-start(bf16[4,64,1024]{2,1,0:T(8,128)(2,1)S(1)} %get-tuple-element.30), channel_id=1, source_target_pairs={{0,2},{2,0},{4,6},{6,4},{8,10},{10,8},{12,14},{14,12},{1,3},{3,1},... | collective-permute-start | bytes 1572872 | tf_op jit(solution)/shard_map/ppermute | solution.py:364
  13.9 12.8 %project.5 = (bf16[4,16,2048]{2,1,0:T(8,128)(2,1)S(1)}, f32[4,16,2048]{2,1,0:T(8,128)S(1)}) custom-call(s32[3]{0:T(128)S(1)} %pad_add_fusion.who_ref, bf16[8192,3584]{1,0:T(8,128)(2,1)} %x_hbm.7, bf16[64,3584]{1,0:T(8,128)(2,1)S(1)} %get-tuple-element.31.sign_source), custom_call_target="tpu_custom_call" | custom-call | flops 1879048192 | bytes 29360128 | tf_op jit(solution)/shard_map/project/pallas_call | solution.py:115
  26.8 2.0 %collective-permute-start.9 = (bf16[256,512]{1,0:T(8,128)(2,1)S(1)}, bf16[256,512]{1,0:T(8,128)(2,1)S(1)}, u32[]{:S(2)}, u32[]{:S(2)}) collective-permute-start(bf16[256,512]{1,0:T(8,128)(2,1)S(1)} %copy-done.1), channel_id=1, source_target_pairs={{0,2},{2,0},{4,6},{6,4},{8,10},{10,8},{12,14},{14,12},{1,3},{3,1},... | collective-permute-start | bytes 786440 | tf_op jit(solution)/shard_map/ppermute | solution.py:364
  29.0 1.6 %collective-permute-start.1 = (bf16[64,1024]{1,0:T(8,128)(2,1)S(1)}, bf16[64,1024]{1,0:T(8,128)(2,1)S(1)}, u32[]{:S(2)}, u32[]{:S(2)}) collective-permute-start(bf16[64,1024]{1,0:T(8,128)(2,1)S(1)} %get-tuple-element.34.refs_0_), channel_id=1, source_target_pairs={{0,4},{2,6},{4,0},{6,2},{8,12},{10,14},{12,8},{14,10},{1,5},{3,7},... | collective-permute-start | bytes 393224 | tf_op jit(solution)/shard_map/ppermute | solution.py:364
  30.6 2.6 %collective-permute-start.2 = (bf16[64,1024]{1,0:T(8,128)(2,1)S(1)}, bf16[64,1024]{1,0:T(8,128)(2,1)S(1)}, u32[]{:S(2)}, u32[]{:S(2)}) collective-permute-start(bf16[64,1024]{1,0:T(8,128)(2,1)S(1)} %get-tuple-element.35), channel_id=1, source_target_pairs={{0,8},{2,10},{4,12},{6,14},{8,0},{10,2},{12,4},{14,6},{1,9},{3,11}... | collective-permute-start | bytes 393224 | tf_op jit(solution)/shard_map/ppermute | solution.py:364
  33.2 0.2 collective-permute-start.3
  33.5 10.3 %project.6 = (bf16[4,16,1536]{2,1,0:T(8,128)(2,1)S(1)}, f32[4,16,1536]{2,1,0:T(8,128)S(1)}) custom-call(s32[3]{0:T(128)S(1)} %pad_add_fusion.who_ref, bf16[8192,3584]{1,0:T(8,128)(2,1)} %x_hbm.7, bf16[64,3584]{1,0:T(8,128)(2,1)S(1)} %get-tuple-element.31.sign_source, bf16[64,1024]{1,0:T(8,128)(2,1)S(1)} %get-tuple-element.34.refs_0_), custom_call_target="tpu_custom_call" | custom-call | flops 1409286144 | bytes 22020096 | tf_op jit(solution)/shard_map/project/pallas_call | solution.py:115
  43.8 0.7 pack.1
  44.6 0.9 collective-permute-start.5
  45.5 3.3 %collective-permute-start.6 = (bf16[64,1536]{1,0:T(8,128)(2,1)S(1)}, bf16[64,1536]{1,0:T(8,128)(2,1)S(1)}, u32[]{:S(2)}, u32[]{:S(2)}) collective-permute-start(bf16[64,1536]{1,0:T(8,128)(2,1)S(1)} %get-tuple-element.42), channel_id=1, source_target_pairs={{0,8},{2,10},{4,12},{6,14},{8,0},{10,2},{12,4},{14,6},{1,9},{3,11}... | collective-permute-start | bytes 589832 | tf_op jit(solution)/shard_map/ppermute | solution.py:364
  49.0 0.3 collective-permute-start.8
  49.3 2.9 %collective-permute-done.5.refs_3_.refs_0_ = bf16[64,1536]{1,0:T(8,128)(2,1)S(1)} collective-permute-done((bf16[64,1536]{1,0:T(8,128)(2,1)S(1)}, bf16[64,1536]{1,0:T(8,128)(2,1)S(1)}, u32[]{:S(2)}, u32[]{:S(2)}) %collective-permute-start.5) | collective-permute-done | bytes 196640 | tf_op jit(solution)/shard_map/ppermute | solution.py:364
  52.2 5.4 %project.7 = (bf16[4,16,512]{2,1,0:T(8,128)(2,1)S(1)}, f32[4,16,512]{2,1,0:T(8,128)S(1)}) custom-call(s32[3]{0:T(128)S(1)} %pad_add_fusion.who_ref, bf16[8192,3584]{1,0:T(8,128)(2,1)} %x_hbm.7, bf16[64,3584]{1,0:T(8,128)(2,1)S(1)} %get-tuple-element.31.sign_source, bf16[64,1024]{1,0:T(8,128)(2,1)S(1)} %get-tuple-element.40.refs_2_.refs_0_, ...), custom_call_target="tpu_custom_call" | custom-call | flops 469762048 | bytes 7340032 | tf_op jit(solution)/shard_map/project/pallas_call | solution.py:115
  57.6 4.7 %collective-permute-done.6.refs_4_.refs_1_ = bf16[64,1536]{1,0:T(8,128)(2,1)S(1)} collective-permute-done((bf16[64,1536]{1,0:T(8,128)(2,1)S(1)}, bf16[64,1536]{1,0:T(8,128)(2,1)S(1)}, u32[]{:S(2)}, u32[]{:S(2)}) %collective-permute-start.6) | collective-permute-done | bytes 196640 | tf_op jit(solution)/shard_map/ppermute | solution.py:364
  62.3 0.5 collective-permute-start.10
  62.8 3.7 %collective-permute-done.10.refs_3_ = bf16[4,16,512]{2,1,0:T(8,128)(2,1)S(1)} collective-permute-done((bf16[4,16,512]{2,1,0:T(8,128)(2,1)S(1)}, bf16[4,16,512]{2,1,0:T(8,128)(2,1)S(1)}, u32[]{:S(2)}, u32[]{:S(2)}) %collective-permute-start.10) | collective-permute-done | bytes 65568 | tf_op jit(solution)/shard_map/ppermute | solution.py:364
  66.6 0.8 merge.3
  67.4 2.9 %collective-permute-start.12 = (bf16[16,2048]{1,0:T(8,128)(2,1)S(1)}, bf16[16,2048]{1,0:T(8,128)(2,1)S(1)}, u32[]{:S(2)}, u32[]{:S(2)}) collective-permute-start(bf16[16,2048]{1,0:T(8,128)(2,1)S(1)} %get-tuple-element.51), channel_id=1, source_target_pairs={{0,8},{2,10},{4,12},{6,14},{8,0},{10,2},{12,4},{14,6},{1,9},{3,11}... | collective-permute-start | bytes 196616 | tf_op jit(solution)/shard_map/ppermute | solution.py:364
  70.3 1.5 %collective-permute-start.13 = (bf16[16,2048]{1,0:T(8,128)(2,1)S(1)}, bf16[16,2048]{1,0:T(8,128)(2,1)S(1)}, u32[]{:S(2)}, u32[]{:S(2)}) collective-permute-start(bf16[16,2048]{1,0:T(8,128)(2,1)S(1)} %get-tuple-element.52), channel_id=1, source_target_pairs={{0,12},{2,14},{4,8},{6,10},{8,4},{10,6},{12,0},{14,2},{1,13},{3,15... | collective-permute-start | bytes 196616 | tf_op jit(solution)/shard_map/ppermute | solution.py:364
  71.8 3.2 %sketch.1 = (f32[64,1024]{1,0:T(8,128)S(1)}, bf16[64,4096]{1,0:T(8,128)(2,1)S(1)}) custom-call(s32[3]{0:T(128)S(1)} %pad_add_fusion.who_ref, s32[1,8192]{1,0:T(1,128)S(1)} %copy-done.3, f32[16,2048]{1,0:T(8,128)S(1)} %get-tuple-element.39.refs_1_, bf16[64,1024]{1,0:T(8,128)(2,1)S(1)} %get-tuple-element.40.refs_2_.refs_0_, ...), custom_call_target="tpu_custom_call" | custom-call | flops 268435456 | bytes 131072 | tf_op jit(solution)/shard_map/sketch/pallas_call | solution.py:337
  75.0 1.4 %collective-permute-done.13.refs_6_ = bf16[16,2048]{1,0:T(8,128)(2,1)S(1)} collective-permute-done((bf16[16,2048]{1,0:T(8,128)(2,1)S(1)}, bf16[16,2048]{1,0:T(8,128)(2,1)S(1)}, u32[]{:S(2)}, u32[]{:S(2)}) %collective-permute-start.13) | collective-permute-done | bytes 65568 | tf_op jit(solution)/shard_map/ppermute | solution.py:364
  76.4 3.1 %score.1 = f32[64,512]{1,0:T(8,128)S(1)} custom-call(s32[3]{0:T(128)S(1)} %pad_add_fusion.who_ref, s32[1,8192]{1,0:T(1,128)S(1)} %copy-done.3, bf16[64,4096]{1,0:T(8,128)(2,1)S(1)} %get-tuple-element.44.refs_1_, f32[64,1024]{1,0:T(8,128)S(1)} %get-tuple-element.45.refs_2_, f32[16,2048]{1,0:T(8,128)S(1)} %get-tuple-element.49.refs_3_, ...), custom_call_target="tpu_custom_call" | custom-call | flops 268435456 | bytes 131072 | tf_op jit(solution)/shard_map/score/pallas_call | solution.py:337
  79.5 0.6 collective-permute-start.16
  80.1 4.5 %collective-permute-done.16 = f32[64,512]{1,0:T(8,128)S(1)} collective-permute-done((f32[64,512]{1,0:T(8,128)S(1)}, f32[64,512]{1,0:T(8,128)S(1)}, u32[]{:S(2)}, u32[]{:S(2)}) %collective-permute-start.16) | collective-permute-done | bytes 131104 | tf_op jit(solution)/shard_map/ppermute | solution.py:364
  84.7 2.0 %collective-permute-start.18 = (bf16[64,512]{1,0:T(8,128)(2,1)S(1)}, bf16[64,512]{1,0:T(8,128)(2,1)S(1)}, u32[]{:S(2)}, u32[]{:S(2)}) collective-permute-start(bf16[64,512]{1,0:T(8,128)(2,1)S(1)} %add_convert_fusion), channel_id=1, source_target_pairs={{0,8},{2,10},{4,12},{6,14},{8,0},{10,2},{12,4},{14,6},{1,9},{3,11}... | collective-permute-start | bytes 196616 | tf_op jit(solution)/shard_map/ppermute | solution.py:364
  86.7 2.3 %collective-permute-start.19 = (bf16[64,512]{1,0:T(8,128)(2,1)S(1)}, bf16[64,512]{1,0:T(8,128)(2,1)S(1)}, u32[]{:S(2)}, u32[]{:S(2)}) collective-permute-start(bf16[64,512]{1,0:T(8,128)(2,1)S(1)} %add_convert_fusion), channel_id=1, source_target_pairs={{0,12},{2,14},{4,8},{6,10},{8,4},{10,6},{12,0},{14,2},{1,13},{3,15... | collective-permute-start | bytes 196616 | tf_op jit(solution)/shard_map/ppermute | solution.py:364
  89.0 0.9 collective-permute-done.18
  89.9 2.9 %collective-permute-done.19 = bf16[64,512]{1,0:T(8,128)(2,1)S(1)} collective-permute-done((bf16[64,512]{1,0:T(8,128)(2,1)S(1)}, bf16[64,512]{1,0:T(8,128)(2,1)S(1)}, u32[]{:S(2)}, u32[]{:S(2)}) %collective-permute-start.19) | collective-permute-done | bytes 65568 | tf_op jit(solution)/shard_map/ppermute | solution.py:364
  92.8 0.7 add_add_fusion
  (29 shorter events, 0.8 us)
Async XLA Ops:
  0.1 1.2 %copy-start = (s32[3584,64]{0,1:T(8,128)S(1)}, s32[3584,64]{0,1:T(8,128)}, u32[]{:S(2)}) copy-start(s32[3584,64]{0,1:T(8,128)} %param.8) | copy-start | bytes 2752516
  1.3 0.9 %copy-start.2 = (s32[1024,64]{0,1:T(8,128)S(1)}, s32[1024,64]{0,1:T(8,128)}, u32[]{:S(2)}) copy-start(s32[1024,64]{0,1:T(8,128)} %param.9) | copy-start | bytes 786436
  2.2 24.6 %copy-start.1 = (bf16[256,512]{1,0:T(8,128)(2,1)S(1)}, bf16[256,512]{1,0:T(8,128)(2,1)}, u32[]{:S(2)}) copy-start(bf16[256,512]{1,0:T(8,128)(2,1)} %refs_7_.1) | copy-start | bytes 786436
  10.9 17.9 %collective-permute-start = (bf16[4,64,1024]{2,1,0:T(8,128)(2,1)S(1)}, bf16[4,64,1024]{2,1,0:T(8,128)(2,1)S(1)}, u32[]{:S(2)}, u32[]{:S(2)}) collective-permute-start(bf16[4,64,1024]{2,1,0:T(8,128)(2,1)S(1)} %get-tuple-element.30), channel_id=1, source_target_pairs={{0,2},{2,0},{4,6},{6,4},{8,10},{10,8},{12,14},{14,12},{1,3},{3,1},... | collective-permute-start | bytes 1572872 | tf_op jit(solution)/shard_map/ppermute | solution.py:364
  26.7 17.1 %collective-permute-start.4 = (bf16[4,16,2048]{2,1,0:T(8,128)(2,1)S(1)}, bf16[4,16,2048]{2,1,0:T(8,128)(2,1)S(1)}, u32[]{:S(2)}, u32[]{:S(2)}) collective-permute-start(bf16[4,16,2048]{2,1,0:T(8,128)(2,1)S(1)} %get-tuple-element.32.refs_2_), channel_id=1, source_target_pairs={{0,2},{2,0},{4,6},{6,4},{8,10},{10,8},{12,14},{14,12},{1,3},{3,1},... | collective-permute-start | bytes 786440 | tf_op jit(solution)/shard_map/ppermute | solution.py:364
  26.8 22.6 %collective-permute-start.9 = (bf16[256,512]{1,0:T(8,128)(2,1)S(1)}, bf16[256,512]{1,0:T(8,128)(2,1)S(1)}, u32[]{:S(2)}, u32[]{:S(2)}) collective-permute-start(bf16[256,512]{1,0:T(8,128)(2,1)S(1)} %copy-done.1), channel_id=1, source_target_pairs={{0,2},{2,0},{4,6},{6,4},{8,10},{10,8},{12,14},{14,12},{1,3},{3,1},... | collective-permute-start | bytes 786440 | tf_op jit(solution)/shard_map/ppermute | solution.py:364
  29.0 14.8 %collective-permute-start.1 = (bf16[64,1024]{1,0:T(8,128)(2,1)S(1)}, bf16[64,1024]{1,0:T(8,128)(2,1)S(1)}, u32[]{:S(2)}, u32[]{:S(2)}) collective-permute-start(bf16[64,1024]{1,0:T(8,128)(2,1)S(1)} %get-tuple-element.34.refs_0_), channel_id=1, source_target_pairs={{0,4},{2,6},{4,0},{6,2},{8,12},{10,14},{12,8},{14,10},{1,5},{3,7},... | collective-permute-start | bytes 393224 | tf_op jit(solution)/shard_map/ppermute | solution.py:364
  30.6 13.2 %collective-permute-start.2 = (bf16[64,1024]{1,0:T(8,128)(2,1)S(1)}, bf16[64,1024]{1,0:T(8,128)(2,1)S(1)}, u32[]{:S(2)}, u32[]{:S(2)}) collective-permute-start(bf16[64,1024]{1,0:T(8,128)(2,1)S(1)} %get-tuple-element.35), channel_id=1, source_target_pairs={{0,8},{2,10},{4,12},{6,14},{8,0},{10,2},{12,4},{14,6},{1,9},{3,11}... | collective-permute-start | bytes 393224 | tf_op jit(solution)/shard_map/ppermute | solution.py:364
  33.2 38.6 %copy-start.3 = (s32[1,8192]{1,0:T(1,128)S(1)}, s32[1,8192]{1,0:T(1,128)}, u32[]{:S(2)}) copy-start(s32[1,8192]{1,0:T(1,128)} %refs_0_.3) | copy-start | bytes 98308
  33.2 10.6 %collective-permute-start.3 = (bf16[64,1024]{1,0:T(8,128)(2,1)S(1)}, bf16[64,1024]{1,0:T(8,128)(2,1)S(1)}, u32[]{:S(2)}, u32[]{:S(2)}) collective-permute-start(bf16[64,1024]{1,0:T(8,128)(2,1)S(1)} %get-tuple-element.36), channel_id=1, source_target_pairs={{0,12},{2,14},{4,8},{6,10},{8,4},{10,6},{12,0},{14,2},{1,13},{3,15... | collective-permute-start | bytes 393224 | tf_op jit(solution)/shard_map/ppermute | solution.py:364
  44.6 7.6 %collective-permute-start.5 = (bf16[64,1536]{1,0:T(8,128)(2,1)S(1)}, bf16[64,1536]{1,0:T(8,128)(2,1)S(1)}, u32[]{:S(2)}, u32[]{:S(2)}) collective-permute-start(bf16[64,1536]{1,0:T(8,128)(2,1)S(1)} %get-tuple-element.41), channel_id=1, source_target_pairs={{0,4},{2,6},{4,0},{6,2},{8,12},{10,14},{12,8},{14,10},{1,5},{3,7},... | collective-permute-start | bytes 589832 | tf_op jit(solution)/shard_map/ppermute | solution.py:364
  45.5 16.8 %collective-permute-start.6 = (bf16[64,1536]{1,0:T(8,128)(2,1)S(1)}, bf16[64,1536]{1,0:T(8,128)(2,1)S(1)}, u32[]{:S(2)}, u32[]{:S(2)}) collective-permute-start(bf16[64,1536]{1,0:T(8,128)(2,1)S(1)} %get-tuple-element.42), channel_id=1, source_target_pairs={{0,8},{2,10},{4,12},{6,14},{8,0},{10,2},{12,4},{14,6},{1,9},{3,11}... | collective-permute-start | bytes 589832 | tf_op jit(solution)/shard_map/ppermute | solution.py:364
  48.8 14.0 %collective-permute-start.7 = (bf16[64,1536]{1,0:T(8,128)(2,1)S(1)}, bf16[64,1536]{1,0:T(8,128)(2,1)S(1)}, u32[]{:S(2)}, u32[]{:S(2)}) collective-permute-start(bf16[64,1536]{1,0:T(8,128)(2,1)S(1)} %get-tuple-element.43), channel_id=1, source_target_pairs={{0,12},{2,14},{4,8},{6,10},{8,4},{10,6},{12,0},{14,2},{1,13},{3,15... | collective-permute-start | bytes 589832 | tf_op jit(solution)/shard_map/ppermute | solution.py:364
  49.0 17.5 %collective-permute-start.8 = (bf16[4,16,1536]{2,1,0:T(8,128)(2,1)S(1)}, bf16[4,16,1536]{2,1,0:T(8,128)(2,1)S(1)}, u32[]{:S(2)}, u32[]{:S(2)}) collective-permute-start(bf16[4,16,1536]{2,1,0:T(8,128)(2,1)S(1)} %get-tuple-element.38.refs_6_), channel_id=1, source_target_pairs={{0,2},{2,0},{4,6},{6,4},{8,10},{10,8},{12,14},{14,12},{1,3},{3,1},... | collective-permute-start | bytes 589832 | tf_op jit(solution)/shard_map/ppermute | solution.py:364
  49.3 25.6 %collective-permute-start.14 = (bf16[256,512]{1,0:T(8,128)(2,1)S(1)}, bf16[256,512]{1,0:T(8,128)(2,1)S(1)}, u32[]{:S(2)}, u32[]{:S(2)}) collective-permute-start(bf16[256,512]{1,0:T(8,128)(2,1)S(1)} %copy-done.1), channel_id=1, source_target_pairs={{0,1},{1,0},{2,3},{3,2},{4,5},{5,4},{6,7},{7,6},{8,9},{9,8},{10,11... | collective-permute-start | bytes 786440 | tf_op jit(solution)/shard_map/ppermute | solution.py:367
  52.2 22.8 %collective-permute-start.15 = (bf16[256,512]{1,0:T(8,128)(2,1)S(1)}, bf16[256,512]{1,0:T(8,128)(2,1)S(1)}, u32[]{:S(2)}, u32[]{:S(2)}) collective-permute-start(bf16[256,512]{1,0:T(8,128)(2,1)S(1)} %collective-permute-done.9.refs_1_.refs_8_), channel_id=1, source_target_pairs={{0,1},{1,0},{2,3},{3,2},{4,5},{5,4},{6,7},{7,6},{8,9},{9,8},{10,11... | collective-permute-start | bytes 786440 | tf_op jit(solution)/shard_map/ppermute | solution.py:367
  62.3 4.3 %collective-permute-start.10 = (bf16[4,16,512]{2,1,0:T(8,128)(2,1)S(1)}, bf16[4,16,512]{2,1,0:T(8,128)(2,1)S(1)}, u32[]{:S(2)}, u32[]{:S(2)}) collective-permute-start(bf16[4,16,512]{2,1,0:T(8,128)(2,1)S(1)} %get-tuple-element.48), channel_id=1, source_target_pairs={{0,2},{2,0},{4,6},{6,4},{8,10},{10,8},{12,14},{14,12},{1,3},{3,1},... | collective-permute-start | bytes 196616 | tf_op jit(solution)/shard_map/ppermute | solution.py:364
  67.3 7.7 %collective-permute-start.11 = (bf16[16,2048]{1,0:T(8,128)(2,1)S(1)}, bf16[16,2048]{1,0:T(8,128)(2,1)S(1)}, u32[]{:S(2)}, u32[]{:S(2)}) collective-permute-start(bf16[16,2048]{1,0:T(8,128)(2,1)S(1)} %get-tuple-element.50), channel_id=1, source_target_pairs={{0,4},{2,6},{4,0},{6,2},{8,12},{10,14},{12,8},{14,10},{1,5},{3,7},... | collective-permute-start | bytes 196616 | tf_op jit(solution)/shard_map/ppermute | solution.py:364
  67.4 7.6 %collective-permute-start.12 = (bf16[16,2048]{1,0:T(8,128)(2,1)S(1)}, bf16[16,2048]{1,0:T(8,128)(2,1)S(1)}, u32[]{:S(2)}, u32[]{:S(2)}) collective-permute-start(bf16[16,2048]{1,0:T(8,128)(2,1)S(1)} %get-tuple-element.51), channel_id=1, source_target_pairs={{0,8},{2,10},{4,12},{6,14},{8,0},{10,2},{12,4},{14,6},{1,9},{3,11}... | collective-permute-start | bytes 196616 | tf_op jit(solution)/shard_map/ppermute | solution.py:364
  70.3 6.1 %collective-permute-start.13 = (bf16[16,2048]{1,0:T(8,128)(2,1)S(1)}, bf16[16,2048]{1,0:T(8,128)(2,1)S(1)}, u32[]{:S(2)}, u32[]{:S(2)}) collective-permute-start(bf16[16,2048]{1,0:T(8,128)(2,1)S(1)} %get-tuple-element.52), channel_id=1, source_target_pairs={{0,12},{2,14},{4,8},{6,10},{8,4},{10,6},{12,0},{14,2},{1,13},{3,15... | collective-permute-start | bytes 196616 | tf_op jit(solution)/shard_map/ppermute | solution.py:364
  79.5 5.0 %collective-permute-start.16 = (f32[64,512]{1,0:T(8,128)S(1)}, f32[64,512]{1,0:T(8,128)S(1)}, u32[]{:S(2)}, u32[]{:S(2)}) collective-permute-start(f32[64,512]{1,0:T(8,128)S(1)} %score.1), channel_id=1, source_target_pairs={{0,2},{2,0},{4,6},{6,4},{8,10},{10,8},{12,14},{14,12},{1,3},{3,1},... | collective-permute-start | bytes 393224 | tf_op jit(solution)/shard_map/ppermute | solution.py:364
  84.6 4.5 %collective-permute-start.17 = (bf16[64,512]{1,0:T(8,128)(2,1)S(1)}, bf16[64,512]{1,0:T(8,128)(2,1)S(1)}, u32[]{:S(2)}, u32[]{:S(2)}) collective-permute-start(bf16[64,512]{1,0:T(8,128)(2,1)S(1)} %add_convert_fusion), channel_id=1, source_target_pairs={{0,4},{2,6},{4,0},{6,2},{8,12},{10,14},{12,8},{14,10},{1,5},{3,7},... | collective-permute-start | bytes 196616 | tf_op jit(solution)/shard_map/ppermute | solution.py:364
  84.7 5.2 %collective-permute-start.18 = (bf16[64,512]{1,0:T(8,128)(2,1)S(1)}, bf16[64,512]{1,0:T(8,128)(2,1)S(1)}, u32[]{:S(2)}, u32[]{:S(2)}) collective-permute-start(bf16[64,512]{1,0:T(8,128)(2,1)S(1)} %add_convert_fusion), channel_id=1, source_target_pairs={{0,8},{2,10},{4,12},{6,14},{8,0},{10,2},{12,4},{14,6},{1,9},{3,11}... | collective-permute-start | bytes 196616 | tf_op jit(solution)/shard_map/ppermute | solution.py:364
  86.7 6.1 %collective-permute-start.19 = (bf16[64,512]{1,0:T(8,128)(2,1)S(1)}, bf16[64,512]{1,0:T(8,128)(2,1)S(1)}, u32[]{:S(2)}, u32[]{:S(2)}) collective-permute-start(bf16[64,512]{1,0:T(8,128)(2,1)S(1)} %add_convert_fusion), channel_id=1, source_target_pairs={{0,12},{2,14},{4,8},{6,10},{8,4},{10,6},{12,0},{14,2},{1,13},{3,15... | collective-permute-start | bytes 196616 | tf_op jit(solution)/shard_map/ppermute | solution.py:364

commit v10 on v9

--- a/solution.py
+++ b/solution.py
@@ -137,13 +137,16 @@
     return copies
 
 
-def merge_kernel(quarters, bases, pairs, waits, *refs):
+def merge_kernel(quarters, bases, pairs, carried, waits, *refs):
     count = bases + 2 * pairs
-    sources, outs = refs[:count], refs[count + waits:count + waits + quarters]
-    targets, sems = refs[count + waits + quarters:-1], refs[-1]
+    sources, refs = refs[:count + carried], refs[count + carried + waits:]
+    outs, carries, refs = refs[:quarters], refs[quarters:quarters + carried], refs[quarters + carried:]
+    targets, sems = refs[:-1], refs[-1]
     copies = fetch_all(sources, targets, sems)
     for copy in copies:
         copy.wait()
+    for k, carry_ref in enumerate(carries):
+        carry_ref[...] = targets[count + k][...]
     for d, out_ref in enumerate(outs):
         at = 0
         if bases:
@@ -156,15 +159,16 @@
             at = at + width
 
 
-def merge(base, arrays, after):
+def merge(base, arrays, after, carry=()):
     quarters, rows = arrays[0].shape[:2]
     tokens = sum(array.shape[2] for array in arrays[::2]) + (base[0].shape[1] if base else 0)
-    operands = list(base) + list(arrays)
-    return pl.pallas_call(
-        functools.partial(merge_kernel, quarters, len(base), len(arrays) // 2, len(after)),
+    operands = list(base) + list(arrays) + list(carry)
+    return pl.pallas_call(
+        functools.partial(merge_kernel, quarters, len(base), len(arrays) // 2, len(carry), len(after)),
         in_specs=[pl.BlockSpec(memory_space=pl.ANY)] * (len(operands) + len(after)),
-        out_specs=[pl.BlockSpec(memory_space=pltpu.VMEM)] * quarters,
-        out_shape=[jax.ShapeDtypeStruct((rows, tokens), jnp.bfloat16 if d else jnp.float32) for d in range(quarters)],
+        out_specs=[pl.BlockSpec(memory_space=pltpu.VMEM)] * (quarters + len(carry)),
+        out_shape=[jax.ShapeDtypeStruct((rows, tokens), jnp.bfloat16 if d else jnp.float32) for d in range(quarters)]
+        + [jax.ShapeDtypeStruct(array.shape, array.dtype) for array in carry],
         scratch_shapes=[pltpu.VMEM(operand.shape, operand.dtype) for operand in operands] + [pltpu.SemaphoreType.DMA((len(operands),))],
         compiler_params=pltpu.CompilerParams(vmem_limit_bytes=VMEM // 6),
         cost_estimate=pl.CostEstimate(flops=quarters * rows * tokens, bytes_accessed=8 * quarters * rows * tokens, transcendentals=0),
@@ -367,7 +371,7 @@
         return lax.ppermute(array, "dp", [(0, 1), (1, 0)])
 
     far = swap(queries, 1)
-    every = [queries, far, cross(queries), cross(far)]
+    cross_near = cross(queries)
 
     scale_in, scale_out = FF ** -0.5, D ** -0.5
     sent_g, kept_g, signs = project(out_grads, proj_out.T, who, scale_out, quarters, False, 0, owned, 1024, proj_in.T)
@@ -381,7 +385,7 @@
     sent_0, chunk_0 = chunk(0, 4, [])
     pair_g = merge([], [kept_g, got_g], [sent_0])
     moved_g = [swap(pair_g[d], 2 * d) for d in range(1, quarters)]
-    sent_1, chunk_1 = chunk(4, 3, [pair_g[1]])
+    sent_1, chunk_1 = chunk(4, 3, [pair_g[1], far, cross_near])
     columns = R // quarters
     packed = columns % 16 == 0
     if packed:
@@ -394,8 +398,9 @@
         right = [own_g] + [swap(own_g, 2 * d) for d in range(1, quarters)]
         pair_0 = merge([], chunk_0, [])
         first = [segment_ids, pair_0[0]] + right + [swap(pair_0[d], 2 * d) for d in range(1, quarters)]
-    sent_2, chunk_2 = chunk(7, 1, [own_g, far])
-    pair_1 = merge([], chunk_1 + chunk_2, [touch(right[1:])])
+    sent_2, chunk_2 = chunk(7, 1, [own_g])
+    pair_1 = merge([], chunk_1 + chunk_2, [touch(right[1:])], [far])
+    every = [queries, far, cross_near, cross(pair_1[quarters])]
     left = [pair_1[0]] + [swap(pair_1[d], 2 * d) for d in range(1, quarters)]
 
     early, entries = owned // 2, columns * R

time: 93.6 us -> 93.9 us (level)
  starting transfers between devices: 24.3 us -> 29.9 us
  waiting for transfers between devices: 20.9 us -> 15.5 us
    ppermute x18, starting transfers between devices: 24.3 us -> 29.8 us  [swap(): lax.ppermute(array, 'tensor', [(k, k ^ distance) for k in range(n_tensor)])]
    ppermute x18, waiting for transfers between devices: 20.9 us -> 15.5 us  [swap(): lax.ppermute(array, 'tensor', [(k, k ^ distance) for k in range(n_tensor)])]
  transfers between devices with their start and end apart: 20 -> 20, of which waited for: 7 -> 6; matrix products, arithmetic and copies ran while one was open for 0% -> 0% of each run, Pallas kernels for 36% -> 34%
where the time goes in v10:
time: 93.9 us; the launch traced here: 93.7 us
  Pallas kernels  45.2 us (48%)
  starting transfers between devices  29.9 us (32%)
  waiting for transfers between devices  15.5 us (17%)
  local copies, waits for them, and re-layouts  2.14 us (2%)
    pallas_call x4, Pallas kernels, project(): pl.pallas_call(functools.partial(project_kernel, scale, first, split, ord...  37.1 us
    ppermute x18, starting transfers between devices, swap(): lax.ppermute(array, 'tensor', [(k, k ^ distance) for k in range(n_tensor)])  29.8 us
    ppermute x18, waiting for transfers between devices, swap(): lax.ppermute(array, 'tensor', [(k, k ^ distance) for k in range(n_tensor)])  15.5 us
    pallas_call x2, Pallas kernels, call_sketch(): pl.pallas_call(kernel, in_specs=[pl.BlockSpec(memory_space=pltpu.SMEM)] +...  6.32 us
    unnamed x8, local copies, waits for them, and re-layouts  2.14 us
  transfers between devices with their start and end apart: 20, of which 6 were waited for; matrix products, arithmetic and copies ran while one was open for 0% of the time, Pallas kernels for 34%

profile of v10, /device:TPU:0, one launch (start us, length us, event | category | flops | bytes accessed | tf_op | source)
XLA Modules:
  0.0 93.7 jit_solution(4642261569968145715)
XLA Ops:
  0.1 1.2 %copy-done = s32[3584,64]{0,1:T(8,128)S(1)} copy-done((s32[3584,64]{0,1:T(8,128)S(1)}, s32[3584,64]{0,1:T(8,128)}, u32[]{:S(2)}) %copy-start) | copy-done | bytes 917528
  1.3 0.9 %copy-done.2 = s32[1024,64]{0,1:T(8,128)S(1)} copy-done((s32[1024,64]{0,1:T(8,128)S(1)}, s32[1024,64]{0,1:T(8,128)}, u32[]{:S(2)}) %copy-start.2) | copy-done | bytes 262168
  2.2 8.6 %project.4 = (bf16[4,64,1024]{2,1,0:T(8,128)(2,1)S(1)}, f32[4,64,1024]{2,1,0:T(8,128)S(1)}, bf16[64,3584]{1,0:T(8,128)(2,1)S(1)}) custom-call(s32[3]{0:T(128)S(1)} %pad_add_fusion.who_ref, bf16[8192,1024]{1,0:T(8,128)(2,1)} %x_hbm.4, s32[64,1024]{1,0:T(8,128)S(1)} %bitcast.6, s32[64,3584]{1,0:T(8,128)S(1)} %bitcast.5), custom_call_target="tpu_custom_call" | custom-call | flops 1073741824 | bytes 16777216 | tf_op jit(solution)/shard_map/project/pallas_call | solution.py:115
  10.9 3.0 %collective-permute-start = (bf16[4,64,1024]{2,1,0:T(8,128)(2,1)S(1)}, bf16[4,64,1024]{2,1,0:T(8,128)(2,1)S(1)}, u32[]{:S(2)}, u32[]{:S(2)}) collective-permute-start(bf16[4,64,1024]{2,1,0:T(8,128)(2,1)S(1)} %get-tuple-element.31), channel_id=1, source_target_pairs={{0,2},{2,0},{4,6},{6,4},{8,10},{10,8},{12,14},{14,12},{1,3},{3,1},... | collective-permute-start | bytes 1572872 | tf_op jit(solution)/shard_map/ppermute | solution.py:368
  14.0 12.8 %project.5 = (bf16[4,16,2048]{2,1,0:T(8,128)(2,1)S(1)}, f32[4,16,2048]{2,1,0:T(8,128)S(1)}) custom-call(s32[3]{0:T(128)S(1)} %pad_add_fusion.who_ref, bf16[8192,3584]{1,0:T(8,128)(2,1)} %x_hbm.7, bf16[64,3584]{1,0:T(8,128)(2,1)S(1)} %get-tuple-element.32.sign_source), custom_call_target="tpu_custom_call" | custom-call | flops 1879048192 | bytes 29360128 | tf_op jit(solution)/shard_map/project/pallas_call | solution.py:115
  26.8 2.0 %collective-permute-start.4 = (bf16[4,16,2048]{2,1,0:T(8,128)(2,1)S(1)}, bf16[4,16,2048]{2,1,0:T(8,128)(2,1)S(1)}, u32[]{:S(2)}, u32[]{:S(2)}) collective-permute-start(bf16[4,16,2048]{2,1,0:T(8,128)(2,1)S(1)} %get-tuple-element.33.refs_2_), channel_id=1, source_target_pairs={{0,2},{2,0},{4,6},{6,4},{8,10},{10,8},{12,14},{14,12},{1,3},{3,1},... | collective-permute-start | bytes 786440 | tf_op jit(solution)/shard_map/ppermute | solution.py:368
  29.0 1.6 %collective-permute-start.1 = (bf16[64,1024]{1,0:T(8,128)(2,1)S(1)}, bf16[64,1024]{1,0:T(8,128)(2,1)S(1)}, u32[]{:S(2)}, u32[]{:S(2)}) collective-permute-start(bf16[64,1024]{1,0:T(8,128)(2,1)S(1)} %get-tuple-element.35.refs_0_), channel_id=1, source_target_pairs={{0,4},{2,6},{4,0},{6,2},{8,12},{10,14},{12,8},{14,10},{1,5},{3,7},... | collective-permute-start | bytes 393224 | tf_op jit(solution)/shard_map/ppermute | solution.py:368
  30.6 2.6 %collective-permute-start.2 = (bf16[64,1024]{1,0:T(8,128)(2,1)S(1)}, bf16[64,1024]{1,0:T(8,128)(2,1)S(1)}, u32[]{:S(2)}, u32[]{:S(2)}) collective-permute-start(bf16[64,1024]{1,0:T(8,128)(2,1)S(1)} %get-tuple-element.36), channel_id=1, source_target_pairs={{0,8},{2,10},{4,12},{6,14},{8,0},{10,2},{12,4},{14,6},{1,9},{3,11}... | collective-permute-start | bytes 393224 | tf_op jit(solution)/shard_map/ppermute | solution.py:368
  33.2 3.2 %collective-permute-start.3 = (bf16[64,1024]{1,0:T(8,128)(2,1)S(1)}, bf16[64,1024]{1,0:T(8,128)(2,1)S(1)}, u32[]{:S(2)}, u32[]{:S(2)}) collective-permute-start(bf16[64,1024]{1,0:T(8,128)(2,1)S(1)} %get-tuple-element.37), channel_id=1, source_target_pairs={{0,12},{2,14},{4,8},{6,10},{8,4},{10,6},{12,0},{14,2},{1,13},{3,15... | collective-permute-start | bytes 393224 | tf_op jit(solution)/shard_map/ppermute | solution.py:368
  36.4 10.3 %project.6 = (bf16[4,16,1536]{2,1,0:T(8,128)(2,1)S(1)}, f32[4,16,1536]{2,1,0:T(8,128)S(1)}) custom-call(s32[3]{0:T(128)S(1)} %pad_add_fusion.who_ref, bf16[8192,3584]{1,0:T(8,128)(2,1)} %x_hbm.7, bf16[64,3584]{1,0:T(8,128)(2,1)S(1)} %get-tuple-element.32.sign_source, bf16[64,1024]{1,0:T(8,128)(2,1)S(1)} %get-tuple-element.35.refs_0_, ...), custom_call_target="tpu_custom_call" | custom-call | flops 1409286144 | bytes 22020096 | tf_op jit(solution)/shard_map/project/pallas_call | solution.py:115
  46.8 0.7 pack.1
  47.6 1.2 %collective-permute-start.8 = (bf16[64,1536]{1,0:T(8,128)(2,1)S(1)}, bf16[64,1536]{1,0:T(8,128)(2,1)S(1)}, u32[]{:S(2)}, u32[]{:S(2)}) collective-permute-start(bf16[64,1536]{1,0:T(8,128)(2,1)S(1)} %get-tuple-element.43), channel_id=1, source_target_pairs={{0,8},{2,10},{4,12},{6,14},{8,0},{10,2},{12,4},{14,6},{1,9},{3,11}... | collective-permute-start | bytes 589832 | tf_op jit(solution)/shard_map/ppermute | solution.py:368
  48.8 3.2 %collective-permute-start.9 = (bf16[64,1536]{1,0:T(8,128)(2,1)S(1)}, bf16[64,1536]{1,0:T(8,128)(2,1)S(1)}, u32[]{:S(2)}, u32[]{:S(2)}) collective-permute-start(bf16[64,1536]{1,0:T(8,128)(2,1)S(1)} %get-tuple-element.44), channel_id=1, source_target_pairs={{0,12},{2,14},{4,8},{6,10},{8,4},{10,6},{12,0},{14,2},{1,13},{3,15... | collective-permute-start | bytes 589832 | tf_op jit(solution)/shard_map/ppermute | solution.py:368
  52.0 1.5 %collective-permute-start.10 = (bf16[4,16,1536]{2,1,0:T(8,128)(2,1)S(1)}, bf16[4,16,1536]{2,1,0:T(8,128)(2,1)S(1)}, u32[]{:S(2)}, u32[]{:S(2)}) collective-permute-start(bf16[4,16,1536]{2,1,0:T(8,128)(2,1)S(1)} %get-tuple-element.39.refs_6_), channel_id=1, source_target_pairs={{0,2},{2,0},{4,6},{6,4},{8,10},{10,8},{12,14},{14,12},{1,3},{3,1},... | collective-permute-start | bytes 589832 | tf_op jit(solution)/shard_map/ppermute | solution.py:368
  53.5 5.4 %project.7 = (bf16[4,16,512]{2,1,0:T(8,128)(2,1)S(1)}, f32[4,16,512]{2,1,0:T(8,128)S(1)}) custom-call(s32[3]{0:T(128)S(1)} %pad_add_fusion.who_ref, bf16[8192,3584]{1,0:T(8,128)(2,1)} %x_hbm.7, bf16[64,3584]{1,0:T(8,128)(2,1)S(1)} %get-tuple-element.32.sign_source, bf16[64,1024]{1,0:T(8,128)(2,1)S(1)} %get-tuple-element.41.refs_2_.refs_0_), custom_call_target="tpu_custom_call" | custom-call | flops 469762048 | bytes 7340032 | tf_op jit(solution)/shard_map/project/pallas_call | solution.py:115
  58.9 0.6 collective-permute-start.11
  59.5 4.4 %collective-permute-done.8.refs_4_.refs_1_ = bf16[64,1536]{1,0:T(8,128)(2,1)S(1)} collective-permute-done((bf16[64,1536]{1,0:T(8,128)(2,1)S(1)}, bf16[64,1536]{1,0:T(8,128)(2,1)S(1)}, u32[]{:S(2)}, u32[]{:S(2)}) %collective-permute-start.8) | collective-permute-done | bytes 196640 | tf_op jit(solution)/shard_map/ppermute | solution.py:368
  63.9 0.8 merge.3
  64.8 2.7 %collective-permute-start.12 = (bf16[16,2048]{1,0:T(8,128)(2,1)S(1)}, bf16[16,2048]{1,0:T(8,128)(2,1)S(1)}, u32[]{:S(2)}, u32[]{:S(2)}) collective-permute-start(bf16[16,2048]{1,0:T(8,128)(2,1)S(1)} %get-tuple-element.51), channel_id=1, source_target_pairs={{0,4},{2,6},{4,0},{6,2},{8,12},{10,14},{12,8},{14,10},{1,5},{3,7},... | collective-permute-start | bytes 196616 | tf_op jit(solution)/shard_map/ppermute | solution.py:368
  67.5 1.1 %collective-permute-start.13 = (bf16[16,2048]{1,0:T(8,128)(2,1)S(1)}, bf16[16,2048]{1,0:T(8,128)(2,1)S(1)}, u32[]{:S(2)}, u32[]{:S(2)}) collective-permute-start(bf16[16,2048]{1,0:T(8,128)(2,1)S(1)} %get-tuple-element.52), channel_id=1, source_target_pairs={{0,8},{2,10},{4,12},{6,14},{8,0},{10,2},{12,4},{14,6},{1,9},{3,11}... | collective-permute-start | bytes 196616 | tf_op jit(solution)/shard_map/ppermute | solution.py:368
  68.6 1.4 %collective-permute-start.14 = (bf16[16,2048]{1,0:T(8,128)(2,1)S(1)}, bf16[16,2048]{1,0:T(8,128)(2,1)S(1)}, u32[]{:S(2)}, u32[]{:S(2)}) collective-permute-start(bf16[16,2048]{1,0:T(8,128)(2,1)S(1)} %get-tuple-element.53), channel_id=1, source_target_pairs={{0,12},{2,14},{4,8},{6,10},{8,4},{10,6},{12,0},{14,2},{1,13},{3,15... | collective-permute-start | bytes 196616 | tf_op jit(solution)/shard_map/ppermute | solution.py:368
  70.0 3.2 %sketch.1 = (f32[64,1024]{1,0:T(8,128)S(1)}, bf16[64,4096]{1,0:T(8,128)(2,1)S(1)}) custom-call(s32[3]{0:T(128)S(1)} %pad_add_fusion.who_ref, s32[1,8192]{1,0:T(1,128)S(1)} %copy-done.3, f32[16,2048]{1,0:T(8,128)S(1)} %get-tuple-element.40.refs_1_, bf16[64,1024]{1,0:T(8,128)(2,1)S(1)} %get-tuple-element.41.refs_2_.refs_0_, ...), custom_call_target="tpu_custom_call" | custom-call | flops 268435456 | bytes 131072 | tf_op jit(solution)/shard_map/sketch/pallas_call | solution.py:341
  73.2 2.7 %collective-permute-done.13.refs_5_ = bf16[16,2048]{1,0:T(8,128)(2,1)S(1)} collective-permute-done((bf16[16,2048]{1,0:T(8,128)(2,1)S(1)}, bf16[16,2048]{1,0:T(8,128)(2,1)S(1)}, u32[]{:S(2)}, u32[]{:S(2)}) %collective-permute-start.13) | collective-permute-done | bytes 65568 | tf_op jit(solution)/shard_map/ppermute | solution.py:368
  75.9 3.1 %score.1 = f32[64,512]{1,0:T(8,128)S(1)} custom-call(s32[3]{0:T(128)S(1)} %pad_add_fusion.who_ref, s32[1,8192]{1,0:T(1,128)S(1)} %copy-done.3, bf16[64,4096]{1,0:T(8,128)(2,1)S(1)} %get-tuple-element.45.refs_1_, f32[64,1024]{1,0:T(8,128)S(1)} %get-tuple-element.46.refs_2_, f32[16,2048]{1,0:T(8,128)S(1)} %get-tuple-element.50.refs_3_, ...), custom_call_target="tpu_custom_call" | custom-call | flops 268435456 | bytes 131072 | tf_op jit(solution)/shard_map/score/pallas_call | solution.py:341
  79.1 1.1 %collective-permute-start.16 = (f32[64,512]{1,0:T(8,128)S(1)}, f32[64,512]{1,0:T(8,128)S(1)}, u32[]{:S(2)}, u32[]{:S(2)}) collective-permute-start(f32[64,512]{1,0:T(8,128)S(1)} %score.1), channel_id=1, source_target_pairs={{0,2},{2,0},{4,6},{6,4},{8,10},{10,8},{12,14},{14,12},{1,3},{3,1},... | collective-permute-start | bytes 393224 | tf_op jit(solution)/shard_map/ppermute | solution.py:368
  80.2 3.9 %collective-permute-done.16 = f32[64,512]{1,0:T(8,128)S(1)} collective-permute-done((f32[64,512]{1,0:T(8,128)S(1)}, f32[64,512]{1,0:T(8,128)S(1)}, u32[]{:S(2)}, u32[]{:S(2)}) %collective-permute-start.16) | collective-permute-done | bytes 131104 | tf_op jit(solution)/shard_map/ppermute | solution.py:368
  84.2 1.7 %collective-permute-start.17 = (bf16[64,512]{1,0:T(8,128)(2,1)S(1)}, bf16[64,512]{1,0:T(8,128)(2,1)S(1)}, u32[]{:S(2)}, u32[]{:S(2)}) collective-permute-start(bf16[64,512]{1,0:T(8,128)(2,1)S(1)} %add_convert_fusion), channel_id=1, source_target_pairs={{0,4},{2,6},{4,0},{6,2},{8,12},{10,14},{12,8},{14,10},{1,5},{3,7},... | collective-permute-start | bytes 196616 | tf_op jit(solution)/shard_map/ppermute | solution.py:368
  85.8 1.1 %collective-permute-start.18 = (bf16[64,512]{1,0:T(8,128)(2,1)S(1)}, bf16[64,512]{1,0:T(8,128)(2,1)S(1)}, u32[]{:S(2)}, u32[]{:S(2)}) collective-permute-start(bf16[64,512]{1,0:T(8,128)(2,1)S(1)} %add_convert_fusion), channel_id=1, source_target_pairs={{0,8},{2,10},{4,12},{6,14},{8,0},{10,2},{12,4},{14,6},{1,9},{3,11}... | collective-permute-start | bytes 196616 | tf_op jit(solution)/shard_map/ppermute | solution.py:368
  86.9 1.7 %collective-permute-start.19 = (bf16[64,512]{1,0:T(8,128)(2,1)S(1)}, bf16[64,512]{1,0:T(8,128)(2,1)S(1)}, u32[]{:S(2)}, u32[]{:S(2)}) collective-permute-start(bf16[64,512]{1,0:T(8,128)(2,1)S(1)} %add_convert_fusion), channel_id=1, source_target_pairs={{0,12},{2,14},{4,8},{6,10},{8,4},{10,6},{12,0},{14,2},{1,13},{3,15... | collective-permute-start | bytes 196616 | tf_op jit(solution)/shard_map/ppermute | solution.py:368
  89.2 3.0 %collective-permute-done.18 = bf16[64,512]{1,0:T(8,128)(2,1)S(1)} collective-permute-done((bf16[64,512]{1,0:T(8,128)(2,1)S(1)}, bf16[64,512]{1,0:T(8,128)(2,1)S(1)}, u32[]{:S(2)}, u32[]{:S(2)}) %collective-permute-start.18) | collective-permute-done | bytes 65568 | tf_op jit(solution)/shard_map/ppermute | solution.py:368
  92.2 0.8 collective-permute-done.19
  93.0 0.7 add_add_fusion
  (29 shorter events, 1.1 us)
Async XLA Ops:
  0.1 1.2 %copy-start = (s32[3584,64]{0,1:T(8,128)S(1)}, s32[3584,64]{0,1:T(8,128)}, u32[]{:S(2)}) copy-start(s32[3584,64]{0,1:T(8,128)} %param.8) | copy-start | bytes 2752516
  1.3 0.9 %copy-start.2 = (s32[1024,64]{0,1:T(8,128)S(1)}, s32[1024,64]{0,1:T(8,128)}, u32[]{:S(2)}) copy-start(s32[1024,64]{0,1:T(8,128)} %param.9) | copy-start | bytes 786436
  10.9 17.9 %collective-permute-start = (bf16[4,64,1024]{2,1,0:T(8,128)(2,1)S(1)}, bf16[4,64,1024]{2,1,0:T(8,128)(2,1)S(1)}, u32[]{:S(2)}, u32[]{:S(2)}) collective-permute-start(bf16[4,64,1024]{2,1,0:T(8,128)(2,1)S(1)} %get-tuple-element.31), channel_id=1, source_target_pairs={{0,2},{2,0},{4,6},{6,4},{8,10},{10,8},{12,14},{14,12},{1,3},{3,1},... | collective-permute-start | bytes 1572872 | tf_op jit(solution)/shard_map/ppermute | solution.py:368
  13.9 19.3 %collective-permute-start.5 = (bf16[256,512]{1,0:T(8,128)(2,1)}, bf16[256,512]{1,0:T(8,128)(2,1)S(1)}, u32[]{:S(2)}, u32[]{:S(2)}) collective-permute-start(bf16[256,512]{1,0:T(8,128)(2,1)} %refs_7_.1), channel_id=1, source_target_pairs={{0,2},{2,0},{4,6},{6,4},{8,10},{10,8},{12,14},{14,12},{1,3},{3,1},... | collective-permute-start | bytes 786440 | tf_op jit(solution)/shard_map/ppermute | solution.py:368
  14.0 22.4 %collective-permute-start.6 = (bf16[256,512]{1,0:T(8,128)(2,1)}, bf16[256,512]{1,0:T(8,128)(2,1)S(1)}, u32[]{:S(2)}, u32[]{:S(2)}) collective-permute-start(bf16[256,512]{1,0:T(8,128)(2,1)} %refs_7_.1), channel_id=1, source_target_pairs={{0,1},{1,0},{2,3},{3,2},{4,5},{5,4},{6,7},{7,6},{8,9},{9,8},{10,11... | collective-permute-start | bytes 786440 | tf_op jit(solution)/shard_map/ppermute | solution.py:371
  26.8 20.0 %collective-permute-start.4 = (bf16[4,16,2048]{2,1,0:T(8,128)(2,1)S(1)}, bf16[4,16,2048]{2,1,0:T(8,128)(2,1)S(1)}, u32[]{:S(2)}, u32[]{:S(2)}) collective-permute-start(bf16[4,16,2048]{2,1,0:T(8,128)(2,1)S(1)} %get-tuple-element.33.refs_2_), channel_id=1, source_target_pairs={{0,2},{2,0},{4,6},{6,4},{8,10},{10,8},{12,14},{14,12},{1,3},{3,1},... | collective-permute-start | bytes 786440 | tf_op jit(solution)/shard_map/ppermute | solution.py:368
  29.0 17.8 %collective-permute-start.1 = (bf16[64,1024]{1,0:T(8,128)(2,1)S(1)}, bf16[64,1024]{1,0:T(8,128)(2,1)S(1)}, u32[]{:S(2)}, u32[]{:S(2)}) collective-permute-start(bf16[64,1024]{1,0:T(8,128)(2,1)S(1)} %get-tuple-element.35.refs_0_), channel_id=1, source_target_pairs={{0,4},{2,6},{4,0},{6,2},{8,12},{10,14},{12,8},{14,10},{1,5},{3,7},... | collective-permute-start | bytes 393224 | tf_op jit(solution)/shard_map/ppermute | solution.py:368
  30.6 16.1 %collective-permute-start.2 = (bf16[64,1024]{1,0:T(8,128)(2,1)S(1)}, bf16[64,1024]{1,0:T(8,128)(2,1)S(1)}, u32[]{:S(2)}, u32[]{:S(2)}) collective-permute-start(bf16[64,1024]{1,0:T(8,128)(2,1)S(1)} %get-tuple-element.36), channel_id=1, source_target_pairs={{0,8},{2,10},{4,12},{6,14},{8,0},{10,2},{12,4},{14,6},{1,9},{3,11}... | collective-permute-start | bytes 393224 | tf_op jit(solution)/shard_map/ppermute | solution.py:368
  33.2 36.8 %copy-start.3 = (s32[1,8192]{1,0:T(1,128)S(1)}, s32[1,8192]{1,0:T(1,128)}, u32[]{:S(2)}) copy-start(s32[1,8192]{1,0:T(1,128)} %refs_0_.3) | copy-start | bytes 98308
  33.2 42.7 %copy-start.1 = (bf16[256,512]{1,0:T(8,128)(2,1)S(1)}, bf16[256,512]{1,0:T(8,128)(2,1)}, u32[]{:S(2)}) copy-start(bf16[256,512]{1,0:T(8,128)(2,1)} %refs_7_.1) | copy-start | bytes 786436
  33.2 13.6 %collective-permute-start.3 = (bf16[64,1024]{1,0:T(8,128)(2,1)S(1)}, bf16[64,1024]{1,0:T(8,128)(2,1)S(1)}, u32[]{:S(2)}, u32[]{:S(2)}) collective-permute-start(bf16[64,1024]{1,0:T(8,128)(2,1)S(1)} %get-tuple-element.37), channel_id=1, source_target_pairs={{0,12},{2,14},{4,8},{6,10},{8,4},{10,6},{12,0},{14,2},{1,13},{3,15... | collective-permute-start | bytes 393224 | tf_op jit(solution)/shard_map/ppermute | solution.py:368
  47.6 11.9 %collective-permute-start.7 = (bf16[64,1536]{1,0:T(8,128)(2,1)S(1)}, bf16[64,1536]{1,0:T(8,128)(2,1)S(1)}, u32[]{:S(2)}, u32[]{:S(2)}) collective-permute-start(bf16[64,1536]{1,0:T(8,128)(2,1)S(1)} %get-tuple-element.42), channel_id=1, source_target_pairs={{0,4},{2,6},{4,0},{6,2},{8,12},{10,14},{12,8},{14,10},{1,5},{3,7},... | collective-permute-start | bytes 589832 | tf_op jit(solution)/shard_map/ppermute | solution.py:368
  47.6 16.2 %collective-permute-start.8 = (bf16[64,1536]{1,0:T(8,128)(2,1)S(1)}, bf16[64,1536]{1,0:T(8,128)(2,1)S(1)}, u32[]{:S(2)}, u32[]{:S(2)}) collective-permute-start(bf16[64,1536]{1,0:T(8,128)(2,1)S(1)} %get-tuple-element.43), channel_id=1, source_target_pairs={{0,8},{2,10},{4,12},{6,14},{8,0},{10,2},{12,4},{14,6},{1,9},{3,11}... | collective-permute-start | bytes 589832 | tf_op jit(solution)/shard_map/ppermute | solution.py:368
  48.8 15.0 %collective-permute-start.9 = (bf16[64,1536]{1,0:T(8,128)(2,1)S(1)}, bf16[64,1536]{1,0:T(8,128)(2,1)S(1)}, u32[]{:S(2)}, u32[]{:S(2)}) collective-permute-start(bf16[64,1536]{1,0:T(8,128)(2,1)S(1)} %get-tuple-element.44), channel_id=1, source_target_pairs={{0,12},{2,14},{4,8},{6,10},{8,4},{10,6},{12,0},{14,2},{1,13},{3,15... | collective-permute-start | bytes 589832 | tf_op jit(solution)/shard_map/ppermute | solution.py:368
  52.0 11.9 %collective-permute-start.10 = (bf16[4,16,1536]{2,1,0:T(8,128)(2,1)S(1)}, bf16[4,16,1536]{2,1,0:T(8,128)(2,1)S(1)}, u32[]{:S(2)}, u32[]{:S(2)}) collective-permute-start(bf16[4,16,1536]{2,1,0:T(8,128)(2,1)S(1)} %get-tuple-element.39.refs_6_), channel_id=1, source_target_pairs={{0,2},{2,0},{4,6},{6,4},{8,10},{10,8},{12,14},{14,12},{1,3},{3,1},... | collective-permute-start | bytes 589832 | tf_op jit(solution)/shard_map/ppermute | solution.py:368
  58.9 5.0 %collective-permute-start.11 = (bf16[4,16,512]{2,1,0:T(8,128)(2,1)S(1)}, bf16[4,16,512]{2,1,0:T(8,128)(2,1)S(1)}, u32[]{:S(2)}, u32[]{:S(2)}) collective-permute-start(bf16[4,16,512]{2,1,0:T(8,128)(2,1)S(1)} %get-tuple-element.49), channel_id=1, source_target_pairs={{0,2},{2,0},{4,6},{6,4},{8,10},{10,8},{12,14},{14,12},{1,3},{3,1},... | collective-permute-start | bytes 196616 | tf_op jit(solution)/shard_map/ppermute | solution.py:368
  64.7 11.2 %collective-permute-start.15 = (bf16[256,512]{1,0:T(8,128)(2,1)S(1)}, bf16[256,512]{1,0:T(8,128)(2,1)S(1)}, u32[]{:S(2)}, u32[]{:S(2)}) collective-permute-start(bf16[256,512]{1,0:T(8,128)(2,1)S(1)} %get-tuple-element.54), channel_id=1, source_target_pairs={{0,1},{1,0},{2,3},{3,2},{4,5},{5,4},{6,7},{7,6},{8,9},{9,8},{10,11... | collective-permute-start | bytes 786440 | tf_op jit(solution)/shard_map/ppermute | solution.py:371
  64.8 8.4 %collective-permute-start.12 = (bf16[16,2048]{1,0:T(8,128)(2,1)S(1)}, bf16[16,2048]{1,0:T(8,128)(2,1)S(1)}, u32[]{:S(2)}, u32[]{:S(2)}) collective-permute-start(bf16[16,2048]{1,0:T(8,128)(2,1)S(1)} %get-tuple-element.51), channel_id=1, source_target_pairs={{0,4},{2,6},{4,0},{6,2},{8,12},{10,14},{12,8},{14,10},{1,5},{3,7},... | collective-permute-start | bytes 196616 | tf_op jit(solution)/shard_map/ppermute | solution.py:368
  67.5 8.4 %collective-permute-start.13 = (bf16[16,2048]{1,0:T(8,128)(2,1)S(1)}, bf16[16,2048]{1,0:T(8,128)(2,1)S(1)}, u32[]{:S(2)}, u32[]{:S(2)}) collective-permute-start(bf16[16,2048]{1,0:T(8,128)(2,1)S(1)} %get-tuple-element.52), channel_id=1, source_target_pairs={{0,8},{2,10},{4,12},{6,14},{8,0},{10,2},{12,4},{14,6},{1,9},{3,11}... | collective-permute-start | bytes 196616 | tf_op jit(solution)/shard_map/ppermute | solution.py:368
  68.6 7.3 %collective-permute-start.14 = (bf16[16,2048]{1,0:T(8,128)(2,1)S(1)}, bf16[16,2048]{1,0:T(8,128)(2,1)S(1)}, u32[]{:S(2)}, u32[]{:S(2)}) collective-permute-start(bf16[16,2048]{1,0:T(8,128)(2,1)S(1)} %get-tuple-element.53), channel_id=1, source_target_pairs={{0,12},{2,14},{4,8},{6,10},{8,4},{10,6},{12,0},{14,2},{1,13},{3,15... | collective-permute-start | bytes 196616 | tf_op jit(solution)/shard_map/ppermute | solution.py:368
  79.1 5.0 %collective-permute-start.16 = (f32[64,512]{1,0:T(8,128)S(1)}, f32[64,512]{1,0:T(8,128)S(1)}, u32[]{:S(2)}, u32[]{:S(2)}) collective-permute-start(f32[64,512]{1,0:T(8,128)S(1)} %score.1), channel_id=1, source_target_pairs={{0,2},{2,0},{4,6},{6,4},{8,10},{10,8},{12,14},{14,12},{1,3},{3,1},... | collective-permute-start | bytes 393224 | tf_op jit(solution)/shard_map/ppermute | solution.py:368
  84.2 5.0 %collective-permute-start.17 = (bf16[64,512]{1,0:T(8,128)(2,1)S(1)}, bf16[64,512]{1,0:T(8,128)(2,1)S(1)}, u32[]{:S(2)}, u32[]{:S(2)}) collective-permute-start(bf16[64,512]{1,0:T(8,128)(2,1)S(1)} %add_convert_fusion), channel_id=1, source_target_pairs={{0,4},{2,6},{4,0},{6,2},{8,12},{10,14},{12,8},{14,10},{1,5},{3,7},... | collective-permute-start | bytes 196616 | tf_op jit(solution)/shard_map/ppermute | solution.py:368
  85.8 6.3 %collective-permute-start.18 = (bf16[64,512]{1,0:T(8,128)(2,1)S(1)}, bf16[64,512]{1,0:T(8,128)(2,1)S(1)}, u32[]{:S(2)}, u32[]{:S(2)}) collective-permute-start(bf16[64,512]{1,0:T(8,128)(2,1)S(1)} %add_convert_fusion), channel_id=1, source_target_pairs={{0,8},{2,10},{4,12},{6,14},{8,0},{10,2},{12,4},{14,6},{1,9},{3,11}... | collective-permute-start | bytes 196616 | tf_op jit(solution)/shard_map/ppermute | solution.py:368
  86.9 6.1 %collective-permute-start.19 = (bf16[64,512]{1,0:T(8,128)(2,1)S(1)}, bf16[64,512]{1,0:T(8,128)(2,1)S(1)}, u32[]{:S(2)}, u32[]{:S(2)}) collective-permute-start(bf16[64,512]{1,0:T(8,128)(2,1)S(1)} %add_convert_fusion), channel_id=1, source_target_pairs={{0,12},{2,14},{4,8},{6,10},{8,4},{10,6},{12,0},{14,2},{1,13},{3,15... | collective-permute-start | bytes 196616 | tf_op jit(solution)/shard_map/ppermute | solution.py:368

commit v11 on v10

--- a/solution.py
+++ b/solution.py
@@ -14,6 +14,7 @@
 SEQ_DEV = 64
 BUFFERS = 4
 VMEM = 48 * 1024 * 1024
+FULL = 60600000
 LAST = (((1,), (1,)), ((), ()))
 
 
@@ -124,7 +125,7 @@
             pltpu.SemaphoreType.DMA((buffers,)),
         ],
         out_shape=shapes,
-        compiler_params=pltpu.CompilerParams(vmem_limit_bytes=VMEM),
+        compiler_params=pltpu.CompilerParams(vmem_limit_bytes=FULL if makes else VMEM),
         cost_estimate=pl.CostEstimate(flops=4 * count * width * R, bytes_accessed=4 * count * width, transcendentals=0),
         name="project",
     )(who, *operands)
@@ -238,21 +239,6 @@
         cost_estimate=pl.CostEstimate(flops=4 * kept.size, bytes_accessed=8 * kept.size, transcendentals=0),
         name="pack",
     )(*operands, *after)
-
-
-def touch_kernel(*refs):
-    refs[-1][...] = jnp.zeros(refs[-1].shape, refs[-1].dtype)
-
-
-def touch(after):
-    return pl.pallas_call(
-        touch_kernel,
-        in_specs=[pl.BlockSpec(memory_space=pl.ANY)] * len(after),
-        out_specs=pl.BlockSpec(memory_space=pltpu.VMEM),
-        out_shape=jax.ShapeDtypeStruct((8, 128), jnp.float32),
-        compiler_params=pltpu.CompilerParams(vmem_limit_bytes=VMEM // 6),
-        name="touch",
-    )(*after)
 
 
 def sketch_rows(half, first, row_ref, col_ref, ids_ref, member_ref, spread_refs, sink):
@@ -371,7 +357,8 @@
         return lax.ppermute(array, "dp", [(0, 1), (1, 0)])
 
     far = swap(queries, 1)
-    cross_near = cross(queries)
+    cross_near, cross_far = cross(queries), cross(far)
+    every = [queries, far, cross_near, cross_far]
 
     scale_in, scale_out = FF ** -0.5, D ** -0.5
     sent_g, kept_g, signs = project(out_grads, proj_out.T, who, scale_out, quarters, False, 0, owned, 1024, proj_in.T)
@@ -382,14 +369,14 @@
         sent, kept = project(activations, signs, who, scale_in, quarters, True, first, count, 512, None, after)
         return sent, [kept, swap(sent, 1)]
 
-    sent_0, chunk_0 = chunk(0, 4, [])
+    sent_0, chunk_0 = chunk(0, 5, [])
     pair_g = merge([], [kept_g, got_g], [sent_0])
     moved_g = [swap(pair_g[d], 2 * d) for d in range(1, quarters)]
-    sent_1, chunk_1 = chunk(4, 3, [pair_g[1], far, cross_near])
+    sent_1, chunk_1 = chunk(5, 3, [pair_g[1], far, cross_near])
     columns = R // quarters
     packed = columns % 16 == 0
     if packed:
-        sums = pack([pair_g[0]] + moved_g, chunk_0[0], chunk_0[1], [sent_1])
+        sums = pack([pair_g[0]] + moved_g, chunk_0[0], chunk_0[1], [sent_1, cross_far])
         own_g, own_a = sums[:2]
         right = [own_g] + [swap(sums[d + 1], 2 * d) for d in range(1, quarters)]
         first = [segment_ids, own_a] + right
@@ -398,12 +385,10 @@
         right = [own_g] + [swap(own_g, 2 * d) for d in range(1, quarters)]
         pair_0 = merge([], chunk_0, [])
         first = [segment_ids, pair_0[0]] + right + [swap(pair_0[d], 2 * d) for d in range(1, quarters)]
-    sent_2, chunk_2 = chunk(7, 1, [own_g])
-    pair_1 = merge([], chunk_1 + chunk_2, [touch(right[1:])], [far])
-    every = [queries, far, cross_near, cross(pair_1[quarters])]
+    pair_1 = merge([], chunk_1, [])
     left = [pair_1[0]] + [swap(pair_1[d], 2 * d) for d in range(1, quarters)]
 
-    early, entries = owned // 2, columns * R
+    early, entries = owned * 5 // 8, columns * R
     shapes = [jax.ShapeDtypeStruct((SEQ_DEV, entries), jnp.float32), jax.ShapeDtypeStruct((R, owned), jnp.bfloat16)]
     base, col = call_sketch(functools.partial(sketch_kernel, quarters, packed), who, first, columns, early, shapes, [], "sketch")
     shapes = [jax.ShapeDtypeStruct((SEQ_DEV, 2 * queries.shape[0]), jnp.float32)]

time: 93.9 us -> 95.3 us (1.015)
  waiting for transfers between devices: 15.5 us -> 24.2 us
  starting transfers between devices: 29.9 us -> 24.1 us
  Pallas kernels: 45.2 us -> 43.7 us
    ppermute x18 -> x17, waiting for transfers between devices: 15.5 us -> 24.2 us  [swap(): lax.ppermute(array, 'tensor', [(k, k ^ distance) for k in range(n_tensor)])]
    ppermute x18 -> x17, starting transfers between devices: 29.8 us -> 23.9 us  [swap(): lax.ppermute(array, 'tensor', [(k, k ^ distance) for k in range(n_tensor)])]
    pallas_call x4 -> x3, Pallas kernels: 37.1 us -> 35.7 us  [project(): pl.pallas_call(functools.partial(project_kernel, scale, first, split, ord...]
    unnamed x8 -> x10, local copies, waits for them, and re-layouts: 2.14 us -> 1.65 us
  transfers between devices with their start and end apart: 20 -> 19, of which waited for: 6 -> 5; matrix products, arithmetic and copies ran while one was open for 0% -> 0% of each run, Pallas kernels for 34% -> 31%
where the time goes in v11:
time: 95.3 us; the launch traced here: 95.1 us
  Pallas kernels  43.7 us (46%)
  waiting for transfers between devices  24.2 us (25%)
  starting transfers between devices  24.1 us (25%)
  local copies, waits for them, and re-layouts  1.65 us (2%)
  other arithmetic  1.32 us (1%)
    pallas_call x3, Pallas kernels, project(): pl.pallas_call(functools.partial(project_kernel, scale, first, split, ord...  35.7 us
    ppermute x17, waiting for transfers between devices, swap(): lax.ppermute(array, 'tensor', [(k, k ^ distance) for k in range(n_tensor)])  24.2 us
    ppermute x17, starting transfers between devices, swap(): lax.ppermute(array, 'tensor', [(k, k ^ distance) for k in range(n_tensor)])  23.9 us
    pallas_call x2, Pallas kernels, call_sketch(): pl.pallas_call(kernel, in_specs=[pl.BlockSpec(memory_space=pltpu.SMEM)] +...  6.32 us
  transfers between devices with their start and end apart: 19, of which 5 were waited for; matrix products, arithmetic and copies ran while one was open for 0% of the time, Pallas kernels for 31%

profile of v11, /device:TPU:0, one launch (start us, length us, event | category | flops | bytes accessed | tf_op | source)
XLA Modules:
  0.0 95.1 jit_solution(715259774827038605)
XLA Ops:
  0.0 0.6 pad_add_fusion.who_ref
  0.6 10.0 %project.3 = (bf16[4,64,1024]{2,1,0:T(8,128)(2,1)}, f32[4,64,1024]{2,1,0:T(8,128)}, bf16[64,3584]{1,0:T(8,128)(2,1)}) custom-call(s32[3]{0:T(128)} %pad_add_fusion.who_ref, bf16[8192,1024]{1,0:T(8,128)(2,1)} %x_hbm.3, s32[64,1024]{1,0:T(8,128)} %bitcast.6, s32[64,3584]{1,0:T(8,128)} %bitcast.5), custom_call_target="tpu_custom_call" | custom-call | flops 1073741824 | bytes 16777216 | tf_op jit(solution)/shard_map/project/pallas_call | solution.py:116
  10.6 3.0 %collective-permute-start = (bf16[4,64,1024]{2,1,0:T(8,128)(2,1)}, bf16[4,64,1024]{2,1,0:T(8,128)(2,1)S(1)}, u32[]{:S(2)}, u32[]{:S(2)}) collective-permute-start(bf16[4,64,1024]{2,1,0:T(8,128)(2,1)} %get-tuple-element.28), channel_id=1, source_target_pairs={{0,2},{2,0},{4,6},{6,4},{8,10},{10,8},{12,14},{14,12},{1,3},{3,1},... | collective-permute-start | bytes 1572872 | tf_op jit(solution)/shard_map/ppermute | solution.py:354
  13.8 1.0 %copy-done = bf16[64,3584]{1,0:T(8,128)(2,1)S(1)} copy-done((bf16[64,3584]{1,0:T(8,128)(2,1)S(1)}, bf16[64,3584]{1,0:T(8,128)(2,1)}, u32[]{:S(2)}) %copy-start) | copy-done | bytes 458776
  14.8 0.6 copy-done.4
  15.4 15.3 %project.4 = (bf16[4,16,2560]{2,1,0:T(8,128)(2,1)S(1)}, f32[4,16,2560]{2,1,0:T(8,128)S(1)}) custom-call(s32[3]{0:T(128)S(1)} %copy-done.4, bf16[8192,3584]{1,0:T(8,128)(2,1)} %x_hbm.5, bf16[64,3584]{1,0:T(8,128)(2,1)S(1)} %copy-done), custom_call_target="tpu_custom_call" | custom-call | flops 2348810240 | bytes 36700160 | tf_op jit(solution)/shard_map/project/pallas_call | solution.py:116
  30.7 2.0 %collective-permute-start.4 = (bf16[4,16,2560]{2,1,0:T(8,128)(2,1)S(1)}, bf16[4,16,2560]{2,1,0:T(8,128)(2,1)S(1)}, u32[]{:S(2)}, u32[]{:S(2)}) collective-permute-start(bf16[4,16,2560]{2,1,0:T(8,128)(2,1)S(1)} %get-tuple-element.30.refs_2_), channel_id=1, source_target_pairs={{0,2},{2,0},{4,6},{6,4},{8,10},{10,8},{12,14},{14,12},{1,3},{3,1},... | collective-permute-start | bytes 983048 | tf_op jit(solution)/shard_map/ppermute | solution.py:354
  32.7 0.2 collective-permute-start.7
  33.0 0.2 merge.2
  33.2 1.6 %collective-permute-start.1 = (bf16[64,1024]{1,0:T(8,128)(2,1)S(1)}, bf16[64,1024]{1,0:T(8,128)(2,1)S(1)}, u32[]{:S(2)}, u32[]{:S(2)}) collective-permute-start(bf16[64,1024]{1,0:T(8,128)(2,1)S(1)} %get-tuple-element.32.refs_0_), channel_id=1, source_target_pairs={{0,4},{2,6},{4,0},{6,2},{8,12},{10,14},{12,8},{14,10},{1,5},{3,7},... | collective-permute-start | bytes 393224 | tf_op jit(solution)/shard_map/ppermute | solution.py:354
  34.8 2.6 %collective-permute-start.2 = (bf16[64,1024]{1,0:T(8,128)(2,1)S(1)}, bf16[64,1024]{1,0:T(8,128)(2,1)S(1)}, u32[]{:S(2)}, u32[]{:S(2)}) collective-permute-start(bf16[64,1024]{1,0:T(8,128)(2,1)S(1)} %get-tuple-element.33), channel_id=1, source_target_pairs={{0,8},{2,10},{4,12},{6,14},{8,0},{10,2},{12,4},{14,6},{1,9},{3,11}... | collective-permute-start | bytes 393224 | tf_op jit(solution)/shard_map/ppermute | solution.py:354
  37.4 0.2 collective-permute-start.3
  37.6 10.3 %project.5 = (bf16[4,16,1536]{2,1,0:T(8,128)(2,1)S(1)}, f32[4,16,1536]{2,1,0:T(8,128)S(1)}) custom-call(s32[3]{0:T(128)S(1)} %copy-done.4, bf16[8192,3584]{1,0:T(8,128)(2,1)} %x_hbm.5, bf16[64,3584]{1,0:T(8,128)(2,1)S(1)} %copy-done, bf16[64,1024]{1,0:T(8,128)(2,1)S(1)} %get-tuple-element.32.refs_0_, ...), custom_call_target="tpu_custom_call" | custom-call | flops 1409286144 | bytes 22020096 | tf_op jit(solution)/shard_map/project/pallas_call | solution.py:116
  48.0 1.0 %pack.1 = (bf16[64,1024]{1,0:T(8,128)(2,1)S(1)}, f32[16,2560]{1,0:T(8,128)S(1)}, bf16[64,1664]{1,0:T(8,128)(2,1)S(1)}, bf16[64,1664]{1,0:T(8,128)(2,1)S(1)}, bf16[64,1664]{1,0:T(8,128)(2,1)S(1)}) custom-call(f32[64,1024]{1,0:T(8,128)S(1)} %get-tuple-element.31.refs_0_, bf16[64,1024]{1,0:T(8,128)(2,1)S(1)} %collective-permute-done.1.refs_1_, ...), custom_call_target="tpu_custom_call" | custom-call | flops 655360 | bytes 1310720 | tf_op jit(solution)/shard_map/pack/pallas_call | solution.py:232
  49.1 3.7 %collective-permute-start.10 = (bf16[64,1664]{1,0:T(8,128)(2,1)S(1)}, bf16[64,1664]{1,0:T(8,128)(2,1)S(1)}, u32[]{:S(2)}, u32[]{:S(2)}) collective-permute-start(bf16[64,1664]{1,0:T(8,128)(2,1)S(1)} %get-tuple-element.41), channel_id=1, source_target_pairs={{0,12},{2,14},{4,8},{6,10},{8,4},{10,6},{12,0},{14,2},{1,13},{3,15... | collective-permute-start | bytes 638984 | tf_op jit(solution)/shard_map/ppermute | solution.py:354
  52.7 0.5 collective-permute-start.11
  53.2 0.1 collective-permute-start.8
  53.3 0.6 collective-permute-start.9
  53.9 4.8 %collective-permute-done.11.refs_1_ = bf16[4,16,1536]{2,1,0:T(8,128)(2,1)S(1)} collective-permute-done((bf16[4,16,1536]{2,1,0:T(8,128)(2,1)S(1)}, bf16[4,16,1536]{2,1,0:T(8,128)(2,1)S(1)}, u32[]{:S(2)}, u32[]{:S(2)}) %collective-permute-start.11) | collective-permute-done | bytes 196640 | tf_op jit(solution)/shard_map/ppermute | solution.py:354
  58.7 0.5 merge.3
  59.3 0.9 collective-permute-start.13
  60.2 3.5 %collective-permute-start.14 = (bf16[16,1536]{1,0:T(8,128)(2,1)S(1)}, bf16[16,1536]{1,0:T(8,128)(2,1)S(1)}, u32[]{:S(2)}, u32[]{:S(2)}) collective-permute-start(bf16[16,1536]{1,0:T(8,128)(2,1)S(1)} %get-tuple-element.48), channel_id=1, source_target_pairs={{0,12},{2,14},{4,8},{6,10},{8,4},{10,6},{12,0},{14,2},{1,13},{3,15... | collective-permute-start | bytes 147464 | tf_op jit(solution)/shard_map/ppermute | solution.py:354
  63.7 9.9 %collective-permute-done.9.refs_4_ = bf16[64,1664]{1,0:T(8,128)(2,1)S(1)} collective-permute-done((bf16[64,1664]{1,0:T(8,128)(2,1)S(1)}, bf16[64,1664]{1,0:T(8,128)(2,1)S(1)}, u32[]{:S(2)}, u32[]{:S(2)}) %collective-permute-start.9) | collective-permute-done | bytes 213024 | tf_op jit(solution)/shard_map/ppermute | solution.py:354
  73.5 3.6 %sketch.1 = (f32[64,1024]{1,0:T(8,128)S(1)}, bf16[64,4096]{1,0:T(8,128)(2,1)S(1)}) custom-call(s32[3]{0:T(128)S(1)} %copy-done.4, s32[1,8192]{1,0:T(1,128)S(1)} %copy-done.3, f32[16,2560]{1,0:T(8,128)S(1)} %get-tuple-element.37.refs_1_, bf16[64,1024]{1,0:T(8,128)(2,1)S(1)} %get-tuple-element.38.refs_2_, bf16[64,1664]{1,0:T(8,128)(2,1)S(1)} %collective-permute-done.8.refs_3_, ...), custom_call_target="tpu_custom_call" | custom-call | flops 335544320 | bytes 163840 | tf_op jit(solution)/shard_map/sketch/pallas_call | solution.py:327
  77.2 2.7 %score.1 = f32[64,512]{1,0:T(8,128)S(1)} custom-call(s32[3]{0:T(128)S(1)} %copy-done.4, s32[1,8192]{1,0:T(1,128)S(1)} %copy-done.3, bf16[64,4096]{1,0:T(8,128)(2,1)S(1)} %get-tuple-element.42.refs_1_, f32[64,1024]{1,0:T(8,128)S(1)} %get-tuple-element.43.refs_2_, f32[16,1536]{1,0:T(8,128)S(1)} %get-tuple-element.45.refs_3_, ...), custom_call_target="tpu_custom_call" | custom-call | flops 201326592 | bytes 98304 | tf_op jit(solution)/shard_map/score/pallas_call | solution.py:327
  79.9 0.6 collective-permute-start.15
  80.5 4.5 %collective-permute-done.15 = f32[64,512]{1,0:T(8,128)S(1)} collective-permute-done((f32[64,512]{1,0:T(8,128)S(1)}, f32[64,512]{1,0:T(8,128)S(1)}, u32[]{:S(2)}, u32[]{:S(2)}) %collective-permute-start.15) | collective-permute-done | bytes 131104 | tf_op jit(solution)/shard_map/ppermute | solution.py:354
  85.1 3.3 %collective-permute-start.17 = (bf16[64,512]{1,0:T(8,128)(2,1)S(1)}, bf16[64,512]{1,0:T(8,128)(2,1)S(1)}, u32[]{:S(2)}, u32[]{:S(2)}) collective-permute-start(bf16[64,512]{1,0:T(8,128)(2,1)S(1)} %add_convert_fusion), channel_id=1, source_target_pairs={{0,8},{2,10},{4,12},{6,14},{8,0},{10,2},{12,4},{14,6},{1,9},{3,11}... | collective-permute-start | bytes 196616 | tf_op jit(solution)/shard_map/ppermute | solution.py:354
  88.4 1.1 %collective-permute-start.18 = (bf16[64,512]{1,0:T(8,128)(2,1)S(1)}, bf16[64,512]{1,0:T(8,128)(2,1)S(1)}, u32[]{:S(2)}, u32[]{:S(2)}) collective-permute-start(bf16[64,512]{1,0:T(8,128)(2,1)S(1)} %add_convert_fusion), channel_id=1, source_target_pairs={{0,12},{2,14},{4,8},{6,10},{8,4},{10,6},{12,0},{14,2},{1,13},{3,15... | collective-permute-start | bytes 196616 | tf_op jit(solution)/shard_map/ppermute | solution.py:354
  89.4 1.2 %collective-permute-done.17 = bf16[64,512]{1,0:T(8,128)(2,1)S(1)} collective-permute-done((bf16[64,512]{1,0:T(8,128)(2,1)S(1)}, bf16[64,512]{1,0:T(8,128)(2,1)S(1)}, u32[]{:S(2)}, u32[]{:S(2)}) %collective-permute-start.17) | collective-permute-done | bytes 65568 | tf_op jit(solution)/shard_map/ppermute | solution.py:354
  90.6 3.8 %collective-permute-done.18 = bf16[64,512]{1,0:T(8,128)(2,1)S(1)} collective-permute-done((bf16[64,512]{1,0:T(8,128)(2,1)S(1)}, bf16[64,512]{1,0:T(8,128)(2,1)S(1)}, u32[]{:S(2)}, u32[]{:S(2)}) %collective-permute-start.18) | collective-permute-done | bytes 65568 | tf_op jit(solution)/shard_map/ppermute | solution.py:354
  94.4 0.7 add_add_fusion
  (27 shorter events, 0.3 us)
Async XLA Ops:
  10.6 22.3 %collective-permute-start = (bf16[4,64,1024]{2,1,0:T(8,128)(2,1)}, bf16[4,64,1024]{2,1,0:T(8,128)(2,1)S(1)}, u32[]{:S(2)}, u32[]{:S(2)}) collective-permute-start(bf16[4,64,1024]{2,1,0:T(8,128)(2,1)} %get-tuple-element.28), channel_id=1, source_target_pairs={{0,2},{2,0},{4,6},{6,4},{8,10},{10,8},{12,14},{14,12},{1,3},{3,1},... | collective-permute-start | bytes 1572872 | tf_op jit(solution)/shard_map/ppermute | solution.py:354
  13.7 19.0 %collective-permute-start.5 = (bf16[256,512]{1,0:T(8,128)(2,1)}, bf16[256,512]{1,0:T(8,128)(2,1)S(1)}, u32[]{:S(2)}, u32[]{:S(2)}) collective-permute-start(bf16[256,512]{1,0:T(8,128)(2,1)} %refs_7_.1), channel_id=1, source_target_pairs={{0,2},{2,0},{4,6},{6,4},{8,10},{10,8},{12,14},{14,12},{1,3},{3,1},... | collective-permute-start | bytes 786440 | tf_op jit(solution)/shard_map/ppermute | solution.py:354
  13.8 23.7 %collective-permute-start.6 = (bf16[256,512]{1,0:T(8,128)(2,1)}, bf16[256,512]{1,0:T(8,128)(2,1)S(1)}, u32[]{:S(2)}, u32[]{:S(2)}) collective-permute-start(bf16[256,512]{1,0:T(8,128)(2,1)} %refs_7_.1), channel_id=1, source_target_pairs={{0,1},{1,0},{2,3},{3,2},{4,5},{5,4},{6,7},{7,6},{8,9},{9,8},{10,11... | collective-permute-start | bytes 786440 | tf_op jit(solution)/shard_map/ppermute | solution.py:357
  13.8 1.0 %copy-start = (bf16[64,3584]{1,0:T(8,128)(2,1)S(1)}, bf16[64,3584]{1,0:T(8,128)(2,1)}, u32[]{:S(2)}) copy-start(bf16[64,3584]{1,0:T(8,128)(2,1)} %get-tuple-element.29.sign_source) | copy-start | bytes 1376260
  14.8 0.6 copy-start.4
  15.4 17.6 %copy-start.1 = (f32[4,64,1024]{2,1,0:T(8,128)S(1)}, f32[4,64,1024]{2,1,0:T(8,128)}, u32[]{:S(2)}) copy-start(f32[4,64,1024]{2,1,0:T(8,128)} %get-tuple-element.27.refs_0_) | copy-start | bytes 3145732
  15.4 58.1 %copy-start.3 = (s32[1,8192]{1,0:T(1,128)S(1)}, s32[1,8192]{1,0:T(1,128)}, u32[]{:S(2)}) copy-start(s32[1,8192]{1,0:T(1,128)} %refs_0_.3) | copy-start | bytes 98308
  15.4 61.8 %copy-start.2 = (bf16[256,512]{1,0:T(8,128)(2,1)S(1)}, bf16[256,512]{1,0:T(8,128)(2,1)}, u32[]{:S(2)}) copy-start(bf16[256,512]{1,0:T(8,128)(2,1)} %refs_7_.1) | copy-start | bytes 786436
  30.7 17.3 %collective-permute-start.4 = (bf16[4,16,2560]{2,1,0:T(8,128)(2,1)S(1)}, bf16[4,16,2560]{2,1,0:T(8,128)(2,1)S(1)}, u32[]{:S(2)}, u32[]{:S(2)}) collective-permute-start(bf16[4,16,2560]{2,1,0:T(8,128)(2,1)S(1)} %get-tuple-element.30.refs_2_), channel_id=1, source_target_pairs={{0,2},{2,0},{4,6},{6,4},{8,10},{10,8},{12,14},{14,12},{1,3},{3,1},... | collective-permute-start | bytes 983048 | tf_op jit(solution)/shard_map/ppermute | solution.py:354
  32.7 15.3 %collective-permute-start.7 = (bf16[256,512]{1,0:T(8,128)(2,1)S(1)}, bf16[256,512]{1,0:T(8,128)(2,1)S(1)}, u32[]{:S(2)}, u32[]{:S(2)}) collective-permute-start(bf16[256,512]{1,0:T(8,128)(2,1)S(1)} %collective-permute-done.5.refs_1_.refs_8_), channel_id=1, source_target_pairs={{0,1},{1,0},{2,3},{3,2},{4,5},{5,4},{6,7},{7,6},{8,9},{9,8},{10,11... | collective-permute-start | bytes 786440 | tf_op jit(solution)/shard_map/ppermute | solution.py:357
  33.2 14.8 %collective-permute-start.1 = (bf16[64,1024]{1,0:T(8,128)(2,1)S(1)}, bf16[64,1024]{1,0:T(8,128)(2,1)S(1)}, u32[]{:S(2)}, u32[]{:S(2)}) collective-permute-start(bf16[64,1024]{1,0:T(8,128)(2,1)S(1)} %get-tuple-element.32.refs_0_), channel_id=1, source_target_pairs={{0,4},{2,6},{4,0},{6,2},{8,12},{10,14},{12,8},{14,10},{1,5},{3,7},... | collective-permute-start | bytes 393224 | tf_op jit(solution)/shard_map/ppermute | solution.py:354
  34.8 13.2 %collective-permute-start.2 = (bf16[64,1024]{1,0:T(8,128)(2,1)S(1)}, bf16[64,1024]{1,0:T(8,128)(2,1)S(1)}, u32[]{:S(2)}, u32[]{:S(2)}) collective-permute-start(bf16[64,1024]{1,0:T(8,128)(2,1)S(1)} %get-tuple-element.33), channel_id=1, source_target_pairs={{0,8},{2,10},{4,12},{6,14},{8,0},{10,2},{12,4},{14,6},{1,9},{3,11}... | collective-permute-start | bytes 393224 | tf_op jit(solution)/shard_map/ppermute | solution.py:354
  37.4 10.6 %collective-permute-start.3 = (bf16[64,1024]{1,0:T(8,128)(2,1)S(1)}, bf16[64,1024]{1,0:T(8,128)(2,1)S(1)}, u32[]{:S(2)}, u32[]{:S(2)}) collective-permute-start(bf16[64,1024]{1,0:T(8,128)(2,1)S(1)} %get-tuple-element.34), channel_id=1, source_target_pairs={{0,12},{2,14},{4,8},{6,10},{8,4},{10,6},{12,0},{14,2},{1,13},{3,15... | collective-permute-start | bytes 393224 | tf_op jit(solution)/shard_map/ppermute | solution.py:354
  49.1 11.1 %collective-permute-start.10 = (bf16[64,1664]{1,0:T(8,128)(2,1)S(1)}, bf16[64,1664]{1,0:T(8,128)(2,1)S(1)}, u32[]{:S(2)}, u32[]{:S(2)}) collective-permute-start(bf16[64,1664]{1,0:T(8,128)(2,1)S(1)} %get-tuple-element.41), channel_id=1, source_target_pairs={{0,12},{2,14},{4,8},{6,10},{8,4},{10,6},{12,0},{14,2},{1,13},{3,15... | collective-permute-start | bytes 638984 | tf_op jit(solution)/shard_map/ppermute | solution.py:354
  52.7 6.0 %collective-permute-start.11 = (bf16[4,16,1536]{2,1,0:T(8,128)(2,1)S(1)}, bf16[4,16,1536]{2,1,0:T(8,128)(2,1)S(1)}, u32[]{:S(2)}, u32[]{:S(2)}) collective-permute-start(bf16[4,16,1536]{2,1,0:T(8,128)(2,1)S(1)} %get-tuple-element.36.refs_6_), channel_id=1, source_target_pairs={{0,2},{2,0},{4,6},{6,4},{8,10},{10,8},{12,14},{14,12},{1,3},{3,1},... | collective-permute-start | bytes 589832 | tf_op jit(solution)/shard_map/ppermute | solution.py:354
  53.2 10.4 %collective-permute-start.8 = (bf16[64,1664]{1,0:T(8,128)(2,1)S(1)}, bf16[64,1664]{1,0:T(8,128)(2,1)S(1)}, u32[]{:S(2)}, u32[]{:S(2)}) collective-permute-start(bf16[64,1664]{1,0:T(8,128)(2,1)S(1)} %get-tuple-element.39), channel_id=1, source_target_pairs={{0,4},{2,6},{4,0},{6,2},{8,12},{10,14},{12,8},{14,10},{1,5},{3,7},... | collective-permute-start | bytes 638984 | tf_op jit(solution)/shard_map/ppermute | solution.py:354
  53.3 20.2 %collective-permute-start.9 = (bf16[64,1664]{1,0:T(8,128)(2,1)S(1)}, bf16[64,1664]{1,0:T(8,128)(2,1)S(1)}, u32[]{:S(2)}, u32[]{:S(2)}) collective-permute-start(bf16[64,1664]{1,0:T(8,128)(2,1)S(1)} %get-tuple-element.40), channel_id=1, source_target_pairs={{0,8},{2,10},{4,12},{6,14},{8,0},{10,2},{12,4},{14,6},{1,9},{3,11}... | collective-permute-start | bytes 638984 | tf_op jit(solution)/shard_map/ppermute | solution.py:354
  59.2 18.0 %collective-permute-start.12 = (bf16[16,1536]{1,0:T(8,128)(2,1)S(1)}, bf16[16,1536]{1,0:T(8,128)(2,1)S(1)}, u32[]{:S(2)}, u32[]{:S(2)}) collective-permute-start(bf16[16,1536]{1,0:T(8,128)(2,1)S(1)} %get-tuple-element.46), channel_id=1, source_target_pairs={{0,4},{2,6},{4,0},{6,2},{8,12},{10,14},{12,8},{14,10},{1,5},{3,7},... | collective-permute-start | bytes 147464 | tf_op jit(solution)/shard_map/ppermute | solution.py:354
  59.3 17.9 %collective-permute-start.13 = (bf16[16,1536]{1,0:T(8,128)(2,1)S(1)}, bf16[16,1536]{1,0:T(8,128)(2,1)S(1)}, u32[]{:S(2)}, u32[]{:S(2)}) collective-permute-start(bf16[16,1536]{1,0:T(8,128)(2,1)S(1)} %get-tuple-element.47), channel_id=1, source_target_pairs={{0,8},{2,10},{4,12},{6,14},{8,0},{10,2},{12,4},{14,6},{1,9},{3,11}... | collective-permute-start | bytes 147464 | tf_op jit(solution)/shard_map/ppermute | solution.py:354
  60.2 17.0 %collective-permute-start.14 = (bf16[16,1536]{1,0:T(8,128)(2,1)S(1)}, bf16[16,1536]{1,0:T(8,128)(2,1)S(1)}, u32[]{:S(2)}, u32[]{:S(2)}) collective-permute-start(bf16[16,1536]{1,0:T(8,128)(2,1)S(1)} %get-tuple-element.48), channel_id=1, source_target_pairs={{0,12},{2,14},{4,8},{6,10},{8,4},{10,6},{12,0},{14,2},{1,13},{3,15... | collective-permute-start | bytes 147464 | tf_op jit(solution)/shard_map/ppermute | solution.py:354
  79.9 5.0 %collective-permute-start.15 = (f32[64,512]{1,0:T(8,128)S(1)}, f32[64,512]{1,0:T(8,128)S(1)}, u32[]{:S(2)}, u32[]{:S(2)}) collective-permute-start(f32[64,512]{1,0:T(8,128)S(1)} %score.1), channel_id=1, source_target_pairs={{0,2},{2,0},{4,6},{6,4},{8,10},{10,8},{12,14},{14,12},{1,3},{3,1},... | collective-permute-start | bytes 393224 | tf_op jit(solution)/shard_map/ppermute | solution.py:354
  85.0 4.5 %collective-permute-start.16 = (bf16[64,512]{1,0:T(8,128)(2,1)S(1)}, bf16[64,512]{1,0:T(8,128)(2,1)S(1)}, u32[]{:S(2)}, u32[]{:S(2)}) collective-permute-start(bf16[64,512]{1,0:T(8,128)(2,1)S(1)} %add_convert_fusion), channel_id=1, source_target_pairs={{0,4},{2,6},{4,0},{6,2},{8,12},{10,14},{12,8},{14,10},{1,5},{3,7},... | collective-permute-start | bytes 196616 | tf_op jit(solution)/shard_map/ppermute | solution.py:354
  85.1 5.6 %collective-permute-start.17 = (bf16[64,512]{1,0:T(8,128)(2,1)S(1)}, bf16[64,512]{1,0:T(8,128)(2,1)S(1)}, u32[]{:S(2)}, u32[]{:S(2)}) collective-permute-start(bf16[64,512]{1,0:T(8,128)(2,1)S(1)} %add_convert_fusion), channel_id=1, source_target_pairs={{0,8},{2,10},{4,12},{6,14},{8,0},{10,2},{12,4},{14,6},{1,9},{3,11}... | collective-permute-start | bytes 196616 | tf_op jit(solution)/shard_map/ppermute | solution.py:354
  88.4 6.1 %collective-permute-start.18 = (bf16[64,512]{1,0:T(8,128)(2,1)S(1)}, bf16[64,512]{1,0:T(8,128)(2,1)S(1)}, u32[]{:S(2)}, u32[]{:S(2)}) collective-permute-start(bf16[64,512]{1,0:T(8,128)(2,1)S(1)} %add_convert_fusion), channel_id=1, source_target_pairs={{0,12},{2,14},{4,8},{6,10},{8,4},{10,6},{12,0},{14,2},{1,13},{3,15... | collective-permute-start | bytes 196616 | tf_op jit(solution)/shard_map/ppermute | solution.py:354

commit v12 on v11

v12 whole, which is shorter than its diff:
```python
import functools
import math

import jax
import jax.numpy as jnp
from jax import lax
from jax.experimental import pallas as pl
from jax.experimental.pallas import tpu as pltpu
from jax.sharding import PartitionSpec as P

D = 8192
FF = 28672
R = 64
SEQ_DEV = 64
BUFFERS = 4
VMEM = 48 * 1024 * 1024
LAST = (((1,), (1,)), ((), ()))


def project_kernel(scale, first, split, columns, group, waits, who_ref, x_hbm, sign_source, *refs):
    makes = group > 0
    other_source, refs = refs[0], refs[makes + waits:]
    sent_ref, kept_ref, made_ref, refs = refs[0], refs[1], refs[2], refs[2 + makes:]
    bits_ref, other_ref = refs[0], refs[1]
    signs_ref, x_buf, sign_sem, sems = refs[-4:]
    half, quarter = who_ref[0], who_ref[1]
    buffers, tile = x_buf.shape[0], x_buf.shape[1]
    quarters = sent_ref.shape[0]
    steps = quarters * split
    total = steps if columns else 2 * steps
    per_quarter = x_hbm.shape[0] // quarters

    def copy(p):
        mine = (p >= steps).astype(jnp.int32)
        s = p - mine * steps
        row = ((s // split) ^ quarter) * per_quarter + lax.rem(s, split) * tile
        row = row + (first if columns else (half ^ 1 ^ mine) * (per_quarter // 2))
        slot = lax.rem(p, buffers)
        return pltpu.make_async_copy(x_hbm.at[pl.ds(pl.multiple_of(row, tile), tile)], x_buf.at[slot], sems.at[slot])

    sign_copy = pltpu.make_async_copy(sign_source, bits_ref, sign_sem.at[0])
    sign_copy.start()

    def begin(p, carry):
        copy(p).start()
        return carry

    lax.fori_loop(0, buffers, begin, 0)
    if makes:
        other_copy = pltpu.make_async_copy(other_source, other_ref, sign_sem.at[1])
        other_copy.start()
    sign_copy.wait()
    signs_ref[...] = (2 * bits_ref[...] - 1).astype(jnp.bfloat16) if makes else bits_ref[...]

    def one(p, carry):
        copy(p).wait()
        mine = (p >= steps).astype(jnp.int32)
        s = p - mine * steps
        part = lax.dot_general(
            signs_ref[...], x_buf[lax.rem(p, buffers)], LAST, preferred_element_type=jnp.float32
        ) * scale
        place = s // split
        here = pl.ds(pl.multiple_of(lax.rem(s, split) * tile, tile), tile)
        if columns:
            sent_ref[place, :, here] = part[:columns].astype(jnp.bfloat16)
            kept_ref[place, :, here] = part[columns:]
        else:
            @pl.when(p < steps)
            def _():
                sent_ref[place, :, here] = part.astype(jnp.bfloat16)

            @pl.when(p >= steps)
            def _():
                kept_ref[place, :, here] = part

        @pl.when(p + buffers < total)
        def _():
            copy(p + buffers).start()

        return carry

    lax.fori_loop(0, total, one, 0)
    if makes:
        other_copy.wait()
        if group % 8:
            made_ref[...] = (2 * other_ref[...] - 1).astype(jnp.bfloat16)
        else:
            blocks = []
            for k in range(R // group):
                side = half ^ 1 ^ (k // quarters)
                blocks.append(other_ref[pl.ds(pl.multiple_of((2 * (k % quarters) + side) * group, 8), group), :])
            for k in range(0, len(blocks), 2):
                pair = jnp.concatenate(blocks[k:k + 2], axis=0)
                made_ref[k * group:(k + 2) * group, :] = (2 * pair - 1).astype(jnp.bfloat16)


def project(x, signs, who, scale, quarters, columns, first, count, tile, other=None, after=()):
    width = x.shape[1]
    makes = other is not None
    group = 0
    tile = min(tile, count)
    rows = columns if columns else R
    if makes:
        group = R // (2 * quarters)
        if group % 8:
            order = jnp.arange(R, dtype=jnp.int32)
            side = who[0] ^ 1 ^ (order // (R // 2))
            order = order % (R // 2)
            other = jnp.take(other, (2 * (order // group) + side) * group + order % group, axis=0)
    shape = (quarters, rows, count)
    shapes = [jax.ShapeDtypeStruct(shape, jnp.bfloat16), jax.ShapeDtypeStruct(shape, jnp.float32)]
    scratch = [pltpu.VMEM(signs.shape, signs.dtype)]
    if makes:
        shapes.append(jax.ShapeDtypeStruct(other.shape, jnp.bfloat16))
        scratch.append(pltpu.VMEM(other.shape, other.dtype))
    split = count // tile
    blocks = quarters * split * (1 if columns else 2)
    buffers = min(BUFFERS, blocks)
    operands = [x, signs] + ([other] if makes else []) + list(after)
    return pl.pallas_call(
        functools.partial(project_kernel, scale, first, split, columns, group, len(after)),
        in_specs=[pl.BlockSpec(memory_space=pltpu.SMEM)] + [pl.BlockSpec(memory_space=pl.ANY)] * len(operands),
        out_specs=[pl.BlockSpec(memory_space=pltpu.VMEM)] * len(shapes),
        scratch_shapes=scratch
        + [
            pltpu.VMEM(signs.shape, jnp.bfloat16),
            pltpu.VMEM((buffers, tile, width), jnp.bfloat16),
            pltpu.SemaphoreType.DMA((2,)),
            pltpu.SemaphoreType.DMA((buffers,)),
        ],
        out_shape=shapes,
        compiler_params=pltpu.CompilerParams(vmem_limit_bytes=VMEM),
        cost_estimate=pl.CostEstimate(flops=2 * blocks * tile * width * R, bytes_accessed=2 * blocks * tile * width, transcendentals=0),
        name="project",
    )(who, *operands)


def fetch_all(sources, targets, sems):
    copies = [pltpu.make_async_copy(source, target, sems.at[k]) for k, (source, target) in enumerate(zip(sources, targets))]
    for copy in copies:
        copy.start()
    return copies


def merge_kernel(quarters, bases, pairs, carried, waits, *refs):
    count = bases + 2 * pairs
    sources, refs = refs[:count + carried], refs[count + carried + waits:]
    outs, carries, refs = refs[:quarters], refs[quarters:quarters + carried], refs[quarters + carried:]
    targets, sems = refs[:-1], refs[-1]
    copies = fetch_all(sources, targets, sems)
    for copy in copies:
        copy.wait()
    for k, carry_ref in enumerate(carries):
        carry_ref[...] = targets[count + k][...]
    for d, out_ref in enumerate(outs):
        at = 0
        if bases:
            at = targets[d].shape[1]
            out_ref[:, :at] = targets[d][...]
        for c in range(bases, count, 2):
            kept_ref, got_ref = targets[c], targets[c + 1]
            width = kept_ref.shape[2]
            out_ref[:, at:at + width] = (kept_ref[d] + got_ref[d].astype(jnp.float32)).astype(out_ref.dtype)
            at = at + width


def merge(base, arrays, after, carry=()):
    quarters, rows = arrays[0].shape[:2]
    tokens = sum(array.shape[2] for array in arrays[::2]) + (base[0].shape[1] if base else 0)
    operands = list(base) + list(arrays) + list(carry)
    return pl.pallas_call(
        functools.partial(merge_kernel, quarters, len(base), len(arrays) // 2, len(carry), len(after)),
        in_specs=[pl.BlockSpec(memory_space=pl.ANY)] * (len(operands) + len(after)),
        out_specs=[pl.BlockSpec(memory_space=pltpu.VMEM)] * (quarters + len(carry)),
        out_shape=[jax.ShapeDtypeStruct((rows, tokens), jnp.bfloat16 if d else jnp.float32) for d in range(quarters)]
        + [jax.ShapeDtypeStruct(array.shape, array.dtype) for array in carry],
        scratch_shapes=[pltpu.VMEM(operand.shape, operand.dtype) for operand in operands] + [pltpu.SemaphoreType.DMA((len(operands),))],
        compiler_params=pltpu.CompilerParams(vmem_limit_bytes=VMEM // 6),
        cost_estimate=pl.CostEstimate(flops=quarters * rows * tokens, bytes_accessed=8 * quarters * rows * tokens, transcendentals=0),
        name="merge",
    )(*operands, *after)


def total_kernel(count, waits, *refs):
    sources, out_ref, targets, sems = refs[:count], refs[count + waits], refs[count + waits + 1:-1], refs[-1]
    for copy in fetch_all(sources, targets, sems):
        copy.wait()
    total = targets[0][...]
    for target in targets[1:]:
        total = total + target[...].astype(jnp.float32)
    out_ref[...] = total.astype(out_ref.dtype)


def total_of(parts, after):
    return pl.pallas_call(
        functools.partial(total_kernel, len(parts), len(after)),
        in_specs=[pl.BlockSpec(memory_space=pl.ANY)] * (len(parts) + len(after)),
        out_specs=pl.BlockSpec(memory_space=pltpu.VMEM),
        out_shape=jax.ShapeDtypeStruct(parts[0].shape, jnp.bfloat16),
        scratch_shapes=[pltpu.VMEM(part.shape, part.dtype) for part in parts] + [pltpu.SemaphoreType.DMA((len(parts),))],
        compiler_params=pltpu.CompilerParams(vmem_limit_bytes=VMEM // 6),
        cost_estimate=pl.CostEstimate(flops=parts[0].size * len(parts), bytes_accessed=2 * parts[0].size * len(parts), transcendentals=0),
        name="total",
    )(*parts, *after)


def stack_kernel(count, waits, *refs):
    sources, out_ref, sems = refs[:count], refs[count + waits], refs[-1]
    rows = sources[0].shape[0]
    targets = [out_ref.at[pl.ds(k * rows, rows)] for k in range(count)]
    for copy in fetch_all(sources, targets, sems):
        copy.wait()


def stack(arrays, after):
    rows, width = arrays[0].shape
    return pl.pallas_call(
        functools.partial(stack_kernel, len(arrays), len(after)),
        in_specs=[pl.BlockSpec(memory_space=pl.ANY)] * (len(arrays) + len(after)),
        out_specs=pl.BlockSpec(memory_space=pltpu.VMEM),
        out_shape=jax.ShapeDtypeStruct((len(arrays) * rows, width), arrays[0].dtype),
        scratch_shapes=[pltpu.SemaphoreType.DMA((len(arrays),))],
        compiler_params=pltpu.CompilerParams(vmem_limit_bytes=VMEM // 6),
        cost_estimate=pl.CostEstimate(flops=0, bytes_accessed=0, transcendentals=0),
        name="stack",
    )(*arrays, *after)


def sketch_rows(quarter, first, row_ref, col_ref, ids_ref, member_ref, spread_refs, sink):
    columns, tokens = row_ref.shape
    width = math.gcd(tokens, 512)
    numbers = lax.broadcasted_iota(jnp.int32, (SEQ_DEV, 1), 0)
    ids = ids_ref[:, pl.ds(pl.multiple_of(quarter * col_ref.shape[1] + first, 128), tokens)]
    member_ref[...] = (ids == numbers).astype(jnp.bfloat16)
    rows = spread_refs[0].shape[0] // R
    for g in range(columns // rows):
        spread_ref = spread_refs[g % 2]
        for at in range(0, tokens, width):
            right = col_ref[:, first + at:first + at + width].astype(jnp.float32)
            for r in range(rows):
                row = row_ref[g * rows + r:g * rows + r + 1, at:at + width]
                spread_ref[r * R:(r + 1) * R, at:at + width] = (row * right).astype(jnp.bfloat16)
        part = lax.dot_general(member_ref[...], spread_ref[...], LAST, preferred_element_type=jnp.float32)
        sink(slice(g * rows * R, (g + 1) * rows * R), part)


def sketch_kernel(lefts, who_ref, *refs):
    count = lefts + 3
    sources, base_ref, col_ref, targets = refs[:count], refs[count], refs[count + 1], refs[count + 2:2 * count + 2]
    sems, row_ref, member_ref, spread_0, spread_1 = refs[2 * count + 2:]
    half, quarter = who_ref[0], who_ref[1]
    for copy in fetch_all(sources, targets, sems):
        copy.wait()
    piece = targets[1].shape[1]
    for k in range(2):
        col_ref[:, pl.ds(pl.multiple_of((half ^ k) * piece, piece), piece)] = targets[1 + k][...]
    row_ref[...] = sum([ref[...].astype(jnp.float32) for ref in targets[4:]], targets[3][...])

    def sink(here, part):
        base_ref[:, here] = part

    sketch_rows(quarter, 0, row_ref, col_ref, targets[0], member_ref, (spread_0, spread_1), sink)


def score_kernel(lefts, asks, first, who_ref, *refs):
    count = lefts + 3 + asks
    sources, out_ref, targets = refs[:count], refs[count], refs[count + 1:2 * count + 1]
    sems, refs = refs[2 * count + 1], refs[2 * count + 2:]
    row_ref, member_ref, spread_0, spread_1 = refs[-4:]
    copies = fetch_all(sources, targets, sems)
    quarter, data = who_ref[1], who_ref[2]
    ids_ref, col_ref, base_ref, left_refs = targets[0], targets[1], targets[2], targets[3:3 + lefts]
    for copy in copies[:3 + lefts]:
        copy.wait()
    row_ref[...] = sum([ref[...].astype(jnp.float32) for ref in left_refs[1:]], left_refs[0][...])
    sketch_ref = refs[0] if asks else out_ref

    def sink(here, part):
        sketch_ref[:, here] = base_ref[:, here] + part

    sketch_rows(quarter, first, row_ref, col_ref, ids_ref, member_ref, (spread_0, spread_1), sink)
    if asks:
        both_ref, query_refs = refs[1], targets[3 + lefts:]
        entries = sketch_ref[...]
        high = entries.astype(jnp.bfloat16)
        both_ref[:SEQ_DEV, :] = high
        both_ref[SEQ_DEV:, :] = (entries - high.astype(jnp.float32)).astype(jnp.bfloat16)
        for copy in copies[3 + lefts:]:
            copy.wait()
        rows, wide = query_refs[0].shape
        for side in range(2):
            total = jnp.zeros((2 * SEQ_DEV, rows), jnp.float32)
            for d in range(lefts):
                query = query_refs[lefts][d * rows:(d + 1) * rows, :] if side else query_refs[d][...]
                near = both_ref[:, pl.ds(pl.multiple_of((quarter ^ d) * wide, wide), wide)]
                total = total + lax.dot_general(near, query, LAST, preferred_element_type=jnp.float32)
            here = pl.ds(pl.multiple_of((data ^ side) * rows, rows), rows)
            out_ref[:, here] = total[:SEQ_DEV] + total[SEQ_DEV:]


def plain_scores(who, entries, asked, crossed):
    quarters = len(asked)
    own = jnp.stack(asked)
    other = crossed.reshape(own.shape)
    both = jnp.where(who[2] == 0, jnp.concatenate([own, other], 1), jnp.concatenate([other, own], 1))
    both = jnp.take(both, jnp.arange(quarters, dtype=jnp.int32) ^ who[1], axis=0)
    both = both.transpose(1, 0, 2).reshape(both.shape[1], -1)
    rounded = lax.reduce_precision(entries, 8, 7)
    low = (entries - rounded).astype(jnp.bfloat16)
    total = lax.dot_general(rounded.astype(jnp.bfloat16), both, LAST, preferred_element_type=jnp.float32)
    return total + lax.dot_general(low, both, LAST, preferred_element_type=jnp.float32)


def call_sketch(kernel, who, operands, columns, tokens, shapes, extra, name):
    rows = min(4, columns)
    return pl.pallas_call(
        kernel,
        in_specs=[pl.BlockSpec(memory_space=pltpu.SMEM)] + [pl.BlockSpec(memory_space=pl.ANY)] * len(operands),
        out_specs=[pl.BlockSpec(memory_space=pltpu.VMEM)] * len(shapes),
        out_shape=shapes,
        scratch_shapes=[pltpu.VMEM(operand.shape, operand.dtype) for operand in operands]
        + [pltpu.SemaphoreType.DMA((len(operands),))]
        + extra
        + [
            pltpu.VMEM((columns, tokens), jnp.float32),
            pltpu.VMEM((SEQ_DEV, tokens), jnp.bfloat16),
            pltpu.VMEM((rows * R, tokens), jnp.bfloat16),
            pltpu.VMEM((rows * R, tokens), jnp.bfloat16),
        ],
        compiler_params=pltpu.CompilerParams(vmem_limit_bytes=VMEM // 3),
        cost_estimate=pl.CostEstimate(flops=2 * tokens * columns * R * SEQ_DEV, bytes_accessed=4 * columns * tokens, transcendentals=0),
        name=name,
    )(who, *operands)


def body(n_tensor, activations, out_grads, proj_in, proj_out, segment_ids, queries):
    quarters = n_tensor // 2
    me = lax.axis_index("tensor").astype(jnp.int32)
    half = me % 2
    who = jnp.stack([half, me // 2, lax.axis_index("dp").astype(jnp.int32)])
    owned = activations.shape[0] // quarters
    early = owned * 3 // 4 if owned % 2048 == 0 else owned // 2
    columns = R // 2

    def swap(array, distance):
        return lax.ppermute(array, "tensor", [(k, k ^ distance) for k in range(n_tensor)])

    def along(arrays):
        return [swap(arrays[d], 2 * d) for d in range(1, quarters)]

    asked = [queries] + along([queries] * quarters)

    scale_in, scale_out = FF ** -0.5, D ** -0.5
    sent_g, kept_g, signs = project(out_grads, proj_out.T, who, scale_out, quarters, 0, 0, owned // 2, 1024, proj_in.T)
    got_g = swap(sent_g, 1)

    def chunk(first, count, after):
        sent, kept = project(activations, signs, who, scale_in, quarters, columns, first, count, 512, None, after)
        return sent, [kept, swap(sent, 1)]

    sent_0, chunk_0 = chunk(0, early, [])
    crossed = lax.ppermute(stack(asked, [sent_0, got_g]), "dp", [(0, 1), (1, 0)])
    pair_g = merge([], [kept_g, got_g], [sent_0])
    moved_g = along(pair_g)
    sent_1, chunk_1 = chunk(early, owned - early, [pair_g[1]])
    own_g = total_of([pair_g[0]] + moved_g, [sent_1, crossed])
    other_g = swap(own_g, 1)
    pair_0 = merge([], chunk_0, [sent_1])
    left_0 = [pair_0[0]] + along(pair_0)
    pair_1 = merge([], chunk_1, [])
    left_1 = [pair_1[0]] + along(pair_1)

    entries = columns * R
    shapes = [jax.ShapeDtypeStruct((SEQ_DEV, entries), jnp.float32), jax.ShapeDtypeStruct((R, owned), jnp.bfloat16)]
    first = [segment_ids, own_g, other_g] + left_0
    base, col = call_sketch(functools.partial(sketch_kernel, quarters), who, first, columns, early, shapes, [], "sketch")
    rest = [segment_ids, col, base] + left_1
    asks = 0 if queries.shape[1] % 128 else quarters + 1
    kernel = functools.partial(score_kernel, quarters, asks, early)
    if not asks:
        shapes = [jax.ShapeDtypeStruct((SEQ_DEV, entries), jnp.float32)]
        total = call_sketch(kernel, who, rest, columns, owned - early, shapes, [], "sketch_rest")[0]
        total = plain_scores(who, total, asked, crossed)
    else:
        shapes = [jax.ShapeDtypeStruct((SEQ_DEV, 2 * queries.shape[0]), jnp.float32)]
        extra = [pltpu.VMEM((SEQ_DEV, entries), jnp.float32), pltpu.VMEM((2 * SEQ_DEV, entries), jnp.bfloat16)]
        rest = rest + asked + [crossed]
        total = call_sketch(kernel, who, rest, columns, owned - early, shapes, extra, "score")[0]
    total = (total + swap(total, 1)).astype(jnp.bfloat16)
    parts = [total] + [swap(total, 2 * d) for d in range(1, quarters)]
    parts = [part.astype(jnp.float32) for part in parts]
    while len(parts) > 1:
        parts = [parts[k] + parts[k + 1] for k in range(0, len(parts), 2)]
    return parts[0]


def solution(mesh):
    return jax.shard_map(
        functools.partial(body, mesh.shape["tensor"]),
        mesh=mesh,
        in_specs=(
            P(("copies", "dp"), "tensor"),
            P(("copies", "dp"), "tensor"),
            P("tensor", None),
            P("tensor", None),
            P(("copies", "dp"), None),
            P(("copies", "dp"), "tensor"),
        ),
        out_specs=P(("copies", "dp"), None),
        check_vma=False,
    )
```

time: 95.3 us -> 93.9 us (0.985)
  starting transfers between devices: 24.1 us -> 33.3 us
  waiting for transfers between devices: 24.2 us -> 15.5 us
  Pallas kernels: 43.7 us -> 41.9 us
    ppermute x17 -> x20, starting transfers between devices: 23.9 us -> 33.2 us  [swap(): lax.ppermute(array, 'tensor', [(k, k ^ distance) for k in range(n_tensor)])]
    ppermute x17 -> x20, waiting for transfers between devices: 24.2 us -> 15.5 us  [swap(): lax.ppermute(array, 'tensor', [(k, k ^ distance) for k in range(n_tensor)])]
    pallas_call x4 -> x5, Pallas kernels: 36.7 us -> 34.7 us  [the longest x3 34 us: project(): pl.pallas_call(functools.partial(project_kernel, scale, first, split, col...]
    unnamed x10 -> x8, local copies, waits for them, and re-layouts: 1.65 us -> 2.14 us
  transfers between devices with their start and end apart: 19 -> 21, of which waited for: 5 -> 7; matrix products, arithmetic and copies ran while one was open for 0% -> 0% of each run, Pallas kernels for 31% -> 33%
where the time goes in v12:
time: 93.9 us; the launch traced here: 93.7 us
  Pallas kernels  41.9 us (45%)
  starting transfers between devices  33.3 us (35%)
  waiting for transfers between devices  15.5 us (17%)
  local copies, waits for them, and re-layouts  2.14 us (2%)
    pallas_call x3, Pallas kernels, project(): pl.pallas_call(functools.partial(project_kernel, scale, first, split, col...  34 us
    ppermute x20, starting transfers between devices, swap(): lax.ppermute(array, 'tensor', [(k, k ^ distance) for k in range(n_tensor)])  33.2 us
    ppermute x20, waiting for transfers between devices, swap(): lax.ppermute(array, 'tensor', [(k, k ^ distance) for k in range(n_tensor)])  15.5 us
    pallas_call x2, Pallas kernels, call_sketch(): pl.pallas_call(kernel, in_specs=[pl.BlockSpec(memory_space=pltpu.SMEM)] +...  6.38 us
    unnamed x8, local copies, waits for them, and re-layouts  2.14 us
  transfers between devices with their start and end apart: 21, of which 7 were waited for; matrix products, arithmetic and copies ran while one was open for 0% of the time, Pallas kernels for 33%

profile of v12, /device:TPU:0, one launch (start us, length us, event | category | flops | bytes accessed | tf_op | source)
XLA Modules:
  0.0 93.7 jit_solution(18340061370806056486)
XLA Ops:
  0.1 1.2 %copy-done.1 = s32[3584,64]{0,1:T(8,128)S(1)} copy-done((s32[3584,64]{0,1:T(8,128)S(1)}, s32[3584,64]{0,1:T(8,128)}, u32[]{:S(2)}) %copy-start.1) | copy-done | bytes 917528
  1.3 0.9 %copy-done.2 = s32[1024,64]{0,1:T(8,128)S(1)} copy-done((s32[1024,64]{0,1:T(8,128)S(1)}, s32[1024,64]{0,1:T(8,128)}, u32[]{:S(2)}) %copy-start.2) | copy-done | bytes 262168
  2.2 8.6 %project.3 = (bf16[4,64,1024]{2,1,0:T(8,128)(2,1)S(1)}, f32[4,64,1024]{2,1,0:T(8,128)S(1)}, bf16[64,3584]{1,0:T(8,128)(2,1)S(1)}) custom-call(s32[3]{0:T(128)S(1)} %pad_add_fusion.who_ref, bf16[8192,1024]{1,0:T(8,128)(2,1)} %x_hbm.3, s32[64,1024]{1,0:T(8,128)S(1)} %bitcast.6, s32[64,3584]{1,0:T(8,128)S(1)} %bitcast.5), custom_call_target="tpu_custom_call" | custom-call | flops 1073741824 | bytes 16777216 | tf_op jit(solution)/shard_map/project/pallas_call | solution.py:120
  10.8 3.0 %collective-permute-start = (bf16[4,64,1024]{2,1,0:T(8,128)(2,1)S(1)}, bf16[4,64,1024]{2,1,0:T(8,128)(2,1)S(1)}, u32[]{:S(2)}, u32[]{:S(2)}) collective-permute-start(bf16[4,64,1024]{2,1,0:T(8,128)(2,1)S(1)} %get-tuple-element.27), channel_id=1, source_target_pairs={{0,2},{2,0},{4,6},{6,4},{8,10},{10,8},{12,14},{14,12},{1,3},{3,1},... | collective-permute-start | bytes 1572872 | tf_op jit(solution)/shard_map/ppermute | solution.py:346
  13.8 1.6 %collective-permute-start.4 = (bf16[256,512]{1,0:T(8,128)(2,1)}, bf16[256,512]{1,0:T(8,128)(2,1)S(1)}, u32[]{:S(2)}, u32[]{:S(2)}) collective-permute-start(bf16[256,512]{1,0:T(8,128)(2,1)} %refs_7_.1), channel_id=1, source_target_pairs={{0,4},{2,6},{4,0},{6,2},{8,12},{10,14},{12,8},{14,10},{1,5},{3,7},... | collective-permute-start | bytes 786440 | tf_op jit(solution)/shard_map/ppermute | solution.py:346
  15.4 2.6 %collective-permute-start.5 = (bf16[256,512]{1,0:T(8,128)(2,1)}, bf16[256,512]{1,0:T(8,128)(2,1)S(1)}, u32[]{:S(2)}, u32[]{:S(2)}) collective-permute-start(bf16[256,512]{1,0:T(8,128)(2,1)} %refs_7_.1), channel_id=1, source_target_pairs={{0,8},{2,10},{4,12},{6,14},{8,0},{10,2},{12,4},{14,6},{1,9},{3,11}... | collective-permute-start | bytes 786440 | tf_op jit(solution)/shard_map/ppermute | solution.py:346
  18.2 17.6 %project.4 = (bf16[4,32,1536]{2,1,0:T(8,128)(2,1)S(1)}, f32[4,32,1536]{2,1,0:T(8,128)S(1)}) custom-call(s32[3]{0:T(128)S(1)} %pad_add_fusion.who_ref, bf16[8192,3584]{1,0:T(8,128)(2,1)} %x_hbm.5, bf16[64,3584]{1,0:T(8,128)(2,1)S(1)} %get-tuple-element.28.sign_source), custom_call_target="tpu_custom_call" | custom-call | flops 2818572288 | bytes 44040192 | tf_op jit(solution)/shard_map/project/pallas_call | solution.py:120
  35.9 1.1 %collective-permute-done.5.refs_2_.refs_9_ = bf16[256,512]{1,0:T(8,128)(2,1)S(1)} collective-permute-done((bf16[256,512]{1,0:T(8,128)(2,1)}, bf16[256,512]{1,0:T(8,128)(2,1)S(1)}, u32[]{:S(2)}, u32[]{:S(2)}) %collective-permute-start.5) | collective-permute-done | bytes 262176 | tf_op jit(solution)/shard_map/ppermute | solution.py:346
  38.0 4.5 %collective-permute-start.1 = (bf16[64,1024]{1,0:T(8,128)(2,1)S(1)}, bf16[64,1024]{1,0:T(8,128)(2,1)S(1)}, u32[]{:S(2)}, u32[]{:S(2)}) collective-permute-start(bf16[64,1024]{1,0:T(8,128)(2,1)S(1)} %get-tuple-element.31.refs_0_), channel_id=1, source_target_pairs={{0,4},{2,6},{4,0},{6,2},{8,12},{10,14},{12,8},{14,10},{1,5},{3,7},... | collective-permute-start | bytes 393224 | tf_op jit(solution)/shard_map/ppermute | solution.py:346
  42.6 1.1 %collective-permute-start.2 = (bf16[64,1024]{1,0:T(8,128)(2,1)S(1)}, bf16[64,1024]{1,0:T(8,128)(2,1)S(1)}, u32[]{:S(2)}, u32[]{:S(2)}) collective-permute-start(bf16[64,1024]{1,0:T(8,128)(2,1)S(1)} %get-tuple-element.32), channel_id=1, source_target_pairs={{0,8},{2,10},{4,12},{6,14},{8,0},{10,2},{12,4},{14,6},{1,9},{3,11}... | collective-permute-start | bytes 393224 | tf_op jit(solution)/shard_map/ppermute | solution.py:346
  43.6 1.4 %collective-permute-start.3 = (bf16[64,1024]{1,0:T(8,128)(2,1)S(1)}, bf16[64,1024]{1,0:T(8,128)(2,1)S(1)}, u32[]{:S(2)}, u32[]{:S(2)}) collective-permute-start(bf16[64,1024]{1,0:T(8,128)(2,1)S(1)} %get-tuple-element.33), channel_id=1, source_target_pairs={{0,12},{2,14},{4,8},{6,10},{8,4},{10,6},{12,0},{14,2},{1,13},{3,15... | collective-permute-start | bytes 393224 | tf_op jit(solution)/shard_map/ppermute | solution.py:346
  45.0 7.8 %project.5 = (bf16[4,32,512]{2,1,0:T(8,128)(2,1)S(1)}, f32[4,32,512]{2,1,0:T(8,128)S(1)}) custom-call(s32[3]{0:T(128)S(1)} %pad_add_fusion.who_ref, bf16[8192,3584]{1,0:T(8,128)(2,1)} %x_hbm.5, bf16[64,3584]{1,0:T(8,128)(2,1)S(1)} %get-tuple-element.28.sign_source, bf16[64,1024]{1,0:T(8,128)(2,1)S(1)} %get-tuple-element.31.refs_0_), custom_call_target="tpu_custom_call" | custom-call | flops 939524096 | bytes 14680064 | tf_op jit(solution)/shard_map/project/pallas_call | solution.py:120
  52.8 1.6 %collective-permute-start.13 = (bf16[4,32,512]{2,1,0:T(8,128)(2,1)S(1)}, bf16[4,32,512]{2,1,0:T(8,128)(2,1)S(1)}, u32[]{:S(2)}, u32[]{:S(2)}) collective-permute-start(bf16[4,32,512]{2,1,0:T(8,128)(2,1)S(1)} %get-tuple-element.34.refs_4_.refs_2_), channel_id=1, source_target_pairs={{0,2},{2,0},{4,6},{6,4},{8,10},{10,8},{12,14},{14,12},{1,3},{3,1},... | collective-permute-start | bytes 393224 | tf_op jit(solution)/shard_map/ppermute | solution.py:346
  54.4 1.0 %collective-permute-done.2.refs_2_ = bf16[64,1024]{1,0:T(8,128)(2,1)S(1)} collective-permute-done((bf16[64,1024]{1,0:T(8,128)(2,1)S(1)}, bf16[64,1024]{1,0:T(8,128)(2,1)S(1)}, u32[]{:S(2)}, u32[]{:S(2)}) %collective-permute-start.2) | collective-permute-done | bytes 131104 | tf_op jit(solution)/shard_map/ppermute | solution.py:346
  55.5 0.6 total.1.refs_1_
  56.1 1.6 %collective-permute-start.8 = (bf16[64,1024]{1,0:T(8,128)(2,1)S(1)}, bf16[64,1024]{1,0:T(8,128)(2,1)S(1)}, u32[]{:S(2)}, u32[]{:S(2)}) collective-permute-start(bf16[64,1024]{1,0:T(8,128)(2,1)S(1)} %total.1.refs_1_), channel_id=1, source_target_pairs={{0,2},{2,0},{4,6},{6,4},{8,10},{10,8},{12,14},{14,12},{1,3},{3,1},... | collective-permute-start | bytes 393224 | tf_op jit(solution)/shard_map/ppermute | solution.py:346
  58.0 2.4 %collective-permute-start.10 = (bf16[32,1536]{1,0:T(8,128)(2,1)S(1)}, bf16[32,1536]{1,0:T(8,128)(2,1)S(1)}, u32[]{:S(2)}, u32[]{:S(2)}) collective-permute-start(bf16[32,1536]{1,0:T(8,128)(2,1)S(1)} %get-tuple-element.37), channel_id=1, source_target_pairs={{0,4},{2,6},{4,0},{6,2},{8,12},{10,14},{12,8},{14,10},{1,5},{3,7},... | collective-permute-start | bytes 294920 | tf_op jit(solution)/shard_map/ppermute | solution.py:346
  60.4 1.0 %collective-permute-start.11 = (bf16[32,1536]{1,0:T(8,128)(2,1)S(1)}, bf16[32,1536]{1,0:T(8,128)(2,1)S(1)}, u32[]{:S(2)}, u32[]{:S(2)}) collective-permute-start(bf16[32,1536]{1,0:T(8,128)(2,1)S(1)} %get-tuple-element.38), channel_id=1, source_target_pairs={{0,8},{2,10},{4,12},{6,14},{8,0},{10,2},{12,4},{14,6},{1,9},{3,11}... | collective-permute-start | bytes 294920 | tf_op jit(solution)/shard_map/ppermute | solution.py:346
  61.4 1.4 %collective-permute-start.12 = (bf16[32,1536]{1,0:T(8,128)(2,1)S(1)}, bf16[32,1536]{1,0:T(8,128)(2,1)S(1)}, u32[]{:S(2)}, u32[]{:S(2)}) collective-permute-start(bf16[32,1536]{1,0:T(8,128)(2,1)S(1)} %get-tuple-element.39), channel_id=1, source_target_pairs={{0,12},{2,14},{4,8},{6,10},{8,4},{10,6},{12,0},{14,2},{1,13},{3,15... | collective-permute-start | bytes 294920 | tf_op jit(solution)/shard_map/ppermute | solution.py:346
  63.1 1.1 %collective-permute-start.14 = (bf16[32,512]{1,0:T(8,128)(2,1)S(1)}, bf16[32,512]{1,0:T(8,128)(2,1)S(1)}, u32[]{:S(2)}, u32[]{:S(2)}) collective-permute-start(bf16[32,512]{1,0:T(8,128)(2,1)S(1)} %get-tuple-element.44), channel_id=1, source_target_pairs={{0,4},{2,6},{4,0},{6,2},{8,12},{10,14},{12,8},{14,10},{1,5},{3,7},... | collective-permute-start | bytes 98312 | tf_op jit(solution)/shard_map/ppermute | solution.py:346
  64.2 2.9 %collective-permute-start.15 = (bf16[32,512]{1,0:T(8,128)(2,1)S(1)}, bf16[32,512]{1,0:T(8,128)(2,1)S(1)}, u32[]{:S(2)}, u32[]{:S(2)}) collective-permute-start(bf16[32,512]{1,0:T(8,128)(2,1)S(1)} %get-tuple-element.45), channel_id=1, source_target_pairs={{0,8},{2,10},{4,12},{6,14},{8,0},{10,2},{12,4},{14,6},{1,9},{3,11}... | collective-permute-start | bytes 98312 | tf_op jit(solution)/shard_map/ppermute | solution.py:346
  67.1 4.0 %collective-permute-done.11.refs_5_ = bf16[32,1536]{1,0:T(8,128)(2,1)S(1)} collective-permute-done((bf16[32,1536]{1,0:T(8,128)(2,1)S(1)}, bf16[32,1536]{1,0:T(8,128)(2,1)S(1)}, u32[]{:S(2)}, u32[]{:S(2)}) %collective-permute-start.11) | collective-permute-done | bytes 98336 | tf_op jit(solution)/shard_map/ppermute | solution.py:346
  71.0 1.2 %collective-permute-start.16 = (bf16[32,512]{1,0:T(8,128)(2,1)S(1)}, bf16[32,512]{1,0:T(8,128)(2,1)S(1)}, u32[]{:S(2)}, u32[]{:S(2)}) collective-permute-start(bf16[32,512]{1,0:T(8,128)(2,1)S(1)} %get-tuple-element.46), channel_id=1, source_target_pairs={{0,12},{2,14},{4,8},{6,10},{8,4},{10,6},{12,0},{14,2},{1,13},{3,15... | collective-permute-start | bytes 98312 | tf_op jit(solution)/shard_map/ppermute | solution.py:346
  72.2 3.7 %sketch.1 = (f32[64,2048]{1,0:T(8,128)S(1)}, bf16[64,2048]{1,0:T(8,128)(2,1)S(1)}) custom-call(s32[3]{0:T(128)S(1)} %pad_add_fusion.who_ref, s32[1,8192]{1,0:T(1,128)S(1)} %copy-done.3, bf16[64,1024]{1,0:T(8,128)(2,1)S(1)} %total.1.refs_1_, bf16[64,1024]{1,0:T(8,128)(2,1)S(1)} %collective-permute-done.8.refs_2_, f32[32,1536]{1,0:T(8,128)S(1)} %get-tuple-element.36.refs_3_, ...), custom_call_target="tpu_custom_call" | custom-call | flops 402653184 | bytes 196608 | tf_op jit(solution)/shard_map/sketch/pallas_call | solution.py:316
  75.9 0.8 collective-permute-done.16.refs_6_
  76.7 2.7 %score.1 = f32[64,512]{1,0:T(8,128)S(1)} custom-call(s32[3]{0:T(128)S(1)} %pad_add_fusion.who_ref, s32[1,8192]{1,0:T(1,128)S(1)} %copy-done.3, bf16[64,2048]{1,0:T(8,128)(2,1)S(1)} %get-tuple-element.40.refs_1_, f32[64,2048]{1,0:T(8,128)S(1)} %get-tuple-element.41.refs_2_, f32[32,512]{1,0:T(8,128)S(1)} %get-tuple-element.43.refs_3_, ...), custom_call_target="tpu_custom_call" | custom-call | flops 134217728 | bytes 65536 | tf_op jit(solution)/shard_map/score/pallas_call | solution.py:316
  80.0 4.5 %collective-permute-done.17 = f32[64,512]{1,0:T(8,128)S(1)} collective-permute-done((f32[64,512]{1,0:T(8,128)S(1)}, f32[64,512]{1,0:T(8,128)S(1)}, u32[]{:S(2)}, u32[]{:S(2)}) %collective-permute-start.17) | collective-permute-done | bytes 131104 | tf_op jit(solution)/shard_map/ppermute | solution.py:346
  84.7 2.3 %collective-permute-start.19 = (bf16[64,512]{1,0:T(8,128)(2,1)S(1)}, bf16[64,512]{1,0:T(8,128)(2,1)S(1)}, u32[]{:S(2)}, u32[]{:S(2)}) collective-permute-start(bf16[64,512]{1,0:T(8,128)(2,1)S(1)} %add_convert_fusion), channel_id=1, source_target_pairs={{0,8},{2,10},{4,12},{6,14},{8,0},{10,2},{12,4},{14,6},{1,9},{3,11}... | collective-permute-start | bytes 196616 | tf_op jit(solution)/shard_map/ppermute | solution.py:346
  87.0 2.0 %collective-permute-start.20 = (bf16[64,512]{1,0:T(8,128)(2,1)S(1)}, bf16[64,512]{1,0:T(8,128)(2,1)S(1)}, u32[]{:S(2)}, u32[]{:S(2)}) collective-permute-start(bf16[64,512]{1,0:T(8,128)(2,1)S(1)} %add_convert_fusion), channel_id=1, source_target_pairs={{0,12},{2,14},{4,8},{6,10},{8,4},{10,6},{12,0},{14,2},{1,13},{3,15... | collective-permute-start | bytes 196616 | tf_op jit(solution)/shard_map/ppermute | solution.py:346
  89.0 0.9 collective-permute-done.19
  89.9 3.2 %collective-permute-done.20 = bf16[64,512]{1,0:T(8,128)(2,1)S(1)} collective-permute-done((bf16[64,512]{1,0:T(8,128)(2,1)S(1)}, bf16[64,512]{1,0:T(8,128)(2,1)S(1)}, u32[]{:S(2)}, u32[]{:S(2)}) %collective-permute-start.20) | collective-permute-done | bytes 65568 | tf_op jit(solution)/shard_map/ppermute | solution.py:346
  93.0 0.7 add_add_fusion
  (31 shorter events, 2.6 us)
Async XLA Ops:
  0.0 37.0 %copy-start = (bf16[256,512]{1,0:T(8,128)(2,1)S(1)}, bf16[256,512]{1,0:T(8,128)(2,1)}, u32[]{:S(2)}) copy-start(bf16[256,512]{1,0:T(8,128)(2,1)} %refs_7_.1) | copy-start | bytes 786436
  0.1 1.2 %copy-start.1 = (s32[3584,64]{0,1:T(8,128)S(1)}, s32[3584,64]{0,1:T(8,128)}, u32[]{:S(2)}) copy-start(s32[3584,64]{0,1:T(8,128)} %param.8) | copy-start | bytes 2752516
  1.3 0.9 %copy-start.2 = (s32[1024,64]{0,1:T(8,128)S(1)}, s32[1024,64]{0,1:T(8,128)}, u32[]{:S(2)}) copy-start(s32[1024,64]{0,1:T(8,128)} %param.9) | copy-start | bytes 786436
  10.8 26.2 %collective-permute-start = (bf16[4,64,1024]{2,1,0:T(8,128)(2,1)S(1)}, bf16[4,64,1024]{2,1,0:T(8,128)(2,1)S(1)}, u32[]{:S(2)}, u32[]{:S(2)}) collective-permute-start(bf16[4,64,1024]{2,1,0:T(8,128)(2,1)S(1)} %get-tuple-element.27), channel_id=1, source_target_pairs={{0,2},{2,0},{4,6},{6,4},{8,10},{10,8},{12,14},{14,12},{1,3},{3,1},... | collective-permute-start | bytes 1572872 | tf_op jit(solution)/shard_map/ppermute | solution.py:346
  13.8 22.0 %collective-permute-start.4 = (bf16[256,512]{1,0:T(8,128)(2,1)}, bf16[256,512]{1,0:T(8,128)(2,1)S(1)}, u32[]{:S(2)}, u32[]{:S(2)}) collective-permute-start(bf16[256,512]{1,0:T(8,128)(2,1)} %refs_7_.1), channel_id=1, source_target_pairs={{0,4},{2,6},{4,0},{6,2},{8,12},{10,14},{12,8},{14,10},{1,5},{3,7},... | collective-permute-start | bytes 786440 | tf_op jit(solution)/shard_map/ppermute | solution.py:346
  15.4 21.6 %collective-permute-start.5 = (bf16[256,512]{1,0:T(8,128)(2,1)}, bf16[256,512]{1,0:T(8,128)(2,1)S(1)}, u32[]{:S(2)}, u32[]{:S(2)}) collective-permute-start(bf16[256,512]{1,0:T(8,128)(2,1)} %refs_7_.1), channel_id=1, source_target_pairs={{0,8},{2,10},{4,12},{6,14},{8,0},{10,2},{12,4},{14,6},{1,9},{3,11}... | collective-permute-start | bytes 786440 | tf_op jit(solution)/shard_map/ppermute | solution.py:346
  18.0 19.0 %collective-permute-start.6 = (bf16[256,512]{1,0:T(8,128)(2,1)}, bf16[256,512]{1,0:T(8,128)(2,1)S(1)}, u32[]{:S(2)}, u32[]{:S(2)}) collective-permute-start(bf16[256,512]{1,0:T(8,128)(2,1)} %refs_7_.1), channel_id=1, source_target_pairs={{0,12},{2,14},{4,8},{6,10},{8,4},{10,6},{12,0},{14,2},{1,13},{3,15... | collective-permute-start | bytes 786440 | tf_op jit(solution)/shard_map/ppermute | solution.py:346
  18.2 54.0 %copy-start.3 = (s32[1,8192]{1,0:T(1,128)S(1)}, s32[1,8192]{1,0:T(1,128)}, u32[]{:S(2)}) copy-start(s32[1,8192]{1,0:T(1,128)} %refs_0_.5) | copy-start | bytes 98308
  37.1 18.3 %collective-permute-start.7 = (bf16[1024,512]{1,0:T(8,128)(2,1)S(1)}, bf16[1024,512]{1,0:T(8,128)(2,1)S(1)}, u32[]{:S(2)}, u32[]{:S(2)}) collective-permute-start(bf16[1024,512]{1,0:T(8,128)(2,1)S(1)} %stack.17), channel_id=1, source_target_pairs={{0,1},{1,0},{2,3},{3,2},{4,5},{5,4},{6,7},{7,6},{8,9},{9,8},{10,11... | collective-permute-start | bytes 3145736 | tf_op jit(solution)/shard_map/ppermute | solution.py:362
  37.2 20.5 %collective-permute-start.9 = (bf16[4,32,1536]{2,1,0:T(8,128)(2,1)S(1)}, bf16[4,32,1536]{2,1,0:T(8,128)(2,1)S(1)}, u32[]{:S(2)}, u32[]{:S(2)}) collective-permute-start(bf16[4,32,1536]{2,1,0:T(8,128)(2,1)S(1)} %get-tuple-element.29.refs_2_.refs_4_), channel_id=1, source_target_pairs={{0,2},{2,0},{4,6},{6,4},{8,10},{10,8},{12,14},{14,12},{1,3},{3,1},... | collective-permute-start | bytes 1179656 | tf_op jit(solution)/shard_map/ppermute | solution.py:346
  38.0 14.8 %collective-permute-start.1 = (bf16[64,1024]{1,0:T(8,128)(2,1)S(1)}, bf16[64,1024]{1,0:T(8,128)(2,1)S(1)}, u32[]{:S(2)}, u32[]{:S(2)}) collective-permute-start(bf16[64,1024]{1,0:T(8,128)(2,1)S(1)} %get-tuple-element.31.refs_0_), channel_id=1, source_target_pairs={{0,4},{2,6},{4,0},{6,2},{8,12},{10,14},{12,8},{14,10},{1,5},{3,7},... | collective-permute-start | bytes 393224 | tf_op jit(solution)/shard_map/ppermute | solution.py:346
  42.6 12.9 %collective-permute-start.2 = (bf16[64,1024]{1,0:T(8,128)(2,1)S(1)}, bf16[64,1024]{1,0:T(8,128)(2,1)S(1)}, u32[]{:S(2)}, u32[]{:S(2)}) collective-permute-start(bf16[64,1024]{1,0:T(8,128)(2,1)S(1)} %get-tuple-element.32), channel_id=1, source_target_pairs={{0,8},{2,10},{4,12},{6,14},{8,0},{10,2},{12,4},{14,6},{1,9},{3,11}... | collective-permute-start | bytes 393224 | tf_op jit(solution)/shard_map/ppermute | solution.py:346
  43.6 11.8 %collective-permute-start.3 = (bf16[64,1024]{1,0:T(8,128)(2,1)S(1)}, bf16[64,1024]{1,0:T(8,128)(2,1)S(1)}, u32[]{:S(2)}, u32[]{:S(2)}) collective-permute-start(bf16[64,1024]{1,0:T(8,128)(2,1)S(1)} %get-tuple-element.33), channel_id=1, source_target_pairs={{0,12},{2,14},{4,8},{6,10},{8,4},{10,6},{12,0},{14,2},{1,13},{3,15... | collective-permute-start | bytes 393224 | tf_op jit(solution)/shard_map/ppermute | solution.py:346
  52.8 10.0 %collective-permute-start.13 = (bf16[4,32,512]{2,1,0:T(8,128)(2,1)S(1)}, bf16[4,32,512]{2,1,0:T(8,128)(2,1)S(1)}, u32[]{:S(2)}, u32[]{:S(2)}) collective-permute-start(bf16[4,32,512]{2,1,0:T(8,128)(2,1)S(1)} %get-tuple-element.34.refs_4_.refs_2_), channel_id=1, source_target_pairs={{0,2},{2,0},{4,6},{6,4},{8,10},{10,8},{12,14},{14,12},{1,3},{3,1},... | collective-permute-start | bytes 393224 | tf_op jit(solution)/shard_map/ppermute | solution.py:346
  56.1 16.1 %collective-permute-start.8 = (bf16[64,1024]{1,0:T(8,128)(2,1)S(1)}, bf16[64,1024]{1,0:T(8,128)(2,1)S(1)}, u32[]{:S(2)}, u32[]{:S(2)}) collective-permute-start(bf16[64,1024]{1,0:T(8,128)(2,1)S(1)} %total.1.refs_1_), channel_id=1, source_target_pairs={{0,2},{2,0},{4,6},{6,4},{8,10},{10,8},{12,14},{14,12},{1,3},{3,1},... | collective-permute-start | bytes 393224 | tf_op jit(solution)/shard_map/ppermute | solution.py:346
  58.0 6.2 %collective-permute-start.10 = (bf16[32,1536]{1,0:T(8,128)(2,1)S(1)}, bf16[32,1536]{1,0:T(8,128)(2,1)S(1)}, u32[]{:S(2)}, u32[]{:S(2)}) collective-permute-start(bf16[32,1536]{1,0:T(8,128)(2,1)S(1)} %get-tuple-element.37), channel_id=1, source_target_pairs={{0,4},{2,6},{4,0},{6,2},{8,12},{10,14},{12,8},{14,10},{1,5},{3,7},... | collective-permute-start | bytes 294920 | tf_op jit(solution)/shard_map/ppermute | solution.py:346
  60.4 10.6 %collective-permute-start.11 = (bf16[32,1536]{1,0:T(8,128)(2,1)S(1)}, bf16[32,1536]{1,0:T(8,128)(2,1)S(1)}, u32[]{:S(2)}, u32[]{:S(2)}) collective-permute-start(bf16[32,1536]{1,0:T(8,128)(2,1)S(1)} %get-tuple-element.38), channel_id=1, source_target_pairs={{0,8},{2,10},{4,12},{6,14},{8,0},{10,2},{12,4},{14,6},{1,9},{3,11}... | collective-permute-start | bytes 294920 | tf_op jit(solution)/shard_map/ppermute | solution.py:346
  61.4 10.8 %collective-permute-start.12 = (bf16[32,1536]{1,0:T(8,128)(2,1)S(1)}, bf16[32,1536]{1,0:T(8,128)(2,1)S(1)}, u32[]{:S(2)}, u32[]{:S(2)}) collective-permute-start(bf16[32,1536]{1,0:T(8,128)(2,1)S(1)} %get-tuple-element.39), channel_id=1, source_target_pairs={{0,12},{2,14},{4,8},{6,10},{8,4},{10,6},{12,0},{14,2},{1,13},{3,15... | collective-permute-start | bytes 294920 | tf_op jit(solution)/shard_map/ppermute | solution.py:346
  63.1 12.8 %collective-permute-start.14 = (bf16[32,512]{1,0:T(8,128)(2,1)S(1)}, bf16[32,512]{1,0:T(8,128)(2,1)S(1)}, u32[]{:S(2)}, u32[]{:S(2)}) collective-permute-start(bf16[32,512]{1,0:T(8,128)(2,1)S(1)} %get-tuple-element.44), channel_id=1, source_target_pairs={{0,4},{2,6},{4,0},{6,2},{8,12},{10,14},{12,8},{14,10},{1,5},{3,7},... | collective-permute-start | bytes 98312 | tf_op jit(solution)/shard_map/ppermute | solution.py:346
  64.2 11.7 %collective-permute-start.15 = (bf16[32,512]{1,0:T(8,128)(2,1)S(1)}, bf16[32,512]{1,0:T(8,128)(2,1)S(1)}, u32[]{:S(2)}, u32[]{:S(2)}) collective-permute-start(bf16[32,512]{1,0:T(8,128)(2,1)S(1)} %get-tuple-element.45), channel_id=1, source_target_pairs={{0,8},{2,10},{4,12},{6,14},{8,0},{10,2},{12,4},{14,6},{1,9},{3,11}... | collective-permute-start | bytes 98312 | tf_op jit(solution)/shard_map/ppermute | solution.py:346
  71.0 5.7 %collective-permute-start.16 = (bf16[32,512]{1,0:T(8,128)(2,1)S(1)}, bf16[32,512]{1,0:T(8,128)(2,1)S(1)}, u32[]{:S(2)}, u32[]{:S(2)}) collective-permute-start(bf16[32,512]{1,0:T(8,128)(2,1)S(1)} %get-tuple-element.46), channel_id=1, source_target_pairs={{0,12},{2,14},{4,8},{6,10},{8,4},{10,6},{12,0},{14,2},{1,13},{3,15... | collective-permute-start | bytes 98312 | tf_op jit(solution)/shard_map/ppermute | solution.py:346
  79.5 5.0 %collective-permute-start.17 = (f32[64,512]{1,0:T(8,128)S(1)}, f32[64,512]{1,0:T(8,128)S(1)}, u32[]{:S(2)}, u32[]{:S(2)}) collective-permute-start(f32[64,512]{1,0:T(8,128)S(1)} %score.1), channel_id=1, source_target_pairs={{0,2},{2,0},{4,6},{6,4},{8,10},{10,8},{12,14},{14,12},{1,3},{3,1},... | collective-permute-start | bytes 393224 | tf_op jit(solution)/shard_map/ppermute | solution.py:346
  84.5 4.5 %collective-permute-start.18 = (bf16[64,512]{1,0:T(8,128)(2,1)S(1)}, bf16[64,512]{1,0:T(8,128)(2,1)S(1)}, u32[]{:S(2)}, u32[]{:S(2)}) collective-permute-start(bf16[64,512]{1,0:T(8,128)(2,1)S(1)} %add_convert_fusion), channel_id=1, source_target_pairs={{0,4},{2,6},{4,0},{6,2},{8,12},{10,14},{12,8},{14,10},{1,5},{3,7},... | collective-permute-start | bytes 196616 | tf_op jit(solution)/shard_map/ppermute | solution.py:346
  84.7 5.2 %collective-permute-start.19 = (bf16[64,512]{1,0:T(8,128)(2,1)S(1)}, bf16[64,512]{1,0:T(8,128)(2,1)S(1)}, u32[]{:S(2)}, u32[]{:S(2)}) collective-permute-start(bf16[64,512]{1,0:T(8,128)(2,1)S(1)} %add_convert_fusion), channel_id=1, source_target_pairs={{0,8},{2,10},{4,12},{6,14},{8,0},{10,2},{12,4},{14,6},{1,9},{3,11}... | collective-permute-start | bytes 196616 | tf_op jit(solution)/shard_map/ppermute | solution.py:346
  87.0 6.1 %collective-permute-start.20 = (bf16[64,512]{1,0:T(8,128)(2,1)S(1)}, bf16[64,512]{1,0:T(8,128)(2,1)S(1)}, u32[]{:S(2)}, u32[]{:S(2)}) collective-permute-start(bf16[64,512]{1,0:T(8,128)(2,1)S(1)} %add_convert_fusion), channel_id=1, source_target_pairs={{0,12},{2,14},{4,8},{6,10},{8,4},{10,6},{12,0},{14,2},{1,13},{3,15... | collective-permute-start | bytes 196616 | tf_op jit(solution)/shard_map/ppermute | solution.py:346

commit v13 on v6

--- a/solution.py
+++ b/solution.py
@@ -141,7 +141,8 @@
 def score_kernel(quarters, width, who_ref, *refs):
     count = 2 * quarters + 5
     sources, out_ref, targets = refs[:count], refs[count], refs[count + 1:2 * count + 1]
-    sems, row_ref, col_ref, member_ref, spread_ref, sketch_ref = refs[2 * count + 1:]
+    sems, row_ref, col_ref, member_ref, sketch_ref = refs[2 * count + 1:-2]
+    spread_refs = refs[-2:]
     copies = fetch_all(sources, targets, sems)
     left_refs, right_refs = targets[:quarters], targets[quarters:2 * quarters]
     ids_ref, query_refs = targets[2 * quarters], targets[2 * quarters + 1:]
@@ -156,14 +157,18 @@
     for d, right_ref in enumerate(right_refs):
         col_ref[:, pl.ds(pl.multiple_of((quarter ^ d) * piece, piece), piece)] = right_ref[...].astype(jnp.float32)
     numbers = lax.broadcasted_iota(jnp.int32, (SEQ_DEV, 1), 0)
-    member_ref[...] = (ids_ref[...] == numbers).astype(jnp.bfloat16)
-    rows = spread_ref.shape[0] // R
-    for first in range(0, row_ref.shape[0], rows):
-        for at in range(0, col_ref.shape[1], width):
+    owned = col_ref.shape[1]
+    ids = ids_ref[:, pl.ds(pl.multiple_of(half * owned, 128), owned)]
+    member_ref[...] = (ids == numbers).astype(jnp.bfloat16)
+    rows = spread_refs[0].shape[0] // R
+    for g in range(row_ref.shape[0] // rows):
+        spread_ref = spread_refs[g % 2]
+        for at in range(0, owned, width):
             right = col_ref[:, at:at + width]
             for r in range(rows):
-                spread_ref[r * R:(r + 1) * R, at:at + width] = (row_ref[first + r:first + r + 1, at:at + width] * right).astype(jnp.bfloat16)
-        sketch_ref[:, first * R:(first + rows) * R] = lax.dot_general(
+                row = row_ref[g * rows + r:g * rows + r + 1, at:at + width]
+                spread_ref[r * R:(r + 1) * R, at:at + width] = (row * right).astype(jnp.bfloat16)
+        sketch_ref[:, g * rows * R:(g + 1) * rows * R] = lax.dot_general(
             member_ref[...], spread_ref[...], LAST, preferred_element_type=jnp.float32
         )
     entries = sketch_ref[...]
@@ -199,8 +204,9 @@
             pltpu.VMEM((columns, tokens), jnp.float32),
             pltpu.VMEM((R, tokens), jnp.float32),
             pltpu.VMEM((SEQ_DEV, tokens), jnp.bfloat16),
+            pltpu.VMEM((SEQ_DEV, columns * R), jnp.float32),
             pltpu.VMEM((rows * R, tokens), jnp.bfloat16),
-            pltpu.VMEM((SEQ_DEV, columns * R), jnp.float32),
+            pltpu.VMEM((rows * R, tokens), jnp.bfloat16),
         ],
         compiler_params=pltpu.CompilerParams(vmem_limit_bytes=VMEM // 3),
         cost_estimate=pl.CostEstimate(flops=2 * tokens * columns * R * SEQ_DEV, bytes_accessed=4 * columns * tokens, transcendentals=0),
@@ -223,7 +229,8 @@
         return lax.ppermute(array, "dp", [(0, 1), (1, 0)])
 
     far = swap(queries, 1)
-    every = [queries, far, cross(queries), cross(far)]
+    cross_near, cross_far = cross(queries), cross(far)
+    every = [queries, far, cross_near, cross_far]
 
     bits_in, bits_out = proj_in.T, proj_out.T
     scale_in, scale_out = FF ** -0.5, D ** -0.5
@@ -234,21 +241,20 @@
     pair_g = [kept_g[d] + got_g[d].astype(jnp.float32) for d in range(quarters)]
     pair_g = [pair_g[0]] + [pair.astype(jnp.bfloat16) for pair in pair_g[1:]]
     moved_g = [swap(pair_g[d], 2 * d) for d in range(1, quarters)]
-    sent_1, kept_1 = project(activations, bits_in, who, scale_in, quarters, True, early, owned - early, 512, [pair_g[1], far])
+    sent_1, kept_1 = project(activations, bits_in, who, scale_in, quarters, True, early, owned - early, 512, [pair_g[1], far, cross_near])
     got_1 = swap(sent_1, 1)
     own_g = sum([moved.astype(jnp.float32) for moved in moved_g], pair_g[0]).astype(jnp.bfloat16)
     right = [own_g] + [swap(own_g, 2 * d) for d in range(1, quarters)]
     pair_a = merge([kept_0, got_0, kept_1, got_1])
     left = [pair_a[0]] + [swap(pair_a[d], 2 * d) for d in range(1, quarters)]
 
-    ids = lax.dynamic_slice(segment_ids, (0, half * owned), (1, owned))
-    total = score(who, left, right, ids, every)
-    distance = 1
-    while 2 * distance < n_tensor:
-        total = total + swap(total, distance)
-        distance = 2 * distance
-    rounded = total.astype(jnp.bfloat16)
-    return rounded.astype(jnp.float32) + swap(rounded, distance).astype(jnp.float32)
+    total = score(who, left, right, segment_ids, every)
+    total = (total + swap(total, 1)).astype(jnp.bfloat16)
+    parts = [total] + [swap(total, 2 * d) for d in range(1, quarters)]
+    parts = [part.astype(jnp.float32) for part in parts]
+    while len(parts) > 1:
+        parts = [parts[k] + parts[k + 1] for k in range(0, len(parts), 2)]
+    return parts[0]
 
 
 def solution(mesh):

time: 94 us -> 92.3 us (0.982)
  starting transfers between devices: 30.3 us -> 25.1 us
  waiting for transfers between devices: 20.7 us -> 24.1 us
    ppermute x16 -> x17, starting transfers between devices: 30.2 us -> 24.9 us  [swap(): lax.ppermute(array, 'tensor', [(k, k ^ distance) for k in range(n_tensor)])]
    ppermute x16 -> x17, waiting for transfers between devices: 20.7 us -> 24.1 us  [swap(): lax.ppermute(array, 'tensor', [(k, k ^ distance) for k in range(n_tensor)])]
  transfers between devices with their start and end apart: 18 -> 19, of which waited for: 6 -> 7; matrix products, arithmetic and copies ran while one was open for 0% -> 0% of each run, Pallas kernels for 28% -> 28%
where the time goes in v13:
time: 92.3 us; the launch traced here: 92.1 us
  Pallas kernels  39.6 us (43%)
  starting transfers between devices  25.1 us (27%)
  waiting for transfers between devices  24.1 us (26%)
  local copies, waits for them, and re-layouts  2.14 us (2%)
  other arithmetic  0.95 us (1%)
    pallas_call x3, Pallas kernels, project(): pl.pallas_call(functools.partial(project_kernel, scale, order, first, spl...  33.6 us
    ppermute x17, starting transfers between devices, swap(): lax.ppermute(array, 'tensor', [(k, k ^ distance) for k in range(n_tensor)])  24.9 us
    ppermute x17, waiting for transfers between devices, swap(): lax.ppermute(array, 'tensor', [(k, k ^ distance) for k in range(n_tensor)])  24.1 us
    pallas_call x1, Pallas kernels, score(): pl.pallas_call(functools.partial(score_kernel, len(left), min(512, tokens...  5.19 us
    unnamed x8, local copies, waits for them, and re-layouts  2.14 us
  transfers between devices with their start and end apart: 19, of which 7 were waited for; matrix products, arithmetic and copies ran while one was open for 0% of the time, Pallas kernels for 28%

profile of v13, /device:TPU:0, one launch (start us, length us, event | category | flops | bytes accessed | tf_op | source)
XLA Modules:
  0.0 92.1 jit_solution(11786510505770667129)
XLA Ops:
  0.1 0.9 %copy-done.1 = s32[1024,64]{0,1:T(8,128)S(1)} copy-done((s32[1024,64]{0,1:T(8,128)S(1)}, s32[1024,64]{0,1:T(8,128)}, u32[]{:S(2)}) %copy-start.1) | copy-done | bytes 262168
  1.0 8.3 %project.4 = (bf16[4,64,1024]{2,1,0:T(8,128)(2,1)S(1)}, f32[4,64,1024]{2,1,0:T(8,128)S(1)}) custom-call(s32[3]{0:T(128)S(1)} %pad_add_fusion.who_ref, bf16[8192,1024]{1,0:T(8,128)(2,1)} %x_hbm.4, s32[64,1024]{1,0:T(8,128)S(1)} %bitcast.21), custom_call_target="tpu_custom_call" | custom-call | flops 1073741824 | bytes 16777216 | tf_op jit(solution)/shard_map/project/pallas_call | solution.py:85
  9.3 3.0 %collective-permute-start.1 = (bf16[4,64,1024]{2,1,0:T(8,128)(2,1)S(1)}, bf16[4,64,1024]{2,1,0:T(8,128)(2,1)S(1)}, u32[]{:S(2)}, u32[]{:S(2)}) collective-permute-start(bf16[4,64,1024]{2,1,0:T(8,128)(2,1)S(1)} %get-tuple-element.18), channel_id=1, source_target_pairs={{0,2},{2,0},{4,6},{6,4},{8,10},{10,8},{12,14},{14,12},{1,3},{3,1},... | collective-permute-start | bytes 1572872 | tf_op jit(solution)/shard_map/ppermute | solution.py:226
  12.5 1.2 %copy-done = s32[3584,64]{0,1:T(8,128)S(1)} copy-done((s32[3584,64]{0,1:T(8,128)S(1)}, s32[3584,64]{0,1:T(8,128)}, u32[]{:S(2)}) %copy-start) | copy-done | bytes 917528
  13.6 15.1 %project.3 = (bf16[4,16,2560]{2,1,0:T(8,128)(2,1)S(1)}, f32[4,16,2560]{2,1,0:T(8,128)S(1)}) custom-call(s32[3]{0:T(128)S(1)} %pad_add_fusion.who_ref, bf16[8192,3584]{1,0:T(8,128)(2,1)} %x_hbm.5, s32[64,3584]{1,0:T(8,128)S(1)} %bitcast.19), custom_call_target="tpu_custom_call" | custom-call | flops 2348810240 | bytes 36700160 | tf_op jit(solution)/shard_map/project/pallas_call | solution.py:85
  28.7 2.0 %collective-permute-start = (bf16[4,16,2560]{2,1,0:T(8,128)(2,1)S(1)}, bf16[4,16,2560]{2,1,0:T(8,128)(2,1)S(1)}, u32[]{:S(2)}, u32[]{:S(2)}) collective-permute-start(bf16[4,16,2560]{2,1,0:T(8,128)(2,1)S(1)} %get-tuple-element.16), channel_id=1, source_target_pairs={{0,2},{2,0},{4,6},{6,4},{8,10},{10,8},{12,14},{14,12},{1,3},{3,1},... | collective-permute-start | bytes 983048 | tf_op jit(solution)/shard_map/ppermute | solution.py:226
  30.8 0.2 collective-permute-start.14
  31.0 0.1 fusion.4
  31.1 3.7 %collective-permute-start.10 = (bf16[64,1024]{1,0:T(8,128)(2,1)S(1)}, bf16[64,1024]{1,0:T(8,128)(2,1)S(1)}, u32[]{:S(2)}, u32[]{:S(2)}) collective-permute-start(bf16[64,1024]{1,0:T(8,128)(2,1)S(1)} %get-tuple-element.26), channel_id=1, source_target_pairs={{0,12},{2,14},{4,8},{6,10},{8,4},{10,6},{12,0},{14,2},{1,13},{3,15... | collective-permute-start | bytes 393224 | tf_op jit(solution)/shard_map/ppermute | solution.py:226
  34.8 0.8 collective-permute-start.9
  35.5 10.2 %project.5 = (bf16[4,16,1536]{2,1,0:T(8,128)(2,1)S(1)}, f32[4,16,1536]{2,1,0:T(8,128)S(1)}) custom-call(s32[3]{0:T(128)S(1)} %pad_add_fusion.who_ref, bf16[8192,3584]{1,0:T(8,128)(2,1)} %x_hbm.5, s32[64,3584]{1,0:T(8,128)S(1)} %bitcast.20, bf16[64,1024]{1,0:T(8,128)(2,1)S(1)} %get-tuple-element.27.refs_0_, ...), custom_call_target="tpu_custom_call" | custom-call | flops 1409286144 | bytes 22020096 | tf_op jit(solution)/shard_map/project/pallas_call | solution.py:85
  45.7 0.8 collective-permute-start.4
  46.6 1.3 %collective-permute-start.11 = (bf16[64,1024]{1,0:T(8,128)(2,1)S(1)}, bf16[64,1024]{1,0:T(8,128)(2,1)S(1)}, u32[]{:S(2)}, u32[]{:S(2)}) collective-permute-start(bf16[64,1024]{1,0:T(8,128)(2,1)S(1)} %fusion.2.refs_4_), channel_id=1, source_target_pairs={{0,4},{2,6},{4,0},{6,2},{8,12},{10,14},{12,8},{14,10},{1,5},{3,7},... | collective-permute-start | bytes 393224 | tf_op jit(solution)/shard_map/ppermute | solution.py:226
  47.9 2.9 %collective-permute-start.12 = (bf16[64,1024]{1,0:T(8,128)(2,1)S(1)}, bf16[64,1024]{1,0:T(8,128)(2,1)S(1)}, u32[]{:S(2)}, u32[]{:S(2)}) collective-permute-start(bf16[64,1024]{1,0:T(8,128)(2,1)S(1)} %fusion.2.refs_4_), channel_id=1, source_target_pairs={{0,8},{2,10},{4,12},{6,14},{8,0},{10,2},{12,4},{14,6},{1,9},{3,11}... | collective-permute-start | bytes 393224 | tf_op jit(solution)/shard_map/ppermute | solution.py:226
  50.8 0.2 collective-permute-start.13
  51.0 1.2 %collective-permute-done.4.refs_3_ = bf16[4,16,1536]{2,1,0:T(8,128)(2,1)S(1)} collective-permute-done((bf16[4,16,1536]{2,1,0:T(8,128)(2,1)S(1)}, bf16[4,16,1536]{2,1,0:T(8,128)(2,1)S(1)}, u32[]{:S(2)}, u32[]{:S(2)}) %collective-permute-start.4) | collective-permute-done | bytes 196640 | tf_op jit(solution)/shard_map/ppermute | solution.py:226
  52.2 0.9 merge.1
  53.1 1.4 %collective-permute-start.5 = (bf16[16,4096]{1,0:T(8,128)(2,1)S(1)}, bf16[16,4096]{1,0:T(8,128)(2,1)S(1)}, u32[]{:S(2)}, u32[]{:S(2)}) collective-permute-start(bf16[16,4096]{1,0:T(8,128)(2,1)S(1)} %get-tuple-element.22), channel_id=1, source_target_pairs={{0,4},{2,6},{4,0},{6,2},{8,12},{10,14},{12,8},{14,10},{1,5},{3,7},... | collective-permute-start | bytes 393224 | tf_op jit(solution)/shard_map/ppermute | solution.py:226
  54.5 2.6 %collective-permute-start.6 = (bf16[16,4096]{1,0:T(8,128)(2,1)S(1)}, bf16[16,4096]{1,0:T(8,128)(2,1)S(1)}, u32[]{:S(2)}, u32[]{:S(2)}) collective-permute-start(bf16[16,4096]{1,0:T(8,128)(2,1)S(1)} %get-tuple-element.23), channel_id=1, source_target_pairs={{0,8},{2,10},{4,12},{6,14},{8,0},{10,2},{12,4},{14,6},{1,9},{3,11}... | collective-permute-start | bytes 393224 | tf_op jit(solution)/shard_map/ppermute | solution.py:226
  57.2 0.4 collective-permute-start.7
  57.5 3.3 %collective-permute-done.12.refs_6_ = bf16[64,1024]{1,0:T(8,128)(2,1)S(1)} collective-permute-done((bf16[64,1024]{1,0:T(8,128)(2,1)S(1)}, bf16[64,1024]{1,0:T(8,128)(2,1)S(1)}, u32[]{:S(2)}, u32[]{:S(2)}) %collective-permute-start.12) | collective-permute-done | bytes 131104 | tf_op jit(solution)/shard_map/ppermute | solution.py:226
  60.9 0.1 collective-permute-done.5.refs_1_
  61.0 10.9 %collective-permute-done.6.refs_2_ = bf16[16,4096]{1,0:T(8,128)(2,1)S(1)} collective-permute-done((bf16[16,4096]{1,0:T(8,128)(2,1)S(1)}, bf16[16,4096]{1,0:T(8,128)(2,1)S(1)}, u32[]{:S(2)}, u32[]{:S(2)}) %collective-permute-start.6) | collective-permute-done | bytes 131104 | tf_op jit(solution)/shard_map/ppermute | solution.py:226
  71.9 5.2 %score.1 = f32[64,512]{1,0:T(8,128)S(1)} custom-call(s32[3]{0:T(128)S(1)} %pad_add_fusion.who_ref, f32[16,4096]{1,0:T(8,128)S(1)} %get-tuple-element.21.refs_0_, bf16[16,4096]{1,0:T(8,128)(2,1)S(1)} %collective-permute-done.5.refs_1_, bf16[16,4096]{1,0:T(8,128)(2,1)S(1)} %collective-permute-done.6.refs_2_, ...), custom_call_target="tpu_custom_call" | custom-call | flops 536870912 | bytes 262144 | tf_op jit(solution)/shard_map/score/pallas_call | solution.py:196
  77.1 1.2 %collective-permute-start.15 = (f32[64,512]{1,0:T(8,128)S(1)}, f32[64,512]{1,0:T(8,128)S(1)}, u32[]{:S(2)}, u32[]{:S(2)}) collective-permute-start(f32[64,512]{1,0:T(8,128)S(1)} %score.1), channel_id=1, source_target_pairs={{0,2},{2,0},{4,6},{6,4},{8,10},{10,8},{12,14},{14,12},{1,3},{3,1},... | collective-permute-start | bytes 393224 | tf_op jit(solution)/shard_map/ppermute | solution.py:226
  78.3 3.9 %collective-permute-done.15 = f32[64,512]{1,0:T(8,128)S(1)} collective-permute-done((f32[64,512]{1,0:T(8,128)S(1)}, f32[64,512]{1,0:T(8,128)S(1)}, u32[]{:S(2)}, u32[]{:S(2)}) %collective-permute-start.15) | collective-permute-done | bytes 131104 | tf_op jit(solution)/shard_map/ppermute | solution.py:226
  82.1 2.0 %collective-permute-start.16 = (bf16[64,512]{1,0:T(8,128)(2,1)S(1)}, bf16[64,512]{1,0:T(8,128)(2,1)S(1)}, u32[]{:S(2)}, u32[]{:S(2)}) collective-permute-start(bf16[64,512]{1,0:T(8,128)(2,1)S(1)} %add_convert_fusion.3), channel_id=1, source_target_pairs={{0,4},{2,6},{4,0},{6,2},{8,12},{10,14},{12,8},{14,10},{1,5},{3,7},... | collective-permute-start | bytes 196616 | tf_op jit(solution)/shard_map/ppermute | solution.py:226
  84.2 1.1 %collective-permute-start.17 = (bf16[64,512]{1,0:T(8,128)(2,1)S(1)}, bf16[64,512]{1,0:T(8,128)(2,1)S(1)}, u32[]{:S(2)}, u32[]{:S(2)}) collective-permute-start(bf16[64,512]{1,0:T(8,128)(2,1)S(1)} %add_convert_fusion.3), channel_id=1, source_target_pairs={{0,8},{2,10},{4,12},{6,14},{8,0},{10,2},{12,4},{14,6},{1,9},{3,11}... | collective-permute-start | bytes 196616 | tf_op jit(solution)/shard_map/ppermute | solution.py:226
  85.2 1.4 %collective-permute-start.18 = (bf16[64,512]{1,0:T(8,128)(2,1)S(1)}, bf16[64,512]{1,0:T(8,128)(2,1)S(1)}, u32[]{:S(2)}, u32[]{:S(2)}) collective-permute-start(bf16[64,512]{1,0:T(8,128)(2,1)S(1)} %add_convert_fusion.3), channel_id=1, source_target_pairs={{0,12},{2,14},{4,8},{6,10},{8,4},{10,6},{12,0},{14,2},{1,13},{3,15... | collective-permute-start | bytes 196616 | tf_op jit(solution)/shard_map/ppermute | solution.py:226
  86.6 3.4 %collective-permute-done.17 = bf16[64,512]{1,0:T(8,128)(2,1)S(1)} collective-permute-done((bf16[64,512]{1,0:T(8,128)(2,1)S(1)}, bf16[64,512]{1,0:T(8,128)(2,1)S(1)}, u32[]{:S(2)}, u32[]{:S(2)}) %collective-permute-start.17) | collective-permute-done | bytes 65568 | tf_op jit(solution)/shard_map/ppermute | solution.py:226
  90.0 1.4 %collective-permute-done.18 = bf16[64,512]{1,0:T(8,128)(2,1)S(1)} collective-permute-done((bf16[64,512]{1,0:T(8,128)(2,1)S(1)}, bf16[64,512]{1,0:T(8,128)(2,1)S(1)}, u32[]{:S(2)}, u32[]{:S(2)}) %collective-permute-start.18) | collective-permute-done | bytes 65568 | tf_op jit(solution)/shard_map/ppermute | solution.py:226
  91.4 0.7 add_add_fusion
  (24 shorter events, 0.3 us)
Async XLA Ops:
  0.1 1.0 %copy-start.1 = (s32[1024,64]{0,1:T(8,128)S(1)}, s32[1024,64]{0,1:T(8,128)}, u32[]{:S(2)}) copy-start(s32[1024,64]{0,1:T(8,128)} %param.9) | copy-start | bytes 786436
  9.3 21.7 %collective-permute-start.1 = (bf16[4,64,1024]{2,1,0:T(8,128)(2,1)S(1)}, bf16[4,64,1024]{2,1,0:T(8,128)(2,1)S(1)}, u32[]{:S(2)}, u32[]{:S(2)}) collective-permute-start(bf16[4,64,1024]{2,1,0:T(8,128)(2,1)S(1)} %get-tuple-element.18), channel_id=1, source_target_pairs={{0,2},{2,0},{4,6},{6,4},{8,10},{10,8},{12,14},{14,12},{1,3},{3,1},... | collective-permute-start | bytes 1572872 | tf_op jit(solution)/shard_map/ppermute | solution.py:226
  12.4 18.4 %collective-permute-start.2 = (bf16[256,512]{1,0:T(8,128)(2,1)}, bf16[256,512]{1,0:T(8,128)(2,1)S(1)}, u32[]{:S(2)}, u32[]{:S(2)}) collective-permute-start(bf16[256,512]{1,0:T(8,128)(2,1)} %refs_9_.1), channel_id=1, source_target_pairs={{0,2},{2,0},{4,6},{6,4},{8,10},{10,8},{12,14},{14,12},{1,3},{3,1},... | collective-permute-start | bytes 786440 | tf_op jit(solution)/shard_map/ppermute | solution.py:226
  12.5 22.3 %collective-permute-start.3 = (bf16[256,512]{1,0:T(8,128)(2,1)}, bf16[256,512]{1,0:T(8,128)(2,1)S(1)}, u32[]{:S(2)}, u32[]{:S(2)}) collective-permute-start(bf16[256,512]{1,0:T(8,128)(2,1)} %refs_9_.1), channel_id=1, source_target_pairs={{0,1},{1,0},{2,3},{3,2},{4,5},{5,4},{6,7},{7,6},{8,9},{9,8},{10,11... | collective-permute-start | bytes 786440 | tf_op jit(solution)/shard_map/ppermute | solution.py:229
  12.5 1.2 %copy-start = (s32[3584,64]{0,1:T(8,128)S(1)}, s32[3584,64]{0,1:T(8,128)}, u32[]{:S(2)}) copy-start(s32[3584,64]{0,1:T(8,128)} %param.8) | copy-start | bytes 2752516
  13.6 58.2 %copy-start.2 = (bf16[256,512]{1,0:T(8,128)(2,1)S(1)}, bf16[256,512]{1,0:T(8,128)(2,1)}, u32[]{:S(2)}) copy-start(bf16[256,512]{1,0:T(8,128)(2,1)} %refs_9_.1) | copy-start | bytes 786436
  13.6 58.2 %copy-start.3 = (s32[1,8192]{1,0:T(1,128)S(1)}, s32[1,8192]{1,0:T(1,128)}, u32[]{:S(2)}) copy-start(s32[1,8192]{1,0:T(1,128)} %refs_8_.1) | copy-start | bytes 98308
  28.7 22.1 %collective-permute-start = (bf16[4,16,2560]{2,1,0:T(8,128)(2,1)S(1)}, bf16[4,16,2560]{2,1,0:T(8,128)(2,1)S(1)}, u32[]{:S(2)}, u32[]{:S(2)}) collective-permute-start(bf16[4,16,2560]{2,1,0:T(8,128)(2,1)S(1)} %get-tuple-element.16), channel_id=1, source_target_pairs={{0,2},{2,0},{4,6},{6,4},{8,10},{10,8},{12,14},{14,12},{1,3},{3,1},... | collective-permute-start | bytes 983048 | tf_op jit(solution)/shard_map/ppermute | solution.py:226
  30.8 23.8 %collective-permute-start.14 = (bf16[256,512]{1,0:T(8,128)(2,1)S(1)}, bf16[256,512]{1,0:T(8,128)(2,1)S(1)}, u32[]{:S(2)}, u32[]{:S(2)}) collective-permute-start(bf16[256,512]{1,0:T(8,128)(2,1)S(1)} %collective-permute-done.2.refs_1_.refs_10_), channel_id=1, source_target_pairs={{0,1},{1,0},{2,3},{3,2},{4,5},{5,4},{6,7},{7,6},{8,9},{9,8},{10,11... | collective-permute-start | bytes 786440 | tf_op jit(solution)/shard_map/ppermute | solution.py:229
  31.1 14.7 %collective-permute-start.10 = (bf16[64,1024]{1,0:T(8,128)(2,1)S(1)}, bf16[64,1024]{1,0:T(8,128)(2,1)S(1)}, u32[]{:S(2)}, u32[]{:S(2)}) collective-permute-start(bf16[64,1024]{1,0:T(8,128)(2,1)S(1)} %get-tuple-element.26), channel_id=1, source_target_pairs={{0,12},{2,14},{4,8},{6,10},{8,4},{10,6},{12,0},{14,2},{1,13},{3,15... | collective-permute-start | bytes 393224 | tf_op jit(solution)/shard_map/ppermute | solution.py:226
  34.7 11.8 %collective-permute-start.8 = (bf16[64,1024]{1,0:T(8,128)(2,1)S(1)}, bf16[64,1024]{1,0:T(8,128)(2,1)S(1)}, u32[]{:S(2)}, u32[]{:S(2)}) collective-permute-start(bf16[64,1024]{1,0:T(8,128)(2,1)S(1)} %get-tuple-element.27.refs_0_), channel_id=1, source_target_pairs={{0,4},{2,6},{4,0},{6,2},{8,12},{10,14},{12,8},{14,10},{1,5},{3,7},... | collective-permute-start | bytes 393224 | tf_op jit(solution)/shard_map/ppermute | solution.py:226
  34.8 11.7 %collective-permute-start.9 = (bf16[64,1024]{1,0:T(8,128)(2,1)S(1)}, bf16[64,1024]{1,0:T(8,128)(2,1)S(1)}, u32[]{:S(2)}, u32[]{:S(2)}) collective-permute-start(bf16[64,1024]{1,0:T(8,128)(2,1)S(1)} %get-tuple-element.25), channel_id=1, source_target_pairs={{0,8},{2,10},{4,12},{6,14},{8,0},{10,2},{12,4},{14,6},{1,9},{3,11}... | collective-permute-start | bytes 393224 | tf_op jit(solution)/shard_map/ppermute | solution.py:226
  45.7 6.5 %collective-permute-start.4 = (bf16[4,16,1536]{2,1,0:T(8,128)(2,1)S(1)}, bf16[4,16,1536]{2,1,0:T(8,128)(2,1)S(1)}, u32[]{:S(2)}, u32[]{:S(2)}) collective-permute-start(bf16[4,16,1536]{2,1,0:T(8,128)(2,1)S(1)} %get-tuple-element.20), channel_id=1, source_target_pairs={{0,2},{2,0},{4,6},{6,4},{8,10},{10,8},{12,14},{14,12},{1,3},{3,1},... | collective-permute-start | bytes 589832 | tf_op jit(solution)/shard_map/ppermute | solution.py:226
  46.6 10.6 %collective-permute-start.11 = (bf16[64,1024]{1,0:T(8,128)(2,1)S(1)}, bf16[64,1024]{1,0:T(8,128)(2,1)S(1)}, u32[]{:S(2)}, u32[]{:S(2)}) collective-permute-start(bf16[64,1024]{1,0:T(8,128)(2,1)S(1)} %fusion.2.refs_4_), channel_id=1, source_target_pairs={{0,4},{2,6},{4,0},{6,2},{8,12},{10,14},{12,8},{14,10},{1,5},{3,7},... | collective-permute-start | bytes 393224 | tf_op jit(solution)/shard_map/ppermute | solution.py:226
  47.9 13.0 %collective-permute-start.12 = (bf16[64,1024]{1,0:T(8,128)(2,1)S(1)}, bf16[64,1024]{1,0:T(8,128)(2,1)S(1)}, u32[]{:S(2)}, u32[]{:S(2)}) collective-permute-start(bf16[64,1024]{1,0:T(8,128)(2,1)S(1)} %fusion.2.refs_4_), channel_id=1, source_target_pairs={{0,8},{2,10},{4,12},{6,14},{8,0},{10,2},{12,4},{14,6},{1,9},{3,11}... | collective-permute-start | bytes 393224 | tf_op jit(solution)/shard_map/ppermute | solution.py:226
  50.8 10.1 %collective-permute-start.13 = (bf16[64,1024]{1,0:T(8,128)(2,1)S(1)}, bf16[64,1024]{1,0:T(8,128)(2,1)S(1)}, u32[]{:S(2)}, u32[]{:S(2)}) collective-permute-start(bf16[64,1024]{1,0:T(8,128)(2,1)S(1)} %fusion.2.refs_4_), channel_id=1, source_target_pairs={{0,12},{2,14},{4,8},{6,10},{8,4},{10,6},{12,0},{14,2},{1,13},{3,15... | collective-permute-start | bytes 393224 | tf_op jit(solution)/shard_map/ppermute | solution.py:226
  53.1 7.9 %collective-permute-start.5 = (bf16[16,4096]{1,0:T(8,128)(2,1)S(1)}, bf16[16,4096]{1,0:T(8,128)(2,1)S(1)}, u32[]{:S(2)}, u32[]{:S(2)}) collective-permute-start(bf16[16,4096]{1,0:T(8,128)(2,1)S(1)} %get-tuple-element.22), channel_id=1, source_target_pairs={{0,4},{2,6},{4,0},{6,2},{8,12},{10,14},{12,8},{14,10},{1,5},{3,7},... | collective-permute-start | bytes 393224 | tf_op jit(solution)/shard_map/ppermute | solution.py:226
  54.5 17.3 %collective-permute-start.6 = (bf16[16,4096]{1,0:T(8,128)(2,1)S(1)}, bf16[16,4096]{1,0:T(8,128)(2,1)S(1)}, u32[]{:S(2)}, u32[]{:S(2)}) collective-permute-start(bf16[16,4096]{1,0:T(8,128)(2,1)S(1)} %get-tuple-element.23), channel_id=1, source_target_pairs={{0,8},{2,10},{4,12},{6,14},{8,0},{10,2},{12,4},{14,6},{1,9},{3,11}... | collective-permute-start | bytes 393224 | tf_op jit(solution)/shard_map/ppermute | solution.py:226
  57.2 14.7 %collective-permute-start.7 = (bf16[16,4096]{1,0:T(8,128)(2,1)S(1)}, bf16[16,4096]{1,0:T(8,128)(2,1)S(1)}, u32[]{:S(2)}, u32[]{:S(2)}) collective-permute-start(bf16[16,4096]{1,0:T(8,128)(2,1)S(1)} %get-tuple-element.24), channel_id=1, source_target_pairs={{0,12},{2,14},{4,8},{6,10},{8,4},{10,6},{12,0},{14,2},{1,13},{3,15... | collective-permute-start | bytes 393224 | tf_op jit(solution)/shard_map/ppermute | solution.py:226
  77.1 5.0 %collective-permute-start.15 = (f32[64,512]{1,0:T(8,128)S(1)}, f32[64,512]{1,0:T(8,128)S(1)}, u32[]{:S(2)}, u32[]{:S(2)}) collective-permute-start(f32[64,512]{1,0:T(8,128)S(1)} %score.1), channel_id=1, source_target_pairs={{0,2},{2,0},{4,6},{6,4},{8,10},{10,8},{12,14},{14,12},{1,3},{3,1},... | collective-permute-start | bytes 393224 | tf_op jit(solution)/shard_map/ppermute | solution.py:226
  82.1 4.5 %collective-permute-start.16 = (bf16[64,512]{1,0:T(8,128)(2,1)S(1)}, bf16[64,512]{1,0:T(8,128)(2,1)S(1)}, u32[]{:S(2)}, u32[]{:S(2)}) collective-permute-start(bf16[64,512]{1,0:T(8,128)(2,1)S(1)} %add_convert_fusion.3), channel_id=1, source_target_pairs={{0,4},{2,6},{4,0},{6,2},{8,12},{10,14},{12,8},{14,10},{1,5},{3,7},... | collective-permute-start | bytes 196616 | tf_op jit(solution)/shard_map/ppermute | solution.py:226
  84.2 5.9 %collective-permute-start.17 = (bf16[64,512]{1,0:T(8,128)(2,1)S(1)}, bf16[64,512]{1,0:T(8,128)(2,1)S(1)}, u32[]{:S(2)}, u32[]{:S(2)}) collective-permute-start(bf16[64,512]{1,0:T(8,128)(2,1)S(1)} %add_convert_fusion.3), channel_id=1, source_target_pairs={{0,8},{2,10},{4,12},{6,14},{8,0},{10,2},{12,4},{14,6},{1,9},{3,11}... | collective-permute-start | bytes 196616 | tf_op jit(solution)/shard_map/ppermute | solution.py:226
  85.2 6.2 %collective-permute-start.18 = (bf16[64,512]{1,0:T(8,128)(2,1)S(1)}, bf16[64,512]{1,0:T(8,128)(2,1)S(1)}, u32[]{:S(2)}, u32[]{:S(2)}) collective-permute-start(bf16[64,512]{1,0:T(8,128)(2,1)S(1)} %add_convert_fusion.3), channel_id=1, source_target_pairs={{0,12},{2,14},{4,8},{6,10},{8,4},{10,6},{12,0},{14,2},{1,13},{3,15... | collective-permute-start | bytes 196616 | tf_op jit(solution)/shard_map/ppermute | solution.py:226

commit v14 on v13

--- a/solution.py
+++ b/solution.py
@@ -244,7 +244,12 @@
     sent_1, kept_1 = project(activations, bits_in, who, scale_in, quarters, True, early, owned - early, 512, [pair_g[1], far, cross_near])
     got_1 = swap(sent_1, 1)
     own_g = sum([moved.astype(jnp.float32) for moved in moved_g], pair_g[0]).astype(jnp.bfloat16)
-    right = [own_g] + [swap(own_g, 2 * d) for d in range(1, quarters)]
+    pieces = {0: own_g}
+    step = quarters // 2
+    while step:
+        pieces.update({d ^ step: swap(piece, 2 * step) for d, piece in list(pieces.items())})
+        step = step // 2
+    right = [pieces[d] for d in range(quarters)]
     pair_a = merge([kept_0, got_0, kept_1, got_1])
     left = [pair_a[0]] + [swap(pair_a[d], 2 * d) for d in range(1, quarters)]
 

time: 92.3 us -> 87.5 us (0.948)
  waiting for transfers between devices: 24.1 us -> 19.2 us
    ppermute x17, waiting for transfers between devices: 24.1 us -> 19.2 us  [swap(): lax.ppermute(array, 'tensor', [(k, k ^ distance) for k in range(n_tensor)])]
  transfers between devices with their start and end apart: 19 -> 19, of which waited for: 7 -> 8; matrix products, arithmetic and copies ran while one was open for 0% -> 0% of each run, Pallas kernels for 28% -> 30%
where the time goes in v14:
time: 87.5 us; the launch traced here: 87.3 us
  Pallas kernels  39.6 us (45%)
  starting transfers between devices  25.4 us (29%)
  waiting for transfers between devices  19.2 us (22%)
  local copies, waits for them, and re-layouts  2.14 us (2%)
  other arithmetic  0.95 us (1%)
    pallas_call x3, Pallas kernels, project(): pl.pallas_call(functools.partial(project_kernel, scale, order, first, spl...  33.6 us
    ppermute x17, starting transfers between devices, swap(): lax.ppermute(array, 'tensor', [(k, k ^ distance) for k in range(n_tensor)])  25.1 us
    ppermute x17, waiting for transfers between devices, swap(): lax.ppermute(array, 'tensor', [(k, k ^ distance) for k in range(n_tensor)])  19.2 us
    pallas_call x1, Pallas kernels, score(): pl.pallas_call(functools.partial(score_kernel, len(left), min(512, tokens...  5.18 us
    unnamed x8, local copies, waits for them, and re-layouts  2.14 us
  transfers between devices with their start and end apart: 19, of which 8 were waited for; matrix products, arithmetic and copies ran while one was open for 0% of the time, Pallas kernels for 30%

profile of v14, /device:TPU:0, one launch (start us, length us, event | category | flops | bytes accessed | tf_op | source)
XLA Modules:
  0.0 87.3 jit_solution(4395092665182374325)
XLA Ops:
  0.1 0.9 %copy-done.1 = s32[1024,64]{0,1:T(8,128)S(1)} copy-done((s32[1024,64]{0,1:T(8,128)S(1)}, s32[1024,64]{0,1:T(8,128)}, u32[]{:S(2)}) %copy-start.1) | copy-done | bytes 262168
  1.0 8.3 %project.4 = (bf16[4,64,1024]{2,1,0:T(8,128)(2,1)S(1)}, f32[4,64,1024]{2,1,0:T(8,128)S(1)}) custom-call(s32[3]{0:T(128)S(1)} %pad_add_fusion.who_ref, bf16[8192,1024]{1,0:T(8,128)(2,1)} %x_hbm.4, s32[64,1024]{1,0:T(8,128)S(1)} %bitcast.21), custom_call_target="tpu_custom_call" | custom-call | flops 1073741824 | bytes 16777216 | tf_op jit(solution)/shard_map/project/pallas_call | solution.py:85
  9.3 3.0 %collective-permute-start.1 = (bf16[4,64,1024]{2,1,0:T(8,128)(2,1)S(1)}, bf16[4,64,1024]{2,1,0:T(8,128)(2,1)S(1)}, u32[]{:S(2)}, u32[]{:S(2)}) collective-permute-start(bf16[4,64,1024]{2,1,0:T(8,128)(2,1)S(1)} %get-tuple-element.18), channel_id=1, source_target_pairs={{0,2},{2,0},{4,6},{6,4},{8,10},{10,8},{12,14},{14,12},{1,3},{3,1},... | collective-permute-start | bytes 1572872 | tf_op jit(solution)/shard_map/ppermute | solution.py:226
  12.5 1.2 %copy-done = s32[3584,64]{0,1:T(8,128)S(1)} copy-done((s32[3584,64]{0,1:T(8,128)S(1)}, s32[3584,64]{0,1:T(8,128)}, u32[]{:S(2)}) %copy-start) | copy-done | bytes 917528
  13.6 15.1 %project.3 = (bf16[4,16,2560]{2,1,0:T(8,128)(2,1)S(1)}, f32[4,16,2560]{2,1,0:T(8,128)S(1)}) custom-call(s32[3]{0:T(128)S(1)} %pad_add_fusion.who_ref, bf16[8192,3584]{1,0:T(8,128)(2,1)} %x_hbm.5, s32[64,3584]{1,0:T(8,128)S(1)} %bitcast.19), custom_call_target="tpu_custom_call" | custom-call | flops 2348810240 | bytes 36700160 | tf_op jit(solution)/shard_map/project/pallas_call | solution.py:85
  28.7 2.0 %collective-permute-start = (bf16[4,16,2560]{2,1,0:T(8,128)(2,1)S(1)}, bf16[4,16,2560]{2,1,0:T(8,128)(2,1)S(1)}, u32[]{:S(2)}, u32[]{:S(2)}) collective-permute-start(bf16[4,16,2560]{2,1,0:T(8,128)(2,1)S(1)} %get-tuple-element.16), channel_id=1, source_target_pairs={{0,2},{2,0},{4,6},{6,4},{8,10},{10,8},{12,14},{14,12},{1,3},{3,1},... | collective-permute-start | bytes 983048 | tf_op jit(solution)/shard_map/ppermute | solution.py:226
  30.8 0.2 collective-permute-start.14
  31.1 3.7 %collective-permute-start.10 = (bf16[64,1024]{1,0:T(8,128)(2,1)S(1)}, bf16[64,1024]{1,0:T(8,128)(2,1)S(1)}, u32[]{:S(2)}, u32[]{:S(2)}) collective-permute-start(bf16[64,1024]{1,0:T(8,128)(2,1)S(1)} %get-tuple-element.26), channel_id=1, source_target_pairs={{0,12},{2,14},{4,8},{6,10},{8,4},{10,6},{12,0},{14,2},{1,13},{3,15... | collective-permute-start | bytes 393224 | tf_op jit(solution)/shard_map/ppermute | solution.py:226
  34.8 0.8 collective-permute-start.9
  35.5 10.2 %project.5 = (bf16[4,16,1536]{2,1,0:T(8,128)(2,1)S(1)}, f32[4,16,1536]{2,1,0:T(8,128)S(1)}) custom-call(s32[3]{0:T(128)S(1)} %pad_add_fusion.who_ref, bf16[8192,3584]{1,0:T(8,128)(2,1)} %x_hbm.5, s32[64,3584]{1,0:T(8,128)S(1)} %bitcast.20, bf16[64,1024]{1,0:T(8,128)(2,1)S(1)} %get-tuple-element.27.refs_0_, ...), custom_call_target="tpu_custom_call" | custom-call | flops 1409286144 | bytes 22020096 | tf_op jit(solution)/shard_map/project/pallas_call | solution.py:85
  45.7 0.8 collective-permute-start.4
  46.6 2.2 %collective-permute-start.12 = (bf16[64,1024]{1,0:T(8,128)(2,1)S(1)}, bf16[64,1024]{1,0:T(8,128)(2,1)S(1)}, u32[]{:S(2)}, u32[]{:S(2)}) collective-permute-start(bf16[64,1024]{1,0:T(8,128)(2,1)S(1)} %fusion.2.refs_4_), channel_id=1, source_target_pairs={{0,8},{2,10},{4,12},{6,14},{8,0},{10,2},{12,4},{14,6},{1,9},{3,11}... | collective-permute-start | bytes 393224 | tf_op jit(solution)/shard_map/ppermute | solution.py:226
  48.8 2.0 %collective-permute-start.11 = (bf16[64,1024]{1,0:T(8,128)(2,1)S(1)}, bf16[64,1024]{1,0:T(8,128)(2,1)S(1)}, u32[]{:S(2)}, u32[]{:S(2)}) collective-permute-start(bf16[64,1024]{1,0:T(8,128)(2,1)S(1)} %fusion.2.refs_4_), channel_id=1, source_target_pairs={{0,4},{2,6},{4,0},{6,2},{8,12},{10,14},{12,8},{14,10},{1,5},{3,7},... | collective-permute-start | bytes 393224 | tf_op jit(solution)/shard_map/ppermute | solution.py:226
  50.8 1.4 %collective-permute-done.4.refs_3_ = bf16[4,16,1536]{2,1,0:T(8,128)(2,1)S(1)} collective-permute-done((bf16[4,16,1536]{2,1,0:T(8,128)(2,1)S(1)}, bf16[4,16,1536]{2,1,0:T(8,128)(2,1)S(1)}, u32[]{:S(2)}, u32[]{:S(2)}) %collective-permute-start.4) | collective-permute-done | bytes 196640 | tf_op jit(solution)/shard_map/ppermute | solution.py:226
  52.2 0.9 merge.1
  53.1 1.4 %collective-permute-start.5 = (bf16[16,4096]{1,0:T(8,128)(2,1)S(1)}, bf16[16,4096]{1,0:T(8,128)(2,1)S(1)}, u32[]{:S(2)}, u32[]{:S(2)}) collective-permute-start(bf16[16,4096]{1,0:T(8,128)(2,1)S(1)} %get-tuple-element.22), channel_id=1, source_target_pairs={{0,4},{2,6},{4,0},{6,2},{8,12},{10,14},{12,8},{14,10},{1,5},{3,7},... | collective-permute-start | bytes 393224 | tf_op jit(solution)/shard_map/ppermute | solution.py:226
  54.5 2.6 %collective-permute-start.6 = (bf16[16,4096]{1,0:T(8,128)(2,1)S(1)}, bf16[16,4096]{1,0:T(8,128)(2,1)S(1)}, u32[]{:S(2)}, u32[]{:S(2)}) collective-permute-start(bf16[16,4096]{1,0:T(8,128)(2,1)S(1)} %get-tuple-element.23), channel_id=1, source_target_pairs={{0,8},{2,10},{4,12},{6,14},{8,0},{10,2},{12,4},{14,6},{1,9},{3,11}... | collective-permute-start | bytes 393224 | tf_op jit(solution)/shard_map/ppermute | solution.py:226
  57.2 0.4 collective-permute-start.7
  57.5 0.5 collective-permute-start.13
  58.0 5.0 %collective-permute-done.5.refs_1_ = bf16[16,4096]{1,0:T(8,128)(2,1)S(1)} collective-permute-done((bf16[16,4096]{1,0:T(8,128)(2,1)S(1)}, bf16[16,4096]{1,0:T(8,128)(2,1)S(1)}, u32[]{:S(2)}, u32[]{:S(2)}) %collective-permute-start.5) | collective-permute-done | bytes 131104 | tf_op jit(solution)/shard_map/ppermute | solution.py:226
  63.0 3.4 %collective-permute-done.6.refs_2_ = bf16[16,4096]{1,0:T(8,128)(2,1)S(1)} collective-permute-done((bf16[16,4096]{1,0:T(8,128)(2,1)S(1)}, bf16[16,4096]{1,0:T(8,128)(2,1)S(1)}, u32[]{:S(2)}, u32[]{:S(2)}) %collective-permute-start.6) | collective-permute-done | bytes 131104 | tf_op jit(solution)/shard_map/ppermute | solution.py:226
  66.4 0.3 collective-permute-done.13.refs_7_
  66.8 5.2 %score.1 = f32[64,512]{1,0:T(8,128)S(1)} custom-call(s32[3]{0:T(128)S(1)} %pad_add_fusion.who_ref, f32[16,4096]{1,0:T(8,128)S(1)} %get-tuple-element.21.refs_0_, bf16[16,4096]{1,0:T(8,128)(2,1)S(1)} %collective-permute-done.5.refs_1_, bf16[16,4096]{1,0:T(8,128)(2,1)S(1)} %collective-permute-done.6.refs_2_, ...), custom_call_target="tpu_custom_call" | custom-call | flops 536870912 | bytes 262144 | tf_op jit(solution)/shard_map/score/pallas_call | solution.py:196
  72.0 1.2 %collective-permute-start.15 = (f32[64,512]{1,0:T(8,128)S(1)}, f32[64,512]{1,0:T(8,128)S(1)}, u32[]{:S(2)}, u32[]{:S(2)}) collective-permute-start(f32[64,512]{1,0:T(8,128)S(1)} %score.1), channel_id=1, source_target_pairs={{0,2},{2,0},{4,6},{6,4},{8,10},{10,8},{12,14},{14,12},{1,3},{3,1},... | collective-permute-start | bytes 393224 | tf_op jit(solution)/shard_map/ppermute | solution.py:226
  73.2 3.8 %collective-permute-done.15 = f32[64,512]{1,0:T(8,128)S(1)} collective-permute-done((f32[64,512]{1,0:T(8,128)S(1)}, f32[64,512]{1,0:T(8,128)S(1)}, u32[]{:S(2)}, u32[]{:S(2)}) %collective-permute-start.15) | collective-permute-done | bytes 131104 | tf_op jit(solution)/shard_map/ppermute | solution.py:226
  77.0 1.7 %collective-permute-start.16 = (bf16[64,512]{1,0:T(8,128)(2,1)S(1)}, bf16[64,512]{1,0:T(8,128)(2,1)S(1)}, u32[]{:S(2)}, u32[]{:S(2)}) collective-permute-start(bf16[64,512]{1,0:T(8,128)(2,1)S(1)} %add_convert_fusion.3), channel_id=1, source_target_pairs={{0,4},{2,6},{4,0},{6,2},{8,12},{10,14},{12,8},{14,10},{1,5},{3,7},... | collective-permute-start | bytes 196616 | tf_op jit(solution)/shard_map/ppermute | solution.py:226
  78.8 1.8 %collective-permute-start.17 = (bf16[64,512]{1,0:T(8,128)(2,1)S(1)}, bf16[64,512]{1,0:T(8,128)(2,1)S(1)}, u32[]{:S(2)}, u32[]{:S(2)}) collective-permute-start(bf16[64,512]{1,0:T(8,128)(2,1)S(1)} %add_convert_fusion.3), channel_id=1, source_target_pairs={{0,8},{2,10},{4,12},{6,14},{8,0},{10,2},{12,4},{14,6},{1,9},{3,11}... | collective-permute-start | bytes 196616 | tf_op jit(solution)/shard_map/ppermute | solution.py:226
  80.6 0.9 %collective-permute-start.18 = (bf16[64,512]{1,0:T(8,128)(2,1)S(1)}, bf16[64,512]{1,0:T(8,128)(2,1)S(1)}, u32[]{:S(2)}, u32[]{:S(2)}) collective-permute-start(bf16[64,512]{1,0:T(8,128)(2,1)S(1)} %add_convert_fusion.3), channel_id=1, source_target_pairs={{0,12},{2,14},{4,8},{6,10},{8,4},{10,6},{12,0},{14,2},{1,13},{3,15... | collective-permute-start | bytes 196616 | tf_op jit(solution)/shard_map/ppermute | solution.py:226
  81.5 0.2 collective-permute-done.16
  81.7 3.4 %collective-permute-done.17 = bf16[64,512]{1,0:T(8,128)(2,1)S(1)} collective-permute-done((bf16[64,512]{1,0:T(8,128)(2,1)S(1)}, bf16[64,512]{1,0:T(8,128)(2,1)S(1)}, u32[]{:S(2)}, u32[]{:S(2)}) %collective-permute-start.17) | collective-permute-done | bytes 65568 | tf_op jit(solution)/shard_map/ppermute | solution.py:226
  85.0 1.6 %collective-permute-done.18 = bf16[64,512]{1,0:T(8,128)(2,1)S(1)} collective-permute-done((bf16[64,512]{1,0:T(8,128)(2,1)S(1)}, bf16[64,512]{1,0:T(8,128)(2,1)S(1)}, u32[]{:S(2)}, u32[]{:S(2)}) %collective-permute-start.18) | collective-permute-done | bytes 65568 | tf_op jit(solution)/shard_map/ppermute | solution.py:226
  86.6 0.7 add_add_fusion
  (24 shorter events, 0.4 us)
Async XLA Ops:
  0.1 1.0 %copy-start.1 = (s32[1024,64]{0,1:T(8,128)S(1)}, s32[1024,64]{0,1:T(8,128)}, u32[]{:S(2)}) copy-start(s32[1024,64]{0,1:T(8,128)} %param.9) | copy-start | bytes 786436
  9.3 21.7 %collective-permute-start.1 = (bf16[4,64,1024]{2,1,0:T(8,128)(2,1)S(1)}, bf16[4,64,1024]{2,1,0:T(8,128)(2,1)S(1)}, u32[]{:S(2)}, u32[]{:S(2)}) collective-permute-start(bf16[4,64,1024]{2,1,0:T(8,128)(2,1)S(1)} %get-tuple-element.18), channel_id=1, source_target_pairs={{0,2},{2,0},{4,6},{6,4},{8,10},{10,8},{12,14},{14,12},{1,3},{3,1},... | collective-permute-start | bytes 1572872 | tf_op jit(solution)/shard_map/ppermute | solution.py:226
  12.4 18.4 %collective-permute-start.2 = (bf16[256,512]{1,0:T(8,128)(2,1)}, bf16[256,512]{1,0:T(8,128)(2,1)S(1)}, u32[]{:S(2)}, u32[]{:S(2)}) collective-permute-start(bf16[256,512]{1,0:T(8,128)(2,1)} %refs_9_.1), channel_id=1, source_target_pairs={{0,2},{2,0},{4,6},{6,4},{8,10},{10,8},{12,14},{14,12},{1,3},{3,1},... | collective-permute-start | bytes 786440 | tf_op jit(solution)/shard_map/ppermute | solution.py:226
  12.5 22.3 %collective-permute-start.3 = (bf16[256,512]{1,0:T(8,128)(2,1)}, bf16[256,512]{1,0:T(8,128)(2,1)S(1)}, u32[]{:S(2)}, u32[]{:S(2)}) collective-permute-start(bf16[256,512]{1,0:T(8,128)(2,1)} %refs_9_.1), channel_id=1, source_target_pairs={{0,1},{1,0},{2,3},{3,2},{4,5},{5,4},{6,7},{7,6},{8,9},{9,8},{10,11... | collective-permute-start | bytes 786440 | tf_op jit(solution)/shard_map/ppermute | solution.py:229
  12.5 1.2 %copy-start = (s32[3584,64]{0,1:T(8,128)S(1)}, s32[3584,64]{0,1:T(8,128)}, u32[]{:S(2)}) copy-start(s32[3584,64]{0,1:T(8,128)} %param.8) | copy-start | bytes 2752516
  13.6 53.1 %copy-start.2 = (bf16[256,512]{1,0:T(8,128)(2,1)S(1)}, bf16[256,512]{1,0:T(8,128)(2,1)}, u32[]{:S(2)}) copy-start(bf16[256,512]{1,0:T(8,128)(2,1)} %refs_9_.1) | copy-start | bytes 786436
  13.6 53.1 %copy-start.3 = (s32[1,8192]{1,0:T(1,128)S(1)}, s32[1,8192]{1,0:T(1,128)}, u32[]{:S(2)}) copy-start(s32[1,8192]{1,0:T(1,128)} %refs_8_.1) | copy-start | bytes 98308
  28.7 22.1 %collective-permute-start = (bf16[4,16,2560]{2,1,0:T(8,128)(2,1)S(1)}, bf16[4,16,2560]{2,1,0:T(8,128)(2,1)S(1)}, u32[]{:S(2)}, u32[]{:S(2)}) collective-permute-start(bf16[4,16,2560]{2,1,0:T(8,128)(2,1)S(1)} %get-tuple-element.16), channel_id=1, source_target_pairs={{0,2},{2,0},{4,6},{6,4},{8,10},{10,8},{12,14},{14,12},{1,3},{3,1},... | collective-permute-start | bytes 983048 | tf_op jit(solution)/shard_map/ppermute | solution.py:226
  30.8 26.4 %collective-permute-start.14 = (bf16[256,512]{1,0:T(8,128)(2,1)S(1)}, bf16[256,512]{1,0:T(8,128)(2,1)S(1)}, u32[]{:S(2)}, u32[]{:S(2)}) collective-permute-start(bf16[256,512]{1,0:T(8,128)(2,1)S(1)} %collective-permute-done.2.refs_1_.refs_10_), channel_id=1, source_target_pairs={{0,1},{1,0},{2,3},{3,2},{4,5},{5,4},{6,7},{7,6},{8,9},{9,8},{10,11... | collective-permute-start | bytes 786440 | tf_op jit(solution)/shard_map/ppermute | solution.py:229
  31.1 14.7 %collective-permute-start.10 = (bf16[64,1024]{1,0:T(8,128)(2,1)S(1)}, bf16[64,1024]{1,0:T(8,128)(2,1)S(1)}, u32[]{:S(2)}, u32[]{:S(2)}) collective-permute-start(bf16[64,1024]{1,0:T(8,128)(2,1)S(1)} %get-tuple-element.26), channel_id=1, source_target_pairs={{0,12},{2,14},{4,8},{6,10},{8,4},{10,6},{12,0},{14,2},{1,13},{3,15... | collective-permute-start | bytes 393224 | tf_op jit(solution)/shard_map/ppermute | solution.py:226
  34.7 11.8 %collective-permute-start.8 = (bf16[64,1024]{1,0:T(8,128)(2,1)S(1)}, bf16[64,1024]{1,0:T(8,128)(2,1)S(1)}, u32[]{:S(2)}, u32[]{:S(2)}) collective-permute-start(bf16[64,1024]{1,0:T(8,128)(2,1)S(1)} %get-tuple-element.27.refs_0_), channel_id=1, source_target_pairs={{0,4},{2,6},{4,0},{6,2},{8,12},{10,14},{12,8},{14,10},{1,5},{3,7},... | collective-permute-start | bytes 393224 | tf_op jit(solution)/shard_map/ppermute | solution.py:226
  34.8 11.7 %collective-permute-start.9 = (bf16[64,1024]{1,0:T(8,128)(2,1)S(1)}, bf16[64,1024]{1,0:T(8,128)(2,1)S(1)}, u32[]{:S(2)}, u32[]{:S(2)}) collective-permute-start(bf16[64,1024]{1,0:T(8,128)(2,1)S(1)} %get-tuple-element.25), channel_id=1, source_target_pairs={{0,8},{2,10},{4,12},{6,14},{8,0},{10,2},{12,4},{14,6},{1,9},{3,11}... | collective-permute-start | bytes 393224 | tf_op jit(solution)/shard_map/ppermute | solution.py:226
  45.7 6.5 %collective-permute-start.4 = (bf16[4,16,1536]{2,1,0:T(8,128)(2,1)S(1)}, bf16[4,16,1536]{2,1,0:T(8,128)(2,1)S(1)}, u32[]{:S(2)}, u32[]{:S(2)}) collective-permute-start(bf16[4,16,1536]{2,1,0:T(8,128)(2,1)S(1)} %get-tuple-element.20), channel_id=1, source_target_pairs={{0,2},{2,0},{4,6},{6,4},{8,10},{10,8},{12,14},{14,12},{1,3},{3,1},... | collective-permute-start | bytes 589832 | tf_op jit(solution)/shard_map/ppermute | solution.py:226
  46.6 11.0 %collective-permute-start.12 = (bf16[64,1024]{1,0:T(8,128)(2,1)S(1)}, bf16[64,1024]{1,0:T(8,128)(2,1)S(1)}, u32[]{:S(2)}, u32[]{:S(2)}) collective-permute-start(bf16[64,1024]{1,0:T(8,128)(2,1)S(1)} %fusion.2.refs_4_), channel_id=1, source_target_pairs={{0,8},{2,10},{4,12},{6,14},{8,0},{10,2},{12,4},{14,6},{1,9},{3,11}... | collective-permute-start | bytes 393224 | tf_op jit(solution)/shard_map/ppermute | solution.py:226
  48.8 9.2 %collective-permute-start.11 = (bf16[64,1024]{1,0:T(8,128)(2,1)S(1)}, bf16[64,1024]{1,0:T(8,128)(2,1)S(1)}, u32[]{:S(2)}, u32[]{:S(2)}) collective-permute-start(bf16[64,1024]{1,0:T(8,128)(2,1)S(1)} %fusion.2.refs_4_), channel_id=1, source_target_pairs={{0,4},{2,6},{4,0},{6,2},{8,12},{10,14},{12,8},{14,10},{1,5},{3,7},... | collective-permute-start | bytes 393224 | tf_op jit(solution)/shard_map/ppermute | solution.py:226
  53.1 10.0 %collective-permute-start.5 = (bf16[16,4096]{1,0:T(8,128)(2,1)S(1)}, bf16[16,4096]{1,0:T(8,128)(2,1)S(1)}, u32[]{:S(2)}, u32[]{:S(2)}) collective-permute-start(bf16[16,4096]{1,0:T(8,128)(2,1)S(1)} %get-tuple-element.22), channel_id=1, source_target_pairs={{0,4},{2,6},{4,0},{6,2},{8,12},{10,14},{12,8},{14,10},{1,5},{3,7},... | collective-permute-start | bytes 393224 | tf_op jit(solution)/shard_map/ppermute | solution.py:226
  54.5 11.9 %collective-permute-start.6 = (bf16[16,4096]{1,0:T(8,128)(2,1)S(1)}, bf16[16,4096]{1,0:T(8,128)(2,1)S(1)}, u32[]{:S(2)}, u32[]{:S(2)}) collective-permute-start(bf16[16,4096]{1,0:T(8,128)(2,1)S(1)} %get-tuple-element.23), channel_id=1, source_target_pairs={{0,8},{2,10},{4,12},{6,14},{8,0},{10,2},{12,4},{14,6},{1,9},{3,11}... | collective-permute-start | bytes 393224 | tf_op jit(solution)/shard_map/ppermute | solution.py:226
  57.2 9.3 %collective-permute-start.7 = (bf16[16,4096]{1,0:T(8,128)(2,1)S(1)}, bf16[16,4096]{1,0:T(8,128)(2,1)S(1)}, u32[]{:S(2)}, u32[]{:S(2)}) collective-permute-start(bf16[16,4096]{1,0:T(8,128)(2,1)S(1)} %get-tuple-element.24), channel_id=1, source_target_pairs={{0,12},{2,14},{4,8},{6,10},{8,4},{10,6},{12,0},{14,2},{1,13},{3,15... | collective-permute-start | bytes 393224 | tf_op jit(solution)/shard_map/ppermute | solution.py:226
  57.5 9.2 %collective-permute-start.13 = (bf16[64,1024]{1,0:T(8,128)(2,1)S(1)}, bf16[64,1024]{1,0:T(8,128)(2,1)S(1)}, u32[]{:S(2)}, u32[]{:S(2)}) collective-permute-start(bf16[64,1024]{1,0:T(8,128)(2,1)S(1)} %collective-permute-done.12.refs_6_), channel_id=1, source_target_pairs={{0,4},{2,6},{4,0},{6,2},{8,12},{10,14},{12,8},{14,10},{1,5},{3,7},... | collective-permute-start | bytes 393224 | tf_op jit(solution)/shard_map/ppermute | solution.py:226
  72.0 5.0 %collective-permute-start.15 = (f32[64,512]{1,0:T(8,128)S(1)}, f32[64,512]{1,0:T(8,128)S(1)}, u32[]{:S(2)}, u32[]{:S(2)}) collective-permute-start(f32[64,512]{1,0:T(8,128)S(1)} %score.1), channel_id=1, source_target_pairs={{0,2},{2,0},{4,6},{6,4},{8,10},{10,8},{12,14},{14,12},{1,3},{3,1},... | collective-permute-start | bytes 393224 | tf_op jit(solution)/shard_map/ppermute | solution.py:226
  77.0 4.6 %collective-permute-start.16 = (bf16[64,512]{1,0:T(8,128)(2,1)S(1)}, bf16[64,512]{1,0:T(8,128)(2,1)S(1)}, u32[]{:S(2)}, u32[]{:S(2)}) collective-permute-start(bf16[64,512]{1,0:T(8,128)(2,1)S(1)} %add_convert_fusion.3), channel_id=1, source_target_pairs={{0,4},{2,6},{4,0},{6,2},{8,12},{10,14},{12,8},{14,10},{1,5},{3,7},... | collective-permute-start | bytes 196616 | tf_op jit(solution)/shard_map/ppermute | solution.py:226
  78.8 6.3 %collective-permute-start.17 = (bf16[64,512]{1,0:T(8,128)(2,1)S(1)}, bf16[64,512]{1,0:T(8,128)(2,1)S(1)}, u32[]{:S(2)}, u32[]{:S(2)}) collective-permute-start(bf16[64,512]{1,0:T(8,128)(2,1)S(1)} %add_convert_fusion.3), channel_id=1, source_target_pairs={{0,8},{2,10},{4,12},{6,14},{8,0},{10,2},{12,4},{14,6},{1,9},{3,11}... | collective-permute-start | bytes 196616 | tf_op jit(solution)/shard_map/ppermute | solution.py:226
  80.6 6.1 %collective-permute-start.18 = (bf16[64,512]{1,0:T(8,128)(2,1)S(1)}, bf16[64,512]{1,0:T(8,128)(2,1)S(1)}, u32[]{:S(2)}, u32[]{:S(2)}) collective-permute-start(bf16[64,512]{1,0:T(8,128)(2,1)S(1)} %add_convert_fusion.3), channel_id=1, source_target_pairs={{0,12},{2,14},{4,8},{6,10},{8,4},{10,6},{12,0},{14,2},{1,13},{3,15... | collective-permute-start | bytes 196616 | tf_op jit(solution)/shard_map/ppermute | solution.py:226

commit v15 on v14

--- a/solution.py
+++ b/solution.py
@@ -225,6 +225,10 @@
     def swap(array, distance):
         return lax.ppermute(array, "tensor", [(k, k ^ distance) for k in range(n_tensor)])
 
+    def along(arrays):
+        moved = {d: swap(arrays[d], 2 * d) for d in range(quarters - 1, 0, -1)}
+        return [moved[d] for d in range(1, quarters)]
+
     def cross(array):
         return lax.ppermute(array, "dp", [(0, 1), (1, 0)])
 
@@ -240,7 +244,7 @@
     got_0 = swap(sent_0, 1)
     pair_g = [kept_g[d] + got_g[d].astype(jnp.float32) for d in range(quarters)]
     pair_g = [pair_g[0]] + [pair.astype(jnp.bfloat16) for pair in pair_g[1:]]
-    moved_g = [swap(pair_g[d], 2 * d) for d in range(1, quarters)]
+    moved_g = along(pair_g)
     sent_1, kept_1 = project(activations, bits_in, who, scale_in, quarters, True, early, owned - early, 512, [pair_g[1], far, cross_near])
     got_1 = swap(sent_1, 1)
     own_g = sum([moved.astype(jnp.float32) for moved in moved_g], pair_g[0]).astype(jnp.bfloat16)
@@ -251,12 +255,12 @@
         step = step // 2
     right = [pieces[d] for d in range(quarters)]
     pair_a = merge([kept_0, got_0, kept_1, got_1])
-    left = [pair_a[0]] + [swap(pair_a[d], 2 * d) for d in range(1, quarters)]
+    left = [pair_a[0]] + along(pair_a)[::-1]
 
     total = score(who, left, right, segment_ids, every)
     total = (total + swap(total, 1)).astype(jnp.bfloat16)
-    parts = [total] + [swap(total, 2 * d) for d in range(1, quarters)]
-    parts = [part.astype(jnp.float32) for part in parts]
+    parts = [total] + along([total] * quarters)
+    parts = [part.astype(jnp.float32) for part in parts[::-1]]
     while len(parts) > 1:
         parts = [parts[k] + parts[k + 1] for k in range(0, len(parts), 2)]
     return parts[0]

time: 87.5 us -> 87.2 us (level)
  waiting for transfers between devices: 19.2 us -> 18.3 us
    ppermute x17, waiting for transfers between devices: 19.2 us -> 18.2 us  [swap(): lax.ppermute(array, 'tensor', [(k, k ^ distance) for k in range(n_tensor)])]
  transfers between devices with their start and end apart: 19 -> 19, of which waited for: 8 -> 7; matrix products, arithmetic and copies ran while one was open for 0% -> 0% of each run, Pallas kernels for 30% -> 30%
where the time goes in v15:
time: 87.2 us; the launch traced here: 87 us
  Pallas kernels  39.6 us (45%)
  starting transfers between devices  26 us (30%)
  waiting for transfers between devices  18.3 us (21%)
  local copies, waits for them, and re-layouts  2.14 us (2%)
  other arithmetic  0.95 us (1%)
    pallas_call x3, Pallas kernels, project(): pl.pallas_call(functools.partial(project_kernel, scale, order, first, spl...  33.6 us
    ppermute x17, starting transfers between devices, swap(): lax.ppermute(array, 'tensor', [(k, k ^ distance) for k in range(n_tensor)])  25.7 us
    ppermute x17, waiting for transfers between devices, swap(): lax.ppermute(array, 'tensor', [(k, k ^ distance) for k in range(n_tensor)])  18.2 us
    pallas_call x1, Pallas kernels, score(): pl.pallas_call(functools.partial(score_kernel, len(left), min(512, tokens...  5.19 us
    unnamed x8, local copies, waits for them, and re-layouts  2.14 us
  transfers between devices with their start and end apart: 19, of which 7 were waited for; matrix products, arithmetic and copies ran while one was open for 0% of the time, Pallas kernels for 30%

profile of v15, /device:TPU:0, one launch (start us, length us, event | category | flops | bytes accessed | tf_op | source)
XLA Modules:
  0.0 87.0 jit_solution(327913458629186407)
XLA Ops:
  0.1 0.9 %copy-done.1 = s32[1024,64]{0,1:T(8,128)S(1)} copy-done((s32[1024,64]{0,1:T(8,128)S(1)}, s32[1024,64]{0,1:T(8,128)}, u32[]{:S(2)}) %copy-start.1) | copy-done | bytes 262168
  1.0 8.3 %project.4 = (bf16[4,64,1024]{2,1,0:T(8,128)(2,1)S(1)}, f32[4,64,1024]{2,1,0:T(8,128)S(1)}) custom-call(s32[3]{0:T(128)S(1)} %pad_add_fusion.who_ref, bf16[8192,1024]{1,0:T(8,128)(2,1)} %x_hbm.4, s32[64,1024]{1,0:T(8,128)S(1)} %bitcast.21), custom_call_target="tpu_custom_call" | custom-call | flops 1073741824 | bytes 16777216 | tf_op jit(solution)/shard_map/project/pallas_call | solution.py:85
  9.3 3.0 %collective-permute-start.1 = (bf16[4,64,1024]{2,1,0:T(8,128)(2,1)S(1)}, bf16[4,64,1024]{2,1,0:T(8,128)(2,1)S(1)}, u32[]{:S(2)}, u32[]{:S(2)}) collective-permute-start(bf16[4,64,1024]{2,1,0:T(8,128)(2,1)S(1)} %get-tuple-element.18), channel_id=1, source_target_pairs={{0,2},{2,0},{4,6},{6,4},{8,10},{10,8},{12,14},{14,12},{1,3},{3,1},... | collective-permute-start | bytes 1572872 | tf_op jit(solution)/shard_map/ppermute | solution.py:226
  12.4 0.1 collective-permute-start.2
  12.5 1.2 %copy-done = s32[3584,64]{0,1:T(8,128)S(1)} copy-done((s32[3584,64]{0,1:T(8,128)S(1)}, s32[3584,64]{0,1:T(8,128)}, u32[]{:S(2)}) %copy-start) | copy-done | bytes 917528
  13.6 15.1 %project.3 = (bf16[4,16,2560]{2,1,0:T(8,128)(2,1)S(1)}, f32[4,16,2560]{2,1,0:T(8,128)S(1)}) custom-call(s32[3]{0:T(128)S(1)} %pad_add_fusion.who_ref, bf16[8192,3584]{1,0:T(8,128)(2,1)} %x_hbm.5, s32[64,3584]{1,0:T(8,128)S(1)} %bitcast.19), custom_call_target="tpu_custom_call" | custom-call | flops 2348810240 | bytes 36700160 | tf_op jit(solution)/shard_map/project/pallas_call | solution.py:85
  28.7 2.0 %collective-permute-start = (bf16[4,16,2560]{2,1,0:T(8,128)(2,1)S(1)}, bf16[4,16,2560]{2,1,0:T(8,128)(2,1)S(1)}, u32[]{:S(2)}, u32[]{:S(2)}) collective-permute-start(bf16[4,16,2560]{2,1,0:T(8,128)(2,1)S(1)} %get-tuple-element.16), channel_id=1, source_target_pairs={{0,2},{2,0},{4,6},{6,4},{8,10},{10,8},{12,14},{14,12},{1,3},{3,1},... | collective-permute-start | bytes 983048 | tf_op jit(solution)/shard_map/ppermute | solution.py:226
  30.8 0.2 collective-permute-start.14
  31.0 0.1 fusion.4
  31.1 3.7 %collective-permute-start.10 = (bf16[64,1024]{1,0:T(8,128)(2,1)S(1)}, bf16[64,1024]{1,0:T(8,128)(2,1)S(1)}, u32[]{:S(2)}, u32[]{:S(2)}) collective-permute-start(bf16[64,1024]{1,0:T(8,128)(2,1)S(1)} %get-tuple-element.26), channel_id=1, source_target_pairs={{0,12},{2,14},{4,8},{6,10},{8,4},{10,6},{12,0},{14,2},{1,13},{3,15... | collective-permute-start | bytes 393224 | tf_op jit(solution)/shard_map/ppermute | solution.py:226
  34.8 0.8 collective-permute-start.9
  35.5 10.2 %project.5 = (bf16[4,16,1536]{2,1,0:T(8,128)(2,1)S(1)}, f32[4,16,1536]{2,1,0:T(8,128)S(1)}) custom-call(s32[3]{0:T(128)S(1)} %pad_add_fusion.who_ref, bf16[8192,3584]{1,0:T(8,128)(2,1)} %x_hbm.5, s32[64,3584]{1,0:T(8,128)S(1)} %bitcast.20, bf16[64,1024]{1,0:T(8,128)(2,1)S(1)} %get-tuple-element.27.refs_0_, ...), custom_call_target="tpu_custom_call" | custom-call | flops 1409286144 | bytes 22020096 | tf_op jit(solution)/shard_map/project/pallas_call | solution.py:85
  45.7 0.8 collective-permute-start.4
  46.5 0.1 fusion.2.refs_4_
  46.6 2.2 %collective-permute-start.12 = (bf16[64,1024]{1,0:T(8,128)(2,1)S(1)}, bf16[64,1024]{1,0:T(8,128)(2,1)S(1)}, u32[]{:S(2)}, u32[]{:S(2)}) collective-permute-start(bf16[64,1024]{1,0:T(8,128)(2,1)S(1)} %fusion.2.refs_4_), channel_id=1, source_target_pairs={{0,8},{2,10},{4,12},{6,14},{8,0},{10,2},{12,4},{14,6},{1,9},{3,11}... | collective-permute-start | bytes 393224 | tf_op jit(solution)/shard_map/ppermute | solution.py:226
  48.8 2.0 %collective-permute-start.11 = (bf16[64,1024]{1,0:T(8,128)(2,1)S(1)}, bf16[64,1024]{1,0:T(8,128)(2,1)S(1)}, u32[]{:S(2)}, u32[]{:S(2)}) collective-permute-start(bf16[64,1024]{1,0:T(8,128)(2,1)S(1)} %fusion.2.refs_4_), channel_id=1, source_target_pairs={{0,4},{2,6},{4,0},{6,2},{8,12},{10,14},{12,8},{14,10},{1,5},{3,7},... | collective-permute-start | bytes 393224 | tf_op jit(solution)/shard_map/ppermute | solution.py:226
  50.8 1.4 %collective-permute-done.4.refs_3_ = bf16[4,16,1536]{2,1,0:T(8,128)(2,1)S(1)} collective-permute-done((bf16[4,16,1536]{2,1,0:T(8,128)(2,1)S(1)}, bf16[4,16,1536]{2,1,0:T(8,128)(2,1)S(1)}, u32[]{:S(2)}, u32[]{:S(2)}) %collective-permute-start.4) | collective-permute-done | bytes 196640 | tf_op jit(solution)/shard_map/ppermute | solution.py:226
  52.2 0.9 %merge.1 = (f32[16,4096]{1,0:T(8,128)S(1)}, bf16[16,4096]{1,0:T(8,128)(2,1)S(1)}, bf16[16,4096]{1,0:T(8,128)(2,1)S(1)}, bf16[16,4096]{1,0:T(8,128)(2,1)S(1)}) custom-call(f32[4,16,2560]{2,1,0:T(8,128)S(1)} %get-tuple-element.15.refs_0_, bf16[4,16,2560]{2,1,0:T(8,128)(2,1)S(1)} %collective-permute-done.refs_1_, f32[4,16,1536]{2,1,0:T(8,128)S(1)} %get-tuple-element.19.refs_2_, ...), custom_call_target="tpu_custom_call" | custom-call | flops 262144 | bytes 2097152 | tf_op jit(solution)/shard_map/merge/pallas_call | solution.py:129
  53.1 3.5 %collective-permute-start.5 = (bf16[16,4096]{1,0:T(8,128)(2,1)S(1)}, bf16[16,4096]{1,0:T(8,128)(2,1)S(1)}, u32[]{:S(2)}, u32[]{:S(2)}) collective-permute-start(bf16[16,4096]{1,0:T(8,128)(2,1)S(1)} %get-tuple-element.22), channel_id=1, source_target_pairs={{0,12},{2,14},{4,8},{6,10},{8,4},{10,6},{12,0},{14,2},{1,13},{3,15... | collective-permute-start | bytes 393224 | tf_op jit(solution)/shard_map/ppermute | solution.py:226
  56.6 0.9 %collective-permute-start.7 = (bf16[16,4096]{1,0:T(8,128)(2,1)S(1)}, bf16[16,4096]{1,0:T(8,128)(2,1)S(1)}, u32[]{:S(2)}, u32[]{:S(2)}) collective-permute-start(bf16[16,4096]{1,0:T(8,128)(2,1)S(1)} %get-tuple-element.24), channel_id=1, source_target_pairs={{0,4},{2,6},{4,0},{6,2},{8,12},{10,14},{12,8},{14,10},{1,5},{3,7},... | collective-permute-start | bytes 393224 | tf_op jit(solution)/shard_map/ppermute | solution.py:226
  57.5 1.1 %collective-permute-start.13 = (bf16[64,1024]{1,0:T(8,128)(2,1)S(1)}, bf16[64,1024]{1,0:T(8,128)(2,1)S(1)}, u32[]{:S(2)}, u32[]{:S(2)}) collective-permute-start(bf16[64,1024]{1,0:T(8,128)(2,1)S(1)} %collective-permute-done.12.refs_6_), channel_id=1, source_target_pairs={{0,4},{2,6},{4,0},{6,2},{8,12},{10,14},{12,8},{14,10},{1,5},{3,7},... | collective-permute-start | bytes 393224 | tf_op jit(solution)/shard_map/ppermute | solution.py:226
  58.6 2.7 %collective-permute-done.5.refs_1_ = bf16[16,4096]{1,0:T(8,128)(2,1)S(1)} collective-permute-done((bf16[16,4096]{1,0:T(8,128)(2,1)S(1)}, bf16[16,4096]{1,0:T(8,128)(2,1)S(1)}, u32[]{:S(2)}, u32[]{:S(2)}) %collective-permute-start.5) | collective-permute-done | bytes 131104 | tf_op jit(solution)/shard_map/ppermute | solution.py:226
  61.4 5.3 %collective-permute-done.6.refs_2_ = bf16[16,4096]{1,0:T(8,128)(2,1)S(1)} collective-permute-done((bf16[16,4096]{1,0:T(8,128)(2,1)S(1)}, bf16[16,4096]{1,0:T(8,128)(2,1)S(1)}, u32[]{:S(2)}, u32[]{:S(2)}) %collective-permute-start.6) | collective-permute-done | bytes 131104 | tf_op jit(solution)/shard_map/ppermute | solution.py:226
  66.7 0.9 collective-permute-done.13.refs_7_
  67.6 5.2 %score.1 = f32[64,512]{1,0:T(8,128)S(1)} custom-call(s32[3]{0:T(128)S(1)} %pad_add_fusion.who_ref, f32[16,4096]{1,0:T(8,128)S(1)} %get-tuple-element.21.refs_0_, bf16[16,4096]{1,0:T(8,128)(2,1)S(1)} %collective-permute-done.5.refs_1_, bf16[16,4096]{1,0:T(8,128)(2,1)S(1)} %collective-permute-done.6.refs_2_, ...), custom_call_target="tpu_custom_call" | custom-call | flops 536870912 | bytes 262144 | tf_op jit(solution)/shard_map/score/pallas_call | solution.py:196
  72.8 1.2 %collective-permute-start.15 = (f32[64,512]{1,0:T(8,128)S(1)}, f32[64,512]{1,0:T(8,128)S(1)}, u32[]{:S(2)}, u32[]{:S(2)}) collective-permute-start(f32[64,512]{1,0:T(8,128)S(1)} %score.1), channel_id=1, source_target_pairs={{0,2},{2,0},{4,6},{6,4},{8,10},{10,8},{12,14},{14,12},{1,3},{3,1},... | collective-permute-start | bytes 393224 | tf_op jit(solution)/shard_map/ppermute | solution.py:226
  73.9 3.9 %collective-permute-done.15 = f32[64,512]{1,0:T(8,128)S(1)} collective-permute-done((f32[64,512]{1,0:T(8,128)S(1)}, f32[64,512]{1,0:T(8,128)S(1)}, u32[]{:S(2)}, u32[]{:S(2)}) %collective-permute-start.15) | collective-permute-done | bytes 131104 | tf_op jit(solution)/shard_map/ppermute | solution.py:226
  77.8 3.4 %collective-permute-start.16 = (bf16[64,512]{1,0:T(8,128)(2,1)S(1)}, bf16[64,512]{1,0:T(8,128)(2,1)S(1)}, u32[]{:S(2)}, u32[]{:S(2)}) collective-permute-start(bf16[64,512]{1,0:T(8,128)(2,1)S(1)} %add_convert_fusion.3), channel_id=1, source_target_pairs={{0,12},{2,14},{4,8},{6,10},{8,4},{10,6},{12,0},{14,2},{1,13},{3,15... | collective-permute-start | bytes 196616 | tf_op jit(solution)/shard_map/ppermute | solution.py:226
  81.2 1.1 %collective-permute-start.18 = (bf16[64,512]{1,0:T(8,128)(2,1)S(1)}, bf16[64,512]{1,0:T(8,128)(2,1)S(1)}, u32[]{:S(2)}, u32[]{:S(2)}) collective-permute-start(bf16[64,512]{1,0:T(8,128)(2,1)S(1)} %add_convert_fusion.3), channel_id=1, source_target_pairs={{0,4},{2,6},{4,0},{6,2},{8,12},{10,14},{12,8},{14,10},{1,5},{3,7},... | collective-permute-start | bytes 196616 | tf_op jit(solution)/shard_map/ppermute | solution.py:226
  82.3 2.0 %collective-permute-done.16 = bf16[64,512]{1,0:T(8,128)(2,1)S(1)} collective-permute-done((bf16[64,512]{1,0:T(8,128)(2,1)S(1)}, bf16[64,512]{1,0:T(8,128)(2,1)S(1)}, u32[]{:S(2)}, u32[]{:S(2)}) %collective-permute-start.16) | collective-permute-done | bytes 65568 | tf_op jit(solution)/shard_map/ppermute | solution.py:226
  84.2 2.1 %collective-permute-done.17 = bf16[64,512]{1,0:T(8,128)(2,1)S(1)} collective-permute-done((bf16[64,512]{1,0:T(8,128)(2,1)S(1)}, bf16[64,512]{1,0:T(8,128)(2,1)S(1)}, u32[]{:S(2)}, u32[]{:S(2)}) %collective-permute-start.17) | collective-permute-done | bytes 65568 | tf_op jit(solution)/shard_map/ppermute | solution.py:226
  86.3 0.7 add_add_fusion
  (24 shorter events, 0.1 us)
Async XLA Ops:
  0.1 1.0 %copy-start.1 = (s32[1024,64]{0,1:T(8,128)S(1)}, s32[1024,64]{0,1:T(8,128)}, u32[]{:S(2)}) copy-start(s32[1024,64]{0,1:T(8,128)} %param.9) | copy-start | bytes 786436
  9.3 21.7 %collective-permute-start.1 = (bf16[4,64,1024]{2,1,0:T(8,128)(2,1)S(1)}, bf16[4,64,1024]{2,1,0:T(8,128)(2,1)S(1)}, u32[]{:S(2)}, u32[]{:S(2)}) collective-permute-start(bf16[4,64,1024]{2,1,0:T(8,128)(2,1)S(1)} %get-tuple-element.18), channel_id=1, source_target_pairs={{0,2},{2,0},{4,6},{6,4},{8,10},{10,8},{12,14},{14,12},{1,3},{3,1},... | collective-permute-start | bytes 1572872 | tf_op jit(solution)/shard_map/ppermute | solution.py:226
  12.4 18.4 %collective-permute-start.2 = (bf16[256,512]{1,0:T(8,128)(2,1)}, bf16[256,512]{1,0:T(8,128)(2,1)S(1)}, u32[]{:S(2)}, u32[]{:S(2)}) collective-permute-start(bf16[256,512]{1,0:T(8,128)(2,1)} %refs_9_.1), channel_id=1, source_target_pairs={{0,2},{2,0},{4,6},{6,4},{8,10},{10,8},{12,14},{14,12},{1,3},{3,1},... | collective-permute-start | bytes 786440 | tf_op jit(solution)/shard_map/ppermute | solution.py:226
  12.5 22.3 %collective-permute-start.3 = (bf16[256,512]{1,0:T(8,128)(2,1)}, bf16[256,512]{1,0:T(8,128)(2,1)S(1)}, u32[]{:S(2)}, u32[]{:S(2)}) collective-permute-start(bf16[256,512]{1,0:T(8,128)(2,1)} %refs_9_.1), channel_id=1, source_target_pairs={{0,1},{1,0},{2,3},{3,2},{4,5},{5,4},{6,7},{7,6},{8,9},{9,8},{10,11... | collective-permute-start | bytes 786440 | tf_op jit(solution)/shard_map/ppermute | solution.py:233
  12.5 1.2 %copy-start = (s32[3584,64]{0,1:T(8,128)S(1)}, s32[3584,64]{0,1:T(8,128)}, u32[]{:S(2)}) copy-start(s32[3584,64]{0,1:T(8,128)} %param.8) | copy-start | bytes 2752516
  13.6 53.9 %copy-start.2 = (bf16[256,512]{1,0:T(8,128)(2,1)S(1)}, bf16[256,512]{1,0:T(8,128)(2,1)}, u32[]{:S(2)}) copy-start(bf16[256,512]{1,0:T(8,128)(2,1)} %refs_9_.1) | copy-start | bytes 786436
  13.6 53.9 %copy-start.3 = (s32[1,8192]{1,0:T(1,128)S(1)}, s32[1,8192]{1,0:T(1,128)}, u32[]{:S(2)}) copy-start(s32[1,8192]{1,0:T(1,128)} %refs_8_.1) | copy-start | bytes 98308
  28.7 22.1 %collective-permute-start = (bf16[4,16,2560]{2,1,0:T(8,128)(2,1)S(1)}, bf16[4,16,2560]{2,1,0:T(8,128)(2,1)S(1)}, u32[]{:S(2)}, u32[]{:S(2)}) collective-permute-start(bf16[4,16,2560]{2,1,0:T(8,128)(2,1)S(1)} %get-tuple-element.16), channel_id=1, source_target_pairs={{0,2},{2,0},{4,6},{6,4},{8,10},{10,8},{12,14},{14,12},{1,3},{3,1},... | collective-permute-start | bytes 983048 | tf_op jit(solution)/shard_map/ppermute | solution.py:226
  30.8 25.9 %collective-permute-start.14 = (bf16[256,512]{1,0:T(8,128)(2,1)S(1)}, bf16[256,512]{1,0:T(8,128)(2,1)S(1)}, u32[]{:S(2)}, u32[]{:S(2)}) collective-permute-start(bf16[256,512]{1,0:T(8,128)(2,1)S(1)} %collective-permute-done.2.refs_1_.refs_10_), channel_id=1, source_target_pairs={{0,1},{1,0},{2,3},{3,2},{4,5},{5,4},{6,7},{7,6},{8,9},{9,8},{10,11... | collective-permute-start | bytes 786440 | tf_op jit(solution)/shard_map/ppermute | solution.py:233
  31.1 14.7 %collective-permute-start.10 = (bf16[64,1024]{1,0:T(8,128)(2,1)S(1)}, bf16[64,1024]{1,0:T(8,128)(2,1)S(1)}, u32[]{:S(2)}, u32[]{:S(2)}) collective-permute-start(bf16[64,1024]{1,0:T(8,128)(2,1)S(1)} %get-tuple-element.26), channel_id=1, source_target_pairs={{0,12},{2,14},{4,8},{6,10},{8,4},{10,6},{12,0},{14,2},{1,13},{3,15... | collective-permute-start | bytes 393224 | tf_op jit(solution)/shard_map/ppermute | solution.py:226
  34.7 11.8 %collective-permute-start.8 = (bf16[64,1024]{1,0:T(8,128)(2,1)S(1)}, bf16[64,1024]{1,0:T(8,128)(2,1)S(1)}, u32[]{:S(2)}, u32[]{:S(2)}) collective-permute-start(bf16[64,1024]{1,0:T(8,128)(2,1)S(1)} %get-tuple-element.27.refs_0_), channel_id=1, source_target_pairs={{0,4},{2,6},{4,0},{6,2},{8,12},{10,14},{12,8},{14,10},{1,5},{3,7},... | collective-permute-start | bytes 393224 | tf_op jit(solution)/shard_map/ppermute | solution.py:226
  34.8 11.7 %collective-permute-start.9 = (bf16[64,1024]{1,0:T(8,128)(2,1)S(1)}, bf16[64,1024]{1,0:T(8,128)(2,1)S(1)}, u32[]{:S(2)}, u32[]{:S(2)}) collective-permute-start(bf16[64,1024]{1,0:T(8,128)(2,1)S(1)} %get-tuple-element.25), channel_id=1, source_target_pairs={{0,8},{2,10},{4,12},{6,14},{8,0},{10,2},{12,4},{14,6},{1,9},{3,11}... | collective-permute-start | bytes 393224 | tf_op jit(solution)/shard_map/ppermute | solution.py:226
  45.7 6.5 %collective-permute-start.4 = (bf16[4,16,1536]{2,1,0:T(8,128)(2,1)S(1)}, bf16[4,16,1536]{2,1,0:T(8,128)(2,1)S(1)}, u32[]{:S(2)}, u32[]{:S(2)}) collective-permute-start(bf16[4,16,1536]{2,1,0:T(8,128)(2,1)S(1)} %get-tuple-element.20), channel_id=1, source_target_pairs={{0,2},{2,0},{4,6},{6,4},{8,10},{10,8},{12,14},{14,12},{1,3},{3,1},... | collective-permute-start | bytes 589832 | tf_op jit(solution)/shard_map/ppermute | solution.py:226
  46.6 11.0 %collective-permute-start.12 = (bf16[64,1024]{1,0:T(8,128)(2,1)S(1)}, bf16[64,1024]{1,0:T(8,128)(2,1)S(1)}, u32[]{:S(2)}, u32[]{:S(2)}) collective-permute-start(bf16[64,1024]{1,0:T(8,128)(2,1)S(1)} %fusion.2.refs_4_), channel_id=1, source_target_pairs={{0,8},{2,10},{4,12},{6,14},{8,0},{10,2},{12,4},{14,6},{1,9},{3,11}... | collective-permute-start | bytes 393224 | tf_op jit(solution)/shard_map/ppermute | solution.py:226
  48.8 9.9 %collective-permute-start.11 = (bf16[64,1024]{1,0:T(8,128)(2,1)S(1)}, bf16[64,1024]{1,0:T(8,128)(2,1)S(1)}, u32[]{:S(2)}, u32[]{:S(2)}) collective-permute-start(bf16[64,1024]{1,0:T(8,128)(2,1)S(1)} %fusion.2.refs_4_), channel_id=1, source_target_pairs={{0,4},{2,6},{4,0},{6,2},{8,12},{10,14},{12,8},{14,10},{1,5},{3,7},... | collective-permute-start | bytes 393224 | tf_op jit(solution)/shard_map/ppermute | solution.py:226
  53.1 8.3 %collective-permute-start.5 = (bf16[16,4096]{1,0:T(8,128)(2,1)S(1)}, bf16[16,4096]{1,0:T(8,128)(2,1)S(1)}, u32[]{:S(2)}, u32[]{:S(2)}) collective-permute-start(bf16[16,4096]{1,0:T(8,128)(2,1)S(1)} %get-tuple-element.22), channel_id=1, source_target_pairs={{0,12},{2,14},{4,8},{6,10},{8,4},{10,6},{12,0},{14,2},{1,13},{3,15... | collective-permute-start | bytes 393224 | tf_op jit(solution)/shard_map/ppermute | solution.py:226
  56.6 10.1 %collective-permute-start.6 = (bf16[16,4096]{1,0:T(8,128)(2,1)S(1)}, bf16[16,4096]{1,0:T(8,128)(2,1)S(1)}, u32[]{:S(2)}, u32[]{:S(2)}) collective-permute-start(bf16[16,4096]{1,0:T(8,128)(2,1)S(1)} %get-tuple-element.23), channel_id=1, source_target_pairs={{0,8},{2,10},{4,12},{6,14},{8,0},{10,2},{12,4},{14,6},{1,9},{3,11}... | collective-permute-start | bytes 393224 | tf_op jit(solution)/shard_map/ppermute | solution.py:226
  56.6 10.1 %collective-permute-start.7 = (bf16[16,4096]{1,0:T(8,128)(2,1)S(1)}, bf16[16,4096]{1,0:T(8,128)(2,1)S(1)}, u32[]{:S(2)}, u32[]{:S(2)}) collective-permute-start(bf16[16,4096]{1,0:T(8,128)(2,1)S(1)} %get-tuple-element.24), channel_id=1, source_target_pairs={{0,4},{2,6},{4,0},{6,2},{8,12},{10,14},{12,8},{14,10},{1,5},{3,7},... | collective-permute-start | bytes 393224 | tf_op jit(solution)/shard_map/ppermute | solution.py:226
  57.5 10.0 %collective-permute-start.13 = (bf16[64,1024]{1,0:T(8,128)(2,1)S(1)}, bf16[64,1024]{1,0:T(8,128)(2,1)S(1)}, u32[]{:S(2)}, u32[]{:S(2)}) collective-permute-start(bf16[64,1024]{1,0:T(8,128)(2,1)S(1)} %collective-permute-done.12.refs_6_), channel_id=1, source_target_pairs={{0,4},{2,6},{4,0},{6,2},{8,12},{10,14},{12,8},{14,10},{1,5},{3,7},... | collective-permute-start | bytes 393224 | tf_op jit(solution)/shard_map/ppermute | solution.py:226
  72.8 5.0 %collective-permute-start.15 = (f32[64,512]{1,0:T(8,128)S(1)}, f32[64,512]{1,0:T(8,128)S(1)}, u32[]{:S(2)}, u32[]{:S(2)}) collective-permute-start(f32[64,512]{1,0:T(8,128)S(1)} %score.1), channel_id=1, source_target_pairs={{0,2},{2,0},{4,6},{6,4},{8,10},{10,8},{12,14},{14,12},{1,3},{3,1},... | collective-permute-start | bytes 393224 | tf_op jit(solution)/shard_map/ppermute | solution.py:226
  77.8 6.4 %collective-permute-start.16 = (bf16[64,512]{1,0:T(8,128)(2,1)S(1)}, bf16[64,512]{1,0:T(8,128)(2,1)S(1)}, u32[]{:S(2)}, u32[]{:S(2)}) collective-permute-start(bf16[64,512]{1,0:T(8,128)(2,1)S(1)} %add_convert_fusion.3), channel_id=1, source_target_pairs={{0,12},{2,14},{4,8},{6,10},{8,4},{10,6},{12,0},{14,2},{1,13},{3,15... | collective-permute-start | bytes 196616 | tf_op jit(solution)/shard_map/ppermute | solution.py:226
  81.2 5.2 %collective-permute-start.17 = (bf16[64,512]{1,0:T(8,128)(2,1)S(1)}, bf16[64,512]{1,0:T(8,128)(2,1)S(1)}, u32[]{:S(2)}, u32[]{:S(2)}) collective-permute-start(bf16[64,512]{1,0:T(8,128)(2,1)S(1)} %add_convert_fusion.3), channel_id=1, source_target_pairs={{0,8},{2,10},{4,12},{6,14},{8,0},{10,2},{12,4},{14,6},{1,9},{3,11}... | collective-permute-start | bytes 196616 | tf_op jit(solution)/shard_map/ppermute | solution.py:226
  81.2 5.2 %collective-permute-start.18 = (bf16[64,512]{1,0:T(8,128)(2,1)S(1)}, bf16[64,512]{1,0:T(8,128)(2,1)S(1)}, u32[]{:S(2)}, u32[]{:S(2)}) collective-permute-start(bf16[64,512]{1,0:T(8,128)(2,1)S(1)} %add_convert_fusion.3), channel_id=1, source_target_pairs={{0,4},{2,6},{4,0},{6,2},{8,12},{10,14},{12,8},{14,10},{1,5},{3,7},... | collective-permute-start | bytes 196616 | tf_op jit(solution)/shard_map/ppermute | solution.py:226

commit v16 on v15

--- a/solution.py
+++ b/solution.py
@@ -160,17 +160,29 @@
     owned = col_ref.shape[1]
     ids = ids_ref[:, pl.ds(pl.multiple_of(half * owned, 128), owned)]
     member_ref[...] = (ids == numbers).astype(jnp.bfloat16)
-    rows = spread_refs[0].shape[0] // R
-    for g in range(row_ref.shape[0] // rows):
-        spread_ref = spread_refs[g % 2]
-        for at in range(0, owned, width):
-            right = col_ref[:, at:at + width]
-            for r in range(rows):
-                row = row_ref[g * rows + r:g * rows + r + 1, at:at + width]
-                spread_ref[r * R:(r + 1) * R, at:at + width] = (row * right).astype(jnp.bfloat16)
-        sketch_ref[:, g * rows * R:(g + 1) * rows * R] = lax.dot_general(
-            member_ref[...], spread_ref[...], LAST, preferred_element_type=jnp.float32
-        )
+    columns = row_ref.shape[0]
+    blocks = owned // width
+    sketch_ref[...] = jnp.zeros(sketch_ref.shape, jnp.float32)
+
+    def fill(spread_ref, block):
+        here = pl.ds(pl.multiple_of(block * width, width), width)
+        right = col_ref[:, here]
+        for r in range(columns):
+            spread_ref[r * R:(r + 1) * R, :] = (row_ref[r:r + 1, here] * right).astype(jnp.bfloat16)
+
+    def add(spread_ref, block):
+        here = pl.ds(pl.multiple_of(block * width, width), width)
+        sketch_ref[...] += lax.dot_general(member_ref[:, here], spread_ref[...], LAST, preferred_element_type=jnp.float32)
+
+    def two(k, carry):
+        fill(spread_refs[1], 2 * k + 1)
+        add(spread_refs[0], 2 * k)
+        fill(spread_refs[0], jnp.minimum(2 * k + 2, blocks - 1))
+        add(spread_refs[1], 2 * k + 1)
+        return carry
+
+    fill(spread_refs[0], 0)
+    lax.fori_loop(0, blocks // 2, two, 0)
     entries = sketch_ref[...]
     high = entries.astype(jnp.bfloat16)
     low = (entries - high.astype(jnp.float32)).astype(jnp.bfloat16)
@@ -191,10 +203,10 @@
 def score(who, left, right, ids, queries):
     operands = left + right + [ids] + queries
     columns, tokens = left[0].shape
-    rows = min(4, columns)
+    width = min(512, tokens // 2)
     shape = (SEQ_DEV, 2 * queries[0].shape[0])
     return pl.pallas_call(
-        functools.partial(score_kernel, len(left), min(512, tokens)),
+        functools.partial(score_kernel, len(left), width),
         in_specs=[pl.BlockSpec(memory_space=pltpu.SMEM)] + [pl.BlockSpec(memory_space=pl.ANY)] * len(operands),
         out_specs=pl.BlockSpec(memory_space=pltpu.VMEM),
         out_shape=jax.ShapeDtypeStruct(shape, jnp.float32),
@@ -205,8 +217,8 @@
             pltpu.VMEM((R, tokens), jnp.float32),
             pltpu.VMEM((SEQ_DEV, tokens), jnp.bfloat16),
             pltpu.VMEM((SEQ_DEV, columns * R), jnp.float32),
-            pltpu.VMEM((rows * R, tokens), jnp.bfloat16),
-            pltpu.VMEM((rows * R, tokens), jnp.bfloat16),
+            pltpu.VMEM((columns * R, width), jnp.bfloat16),
+            pltpu.VMEM((columns * R, width), jnp.bfloat16),
         ],
         compiler_params=pltpu.CompilerParams(vmem_limit_bytes=VMEM // 3),
         cost_estimate=pl.CostEstimate(flops=2 * tokens * columns * R * SEQ_DEV, bytes_accessed=4 * columns * tokens, transcendentals=0),

time: 87.2 us -> 88.2 us (1.011)
  Pallas kernels: 39.6 us -> 40.6 us
    pallas_call x1, Pallas kernels: 5.19 us -> 6.14 us  [score(): pl.pallas_call(functools.partial(score_kernel, len(left), width), in_spec...]
where the time goes in v16:
time: 88.2 us; the launch traced here: 88 us
  Pallas kernels  40.6 us (46%)
  starting transfers between devices  26 us (29%)
  waiting for transfers between devices  18.3 us (21%)
  local copies, waits for them, and re-layouts  2.14 us (2%)
  other arithmetic  0.95 us (1%)
    pallas_call x3, Pallas kernels, project(): pl.pallas_call(functools.partial(project_kernel, scale, order, first, spl...  33.6 us
    ppermute x17, starting transfers between devices, swap(): lax.ppermute(array, 'tensor', [(k, k ^ distance) for k in range(n_tensor)])  25.7 us
    ppermute x17, waiting for transfers between devices, swap(): lax.ppermute(array, 'tensor', [(k, k ^ distance) for k in range(n_tensor)])  18.3 us
    pallas_call x1, Pallas kernels, score(): pl.pallas_call(functools.partial(score_kernel, len(left), width), in_spec...  6.14 us
    unnamed x8, local copies, waits for them, and re-layouts  2.14 us
  transfers between devices with their start and end apart: 19, of which 7 were waited for; matrix products, arithmetic and copies ran while one was open for 0% of the time, Pallas kernels for 30%

profile of v16, /device:TPU:0, one launch (start us, length us, event | category | flops | bytes accessed | tf_op | source)
XLA Modules:
  0.0 88.0 jit_solution(3022922991206281617)
XLA Ops:
  0.1 0.9 %copy-done.1 = s32[1024,64]{0,1:T(8,128)S(1)} copy-done((s32[1024,64]{0,1:T(8,128)S(1)}, s32[1024,64]{0,1:T(8,128)}, u32[]{:S(2)}) %copy-start.1) | copy-done | bytes 262168
  1.0 8.3 %project.4 = (bf16[4,64,1024]{2,1,0:T(8,128)(2,1)S(1)}, f32[4,64,1024]{2,1,0:T(8,128)S(1)}) custom-call(s32[3]{0:T(128)S(1)} %pad_add_fusion.who_ref, bf16[8192,1024]{1,0:T(8,128)(2,1)} %x_hbm.4, s32[64,1024]{1,0:T(8,128)S(1)} %bitcast.21), custom_call_target="tpu_custom_call" | custom-call | flops 1073741824 | bytes 16777216 | tf_op jit(solution)/shard_map/project/pallas_call | solution.py:85
  9.3 3.0 %collective-permute-start.1 = (bf16[4,64,1024]{2,1,0:T(8,128)(2,1)S(1)}, bf16[4,64,1024]{2,1,0:T(8,128)(2,1)S(1)}, u32[]{:S(2)}, u32[]{:S(2)}) collective-permute-start(bf16[4,64,1024]{2,1,0:T(8,128)(2,1)S(1)} %get-tuple-element.18), channel_id=1, source_target_pairs={{0,2},{2,0},{4,6},{6,4},{8,10},{10,8},{12,14},{14,12},{1,3},{3,1},... | collective-permute-start | bytes 1572872 | tf_op jit(solution)/shard_map/ppermute | solution.py:238
  12.4 0.1 collective-permute-start.2
  12.5 1.2 %copy-done = s32[3584,64]{0,1:T(8,128)S(1)} copy-done((s32[3584,64]{0,1:T(8,128)S(1)}, s32[3584,64]{0,1:T(8,128)}, u32[]{:S(2)}) %copy-start) | copy-done | bytes 917528
  13.6 15.1 %project.3 = (bf16[4,16,2560]{2,1,0:T(8,128)(2,1)S(1)}, f32[4,16,2560]{2,1,0:T(8,128)S(1)}) custom-call(s32[3]{0:T(128)S(1)} %pad_add_fusion.who_ref, bf16[8192,3584]{1,0:T(8,128)(2,1)} %x_hbm.5, s32[64,3584]{1,0:T(8,128)S(1)} %bitcast.19), custom_call_target="tpu_custom_call" | custom-call | flops 2348810240 | bytes 36700160 | tf_op jit(solution)/shard_map/project/pallas_call | solution.py:85
  28.7 2.0 %collective-permute-start = (bf16[4,16,2560]{2,1,0:T(8,128)(2,1)S(1)}, bf16[4,16,2560]{2,1,0:T(8,128)(2,1)S(1)}, u32[]{:S(2)}, u32[]{:S(2)}) collective-permute-start(bf16[4,16,2560]{2,1,0:T(8,128)(2,1)S(1)} %get-tuple-element.16), channel_id=1, source_target_pairs={{0,2},{2,0},{4,6},{6,4},{8,10},{10,8},{12,14},{14,12},{1,3},{3,1},... | collective-permute-start | bytes 983048 | tf_op jit(solution)/shard_map/ppermute | solution.py:238
  30.8 0.2 collective-permute-start.14
  31.0 0.1 fusion.4
  31.1 3.7 %collective-permute-start.10 = (bf16[64,1024]{1,0:T(8,128)(2,1)S(1)}, bf16[64,1024]{1,0:T(8,128)(2,1)S(1)}, u32[]{:S(2)}, u32[]{:S(2)}) collective-permute-start(bf16[64,1024]{1,0:T(8,128)(2,1)S(1)} %get-tuple-element.26), channel_id=1, source_target_pairs={{0,12},{2,14},{4,8},{6,10},{8,4},{10,6},{12,0},{14,2},{1,13},{3,15... | collective-permute-start | bytes 393224 | tf_op jit(solution)/shard_map/ppermute | solution.py:238
  34.8 0.8 collective-permute-start.9
  35.5 10.2 %project.5 = (bf16[4,16,1536]{2,1,0:T(8,128)(2,1)S(1)}, f32[4,16,1536]{2,1,0:T(8,128)S(1)}) custom-call(s32[3]{0:T(128)S(1)} %pad_add_fusion.who_ref, bf16[8192,3584]{1,0:T(8,128)(2,1)} %x_hbm.5, s32[64,3584]{1,0:T(8,128)S(1)} %bitcast.20, bf16[64,1024]{1,0:T(8,128)(2,1)S(1)} %get-tuple-element.27.refs_0_, ...), custom_call_target="tpu_custom_call" | custom-call | flops 1409286144 | bytes 22020096 | tf_op jit(solution)/shard_map/project/pallas_call | solution.py:85
  45.7 0.8 collective-permute-start.4
  46.5 0.1 fusion.2.refs_4_
  46.6 2.2 %collective-permute-start.12 = (bf16[64,1024]{1,0:T(8,128)(2,1)S(1)}, bf16[64,1024]{1,0:T(8,128)(2,1)S(1)}, u32[]{:S(2)}, u32[]{:S(2)}) collective-permute-start(bf16[64,1024]{1,0:T(8,128)(2,1)S(1)} %fusion.2.refs_4_), channel_id=1, source_target_pairs={{0,8},{2,10},{4,12},{6,14},{8,0},{10,2},{12,4},{14,6},{1,9},{3,11}... | collective-permute-start | bytes 393224 | tf_op jit(solution)/shard_map/ppermute | solution.py:238
  48.8 2.0 %collective-permute-start.11 = (bf16[64,1024]{1,0:T(8,128)(2,1)S(1)}, bf16[64,1024]{1,0:T(8,128)(2,1)S(1)}, u32[]{:S(2)}, u32[]{:S(2)}) collective-permute-start(bf16[64,1024]{1,0:T(8,128)(2,1)S(1)} %fusion.2.refs_4_), channel_id=1, source_target_pairs={{0,4},{2,6},{4,0},{6,2},{8,12},{10,14},{12,8},{14,10},{1,5},{3,7},... | collective-permute-start | bytes 393224 | tf_op jit(solution)/shard_map/ppermute | solution.py:238
  50.8 1.4 %collective-permute-done.4.refs_3_ = bf16[4,16,1536]{2,1,0:T(8,128)(2,1)S(1)} collective-permute-done((bf16[4,16,1536]{2,1,0:T(8,128)(2,1)S(1)}, bf16[4,16,1536]{2,1,0:T(8,128)(2,1)S(1)}, u32[]{:S(2)}, u32[]{:S(2)}) %collective-permute-start.4) | collective-permute-done | bytes 196640 | tf_op jit(solution)/shard_map/ppermute | solution.py:238
  52.2 0.9 merge.1
  53.1 3.5 %collective-permute-start.5 = (bf16[16,4096]{1,0:T(8,128)(2,1)S(1)}, bf16[16,4096]{1,0:T(8,128)(2,1)S(1)}, u32[]{:S(2)}, u32[]{:S(2)}) collective-permute-start(bf16[16,4096]{1,0:T(8,128)(2,1)S(1)} %get-tuple-element.22), channel_id=1, source_target_pairs={{0,12},{2,14},{4,8},{6,10},{8,4},{10,6},{12,0},{14,2},{1,13},{3,15... | collective-permute-start | bytes 393224 | tf_op jit(solution)/shard_map/ppermute | solution.py:238
  56.6 0.9 %collective-permute-start.7 = (bf16[16,4096]{1,0:T(8,128)(2,1)S(1)}, bf16[16,4096]{1,0:T(8,128)(2,1)S(1)}, u32[]{:S(2)}, u32[]{:S(2)}) collective-permute-start(bf16[16,4096]{1,0:T(8,128)(2,1)S(1)} %get-tuple-element.24), channel_id=1, source_target_pairs={{0,4},{2,6},{4,0},{6,2},{8,12},{10,14},{12,8},{14,10},{1,5},{3,7},... | collective-permute-start | bytes 393224 | tf_op jit(solution)/shard_map/ppermute | solution.py:238
  57.5 1.1 %collective-permute-start.13 = (bf16[64,1024]{1,0:T(8,128)(2,1)S(1)}, bf16[64,1024]{1,0:T(8,128)(2,1)S(1)}, u32[]{:S(2)}, u32[]{:S(2)}) collective-permute-start(bf16[64,1024]{1,0:T(8,128)(2,1)S(1)} %collective-permute-done.12.refs_6_), channel_id=1, source_target_pairs={{0,4},{2,6},{4,0},{6,2},{8,12},{10,14},{12,8},{14,10},{1,5},{3,7},... | collective-permute-start | bytes 393224 | tf_op jit(solution)/shard_map/ppermute | solution.py:238
  58.6 2.7 %collective-permute-done.5.refs_1_ = bf16[16,4096]{1,0:T(8,128)(2,1)S(1)} collective-permute-done((bf16[16,4096]{1,0:T(8,128)(2,1)S(1)}, bf16[16,4096]{1,0:T(8,128)(2,1)S(1)}, u32[]{:S(2)}, u32[]{:S(2)}) %collective-permute-start.5) | collective-permute-done | bytes 131104 | tf_op jit(solution)/shard_map/ppermute | solution.py:238
  61.4 5.3 %collective-permute-done.6.refs_2_ = bf16[16,4096]{1,0:T(8,128)(2,1)S(1)} collective-permute-done((bf16[16,4096]{1,0:T(8,128)(2,1)S(1)}, bf16[16,4096]{1,0:T(8,128)(2,1)S(1)}, u32[]{:S(2)}, u32[]{:S(2)}) %collective-permute-start.6) | collective-permute-done | bytes 131104 | tf_op jit(solution)/shard_map/ppermute | solution.py:238
  66.7 0.9 collective-permute-done.13.refs_7_
  67.6 6.1 %score.1 = f32[64,512]{1,0:T(8,128)S(1)} custom-call(s32[3]{0:T(128)S(1)} %pad_add_fusion.who_ref, f32[16,4096]{1,0:T(8,128)S(1)} %get-tuple-element.21.refs_0_, bf16[16,4096]{1,0:T(8,128)(2,1)S(1)} %collective-permute-done.5.refs_1_, bf16[16,4096]{1,0:T(8,128)(2,1)S(1)} %collective-permute-done.6.refs_2_, ...), custom_call_target="tpu_custom_call" | custom-call | flops 536870912 | bytes 262144 | tf_op jit(solution)/shard_map/score/pallas_call | solution.py:208
  73.7 1.2 %collective-permute-start.15 = (f32[64,512]{1,0:T(8,128)S(1)}, f32[64,512]{1,0:T(8,128)S(1)}, u32[]{:S(2)}, u32[]{:S(2)}) collective-permute-start(f32[64,512]{1,0:T(8,128)S(1)} %score.1), channel_id=1, source_target_pairs={{0,2},{2,0},{4,6},{6,4},{8,10},{10,8},{12,14},{14,12},{1,3},{3,1},... | collective-permute-start | bytes 393224 | tf_op jit(solution)/shard_map/ppermute | solution.py:238
  74.9 3.9 %collective-permute-done.15 = f32[64,512]{1,0:T(8,128)S(1)} collective-permute-done((f32[64,512]{1,0:T(8,128)S(1)}, f32[64,512]{1,0:T(8,128)S(1)}, u32[]{:S(2)}, u32[]{:S(2)}) %collective-permute-start.15) | collective-permute-done | bytes 131104 | tf_op jit(solution)/shard_map/ppermute | solution.py:238
  78.8 3.4 %collective-permute-start.16 = (bf16[64,512]{1,0:T(8,128)(2,1)S(1)}, bf16[64,512]{1,0:T(8,128)(2,1)S(1)}, u32[]{:S(2)}, u32[]{:S(2)}) collective-permute-start(bf16[64,512]{1,0:T(8,128)(2,1)S(1)} %add_convert_fusion.3), channel_id=1, source_target_pairs={{0,12},{2,14},{4,8},{6,10},{8,4},{10,6},{12,0},{14,2},{1,13},{3,15... | collective-permute-start | bytes 196616 | tf_op jit(solution)/shard_map/ppermute | solution.py:238
  82.1 1.1 %collective-permute-start.18 = (bf16[64,512]{1,0:T(8,128)(2,1)S(1)}, bf16[64,512]{1,0:T(8,128)(2,1)S(1)}, u32[]{:S(2)}, u32[]{:S(2)}) collective-permute-start(bf16[64,512]{1,0:T(8,128)(2,1)S(1)} %add_convert_fusion.3), channel_id=1, source_target_pairs={{0,4},{2,6},{4,0},{6,2},{8,12},{10,14},{12,8},{14,10},{1,5},{3,7},... | collective-permute-start | bytes 196616 | tf_op jit(solution)/shard_map/ppermute | solution.py:238
  83.2 2.0 %collective-permute-done.16 = bf16[64,512]{1,0:T(8,128)(2,1)S(1)} collective-permute-done((bf16[64,512]{1,0:T(8,128)(2,1)S(1)}, bf16[64,512]{1,0:T(8,128)(2,1)S(1)}, u32[]{:S(2)}, u32[]{:S(2)}) %collective-permute-start.16) | collective-permute-done | bytes 65568 | tf_op jit(solution)/shard_map/ppermute | solution.py:238
  85.2 2.1 %collective-permute-done.17 = bf16[64,512]{1,0:T(8,128)(2,1)S(1)} collective-permute-done((bf16[64,512]{1,0:T(8,128)(2,1)S(1)}, bf16[64,512]{1,0:T(8,128)(2,1)S(1)}, u32[]{:S(2)}, u32[]{:S(2)}) %collective-permute-start.17) | collective-permute-done | bytes 65568 | tf_op jit(solution)/shard_map/ppermute | solution.py:238
  87.3 0.7 add_add_fusion
  (24 shorter events, 0.1 us)
Async XLA Ops:
  0.1 1.0 %copy-start.1 = (s32[1024,64]{0,1:T(8,128)S(1)}, s32[1024,64]{0,1:T(8,128)}, u32[]{:S(2)}) copy-start(s32[1024,64]{0,1:T(8,128)} %param.9) | copy-start | bytes 786436
  9.3 21.7 %collective-permute-start.1 = (bf16[4,64,1024]{2,1,0:T(8,128)(2,1)S(1)}, bf16[4,64,1024]{2,1,0:T(8,128)(2,1)S(1)}, u32[]{:S(2)}, u32[]{:S(2)}) collective-permute-start(bf16[4,64,1024]{2,1,0:T(8,128)(2,1)S(1)} %get-tuple-element.18), channel_id=1, source_target_pairs={{0,2},{2,0},{4,6},{6,4},{8,10},{10,8},{12,14},{14,12},{1,3},{3,1},... | collective-permute-start | bytes 1572872 | tf_op jit(solution)/shard_map/ppermute | solution.py:238
  12.4 18.4 %collective-permute-start.2 = (bf16[256,512]{1,0:T(8,128)(2,1)}, bf16[256,512]{1,0:T(8,128)(2,1)S(1)}, u32[]{:S(2)}, u32[]{:S(2)}) collective-permute-start(bf16[256,512]{1,0:T(8,128)(2,1)} %refs_9_.1), channel_id=1, source_target_pairs={{0,2},{2,0},{4,6},{6,4},{8,10},{10,8},{12,14},{14,12},{1,3},{3,1},... | collective-permute-start | bytes 786440 | tf_op jit(solution)/shard_map/ppermute | solution.py:238
  12.5 22.3 %collective-permute-start.3 = (bf16[256,512]{1,0:T(8,128)(2,1)}, bf16[256,512]{1,0:T(8,128)(2,1)S(1)}, u32[]{:S(2)}, u32[]{:S(2)}) collective-permute-start(bf16[256,512]{1,0:T(8,128)(2,1)} %refs_9_.1), channel_id=1, source_target_pairs={{0,1},{1,0},{2,3},{3,2},{4,5},{5,4},{6,7},{7,6},{8,9},{9,8},{10,11... | collective-permute-start | bytes 786440 | tf_op jit(solution)/shard_map/ppermute | solution.py:245
  12.5 1.2 %copy-start = (s32[3584,64]{0,1:T(8,128)S(1)}, s32[3584,64]{0,1:T(8,128)}, u32[]{:S(2)}) copy-start(s32[3584,64]{0,1:T(8,128)} %param.8) | copy-start | bytes 2752516
  13.6 53.9 %copy-start.2 = (bf16[256,512]{1,0:T(8,128)(2,1)S(1)}, bf16[256,512]{1,0:T(8,128)(2,1)}, u32[]{:S(2)}) copy-start(bf16[256,512]{1,0:T(8,128)(2,1)} %refs_9_.1) | copy-start | bytes 786436
  13.6 53.9 %copy-start.3 = (s32[1,8192]{1,0:T(1,128)S(1)}, s32[1,8192]{1,0:T(1,128)}, u32[]{:S(2)}) copy-start(s32[1,8192]{1,0:T(1,128)} %refs_8_.1) | copy-start | bytes 98308
  28.7 22.1 %collective-permute-start = (bf16[4,16,2560]{2,1,0:T(8,128)(2,1)S(1)}, bf16[4,16,2560]{2,1,0:T(8,128)(2,1)S(1)}, u32[]{:S(2)}, u32[]{:S(2)}) collective-permute-start(bf16[4,16,2560]{2,1,0:T(8,128)(2,1)S(1)} %get-tuple-element.16), channel_id=1, source_target_pairs={{0,2},{2,0},{4,6},{6,4},{8,10},{10,8},{12,14},{14,12},{1,3},{3,1},... | collective-permute-start | bytes 983048 | tf_op jit(solution)/shard_map/ppermute | solution.py:238
  30.8 25.9 %collective-permute-start.14 = (bf16[256,512]{1,0:T(8,128)(2,1)S(1)}, bf16[256,512]{1,0:T(8,128)(2,1)S(1)}, u32[]{:S(2)}, u32[]{:S(2)}) collective-permute-start(bf16[256,512]{1,0:T(8,128)(2,1)S(1)} %collective-permute-done.2.refs_1_.refs_10_), channel_id=1, source_target_pairs={{0,1},{1,0},{2,3},{3,2},{4,5},{5,4},{6,7},{7,6},{8,9},{9,8},{10,11... | collective-permute-start | bytes 786440 | tf_op jit(solution)/shard_map/ppermute | solution.py:245
  31.1 14.7 %collective-permute-start.10 = (bf16[64,1024]{1,0:T(8,128)(2,1)S(1)}, bf16[64,1024]{1,0:T(8,128)(2,1)S(1)}, u32[]{:S(2)}, u32[]{:S(2)}) collective-permute-start(bf16[64,1024]{1,0:T(8,128)(2,1)S(1)} %get-tuple-element.26), channel_id=1, source_target_pairs={{0,12},{2,14},{4,8},{6,10},{8,4},{10,6},{12,0},{14,2},{1,13},{3,15... | collective-permute-start | bytes 393224 | tf_op jit(solution)/shard_map/ppermute | solution.py:238
  34.7 11.8 %collective-permute-start.8 = (bf16[64,1024]{1,0:T(8,128)(2,1)S(1)}, bf16[64,1024]{1,0:T(8,128)(2,1)S(1)}, u32[]{:S(2)}, u32[]{:S(2)}) collective-permute-start(bf16[64,1024]{1,0:T(8,128)(2,1)S(1)} %get-tuple-element.27.refs_0_), channel_id=1, source_target_pairs={{0,4},{2,6},{4,0},{6,2},{8,12},{10,14},{12,8},{14,10},{1,5},{3,7},... | collective-permute-start | bytes 393224 | tf_op jit(solution)/shard_map/ppermute | solution.py:238
  34.8 11.7 %collective-permute-start.9 = (bf16[64,1024]{1,0:T(8,128)(2,1)S(1)}, bf16[64,1024]{1,0:T(8,128)(2,1)S(1)}, u32[]{:S(2)}, u32[]{:S(2)}) collective-permute-start(bf16[64,1024]{1,0:T(8,128)(2,1)S(1)} %get-tuple-element.25), channel_id=1, source_target_pairs={{0,8},{2,10},{4,12},{6,14},{8,0},{10,2},{12,4},{14,6},{1,9},{3,11}... | collective-permute-start | bytes 393224 | tf_op jit(solution)/shard_map/ppermute | solution.py:238
  45.7 6.5 %collective-permute-start.4 = (bf16[4,16,1536]{2,1,0:T(8,128)(2,1)S(1)}, bf16[4,16,1536]{2,1,0:T(8,128)(2,1)S(1)}, u32[]{:S(2)}, u32[]{:S(2)}) collective-permute-start(bf16[4,16,1536]{2,1,0:T(8,128)(2,1)S(1)} %get-tuple-element.20), channel_id=1, source_target_pairs={{0,2},{2,0},{4,6},{6,4},{8,10},{10,8},{12,14},{14,12},{1,3},{3,1},... | collective-permute-start | bytes 589832 | tf_op jit(solution)/shard_map/ppermute | solution.py:238
  46.6 11.0 %collective-permute-start.12 = (bf16[64,1024]{1,0:T(8,128)(2,1)S(1)}, bf16[64,1024]{1,0:T(8,128)(2,1)S(1)}, u32[]{:S(2)}, u32[]{:S(2)}) collective-permute-start(bf16[64,1024]{1,0:T(8,128)(2,1)S(1)} %fusion.2.refs_4_), channel_id=1, source_target_pairs={{0,8},{2,10},{4,12},{6,14},{8,0},{10,2},{12,4},{14,6},{1,9},{3,11}... | collective-permute-start | bytes 393224 | tf_op jit(solution)/shard_map/ppermute | solution.py:238
  48.8 9.9 %collective-permute-start.11 = (bf16[64,1024]{1,0:T(8,128)(2,1)S(1)}, bf16[64,1024]{1,0:T(8,128)(2,1)S(1)}, u32[]{:S(2)}, u32[]{:S(2)}) collective-permute-start(bf16[64,1024]{1,0:T(8,128)(2,1)S(1)} %fusion.2.refs_4_), channel_id=1, source_target_pairs={{0,4},{2,6},{4,0},{6,2},{8,12},{10,14},{12,8},{14,10},{1,5},{3,7},... | collective-permute-start | bytes 393224 | tf_op jit(solution)/shard_map/ppermute | solution.py:238
  53.1 8.3 %collective-permute-start.5 = (bf16[16,4096]{1,0:T(8,128)(2,1)S(1)}, bf16[16,4096]{1,0:T(8,128)(2,1)S(1)}, u32[]{:S(2)}, u32[]{:S(2)}) collective-permute-start(bf16[16,4096]{1,0:T(8,128)(2,1)S(1)} %get-tuple-element.22), channel_id=1, source_target_pairs={{0,12},{2,14},{4,8},{6,10},{8,4},{10,6},{12,0},{14,2},{1,13},{3,15... | collective-permute-start | bytes 393224 | tf_op jit(solution)/shard_map/ppermute | solution.py:238
  56.6 10.1 %collective-permute-start.6 = (bf16[16,4096]{1,0:T(8,128)(2,1)S(1)}, bf16[16,4096]{1,0:T(8,128)(2,1)S(1)}, u32[]{:S(2)}, u32[]{:S(2)}) collective-permute-start(bf16[16,4096]{1,0:T(8,128)(2,1)S(1)} %get-tuple-element.23), channel_id=1, source_target_pairs={{0,8},{2,10},{4,12},{6,14},{8,0},{10,2},{12,4},{14,6},{1,9},{3,11}... | collective-permute-start | bytes 393224 | tf_op jit(solution)/shard_map/ppermute | solution.py:238
  56.6 10.1 %collective-permute-start.7 = (bf16[16,4096]{1,0:T(8,128)(2,1)S(1)}, bf16[16,4096]{1,0:T(8,128)(2,1)S(1)}, u32[]{:S(2)}, u32[]{:S(2)}) collective-permute-start(bf16[16,4096]{1,0:T(8,128)(2,1)S(1)} %get-tuple-element.24), channel_id=1, source_target_pairs={{0,4},{2,6},{4,0},{6,2},{8,12},{10,14},{12,8},{14,10},{1,5},{3,7},... | collective-permute-start | bytes 393224 | tf_op jit(solution)/shard_map/ppermute | solution.py:238
  57.5 10.0 %collective-permute-start.13 = (bf16[64,1024]{1,0:T(8,128)(2,1)S(1)}, bf16[64,1024]{1,0:T(8,128)(2,1)S(1)}, u32[]{:S(2)}, u32[]{:S(2)}) collective-permute-start(bf16[64,1024]{1,0:T(8,128)(2,1)S(1)} %collective-permute-done.12.refs_6_), channel_id=1, source_target_pairs={{0,4},{2,6},{4,0},{6,2},{8,12},{10,14},{12,8},{14,10},{1,5},{3,7},... | collective-permute-start | bytes 393224 | tf_op jit(solution)/shard_map/ppermute | solution.py:238
  73.7 5.0 %collective-permute-start.15 = (f32[64,512]{1,0:T(8,128)S(1)}, f32[64,512]{1,0:T(8,128)S(1)}, u32[]{:S(2)}, u32[]{:S(2)}) collective-permute-start(f32[64,512]{1,0:T(8,128)S(1)} %score.1), channel_id=1, source_target_pairs={{0,2},{2,0},{4,6},{6,4},{8,10},{10,8},{12,14},{14,12},{1,3},{3,1},... | collective-permute-start | bytes 393224 | tf_op jit(solution)/shard_map/ppermute | solution.py:238
  78.8 6.4 %collective-permute-start.16 = (bf16[64,512]{1,0:T(8,128)(2,1)S(1)}, bf16[64,512]{1,0:T(8,128)(2,1)S(1)}, u32[]{:S(2)}, u32[]{:S(2)}) collective-permute-start(bf16[64,512]{1,0:T(8,128)(2,1)S(1)} %add_convert_fusion.3), channel_id=1, source_target_pairs={{0,12},{2,14},{4,8},{6,10},{8,4},{10,6},{12,0},{14,2},{1,13},{3,15... | collective-permute-start | bytes 196616 | tf_op jit(solution)/shard_map/ppermute | solution.py:238
  82.1 5.2 %collective-permute-start.17 = (bf16[64,512]{1,0:T(8,128)(2,1)S(1)}, bf16[64,512]{1,0:T(8,128)(2,1)S(1)}, u32[]{:S(2)}, u32[]{:S(2)}) collective-permute-start(bf16[64,512]{1,0:T(8,128)(2,1)S(1)} %add_convert_fusion.3), channel_id=1, source_target_pairs={{0,8},{2,10},{4,12},{6,14},{8,0},{10,2},{12,4},{14,6},{1,9},{3,11}... | collective-permute-start | bytes 196616 | tf_op jit(solution)/shard_map/ppermute | solution.py:238
  82.1 5.2 %collective-permute-start.18 = (bf16[64,512]{1,0:T(8,128)(2,1)S(1)}, bf16[64,512]{1,0:T(8,128)(2,1)S(1)}, u32[]{:S(2)}, u32[]{:S(2)}) collective-permute-start(bf16[64,512]{1,0:T(8,128)(2,1)S(1)} %add_convert_fusion.3), channel_id=1, source_target_pairs={{0,4},{2,6},{4,0},{6,2},{8,12},{10,14},{12,8},{14,10},{1,5},{3,7},... | collective-permute-start | bytes 196616 | tf_op jit(solution)/shard_map/ppermute | solution.py:238

commit v17 on v15

--- a/solution.py
+++ b/solution.py
@@ -11,7 +11,7 @@
 FF = 28672
 R = 64
 SEQ_DEV = 64
-BUFFERS = 4
+BUFFERS = 6
 VMEM = 48 * 1024 * 1024
 LAST = (((1,), (1,)), ((), ()))
 

time: 87.2 us -> 87.2 us (level)
  no operation moved by 1% of the time
where the time goes in v17:
time: 87.2 us; the launch traced here: 87 us
  Pallas kernels  39.7 us (46%)
  starting transfers between devices  26 us (30%)
  waiting for transfers between devices  18.3 us (21%)
  local copies, waits for them, and re-layouts  2.14 us (2%)
  other arithmetic  0.95 us (1%)
    pallas_call x3, Pallas kernels, project(): pl.pallas_call(functools.partial(project_kernel, scale, order, first, spl...  33.6 us
    ppermute x17, starting transfers between devices, swap(): lax.ppermute(array, 'tensor', [(k, k ^ distance) for k in range(n_tensor)])  25.7 us
    ppermute x17, waiting for transfers between devices, swap(): lax.ppermute(array, 'tensor', [(k, k ^ distance) for k in range(n_tensor)])  18.2 us
    pallas_call x1, Pallas kernels, score(): pl.pallas_call(functools.partial(score_kernel, len(left), min(512, tokens...  5.19 us
    unnamed x8, local copies, waits for them, and re-layouts  2.14 us
  transfers between devices with their start and end apart: 19, of which 7 were waited for; matrix products, arithmetic and copies ran while one was open for 0% of the time, Pallas kernels for 30%

profile of v17, /device:TPU:0, one launch (start us, length us, event | category | flops | bytes accessed | tf_op | source)
XLA Modules:
  0.0 87.0 jit_solution(11265923880130894049)
XLA Ops:
  0.1 0.9 %copy-done.1 = s32[1024,64]{0,1:T(8,128)S(1)} copy-done((s32[1024,64]{0,1:T(8,128)S(1)}, s32[1024,64]{0,1:T(8,128)}, u32[]{:S(2)}) %copy-start.1) | copy-done | bytes 262168
  1.0 8.3 %project.4 = (bf16[4,64,1024]{2,1,0:T(8,128)(2,1)S(1)}, f32[4,64,1024]{2,1,0:T(8,128)S(1)}) custom-call(s32[3]{0:T(128)S(1)} %pad_add_fusion.who_ref, bf16[8192,1024]{1,0:T(8,128)(2,1)} %x_hbm.4, s32[64,1024]{1,0:T(8,128)S(1)} %bitcast.21), custom_call_target="tpu_custom_call" | custom-call | flops 1073741824 | bytes 16777216 | tf_op jit(solution)/shard_map/project/pallas_call | solution.py:85
  9.3 3.0 %collective-permute-start.1 = (bf16[4,64,1024]{2,1,0:T(8,128)(2,1)S(1)}, bf16[4,64,1024]{2,1,0:T(8,128)(2,1)S(1)}, u32[]{:S(2)}, u32[]{:S(2)}) collective-permute-start(bf16[4,64,1024]{2,1,0:T(8,128)(2,1)S(1)} %get-tuple-element.18), channel_id=1, source_target_pairs={{0,2},{2,0},{4,6},{6,4},{8,10},{10,8},{12,14},{14,12},{1,3},{3,1},... | collective-permute-start | bytes 1572872 | tf_op jit(solution)/shard_map/ppermute | solution.py:226
  12.4 0.1 collective-permute-start.2
  12.5 1.2 %copy-done = s32[3584,64]{0,1:T(8,128)S(1)} copy-done((s32[3584,64]{0,1:T(8,128)S(1)}, s32[3584,64]{0,1:T(8,128)}, u32[]{:S(2)}) %copy-start) | copy-done | bytes 917528
  13.6 15.1 %project.3 = (bf16[4,16,2560]{2,1,0:T(8,128)(2,1)S(1)}, f32[4,16,2560]{2,1,0:T(8,128)S(1)}) custom-call(s32[3]{0:T(128)S(1)} %pad_add_fusion.who_ref, bf16[8192,3584]{1,0:T(8,128)(2,1)} %x_hbm.5, s32[64,3584]{1,0:T(8,128)S(1)} %bitcast.19), custom_call_target="tpu_custom_call" | custom-call | flops 2348810240 | bytes 36700160 | tf_op jit(solution)/shard_map/project/pallas_call | solution.py:85
  28.7 2.0 %collective-permute-start = (bf16[4,16,2560]{2,1,0:T(8,128)(2,1)S(1)}, bf16[4,16,2560]{2,1,0:T(8,128)(2,1)S(1)}, u32[]{:S(2)}, u32[]{:S(2)}) collective-permute-start(bf16[4,16,2560]{2,1,0:T(8,128)(2,1)S(1)} %get-tuple-element.16), channel_id=1, source_target_pairs={{0,2},{2,0},{4,6},{6,4},{8,10},{10,8},{12,14},{14,12},{1,3},{3,1},... | collective-permute-start | bytes 983048 | tf_op jit(solution)/shard_map/ppermute | solution.py:226
  30.8 0.2 collective-permute-start.14
  31.0 0.1 fusion.4
  31.1 3.7 %collective-permute-start.10 = (bf16[64,1024]{1,0:T(8,128)(2,1)S(1)}, bf16[64,1024]{1,0:T(8,128)(2,1)S(1)}, u32[]{:S(2)}, u32[]{:S(2)}) collective-permute-start(bf16[64,1024]{1,0:T(8,128)(2,1)S(1)} %get-tuple-element.26), channel_id=1, source_target_pairs={{0,12},{2,14},{4,8},{6,10},{8,4},{10,6},{12,0},{14,2},{1,13},{3,15... | collective-permute-start | bytes 393224 | tf_op jit(solution)/shard_map/ppermute | solution.py:226
  34.8 0.8 collective-permute-start.9
  35.6 10.2 %project.5 = (bf16[4,16,1536]{2,1,0:T(8,128)(2,1)S(1)}, f32[4,16,1536]{2,1,0:T(8,128)S(1)}) custom-call(s32[3]{0:T(128)S(1)} %pad_add_fusion.who_ref, bf16[8192,3584]{1,0:T(8,128)(2,1)} %x_hbm.5, s32[64,3584]{1,0:T(8,128)S(1)} %bitcast.20, bf16[64,1024]{1,0:T(8,128)(2,1)S(1)} %get-tuple-element.27.refs_0_, ...), custom_call_target="tpu_custom_call" | custom-call | flops 1409286144 | bytes 22020096 | tf_op jit(solution)/shard_map/project/pallas_call | solution.py:85
  45.8 0.7 collective-permute-start.4
  46.5 0.1 fusion.2.refs_4_
  46.6 2.2 %collective-permute-start.12 = (bf16[64,1024]{1,0:T(8,128)(2,1)S(1)}, bf16[64,1024]{1,0:T(8,128)(2,1)S(1)}, u32[]{:S(2)}, u32[]{:S(2)}) collective-permute-start(bf16[64,1024]{1,0:T(8,128)(2,1)S(1)} %fusion.2.refs_4_), channel_id=1, source_target_pairs={{0,8},{2,10},{4,12},{6,14},{8,0},{10,2},{12,4},{14,6},{1,9},{3,11}... | collective-permute-start | bytes 393224 | tf_op jit(solution)/shard_map/ppermute | solution.py:226
  48.8 2.0 %collective-permute-start.11 = (bf16[64,1024]{1,0:T(8,128)(2,1)S(1)}, bf16[64,1024]{1,0:T(8,128)(2,1)S(1)}, u32[]{:S(2)}, u32[]{:S(2)}) collective-permute-start(bf16[64,1024]{1,0:T(8,128)(2,1)S(1)} %fusion.2.refs_4_), channel_id=1, source_target_pairs={{0,4},{2,6},{4,0},{6,2},{8,12},{10,14},{12,8},{14,10},{1,5},{3,7},... | collective-permute-start | bytes 393224 | tf_op jit(solution)/shard_map/ppermute | solution.py:226
  50.8 1.4 %collective-permute-done.4.refs_3_ = bf16[4,16,1536]{2,1,0:T(8,128)(2,1)S(1)} collective-permute-done((bf16[4,16,1536]{2,1,0:T(8,128)(2,1)S(1)}, bf16[4,16,1536]{2,1,0:T(8,128)(2,1)S(1)}, u32[]{:S(2)}, u32[]{:S(2)}) %collective-permute-start.4) | collective-permute-done | bytes 196640 | tf_op jit(solution)/shard_map/ppermute | solution.py:226
  52.2 0.9 %merge.1 = (f32[16,4096]{1,0:T(8,128)S(1)}, bf16[16,4096]{1,0:T(8,128)(2,1)S(1)}, bf16[16,4096]{1,0:T(8,128)(2,1)S(1)}, bf16[16,4096]{1,0:T(8,128)(2,1)S(1)}) custom-call(f32[4,16,2560]{2,1,0:T(8,128)S(1)} %get-tuple-element.15.refs_0_, bf16[4,16,2560]{2,1,0:T(8,128)(2,1)S(1)} %collective-permute-done.refs_1_, f32[4,16,1536]{2,1,0:T(8,128)S(1)} %get-tuple-element.19.refs_2_, ...), custom_call_target="tpu_custom_call" | custom-call | flops 262144 | bytes 2097152 | tf_op jit(solution)/shard_map/merge/pallas_call | solution.py:129
  53.1 3.5 %collective-permute-start.5 = (bf16[16,4096]{1,0:T(8,128)(2,1)S(1)}, bf16[16,4096]{1,0:T(8,128)(2,1)S(1)}, u32[]{:S(2)}, u32[]{:S(2)}) collective-permute-start(bf16[16,4096]{1,0:T(8,128)(2,1)S(1)} %get-tuple-element.22), channel_id=1, source_target_pairs={{0,12},{2,14},{4,8},{6,10},{8,4},{10,6},{12,0},{14,2},{1,13},{3,15... | collective-permute-start | bytes 393224 | tf_op jit(solution)/shard_map/ppermute | solution.py:226
  56.6 0.9 %collective-permute-start.7 = (bf16[16,4096]{1,0:T(8,128)(2,1)S(1)}, bf16[16,4096]{1,0:T(8,128)(2,1)S(1)}, u32[]{:S(2)}, u32[]{:S(2)}) collective-permute-start(bf16[16,4096]{1,0:T(8,128)(2,1)S(1)} %get-tuple-element.24), channel_id=1, source_target_pairs={{0,4},{2,6},{4,0},{6,2},{8,12},{10,14},{12,8},{14,10},{1,5},{3,7},... | collective-permute-start | bytes 393224 | tf_op jit(solution)/shard_map/ppermute | solution.py:226
  57.5 1.1 %collective-permute-start.13 = (bf16[64,1024]{1,0:T(8,128)(2,1)S(1)}, bf16[64,1024]{1,0:T(8,128)(2,1)S(1)}, u32[]{:S(2)}, u32[]{:S(2)}) collective-permute-start(bf16[64,1024]{1,0:T(8,128)(2,1)S(1)} %collective-permute-done.12.refs_6_), channel_id=1, source_target_pairs={{0,4},{2,6},{4,0},{6,2},{8,12},{10,14},{12,8},{14,10},{1,5},{3,7},... | collective-permute-start | bytes 393224 | tf_op jit(solution)/shard_map/ppermute | solution.py:226
  58.7 2.7 %collective-permute-done.5.refs_1_ = bf16[16,4096]{1,0:T(8,128)(2,1)S(1)} collective-permute-done((bf16[16,4096]{1,0:T(8,128)(2,1)S(1)}, bf16[16,4096]{1,0:T(8,128)(2,1)S(1)}, u32[]{:S(2)}, u32[]{:S(2)}) %collective-permute-start.5) | collective-permute-done | bytes 131104 | tf_op jit(solution)/shard_map/ppermute | solution.py:226
  61.4 5.3 %collective-permute-done.6.refs_2_ = bf16[16,4096]{1,0:T(8,128)(2,1)S(1)} collective-permute-done((bf16[16,4096]{1,0:T(8,128)(2,1)S(1)}, bf16[16,4096]{1,0:T(8,128)(2,1)S(1)}, u32[]{:S(2)}, u32[]{:S(2)}) %collective-permute-start.6) | collective-permute-done | bytes 131104 | tf_op jit(solution)/shard_map/ppermute | solution.py:226
  66.7 0.8 collective-permute-done.13.refs_7_
  67.6 5.2 %score.1 = f32[64,512]{1,0:T(8,128)S(1)} custom-call(s32[3]{0:T(128)S(1)} %pad_add_fusion.who_ref, f32[16,4096]{1,0:T(8,128)S(1)} %get-tuple-element.21.refs_0_, bf16[16,4096]{1,0:T(8,128)(2,1)S(1)} %collective-permute-done.5.refs_1_, bf16[16,4096]{1,0:T(8,128)(2,1)S(1)} %collective-permute-done.6.refs_2_, ...), custom_call_target="tpu_custom_call" | custom-call | flops 536870912 | bytes 262144 | tf_op jit(solution)/shard_map/score/pallas_call | solution.py:196
  72.7 1.2 %collective-permute-start.15 = (f32[64,512]{1,0:T(8,128)S(1)}, f32[64,512]{1,0:T(8,128)S(1)}, u32[]{:S(2)}, u32[]{:S(2)}) collective-permute-start(f32[64,512]{1,0:T(8,128)S(1)} %score.1), channel_id=1, source_target_pairs={{0,2},{2,0},{4,6},{6,4},{8,10},{10,8},{12,14},{14,12},{1,3},{3,1},... | collective-permute-start | bytes 393224 | tf_op jit(solution)/shard_map/ppermute | solution.py:226
  73.9 3.8 %collective-permute-done.15 = f32[64,512]{1,0:T(8,128)S(1)} collective-permute-done((f32[64,512]{1,0:T(8,128)S(1)}, f32[64,512]{1,0:T(8,128)S(1)}, u32[]{:S(2)}, u32[]{:S(2)}) %collective-permute-start.15) | collective-permute-done | bytes 131104 | tf_op jit(solution)/shard_map/ppermute | solution.py:226
  77.8 3.4 %collective-permute-start.16 = (bf16[64,512]{1,0:T(8,128)(2,1)S(1)}, bf16[64,512]{1,0:T(8,128)(2,1)S(1)}, u32[]{:S(2)}, u32[]{:S(2)}) collective-permute-start(bf16[64,512]{1,0:T(8,128)(2,1)S(1)} %add_convert_fusion.3), channel_id=1, source_target_pairs={{0,12},{2,14},{4,8},{6,10},{8,4},{10,6},{12,0},{14,2},{1,13},{3,15... | collective-permute-start | bytes 196616 | tf_op jit(solution)/shard_map/ppermute | solution.py:226
  81.2 1.1 %collective-permute-start.18 = (bf16[64,512]{1,0:T(8,128)(2,1)S(1)}, bf16[64,512]{1,0:T(8,128)(2,1)S(1)}, u32[]{:S(2)}, u32[]{:S(2)}) collective-permute-start(bf16[64,512]{1,0:T(8,128)(2,1)S(1)} %add_convert_fusion.3), channel_id=1, source_target_pairs={{0,4},{2,6},{4,0},{6,2},{8,12},{10,14},{12,8},{14,10},{1,5},{3,7},... | collective-permute-start | bytes 196616 | tf_op jit(solution)/shard_map/ppermute | solution.py:226
  82.3 1.7 %collective-permute-done.16 = bf16[64,512]{1,0:T(8,128)(2,1)S(1)} collective-permute-done((bf16[64,512]{1,0:T(8,128)(2,1)S(1)}, bf16[64,512]{1,0:T(8,128)(2,1)S(1)}, u32[]{:S(2)}, u32[]{:S(2)}) %collective-permute-start.16) | collective-permute-done | bytes 65568 | tf_op jit(solution)/shard_map/ppermute | solution.py:226
  83.9 2.4 %collective-permute-done.17 = bf16[64,512]{1,0:T(8,128)(2,1)S(1)} collective-permute-done((bf16[64,512]{1,0:T(8,128)(2,1)S(1)}, bf16[64,512]{1,0:T(8,128)(2,1)S(1)}, u32[]{:S(2)}, u32[]{:S(2)}) %collective-permute-start.17) | collective-permute-done | bytes 65568 | tf_op jit(solution)/shard_map/ppermute | solution.py:226
  86.4 0.7 add_add_fusion
  (24 shorter events, 0.1 us)
Async XLA Ops:
  0.1 1.0 %copy-start.1 = (s32[1024,64]{0,1:T(8,128)S(1)}, s32[1024,64]{0,1:T(8,128)}, u32[]{:S(2)}) copy-start(s32[1024,64]{0,1:T(8,128)} %param.9) | copy-start | bytes 786436
  9.3 21.7 %collective-permute-start.1 = (bf16[4,64,1024]{2,1,0:T(8,128)(2,1)S(1)}, bf16[4,64,1024]{2,1,0:T(8,128)(2,1)S(1)}, u32[]{:S(2)}, u32[]{:S(2)}) collective-permute-start(bf16[4,64,1024]{2,1,0:T(8,128)(2,1)S(1)} %get-tuple-element.18), channel_id=1, source_target_pairs={{0,2},{2,0},{4,6},{6,4},{8,10},{10,8},{12,14},{14,12},{1,3},{3,1},... | collective-permute-start | bytes 1572872 | tf_op jit(solution)/shard_map/ppermute | solution.py:226
  12.4 18.4 %collective-permute-start.2 = (bf16[256,512]{1,0:T(8,128)(2,1)}, bf16[256,512]{1,0:T(8,128)(2,1)S(1)}, u32[]{:S(2)}, u32[]{:S(2)}) collective-permute-start(bf16[256,512]{1,0:T(8,128)(2,1)} %refs_9_.1), channel_id=1, source_target_pairs={{0,2},{2,0},{4,6},{6,4},{8,10},{10,8},{12,14},{14,12},{1,3},{3,1},... | collective-permute-start | bytes 786440 | tf_op jit(solution)/shard_map/ppermute | solution.py:226
  12.5 22.3 %collective-permute-start.3 = (bf16[256,512]{1,0:T(8,128)(2,1)}, bf16[256,512]{1,0:T(8,128)(2,1)S(1)}, u32[]{:S(2)}, u32[]{:S(2)}) collective-permute-start(bf16[256,512]{1,0:T(8,128)(2,1)} %refs_9_.1), channel_id=1, source_target_pairs={{0,1},{1,0},{2,3},{3,2},{4,5},{5,4},{6,7},{7,6},{8,9},{9,8},{10,11... | collective-permute-start | bytes 786440 | tf_op jit(solution)/shard_map/ppermute | solution.py:233
  12.5 1.2 %copy-start = (s32[3584,64]{0,1:T(8,128)S(1)}, s32[3584,64]{0,1:T(8,128)}, u32[]{:S(2)}) copy-start(s32[3584,64]{0,1:T(8,128)} %param.8) | copy-start | bytes 2752516
  13.6 53.9 %copy-start.2 = (bf16[256,512]{1,0:T(8,128)(2,1)S(1)}, bf16[256,512]{1,0:T(8,128)(2,1)}, u32[]{:S(2)}) copy-start(bf16[256,512]{1,0:T(8,128)(2,1)} %refs_9_.1) | copy-start | bytes 786436
  13.6 53.9 %copy-start.3 = (s32[1,8192]{1,0:T(1,128)S(1)}, s32[1,8192]{1,0:T(1,128)}, u32[]{:S(2)}) copy-start(s32[1,8192]{1,0:T(1,128)} %refs_8_.1) | copy-start | bytes 98308
  28.7 22.1 %collective-permute-start = (bf16[4,16,2560]{2,1,0:T(8,128)(2,1)S(1)}, bf16[4,16,2560]{2,1,0:T(8,128)(2,1)S(1)}, u32[]{:S(2)}, u32[]{:S(2)}) collective-permute-start(bf16[4,16,2560]{2,1,0:T(8,128)(2,1)S(1)} %get-tuple-element.16), channel_id=1, source_target_pairs={{0,2},{2,0},{4,6},{6,4},{8,10},{10,8},{12,14},{14,12},{1,3},{3,1},... | collective-permute-start | bytes 983048 | tf_op jit(solution)/shard_map/ppermute | solution.py:226
  30.8 25.9 %collective-permute-start.14 = (bf16[256,512]{1,0:T(8,128)(2,1)S(1)}, bf16[256,512]{1,0:T(8,128)(2,1)S(1)}, u32[]{:S(2)}, u32[]{:S(2)}) collective-permute-start(bf16[256,512]{1,0:T(8,128)(2,1)S(1)} %collective-permute-done.2.refs_1_.refs_10_), channel_id=1, source_target_pairs={{0,1},{1,0},{2,3},{3,2},{4,5},{5,4},{6,7},{7,6},{8,9},{9,8},{10,11... | collective-permute-start | bytes 786440 | tf_op jit(solution)/shard_map/ppermute | solution.py:233
  31.1 14.7 %collective-permute-start.10 = (bf16[64,1024]{1,0:T(8,128)(2,1)S(1)}, bf16[64,1024]{1,0:T(8,128)(2,1)S(1)}, u32[]{:S(2)}, u32[]{:S(2)}) collective-permute-start(bf16[64,1024]{1,0:T(8,128)(2,1)S(1)} %get-tuple-element.26), channel_id=1, source_target_pairs={{0,12},{2,14},{4,8},{6,10},{8,4},{10,6},{12,0},{14,2},{1,13},{3,15... | collective-permute-start | bytes 393224 | tf_op jit(solution)/shard_map/ppermute | solution.py:226
  34.8 11.7 %collective-permute-start.8 = (bf16[64,1024]{1,0:T(8,128)(2,1)S(1)}, bf16[64,1024]{1,0:T(8,128)(2,1)S(1)}, u32[]{:S(2)}, u32[]{:S(2)}) collective-permute-start(bf16[64,1024]{1,0:T(8,128)(2,1)S(1)} %get-tuple-element.27.refs_0_), channel_id=1, source_target_pairs={{0,4},{2,6},{4,0},{6,2},{8,12},{10,14},{12,8},{14,10},{1,5},{3,7},... | collective-permute-start | bytes 393224 | tf_op jit(solution)/shard_map/ppermute | solution.py:226
  34.8 11.7 %collective-permute-start.9 = (bf16[64,1024]{1,0:T(8,128)(2,1)S(1)}, bf16[64,1024]{1,0:T(8,128)(2,1)S(1)}, u32[]{:S(2)}, u32[]{:S(2)}) collective-permute-start(bf16[64,1024]{1,0:T(8,128)(2,1)S(1)} %get-tuple-element.25), channel_id=1, source_target_pairs={{0,8},{2,10},{4,12},{6,14},{8,0},{10,2},{12,4},{14,6},{1,9},{3,11}... | collective-permute-start | bytes 393224 | tf_op jit(solution)/shard_map/ppermute | solution.py:226
  45.8 6.4 %collective-permute-start.4 = (bf16[4,16,1536]{2,1,0:T(8,128)(2,1)S(1)}, bf16[4,16,1536]{2,1,0:T(8,128)(2,1)S(1)}, u32[]{:S(2)}, u32[]{:S(2)}) collective-permute-start(bf16[4,16,1536]{2,1,0:T(8,128)(2,1)S(1)} %get-tuple-element.20), channel_id=1, source_target_pairs={{0,2},{2,0},{4,6},{6,4},{8,10},{10,8},{12,14},{14,12},{1,3},{3,1},... | collective-permute-start | bytes 589832 | tf_op jit(solution)/shard_map/ppermute | solution.py:226
  46.6 11.0 %collective-permute-start.12 = (bf16[64,1024]{1,0:T(8,128)(2,1)S(1)}, bf16[64,1024]{1,0:T(8,128)(2,1)S(1)}, u32[]{:S(2)}, u32[]{:S(2)}) collective-permute-start(bf16[64,1024]{1,0:T(8,128)(2,1)S(1)} %fusion.2.refs_4_), channel_id=1, source_target_pairs={{0,8},{2,10},{4,12},{6,14},{8,0},{10,2},{12,4},{14,6},{1,9},{3,11}... | collective-permute-start | bytes 393224 | tf_op jit(solution)/shard_map/ppermute | solution.py:226
  48.8 9.9 %collective-permute-start.11 = (bf16[64,1024]{1,0:T(8,128)(2,1)S(1)}, bf16[64,1024]{1,0:T(8,128)(2,1)S(1)}, u32[]{:S(2)}, u32[]{:S(2)}) collective-permute-start(bf16[64,1024]{1,0:T(8,128)(2,1)S(1)} %fusion.2.refs_4_), channel_id=1, source_target_pairs={{0,4},{2,6},{4,0},{6,2},{8,12},{10,14},{12,8},{14,10},{1,5},{3,7},... | collective-permute-start | bytes 393224 | tf_op jit(solution)/shard_map/ppermute | solution.py:226
  53.1 8.3 %collective-permute-start.5 = (bf16[16,4096]{1,0:T(8,128)(2,1)S(1)}, bf16[16,4096]{1,0:T(8,128)(2,1)S(1)}, u32[]{:S(2)}, u32[]{:S(2)}) collective-permute-start(bf16[16,4096]{1,0:T(8,128)(2,1)S(1)} %get-tuple-element.22), channel_id=1, source_target_pairs={{0,12},{2,14},{4,8},{6,10},{8,4},{10,6},{12,0},{14,2},{1,13},{3,15... | collective-permute-start | bytes 393224 | tf_op jit(solution)/shard_map/ppermute | solution.py:226
  56.6 10.1 %collective-permute-start.6 = (bf16[16,4096]{1,0:T(8,128)(2,1)S(1)}, bf16[16,4096]{1,0:T(8,128)(2,1)S(1)}, u32[]{:S(2)}, u32[]{:S(2)}) collective-permute-start(bf16[16,4096]{1,0:T(8,128)(2,1)S(1)} %get-tuple-element.23), channel_id=1, source_target_pairs={{0,8},{2,10},{4,12},{6,14},{8,0},{10,2},{12,4},{14,6},{1,9},{3,11}... | collective-permute-start | bytes 393224 | tf_op jit(solution)/shard_map/ppermute | solution.py:226
  56.6 10.1 %collective-permute-start.7 = (bf16[16,4096]{1,0:T(8,128)(2,1)S(1)}, bf16[16,4096]{1,0:T(8,128)(2,1)S(1)}, u32[]{:S(2)}, u32[]{:S(2)}) collective-permute-start(bf16[16,4096]{1,0:T(8,128)(2,1)S(1)} %get-tuple-element.24), channel_id=1, source_target_pairs={{0,4},{2,6},{4,0},{6,2},{8,12},{10,14},{12,8},{14,10},{1,5},{3,7},... | collective-permute-start | bytes 393224 | tf_op jit(solution)/shard_map/ppermute | solution.py:226
  57.5 10.0 %collective-permute-start.13 = (bf16[64,1024]{1,0:T(8,128)(2,1)S(1)}, bf16[64,1024]{1,0:T(8,128)(2,1)S(1)}, u32[]{:S(2)}, u32[]{:S(2)}) collective-permute-start(bf16[64,1024]{1,0:T(8,128)(2,1)S(1)} %collective-permute-done.12.refs_6_), channel_id=1, source_target_pairs={{0,4},{2,6},{4,0},{6,2},{8,12},{10,14},{12,8},{14,10},{1,5},{3,7},... | collective-permute-start | bytes 393224 | tf_op jit(solution)/shard_map/ppermute | solution.py:226
  72.7 5.0 %collective-permute-start.15 = (f32[64,512]{1,0:T(8,128)S(1)}, f32[64,512]{1,0:T(8,128)S(1)}, u32[]{:S(2)}, u32[]{:S(2)}) collective-permute-start(f32[64,512]{1,0:T(8,128)S(1)} %score.1), channel_id=1, source_target_pairs={{0,2},{2,0},{4,6},{6,4},{8,10},{10,8},{12,14},{14,12},{1,3},{3,1},... | collective-permute-start | bytes 393224 | tf_op jit(solution)/shard_map/ppermute | solution.py:226
  77.8 6.1 %collective-permute-start.16 = (bf16[64,512]{1,0:T(8,128)(2,1)S(1)}, bf16[64,512]{1,0:T(8,128)(2,1)S(1)}, u32[]{:S(2)}, u32[]{:S(2)}) collective-permute-start(bf16[64,512]{1,0:T(8,128)(2,1)S(1)} %add_convert_fusion.3), channel_id=1, source_target_pairs={{0,12},{2,14},{4,8},{6,10},{8,4},{10,6},{12,0},{14,2},{1,13},{3,15... | collective-permute-start | bytes 196616 | tf_op jit(solution)/shard_map/ppermute | solution.py:226
  81.2 5.2 %collective-permute-start.17 = (bf16[64,512]{1,0:T(8,128)(2,1)S(1)}, bf16[64,512]{1,0:T(8,128)(2,1)S(1)}, u32[]{:S(2)}, u32[]{:S(2)}) collective-permute-start(bf16[64,512]{1,0:T(8,128)(2,1)S(1)} %add_convert_fusion.3), channel_id=1, source_target_pairs={{0,8},{2,10},{4,12},{6,14},{8,0},{10,2},{12,4},{14,6},{1,9},{3,11}... | collective-permute-start | bytes 196616 | tf_op jit(solution)/shard_map/ppermute | solution.py:226
  81.2 5.2 %collective-permute-start.18 = (bf16[64,512]{1,0:T(8,128)(2,1)S(1)}, bf16[64,512]{1,0:T(8,128)(2,1)S(1)}, u32[]{:S(2)}, u32[]{:S(2)}) collective-permute-start(bf16[64,512]{1,0:T(8,128)(2,1)S(1)} %add_convert_fusion.3), channel_id=1, source_target_pairs={{0,4},{2,6},{4,0},{6,2},{8,12},{10,14},{12,8},{14,10},{1,5},{3,7},... | collective-permute-start | bytes 196616 | tf_op jit(solution)/shard_map/ppermute | solution.py:226
